TPU v7x, 32 devices: a whole 2x2x4 slice. The times are simulated.
32 devices in a mesh: section: 4 (over x, core), tp: 2 (over y), doc: 4 (over z).
Axes of the slice: x: 2, y: 2, z: 4, core: 2. Of those that a mesh axis runs over, the one named last changes fastest.
Arguments:
- token_ids: int32 [8, 2, 32], P('doc'), may hold values from 0 to 16383
- seg_lengths: int32 [8, 2], P('doc'), may hold values from 1 to 32
- emb_table: bfloat16 [16384, 4096], P('section', 'tp'), may hold values from -6 to 6
- mem_init: bfloat16 [16, 4096], P(None, 'tp'), may hold values from -6 to 6
- norm_gain: float32 [4, 4096], P('section'), may hold values from 0.1 to 1.9
- w_query: bfloat16 [4, 4096, 2048], P('section', 'doc', 'tp'), may hold values from -0.09375 to 0.09375
- w_key: bfloat16 [4, 4096, 2048], P('section', 'doc', 'tp'), may hold values from -0.09375 to 0.09375
- w_value: bfloat16 [4, 4096, 2048], P('section', 'doc', 'tp'), may hold values from -0.09375 to 0.09375
- w_out: bfloat16 [4, 2048, 4096], P('section', None, 'tp'), may hold values from -0.125 to 0.125
- layer_mix: float32 [4], P('section'), may hold values from 0.5 to 4.5
Outputs:
- pooled: float32 [8, 4096], P(None, 'tp')
All inputs are finite; a program needn't handle non-finite values.
Results may differ from a plain program's by a relative error of at most 0.013.
Values may be sent and summed in bfloat16 or wider, within the bound.
No kernel may reach another device: no remote copies, remote signals or barrier semaphores. Data moves between devices by JAX's collectives and lax.ppermute only.
A program may use at most 192 MiB of HBM per device.

v0:
```python
import math

import jax
import jax.numpy as jnp
from jax import lax
from jax.sharding import PartitionSpec as P

HD = 128
M = 16
L = 32
SEGS = 2


EPSILON = 1e-05
NEGATIVE = -1e30


def from_behind(block, axis, distance):
    devices = range(lax.axis_size(axis))
    route = [((i - distance) % len(devices), i) for i in devices]
    return lax.ppermute(block, axis, route)


def visible_rows(row_count, length):
    position = jnp.arange(row_count)
    key_ok = (position < M) | (position - M < length)
    ordered = (
        (position[None, :] < M) | (position[:, None] < M) | (position[None, :] <= position[:, None])
    )
    return key_ok[None, :] & ordered


def attend(features, length, query_proj, key_proj, value_proj, norm_row):
    row_count = features.shape[0]
    local_heads = query_proj.shape[1] // HD
    floats = features.astype(jnp.float32)
    mean_square = jnp.mean(floats * floats, -1, keepdims=True)
    normed = (floats * lax.rsqrt(mean_square + EPSILON) * norm_row).astype(jnp.bfloat16)
    head_shape = (row_count, local_heads, HD)
    queries = (
        jnp.dot(normed, query_proj, preferred_element_type=jnp.float32)
        .astype(jnp.bfloat16)
        .reshape(head_shape)
    )
    keys = (
        jnp.dot(normed, key_proj, preferred_element_type=jnp.float32)
        .astype(jnp.bfloat16)
        .reshape(head_shape)
    )
    values = (
        jnp.dot(normed, value_proj, preferred_element_type=jnp.float32)
        .astype(jnp.bfloat16)
        .reshape(head_shape)
    )
    scores = jnp.einsum("qhe,khe->hqk", queries, keys, preferred_element_type=jnp.float32) * (
        1.0 / math.sqrt(HD)
    )
    allowed = visible_rows(row_count, length)[None]
    scores = jnp.where(allowed, scores, NEGATIVE)
    weights = jnp.where(allowed, jnp.exp(scores), 0.0)
    probs = (weights / jnp.sum(weights, -1, keepdims=True)).astype(jnp.bfloat16)
    mixed = jnp.einsum("hqk,khe->qhe", probs, values, preferred_element_type=jnp.float32).astype(
        jnp.bfloat16
    )
    return mixed.reshape(row_count, local_heads * HD)


def body(
    token_ids,
    seg_lengths,
    emb_table,
    mem_init,
    norm_gain,
    w_query,
    w_key,
    w_value,
    w_out,
    layer_mix,
):
    phases = lax.axis_size("section")
    phase_index = lax.axis_index("section")
    doc_local = token_ids.shape[0]
    vocab_rows = emb_table.shape[0]
    width_local = emb_table.shape[1]
    flat_ids = token_ids.reshape(-1)
    local_ids = flat_ids - phase_index * vocab_rows
    owned = (local_ids >= 0) & (local_ids < vocab_rows)
    picked_rows = jnp.take(emb_table, jnp.clip(local_ids, 0, vocab_rows - 1), axis=0)
    partial_rows = jnp.where(owned[:, None], picked_rows.astype(jnp.float32), 0.0)
    embedded = lax.psum(partial_rows.astype(jnp.bfloat16), "section")
    embedded = embedded.reshape(doc_local * SEGS, L, width_local)
    query_proj, key_proj, value_proj = (
        lax.all_gather(w_query[0], "doc", axis=0, tiled=True),
        lax.all_gather(w_key[0], "doc", axis=0, tiled=True),
        lax.all_gather(w_value[0], "doc", axis=0, tiled=True),
    )
    out_proj = w_out[0]
    norm_row = norm_gain[0]
    mixing = layer_mix[0]
    row_count = M + L
    head_cols = query_proj.shape[1]
    total_turns = (SEGS - 1) * phases + doc_local + phases - 1

    def turn(turn_index, carried):
        incoming, returned, pooled = carried
        offset = turn_index - phase_index
        segment = offset // phases
        document = offset % phases
        active = (offset >= 0) & (document < doc_local) & (segment < SEGS)
        segment = jnp.clip(segment, 0, SEGS - 1)
        document = jnp.clip(document, 0, doc_local - 1)
        tokens = lax.dynamic_index_in_dim(embedded, document * SEGS + segment, 0, keepdims=False)
        earlier = incoming[:M]
        memory = jnp.where(segment == 0, mem_init, earlier)
        hidden = jnp.where(phase_index == 0, jnp.concatenate([memory, tokens], 0), incoming)
        length = seg_lengths[document, segment]
        features = lax.all_gather(hidden, "tp", axis=1, tiled=True)
        heads_out = lax.cond(
            active,
            lambda: attend(features, length, query_proj, key_proj, value_proj, norm_row),
            lambda: jnp.zeros((row_count, head_cols), jnp.bfloat16),
        )
        every_head = lax.all_gather(heads_out, "tp", axis=1, tiled=True)
        update = lax.cond(
            active,
            lambda: jnp.dot(every_head, out_proj, preferred_element_type=jnp.float32),
            lambda: jnp.zeros((row_count, width_local), jnp.float32),
        )
        result = (hidden.astype(jnp.float32) + update).astype(jnp.bfloat16)
        token_ok = jnp.arange(L) < length
        summed = jnp.sum(
            jnp.where(token_ok[:, None], result[M:].astype(jnp.float32), 0.0), 0
        ) / length.astype(jnp.float32)
        scale_now = jnp.where(active & (segment == SEGS - 1), mixing, 0.0)
        picked = (jnp.arange(doc_local) == document).astype(jnp.float32)
        pooled = pooled + picked[:, None] * (scale_now * summed)[None, :]
        incoming = from_behind(result, "section", 1)
        return (incoming, returned, pooled)

    start_state = (
        jnp.zeros((row_count, width_local), jnp.bfloat16),
        jnp.zeros((M, width_local), jnp.bfloat16),
        jnp.zeros((doc_local, width_local), jnp.float32),
    )
    final_state = lax.fori_loop(0, total_turns, turn, start_state)
    pooled = final_state[2]
    layer_total = lax.psum(pooled, "section")
    return lax.all_gather(layer_total, "doc", axis=0, tiled=True)


def solution(mesh):
    return jax.shard_map(
        body,
        mesh=mesh,
        in_specs=(
            P("doc", None, None),
            P("doc", None),
            P("section", "tp"),
            P(None, "tp"),
            P("section", None),
            P("section", "doc", "tp"),
            P("section", "doc", "tp"),
            P("section", "doc", "tp"),
            P("section", None, "tp"),
            P("section"),
        ),
        out_specs=P(None, "tp"),
        check_vma=False,
    )
```

profile of v0, /device:TPU:0, one launch (start us, length us, event | category | flops | bytes accessed | tf_op | source)
XLA Modules:
  0.0 784.1 jit_solution(3177141854226608672)
XLA Ops:
  9.1 9.4 %gather_fusion = bf16[128,2048]{1,0:T(8,128)(2,1)S(1)} fusion(bf16[4096,2048]{1,0:T(8,128)(2,1)} %param.18, s32[1024]{0:T(1024)S(1)} %pad_clamp_fusion), kind=kCustom, calls=%fused_computation | custom fusion | bytes 1049088 | tf_op jit(solution)/shard_map/jit(_take)/gather | solution.py:88
  18.4 1.1 select_convert_fusion
  21.4 34.5 %all-reduce.2.cloned.1.call-done = bf16[4,32,2048]{2,1,0:T(8,128)(2,1)} async-done(((bf16[4,32,2048]{2,1,0:T(8,128)(2,1)}), bf16[4,32,2048]{2,1,0:T(8,128)(2,1)}) %all-reduce.2.cloned.1.call-update) | async-done | bytes 524304 | tf_op jit(solution)/shard_map/psum | solution.py:90
  55.9 118.0 %all-gather.8.cloned.1.call-done = bf16[1,4096,1024]{2,1,0:T(8,128)(2,1)} async-done(((bf16[1,1024,1024]{2,1,0:T(8,128)(2,1)}), bf16[1,4096,1024]{2,1,0:T(8,128)(2,1)}) %all-gather.8.cloned.1.call-update) | async-done | bytes 8388624 | tf_op jit(solution)/shard_map/all_gather | solution.py:95
  173.8 149.2 %all-gather.10.cloned.1.call-done = bf16[1,4096,1024]{2,1,0:T(8,128)(2,1)} async-done(((bf16[1,1024,1024]{2,1,0:T(8,128)(2,1)}), bf16[1,4096,1024]{2,1,0:T(8,128)(2,1)}) %all-gather.10.cloned.1.call-update) | async-done | bytes 8388624 | tf_op jit(solution)/shard_map/all_gather | solution.py:93
  323.0 149.2 %all-gather.12.cloned.1.call-done = bf16[1,4096,1024]{2,1,0:T(8,128)(2,1)} async-done(((bf16[1,1024,1024]{2,1,0:T(8,128)(2,1)}), bf16[1,4096,1024]{2,1,0:T(8,128)(2,1)}) %all-gather.12.cloned.1.call-update) | async-done | bytes 8388624 | tf_op jit(solution)/shard_map/all_gather | solution.py:94
  472.2 280.3 %while.18 = (s32[]{:T(128)}, bf16[48,2048]{1,0:T(8,128)(2,1)S(1)}, f32[2,2048]{1,0:T(2,128)S(1)}, pred[]{:T(512)}, s32[]{:T(128)}, /*index=5*/bf16[16,2048]{1,0:...) while((s32[]{:T(128)}, bf16[48,2048]{1,0:T(8,128)(2,1)S(1)}, ...), condition=%wide.region_9.10_spmd.clone, body=%wide.region_1.9_spmd.clone.sunk | while | flops 1624327808 | bytes 99228344 | solution.py:145
  472.3 0.9 dynamic-slice_bitcast_fusion.2
  473.3 7.5 all_gather.40
  481.5 10.6 %conditional.6 = (bf16[48,1024]{1,0:T(8,128)(2,1)S(1)}) conditional(s32[]{:T(128)} %convert_element_type.148, () %tuple.62, (bf16[48,4096]{1,0:T(8,128)(2,1)S(1)}, f32[1,4096]{1,0:T(1,128)S(1)}, bf16[4096,1024]{1,0:T(8,128)(2,1)}, s32[]{:T(128)}, bf16[4096,1024]{1,0:T(8,128)(2,1)}, /*index=5*/bf16[4096,1024]{1,0:T(8,128)(2,1)}) %tuple.63), branch_computations={%region_2.2_spmd, %region_3.5_spmd} | conditional | flops 1220644480 | bytes 86546328 | solution.py:118
  481.7 5.2 fusion.5
  487.5 1.6 fusion.6
  490.1 1.6 fusion.4
  492.1 5.3 all_gather.41
  497.4 4.9 conditional.7
  497.4 4.9 fusion.25
  504.7 2.8 collective-permute-done
  508.5 6.3 all_gather.40
  515.5 10.6 %conditional.6 = (bf16[48,1024]{1,0:T(8,128)(2,1)S(1)}) conditional(s32[]{:T(128)} %convert_element_type.148, () %tuple.62, (bf16[48,4096]{1,0:T(8,128)(2,1)S(1)}, f32[1,4096]{1,0:T(1,128)S(1)}, bf16[4096,1024]{1,0:T(8,128)(2,1)}, s32[]{:T(128)}, bf16[4096,1024]{1,0:T(8,128)(2,1)}, /*index=5*/bf16[4096,1024]{1,0:T(8,128)(2,1)}) %tuple.63), branch_computations={%region_2.2_spmd, %region_3.5_spmd} | conditional | flops 1220644480 | bytes 86546328 | solution.py:118
  515.7 5.2 fusion.5
  521.5 1.6 fusion.6
  524.2 1.6 fusion.4
  526.1 5.3 all_gather.41
  531.4 4.9 conditional.7
  531.4 4.9 fusion.25
  538.7 2.8 collective-permute-done
  542.5 6.3 all_gather.40
  549.5 5.3 all_gather.41
  554.9 9.9 %collective-permute-start = (bf16[48,2048]{1,0:T(8,128)(2,1)S(1)}, bf16[48,2048]{1,0:T(8,128)(2,1)S(1)}, u32[]{:S(2)}, u32[]{:S(2)}) collective-permute-start(bf16[48,2048]{1,0:T(8,128)(2,1)S(1)} %add_convert_fusion.2), channel_id=1, source_target_pairs={{24,0},{0,8},{8,16},{16,24},{25,1},{1,9},{9,17},{17,25},{26,2},{2,... | collective-permute-start | bytes 589832 | tf_op jit(solution)/shard_map/while/body/eval_jaxpr/ppermute | solution.py:21
  567.1 0.9 dynamic-slice_bitcast_fusion.2
  568.1 7.8 all_gather.40
  576.6 5.3 all_gather.41
  584.3 11.1 %collective-permute-done = bf16[48,2048]{1,0:T(8,128)(2,1)S(1)} collective-permute-done((bf16[48,2048]{1,0:T(8,128)(2,1)S(1)}, bf16[48,2048]{1,0:T(8,128)(2,1)S(1)}, u32[]{:S(2)}, u32[]{:S(2)}) %collective-permute-start) | collective-permute-done | bytes 196640 | tf_op jit(solution)/shard_map/while/body/eval_jaxpr/ppermute | solution.py:21
  596.4 6.3 all_gather.40
  603.4 10.6 %conditional.6 = (bf16[48,1024]{1,0:T(8,128)(2,1)S(1)}) conditional(s32[]{:T(128)} %convert_element_type.148, () %tuple.62, (bf16[48,4096]{1,0:T(8,128)(2,1)S(1)}, f32[1,4096]{1,0:T(1,128)S(1)}, bf16[4096,1024]{1,0:T(8,128)(2,1)}, s32[]{:T(128)}, bf16[4096,1024]{1,0:T(8,128)(2,1)}, /*index=5*/bf16[4096,1024]{1,0:T(8,128)(2,1)}) %tuple.63), branch_computations={%region_2.2_spmd, %region_3.5_spmd} | conditional | flops 1220644480 | bytes 86546328 | solution.py:118
  603.6 5.2 fusion.5
  609.4 1.6 fusion.6
  612.1 1.6 fusion.4
  614.0 5.3 all_gather.41
  619.3 4.9 conditional.7
  619.3 4.9 fusion.25
  626.6 3.4 collective-permute-done
  631.0 6.3 all_gather.40
  638.0 10.6 %conditional.6 = (bf16[48,1024]{1,0:T(8,128)(2,1)S(1)}) conditional(s32[]{:T(128)} %convert_element_type.148, () %tuple.62, (bf16[48,4096]{1,0:T(8,128)(2,1)S(1)}, f32[1,4096]{1,0:T(1,128)S(1)}, bf16[4096,1024]{1,0:T(8,128)(2,1)}, s32[]{:T(128)}, bf16[4096,1024]{1,0:T(8,128)(2,1)}, /*index=5*/bf16[4096,1024]{1,0:T(8,128)(2,1)}) %tuple.63), branch_computations={%region_2.2_spmd, %region_3.5_spmd} | conditional | flops 1220644480 | bytes 86546328 | solution.py:118
  638.2 5.2 fusion.5
  644.0 1.6 fusion.6
  646.7 1.6 fusion.4
  648.6 5.3 all_gather.41
  653.9 4.9 conditional.7
  653.9 4.9 fusion.25
  661.2 2.8 collective-permute-done
  665.0 6.3 all_gather.40
  672.1 5.3 all_gather.41
  677.4 9.9 %collective-permute-start = (bf16[48,2048]{1,0:T(8,128)(2,1)S(1)}, bf16[48,2048]{1,0:T(8,128)(2,1)S(1)}, u32[]{:S(2)}, u32[]{:S(2)}) collective-permute-start(bf16[48,2048]{1,0:T(8,128)(2,1)S(1)} %add_convert_fusion.2), channel_id=1, source_target_pairs={{24,0},{0,8},{8,16},{16,24},{25,1},{1,9},{9,17},{17,25},{26,2},{2,... | collective-permute-start | bytes 589832 | tf_op jit(solution)/shard_map/while/body/eval_jaxpr/ppermute | solution.py:21
  689.7 0.9 dynamic-slice_bitcast_fusion.2
  690.6 7.8 all_gather.40
  699.1 5.3 all_gather.41
  706.8 10.5 %collective-permute-done = bf16[48,2048]{1,0:T(8,128)(2,1)S(1)} collective-permute-done((bf16[48,2048]{1,0:T(8,128)(2,1)S(1)}, bf16[48,2048]{1,0:T(8,128)(2,1)S(1)}, u32[]{:S(2)}, u32[]{:S(2)}) %collective-permute-start) | collective-permute-done | bytes 196640 | tf_op jit(solution)/shard_map/while/body/eval_jaxpr/ppermute | solution.py:21
  718.3 6.3 all_gather.40
  725.4 6.0 all_gather.41
  731.5 4.6 collective-permute-start
  738.3 14.2 %collective-permute-done = bf16[48,2048]{1,0:T(8,128)(2,1)S(1)} collective-permute-done((bf16[48,2048]{1,0:T(8,128)(2,1)S(1)}, bf16[48,2048]{1,0:T(8,128)(2,1)S(1)}, u32[]{:S(2)}, u32[]{:S(2)}) %collective-permute-start) | collective-permute-done | bytes 196640 | tf_op jit(solution)/shard_map/while/body/eval_jaxpr/ppermute | solution.py:21
  752.5 10.1 %psum.15 = f32[2,2048]{1,0:T(2,128)S(1)} all-reduce(f32[2,2048]{1,0:T(2,128)S(1)} %get-tuple-element.366), channel_id=1, replica_groups=mesh['section'=4,'tp'=2,'doc'=4] {'section'}, use_global_device_ids=true, to_apply=%region_10.11 | all-reduce | flops 4096 | bytes 32768 | tf_op jit(solution)/shard_map/psum | solution.py:147
  762.6 13.1 %all-gather.3 = f32[4,2,2048]{2,1,0:T(2,128)S(1)} all-gather(f32[1,2,2048]{2,1,0:T(2,128)S(1)} %bitcast.55), channel_id=1, replica_groups=mesh['section'=4,'tp'=2,'doc'=4] {'doc'}, dimensions={0}, use_global_device_ids=true | all-gather | bytes 81920 | tf_op jit(solution)/shard_map/all_gather | solution.py:148
  (196 shorter events, 33.4 us)
Async XLA Ops:
  7.4 464.8 %copy-start.3 = (s32[2,2]{1,0:T(2,128)S(1)}, s32[2,2]{1,0:T(2,128)}, u32[]{:S(2)}) copy-start(s32[2,2]{1,0:T(2,128)} %param.17) | copy-start | bytes 52
  7.4 464.8 %copy-start.2 = (bf16[16,2048]{1,0:T(8,128)(2,1)S(1)}, bf16[16,2048]{1,0:T(8,128)(2,1)}, u32[]{:S(2)}) copy-start(bf16[16,2048]{1,0:T(8,128)(2,1)} %param.19) | copy-start | bytes 196612
  7.4 464.9 %copy-start.1 = (f32[1,4096]{1,0:T(1,128)S(1)}, f32[1,4096]{1,0:T(1,128)}, u32[]{:S(2)}) copy-start(f32[1,4096]{1,0:T(1,128)} %param.20) | copy-start | bytes 49156
  7.4 48.5 %all-reduce.2.cloned.1.call-start = ((), (), s32[]{:S(2)}) async-start(), calls=%async_computation | async-start | bytes 1048576 | tf_op jit(solution)/shard_map/psum | solution.py:90
  19.6 154.2 %all-gather.8.cloned.1.call-start = ((), (), s32[]{:S(2)}) async-start(), calls=%async_computation.1 | async-start | bytes 10485760 | tf_op jit(solution)/shard_map/all_gather | solution.py:95
  20.2 302.8 %all-gather.10.cloned.1.call-start = ((), (), s32[]{:S(2)}) async-start(), calls=%async_computation.2 | async-start | bytes 10485760 | tf_op jit(solution)/shard_map/all_gather | solution.py:93
  20.8 451.4 %all-gather.12.cloned.1.call-start = ((), (), s32[]{:S(2)}) async-start(), calls=%async_computation.3 | async-start | bytes 10485760 | tf_op jit(solution)/shard_map/all_gather | solution.py:94
  481.7 5.8 copy-start
  481.7 8.4 %slice-start = ((s8[8388608]{0:T(1024)(128)(4,1)}), s8[4194304]{0:T(1024)(128)(4,1)S(1)}, s32[]{:S(2)}) async-start(s8[8388608]{0:T(1024)(128)(4,1)} %bitcast.45), calls=%async_computation.4 | async-start | bytes 8388608 | tf_op jit(solution)/shard_map/while/body/eval_jaxpr/cond
  487.5 2.7 slice-start.1
  502.4 5.1 collective-permute-start
  515.7 5.8 copy-start
  515.7 8.4 %slice-start = ((s8[8388608]{0:T(1024)(128)(4,1)}), s8[4194304]{0:T(1024)(128)(4,1)S(1)}, s32[]{:S(2)}) async-start(s8[8388608]{0:T(1024)(128)(4,1)} %bitcast.45), calls=%async_computation.4 | async-start | bytes 8388608 | tf_op jit(solution)/shard_map/while/body/eval_jaxpr/cond
  521.5 2.7 slice-start.1
  536.4 5.1 collective-permute-start
  554.9 12.1 %collective-permute-start = (bf16[48,2048]{1,0:T(8,128)(2,1)S(1)}, bf16[48,2048]{1,0:T(8,128)(2,1)S(1)}, u32[]{:S(2)}, u32[]{:S(2)}) collective-permute-start(bf16[48,2048]{1,0:T(8,128)(2,1)S(1)} %add_convert_fusion.2), channel_id=1, source_target_pairs={{24,0},{0,8},{8,16},{16,24},{25,1},{1,9},{9,17},{17,25},{26,2},{2,... | collective-permute-start | bytes 589832 | tf_op jit(solution)/shard_map/while/body/eval_jaxpr/ppermute | solution.py:21
  581.9 13.5 %collective-permute-start = (bf16[48,2048]{1,0:T(8,128)(2,1)S(1)}, bf16[48,2048]{1,0:T(8,128)(2,1)S(1)}, u32[]{:S(2)}, u32[]{:S(2)}) collective-permute-start(bf16[48,2048]{1,0:T(8,128)(2,1)S(1)} %add_convert_fusion.2), channel_id=1, source_target_pairs={{24,0},{0,8},{8,16},{16,24},{25,1},{1,9},{9,17},{17,25},{26,2},{2,... | collective-permute-start | bytes 589832 | tf_op jit(solution)/shard_map/while/body/eval_jaxpr/ppermute | solution.py:21
  603.6 5.8 copy-start
  603.6 8.4 %slice-start = ((s8[8388608]{0:T(1024)(128)(4,1)}), s8[4194304]{0:T(1024)(128)(4,1)S(1)}, s32[]{:S(2)}) async-start(s8[8388608]{0:T(1024)(128)(4,1)} %bitcast.45), calls=%async_computation.4 | async-start | bytes 8388608 | tf_op jit(solution)/shard_map/while/body/eval_jaxpr/cond
  609.4 2.7 slice-start.1
  624.3 5.7 collective-permute-start
  638.2 5.8 copy-start
  638.2 8.4 %slice-start = ((s8[8388608]{0:T(1024)(128)(4,1)}), s8[4194304]{0:T(1024)(128)(4,1)S(1)}, s32[]{:S(2)}) async-start(s8[8388608]{0:T(1024)(128)(4,1)} %bitcast.45), calls=%async_computation.4 | async-start | bytes 8388608 | tf_op jit(solution)/shard_map/while/body/eval_jaxpr/cond
  644.0 2.7 slice-start.1
  658.9 5.1 collective-permute-start
  677.4 12.1 %collective-permute-start = (bf16[48,2048]{1,0:T(8,128)(2,1)S(1)}, bf16[48,2048]{1,0:T(8,128)(2,1)S(1)}, u32[]{:S(2)}, u32[]{:S(2)}) collective-permute-start(bf16[48,2048]{1,0:T(8,128)(2,1)S(1)} %add_convert_fusion.2), channel_id=1, source_target_pairs={{24,0},{0,8},{8,16},{16,24},{25,1},{1,9},{9,17},{17,25},{26,2},{2,... | collective-permute-start | bytes 589832 | tf_op jit(solution)/shard_map/while/body/eval_jaxpr/ppermute | solution.py:21
  704.5 12.9 %collective-permute-start = (bf16[48,2048]{1,0:T(8,128)(2,1)S(1)}, bf16[48,2048]{1,0:T(8,128)(2,1)S(1)}, u32[]{:S(2)}, u32[]{:S(2)}) collective-permute-start(bf16[48,2048]{1,0:T(8,128)(2,1)S(1)} %add_convert_fusion.2), channel_id=1, source_target_pairs={{24,0},{0,8},{8,16},{16,24},{25,1},{1,9},{9,17},{17,25},{26,2},{2,... | collective-permute-start | bytes 589832 | tf_op jit(solution)/shard_map/while/body/eval_jaxpr/ppermute | solution.py:21
  731.5 21.1 %collective-permute-start = (bf16[48,2048]{1,0:T(8,128)(2,1)S(1)}, bf16[48,2048]{1,0:T(8,128)(2,1)S(1)}, u32[]{:S(2)}, u32[]{:S(2)}) collective-permute-start(bf16[48,2048]{1,0:T(8,128)(2,1)S(1)} %add_convert_fusion.2), channel_id=1, source_target_pairs={{24,0},{0,8},{8,16},{16,24},{25,1},{1,9},{9,17},{17,25},{26,2},{2,... | collective-permute-start | bytes 589832 | tf_op jit(solution)/shard_map/while/body/eval_jaxpr/ppermute | solution.py:21
Sparse Core Ops, SparseCore 0:
  19.7 36.1 all-reduce.1
Sparse Core Ops, SparseCore 1:
  21.6 152.1 all-gather.7
  175.3 147.7 all-gather.9
  324.5 147.7 all-gather.11
where the time goes:
time: 785 us; the launch traced here: 784 us
  waiting for transfers between devices  500 us (64%)
  blocking collectives  133 us (17%)
  matrix products  55.3 us (7%)
  local copies, waits for them, and re-layouts  27.2 us (3%)
  starting transfers between devices  24.8 us (3%)
  other arithmetic  15.4 us (2%)
  between operations  15.1 us (2%)
  loops' own time  13.4 us (2%)
    all_gather x1, waiting for transfers between devices, body(): lax.all_gather(w_key[0], 'doc', axis=0, tiled=True)  149 us
    all_gather x1, waiting for transfers between devices, body(): lax.all_gather(w_query[0], 'doc', axis=0, tiled=True)  149 us
    all_gather x1, waiting for transfers between devices, body(): lax.all_gather(w_value[0], 'doc', axis=0, tiled=True)  118 us
    all_gather x9, blocking collectives, turn(): features = lax.all_gather(hidden, 'tp', axis=1, tiled=True)  61.1 us
    all_gather x9, blocking collectives, turn(): every_head = lax.all_gather(heads_out, 'tp', axis=1, tiled=True)  48.3 us
    ppermute x9, waiting for transfers between devices, from_behind(): return lax.ppermute(block, axis, route)  47.7 us
    psum x1, waiting for transfers between devices, body(): embedded = lax.psum(partial_rows.astype(jnp.bfloat16), 'section')  34.5 us
    ppermute x9, starting transfers between devices, from_behind(): return lax.ppermute(block, axis, route)  24.7 us
  transfers between devices with their start and end apart: 13, of which 11 were waited for; matrix products, arithmetic and copies ran while one was open for 1% of the time, Pallas kernels for 0%

commit v1 on v0

v1 whole, which is shorter than its diff:
```python
import functools
import math

import jax
import jax.numpy as jnp
from jax import lax
from jax.experimental import pallas as pl
from jax.experimental.pallas import tpu as pltpu
from jax.sharding import PartitionSpec as P

HD = 128
M = 16
EPSILON = 1e-05
AXES = ("section", "tp", "doc")
VMEM_LIMIT = 48 * 1024 * 1024
C_FIRST, C_INIT, C_TP, C_POOL, C_LEN = 0, 1, 2, 3, 4


def attend_kernel(
    turn, docs, tokens, blocks, meta, where, *refs
):
    halves = refs[0]
    other = refs[1]
    tok, tok_other, mem, mem_other, gain = refs[2:7]
    weights = refs[7 : 7 + blocks]
    mixed_ref, keep_ref = refs[7 + blocks : 9 + blocks]
    normed, acc, wbuf, sems = refs[9 + blocks :]
    rows = M + tokens
    half = halves.shape[1]
    depth = wbuf.shape[1]
    cols = wbuf.shape[2] // 3
    copies = []
    for b in range(blocks):
        copy = pltpu.make_async_copy(weights[b], wbuf.at[b], sems.at[b])
        copy.start()
        copies.append(copy)
    first = meta[turn, C_FIRST] == 1
    initial = meta[turn, C_INIT] == 1
    tp = meta[turn, C_TP]

    def prepare(doc, _):
        base = pl.multiple_of(doc * rows, 16)
        tbase = pl.multiple_of(doc * tokens, 16)
        parts = []
        for block, tk, mm in ((halves, tok, mem), (other, tok_other, mem_other)):
            head = jnp.where(initial, mm[...], block[pl.ds(base, M), :])
            body = jnp.where(
                first, tk[pl.ds(tbase, tokens), :], block[pl.ds(base + M, tokens), :]
            )
            parts.append(jnp.concatenate([head, body], 0))
        keep_ref[pl.ds(base, rows), :] = parts[0]
        floats = [p.astype(jnp.float32) for p in parts]
        square = sum(jnp.sum(f * f, -1, keepdims=True) for f in floats)
        scale = lax.rsqrt(square * (1.0 / (2 * half)) + EPSILON)
        for j, f in enumerate(floats):
            at = pl.multiple_of((tp if j == 0 else 1 - tp) * half, 128)
            normed[pl.ds(base, rows), pl.ds(at, half)] = (
                f * scale * gain[:, pl.ds(at, half)]
            ).astype(jnp.bfloat16)
        return 0

    lax.fori_loop(0, docs, prepare, 0)
    for b in range(blocks):
        copies[b].wait()
        at = pl.multiple_of(where[b] * depth, 128)
        left = normed[:, pl.ds(at, depth)]
        for c in range(3):
            span = pl.ds(c * cols, cols)
            part = jnp.dot(left, wbuf[b, :, span], preferred_element_type=jnp.float32)
            if b == 0:
                acc[:, span] = part
            else:
                acc[:, span] += part

    row = lax.broadcasted_iota(jnp.int32, (rows, rows), 0)
    col = lax.broadcasted_iota(jnp.int32, (rows, rows), 1)
    ordered = (col < M) | (row < M) | (col <= row)

    def one(doc, _):
        base = pl.multiple_of(doc * rows, 16)
        length = meta[turn, C_LEN + doc]
        allowed = ordered & ((col < M) | (col - M < length))
        for h in range(cols // HD):
            q, k, v = (
                acc[pl.ds(base, rows), c * cols + h * HD : c * cols + (h + 1) * HD].astype(
                    jnp.bfloat16
                )
                for c in range(3)
            )
            scores = lax.dot_general(
                q, k, (((1,), (1,)), ((), ())), preferred_element_type=jnp.float32
            ) * (1.0 / math.sqrt(HD))
            raw = jnp.where(allowed, jnp.exp(jnp.where(allowed, scores, -1e30)), 0.0)
            probs = (raw / jnp.sum(raw, -1, keepdims=True)).astype(jnp.bfloat16)
            mixed_ref[pl.ds(base, rows), h * HD : (h + 1) * HD] = jnp.dot(
                probs, v, preferred_element_type=jnp.float32
            ).astype(jnp.bfloat16)
        return 0

    lax.fori_loop(0, docs, one, 0)


def project_kernel(turn, docs, tokens, parts, pool, meta, place, mix, *refs):
    mixed = refs[:parts]
    keep, weight = refs[parts : parts + 2]
    outs = refs[parts + 2 :]
    if pool:
        out, pooled, wbuf, sems = outs
    else:
        out, wbuf, sems = outs
    rows = M + tokens
    depth = mixed[0].shape[1]
    width = keep.shape[1]
    copies = []
    for b in range(parts):
        at = pl.multiple_of(place[b] * depth, 128)
        copy = pltpu.make_async_copy(weight.at[pl.ds(at, depth), :], wbuf.at[b], sems.at[b])
        copy.start()
        copies.append(copy)
    for copy in copies:
        copy.wait()
    step = min(width, 512)
    for c in range(0, width, step):
        total = keep[:, c : c + step].astype(jnp.float32)
        for b in range(parts):
            total += jnp.dot(
                mixed[b][...], wbuf[b, :, c : c + step], preferred_element_type=jnp.float32
            )
        out[:, c : c + step] = total.astype(jnp.bfloat16)
    if pool:
        wanted = meta[turn, C_POOL] == 1
        place_row = lax.broadcasted_iota(jnp.int32, (rows, width), 0)
        for doc in range(docs):
            length = meta[turn, C_LEN + doc]
            ok = (place_row >= M) & (place_row - M < length) & wanted
            values = out[doc * rows : (doc + 1) * rows, :].astype(jnp.float32)
            summed = jnp.sum(jnp.where(ok, values, 0.0), 0, keepdims=True)
            pooled[doc : doc + 1, :] = summed * (mix[0] / jnp.maximum(length, 1).astype(jnp.float32))


def body(
    token_ids,
    seg_lengths,
    emb_table,
    mem_init,
    norm_gain,
    w_query,
    w_key,
    w_value,
    w_out,
    layer_mix,
):
    S, T, D = (lax.axis_size(a) for a in AXES)
    s, t, z = (lax.axis_index(a) for a in AXES)
    docs_local, segs, tokens = token_ids.shape
    docs = docs_local * D
    n = docs // S
    rows = M + tokens
    R = n * rows
    half = emb_table.shape[1]
    depth = w_query.shape[1]
    cols = w_query.shape[2] // 2
    lo, hi = D // 2 - 1, D // 2
    planes = (lo, hi)
    turns = segs * S + S - 1

    def lin(a, b, c):
        return (a * T + b) * D + c

    def send(block, pairs):
        return lax.ppermute(block, AXES, [(lin(*a), lin(*b)) for a, b in pairs])

    def block_of(side):
        return jnp.concatenate(
            [lax.dynamic_slice_in_dim(w[0], side * cols, cols, 1) for w in (w_query, w_key, w_value)],
            1,
        )

    weights = [block_of((z == hi).astype(jnp.int32))]
    where = [z]
    for source in range(D):
        if source == lo:
            continue
        pairs = []
        for a in range(S):
            for b in range(T):
                pairs.append(((a, b, source), (a, b, lo)))
                pairs.append(((a, b, D - 1 - source), (a, b, hi)))
        weights.append(send(block_of((z == D - 1 - source).astype(jnp.int32)), pairs))
        where.append(jnp.where(z == hi, D - 1 - source, source))
    where = jnp.stack(where).astype(jnp.int32)

    packed = jnp.concatenate([token_ids, seg_lengths[:, :, None]], 2)
    packed = lax.all_gather(packed, "doc", axis=0, tiled=True)
    ids, lengths = packed[:, :, :tokens], packed[:, :, tokens]

    vocab = emb_table.shape[0]
    tok, tok_other = [], []
    for seg in range(segs):
        local = ids[:, seg].reshape(-1) - s * vocab
        owned = (local >= 0) & (local < vocab)
        picked = jnp.take(emb_table, jnp.clip(local, 0, vocab - 1), axis=0)
        picked = jnp.where(owned[:, None], picked, jnp.zeros_like(picked))
        full = picked
        for a in range(1, S):
            full = full + send(picked, [((a, b, c), (0, b, c)) for b in range(T) for c in planes])
        tok.append(full)
        tok_other.append(send(full, [((0, b, c), (0, T - 1 - b, c)) for b in range(T) for c in planes]))
    mem_other = send(mem_init, [((0, b, c), (0, T - 1 - b, c)) for b in range(T) for c in planes])

    offset = jnp.arange(turns) - s
    group = offset % S
    segment = jnp.clip(offset // S, 0, segs - 1)
    grouped = lengths.reshape(S, n, segs)
    lens = grouped[group, :, segment]
    active = (offset >= 0) & (offset < segs * S)
    flags = jnp.stack(
        [
            jnp.full((turns,), s == 0),
            (s == 0) & (offset < S),
            jnp.full((turns,), t),
            active & (segment == segs - 1),
        ],
        1,
    ).astype(jnp.int32)
    meta = jnp.concatenate([flags, lens], 1).astype(jnp.int32)

    shifts = [(j, i) for i in range(2) for j in range(T)]
    side = (z == hi).astype(jnp.int32)
    place = jnp.stack([((t + j) % T) * 2 + (side + i) % 2 for j, i in shifts]).astype(jnp.int32)

    smem = pl.BlockSpec(memory_space=pltpu.SMEM)
    vmem = pl.BlockSpec(memory_space=pltpu.VMEM)
    anyw = pl.BlockSpec(memory_space=pl.ANY)
    out_proj = w_out[0]
    parts = len(shifts)

    own = jnp.zeros((R, half), jnp.bfloat16)
    other = jnp.zeros((R, half), jnp.bfloat16)
    pools = []
    for k in range(turns):
        g, seg = k % S, k // S
        rows_of = slice(g * n * tokens, (g + 1) * n * tokens)
        tk, tko = (a[min(seg, segs - 1)][rows_of] for a in (tok, tok_other))
        mixed, keep = pl.pallas_call(
            functools.partial(attend_kernel, k, n, tokens, D),
            out_shape=(
                jax.ShapeDtypeStruct((R, cols), jnp.bfloat16),
                jax.ShapeDtypeStruct((R, half), jnp.bfloat16),
            ),
            in_specs=[smem, smem] + [vmem] * 7 + [anyw] * D,
            out_specs=(vmem, vmem),
            scratch_shapes=[
                pltpu.VMEM((R, 2 * half), jnp.bfloat16),
                pltpu.VMEM((R, 3 * cols), jnp.float32),
                pltpu.VMEM((D, depth, 3 * cols), jnp.bfloat16),
                pltpu.SemaphoreType.DMA((D,)),
            ],
            compiler_params=pltpu.CompilerParams(vmem_limit_bytes=VMEM_LIMIT),
        )(meta, where, own, other, tk, tko, mem_init, mem_other, norm_gain, *weights)
        live = [a for a in range(S) if 0 <= k - a < segs * S]
        shared = [mixed]
        for j, i in shifts[1:]:
            pairs = [
                ((a, (b + j) % T, planes[(c + i) % 2]), (a, b, planes[c]))
                for a in live
                for b in range(T)
                for c in range(2)
            ]
            shared.append(send(mixed, pairs))
        pool = k >= (segs - 1) * S
        shapes = [jax.ShapeDtypeStruct((R, half), jnp.bfloat16)]
        if pool:
            shapes.append(jax.ShapeDtypeStruct((n, half), jnp.float32))
        result = pl.pallas_call(
            functools.partial(project_kernel, k, n, tokens, parts, pool),
            out_shape=tuple(shapes),
            in_specs=[smem, smem, smem] + [vmem] * (parts + 1) + [anyw],
            out_specs=tuple([vmem] * len(shapes)),
            scratch_shapes=[
                pltpu.VMEM((parts, cols, half), jnp.bfloat16),
                pltpu.SemaphoreType.DMA((parts,)),
            ],
            compiler_params=pltpu.CompilerParams(vmem_limit_bytes=VMEM_LIMIT),
        )(meta, place, layer_mix, *shared, keep, out_proj)
        if pool:
            pools.append(result[1])
        goes = [a for a in live if not (a == S - 1 and (k - a) // S == segs - 1)]
        if goes:
            own = send(
                result[0],
                [((a, b, c), ((a + 1) % S, b, c)) for a in goes for b in range(T) for c in planes],
            )
            other = send(
                result[0],
                [
                    ((a, b, c), ((a + 1) % S, T - 1 - b, c))
                    for a in goes
                    for b in range(T)
                    for c in planes
                ],
            )

    mine = lax.dynamic_slice_in_dim(jnp.stack(pools), s, S, 0).reshape(docs, half)
    mine = jnp.where((z == lo) | (z == hi), mine, 0.0)
    total = lax.psum(mine, "section")
    spread = total
    for k in range(1, D // 2):
        pairs = [
            ((a, b, c), (a, b, c + e)) for a in range(S) for b in range(T) for c, e in ((lo, -k), (hi, k))
        ]
        spread = spread + send(total, pairs)
    return spread


def solution(mesh):
    return jax.shard_map(
        body,
        mesh=mesh,
        in_specs=(
            P("doc", None, None),
            P("doc", None),
            P("section", "tp"),
            P(None, "tp"),
            P("section", None),
            P("section", "doc", "tp"),
            P("section", "doc", "tp"),
            P("section", "doc", "tp"),
            P("section", None, "tp"),
            P("section"),
        ),
        out_specs=P(None, "tp"),
        check_vma=False,
    )
```

time: 785 us -> 680 us (0.87); the launches traced: 784 us -> 670 us
  waiting for transfers between devices: 500 us -> 175 us
  starting transfers between devices: 24.8 us -> 278 us
  Pallas kernels: 0 us -> 131 us
  blocking collectives: 133 us -> 13.5 us
  matrix products: 55.3 us -> 0 us
  loops' own time: 13.4 us -> 0 us
  local copies, waits for them, and re-layouts: 27.2 us -> 39.8 us
    all_gather x3 -> x0, waiting for transfers between devices: 416 us -> none  [the longest x1 149 us: body(): lax.all_gather(w_key[0], 'doc', axis=0, tiled=True)]
    ppermute x9 -> x66, starting transfers between devices: 24.7 us -> 278 us  [send(): return lax.ppermute(block, AXES, [(lin(*a), lin(*b)) for a, b in pairs])]
    pallas_call x0 -> x21, Pallas kernels: none -> 131 us  [the longest x11 72.6 us: body(): pl.pallas_call(functools.partial(attend_kernel, k, n, tokens, D), out_sha...]
    all_gather x19 -> x1, blocking collectives: 123 us -> 13.5 us  [body(): packed = lax.all_gather(packed, 'doc', axis=0, tiled=True)]
    dot_general x24 -> x0, matrix products: 55.3 us -> none  [the longest x4 20.6 us: attend(): jnp.dot(normed, query_proj, preferred_element_type=jnp.float32)]
    ppermute x9 -> x66, waiting for transfers between devices: 47.7 us -> 97.8 us  [send(): return lax.ppermute(block, AXES, [(lin(*a), lin(*b)) for a, b in pairs])]
    psum x1, waiting for transfers between devices: 34.5 us -> 77 us  [body(): total = lax.psum(mine, 'section')]
    another operation x19 -> x0, loops' own time: 13.4 us -> none  [the longest x1 13.1 us: body(): final_state = lax.fori_loop(0, total_turns, turn, start_state)]
  transfers between devices with their start and end apart: 13 -> 67, of which waited for: 11 -> 4; matrix products, arithmetic and copies ran while one was open for 1% -> 5% of each run, Pallas kernels for 0% -> 7%
where the time goes in v1:
time: 680 us; the launch traced here: 670 us
  starting transfers between devices  278 us (41%)
  waiting for transfers between devices  175 us (26%)
  Pallas kernels  131 us (19%)
  local copies, waits for them, and re-layouts  39.8 us (6%)
  other arithmetic  16.8 us (2%)
  between operations  16.2 us (2%)
  blocking collectives  13.5 us (2%)
    ppermute x66, starting transfers between devices, send(): return lax.ppermute(block, AXES, [(lin(*a), lin(*b)) for a, b in pairs])  278 us
    ppermute x66, waiting for transfers between devices, send(): return lax.ppermute(block, AXES, [(lin(*a), lin(*b)) for a, b in pairs])  97.8 us
    psum x1, waiting for transfers between devices, body(): total = lax.psum(mine, 'section')  77 us
    pallas_call x11, Pallas kernels, body(): pl.pallas_call(functools.partial(attend_kernel, k, n, tokens, D), out_sha...  72.6 us
    pallas_call x10, Pallas kernels, body(): pl.pallas_call(functools.partial(project_kernel, k, n, tokens, parts, poo...  58.2 us
    gather x2, local copies, waits for them, and re-layouts, body(): picked = jnp.take(emb_table, jnp.clip(local, 0, vocab - 1), axis=0)  21.6 us
  transfers between devices with their start and end apart: 67, of which 4 were waited for; matrix products, arithmetic and copies ran while one was open for 5% of the time, Pallas kernels for 7%

profile of v1, /device:TPU:0, one launch (start us, length us, event | category | flops | bytes accessed | tf_op | source)
XLA Modules:
  0.0 669.7 jit_solution(3795189216218097514)
XLA Ops:
  8.1 13.5 %all_gather.3 = s32[8,2,33]{2,1,0:T(2,128)S(1)} all-gather(s32[2,2,33]{2,1,0:T(2,128)S(1)} %pad_add_fusion), channel_id=1, replica_groups=mesh['section'=4,'tp'=2,'doc'=4] {'doc'}, dimensions={0}, use_global_device_ids=true | all-gather | bytes 2640 | tf_op jit(solution)/shard_map/all_gather | solution.py:194
  22.0 10.3 %gather_fusion.1 = bf16[256,2048]{1,0:T(8,128)(2,1)S(1)} fusion(bf16[4096,2048]{1,0:T(8,128)(2,1)} %param.14, s32[1024]{0:T(1024)S(1)} %pad_clamp_fusion.1), kind=kCustom, calls=%fused_computation.clone | custom fusion | bytes 2098176 | tf_op jit(solution)/shard_map/jit(_take)/gather | solution.py:202
  32.3 1.2 select_select_fusion.1
  33.5 1.8 collective-permute-start
  35.3 1.6 collective-permute-start.1
  36.9 1.6 collective-permute-start.2
  38.6 4.5 dynamic-slice_bitcast_fusion
  43.1 1.5 dynamic-slice_bitcast_fusion.2
  44.6 1.7 pad_maximum_fusion.1
  46.3 7.8 %collective-permute-start.5 = (bf16[1024,1536]{1,0:T(8,128)(2,1)}, bf16[1024,1536]{1,0:T(8,128)(2,1)}, u32[]{:S(2)}, u32[]{:S(2)}) collective-permute-start(bf16[1024,1536]{1,0:T(8,128)(2,1)} %pad_maximum_fusion.1), channel_id=1, source_target_pairs={{0,1},{3,2},{4,5},{7,6},{8,9},{11,10},{12,13},{15,14},{16,17},{19,... | collective-permute-start | bytes 9437192 | tf_op jit(solution)/shard_map/ppermute | solution.py:171
  54.1 1.9 pad_maximum_fusion.2
  56.0 2.3 collective-permute-start.6
  58.3 1.7 pad_maximum_fusion.3
  60.0 8.8 %collective-permute-start.7 = (bf16[1024,1536]{1,0:T(8,128)(2,1)}, bf16[1024,1536]{1,0:T(8,128)(2,1)}, u32[]{:S(2)}, u32[]{:S(2)}) collective-permute-start(bf16[1024,1536]{1,0:T(8,128)(2,1)} %pad_maximum_fusion.3), channel_id=1, source_target_pairs={{3,1},{0,2},{7,5},{4,6},{11,9},{8,10},{15,13},{12,14},{19,17},{16,... | collective-permute-start | bytes 9437192 | tf_op jit(solution)/shard_map/ppermute | solution.py:171
  69.2 11.3 %gather_fusion.2 = bf16[256,2048]{1,0:T(8,128)(2,1)} fusion(bf16[4096,2048]{1,0:T(8,128)(2,1)} %param.14, s32[1024]{0:T(1024)S(1)} %pad_clamp_fusion), kind=kCustom, calls=%fused_computation.1.clone | custom fusion | bytes 2098176 | tf_op jit(solution)/shard_map/jit(_take)/gather | solution.py:202
  81.5 2.1 pad_maximum_fusion.refs_7_
  83.5 1.3 collective-permute-start.4
  84.8 2.2 add_add_fusion.1
  87.9 1.2 select_select_fusion
  89.1 1.0 fusion.26
  90.0 1.6 collective-permute-start.28
  91.7 1.6 collective-permute-start.29
  93.3 28.0 %collective-permute-done.5.refs_8_ = bf16[1024,1536]{1,0:T(8,128)(2,1)} collective-permute-done((bf16[1024,1536]{1,0:T(8,128)(2,1)}, bf16[1024,1536]{1,0:T(8,128)(2,1)}, u32[]{:S(2)}, u32[]{:S(2)}) %collective-permute-start.5) | collective-permute-done | bytes 3145760 | tf_op jit(solution)/shard_map/ppermute | solution.py:171
  121.3 1.7 collective-permute-start.30
  122.9 0.9 fusion.25
  123.9 64.6 %collective-permute-done.7.refs_10_ = bf16[1024,1536]{1,0:T(8,128)(2,1)} collective-permute-done((bf16[1024,1536]{1,0:T(8,128)(2,1)}, bf16[1024,1536]{1,0:T(8,128)(2,1)}, u32[]{:S(2)}, u32[]{:S(2)}) %collective-permute-start.7) | collective-permute-done | bytes 3145760 | tf_op jit(solution)/shard_map/ppermute | solution.py:171
  188.5 6.5 shard_map.100
  198.6 1.0 copy-done.21
  199.6 5.7 shard_map.101
  206.7 6.5 shard_map.102
  215.3 5.7 shard_map.103
  221.0 0.8 collective-permute-start.16
  222.6 2.2 add_add_fusion
  225.6 6.5 shard_map.104
  234.2 5.7 shard_map.105
  240.6 0.9 collective-permute-start.22
  241.5 6.5 shard_map.106
  250.2 5.7 shard_map.107
  257.5 6.5 shard_map.108
  266.1 5.8 shard_map.109
  273.3 6.5 shard_map.110
  281.9 5.8 shard_map.111
  289.1 6.5 shard_map.112
  296.3 0.9 collective-permute-start.43
  297.9 5.8 shard_map.113
  305.1 7.2 %shard_map.114 = (bf16[96,512]{1,0:T(8,128)(2,1)}, bf16[96,2048]{1,0:T(8,128)(2,1)S(1)}) custom-call(s32[11,6]{1,0:T(8,128)S(1)} %concatenate.23.meta, s32[4]{0:T(128)S(1)} %pad_add_fusion.2.where, bf16[96,2048]{1,0:T(8,128)(2,1)S(1)} %collective-permute-done.45.refs_0_, bf16[96,2048]{1,0:T(8,128)(2,1)S(1)} %collective-permute-done.46.refs_1_, ...), custom_call_target="tpu_custom_call" | custom-call | tf_op jit(solution)/shard_map/pallas_call | solution.py:245
  313.1 1.3 collective-permute-start.47
  314.4 1.3 collective-permute-start.48
  315.6 1.3 collective-permute-start.49
  317.0 1.0 copy-done.23
  318.0 6.1 shard_map.115
  325.6 6.5 shard_map.116
  332.1 196.2 %collective-permute-start.52 = (bf16[96,512]{1,0:T(8,128)(2,1)S(1)}, bf16[96,512]{1,0:T(8,128)(2,1)S(1)}, u32[]{:S(2)}, u32[]{:S(2)}) collective-permute-start(bf16[96,512]{1,0:T(8,128)(2,1)S(1)} %get-tuple-element.65.refs_0_), channel_id=1, source_target_pairs={{13,9},{14,10},{9,13},{10,14},{21,17},{22,18},{17,21},{18,22},{29,... | collective-permute-start | bytes 294920 | tf_op jit(solution)/shard_map/ppermute | solution.py:171
  529.0 7.8 %collective-permute-start.54 = (bf16[96,512]{1,0:T(8,128)(2,1)S(1)}, bf16[96,512]{1,0:T(8,128)(2,1)S(1)}, u32[]{:S(2)}, u32[]{:S(2)}) collective-permute-start(bf16[96,512]{1,0:T(8,128)(2,1)S(1)} %get-tuple-element.65.refs_0_), channel_id=1, source_target_pairs={{14,9},{13,10},{10,13},{9,14},{22,17},{21,18},{18,21},{17,22},{30,... | collective-permute-start | bytes 294920 | tf_op jit(solution)/shard_map/ppermute | solution.py:171
  536.9 5.8 shard_map.117
  544.1 6.5 shard_map.118
  552.7 6.1 shard_map.119
  559.5 0.9 collective-permute-start.61
  560.5 6.8 %shard_map.120 = (bf16[96,512]{1,0:T(8,128)(2,1)S(1)}, bf16[96,2048]{1,0:T(8,128)(2,1)S(1)}) custom-call(s32[11,6]{1,0:T(8,128)S(1)} %concatenate.23.meta, s32[4]{0:T(128)S(1)} %pad_add_fusion.2.where, bf16[96,2048]{1,0:T(8,128)(2,1)S(1)} %collective-permute-done.60.refs_0_, bf16[96,2048]{1,0:T(8,128)(2,1)S(1)} %collective-permute-done.61.refs_1_, ...), custom_call_target="tpu_custom_call" | custom-call | tf_op jit(solution)/shard_map/pallas_call | solution.py:245
  569.5 3.6 shard_map.121
  573.8 77.0 %all-reduce.2.cloned.1.call-done = f32[8,2048]{1,0:T(8,128)} async-done(((f32[8,2048]{1,0:T(8,128)}), f32[8,2048]{1,0:T(8,128)}) %all-reduce.2.cloned.1.call-update) | async-done | bytes 65552 | tf_op jit(solution)/shard_map/psum | solution.py:306
  650.8 5.0 collective-permute-start.65
  655.8 5.1 collective-permute-done.65
  660.9 1.5 add.146
  (220 shorter events, 37.3 us)
Async XLA Ops:
  6.5 644.3 %all-reduce.2.cloned.1.call-start = ((), (), s32[]{:S(2)}) async-start(), calls=%async_computation | async-start | bytes 131072 | tf_op jit(solution)/shard_map/psum | solution.py:306
  33.5 26.6 %collective-permute-start = (bf16[256,2048]{1,0:T(8,128)(2,1)}, bf16[256,2048]{1,0:T(8,128)(2,1)}, u32[]{:S(2)}, u32[]{:S(2)}) collective-permute-start(bf16[256,2048]{1,0:T(8,128)(2,1)} %select_select_fusion.1), channel_id=1, source_target_pairs={{9,1},{10,2},{13,5},{14,6}} | collective-permute-start | bytes 3145736 | tf_op jit(solution)/shard_map/ppermute | solution.py:171
  35.3 48.2 %collective-permute-start.1 = (bf16[256,2048]{1,0:T(8,128)(2,1)}, bf16[256,2048]{1,0:T(8,128)(2,1)}, u32[]{:S(2)}, u32[]{:S(2)}) collective-permute-start(bf16[256,2048]{1,0:T(8,128)(2,1)} %select_select_fusion.1), channel_id=1, source_target_pairs={{17,1},{18,2},{21,5},{22,6}} | collective-permute-start | bytes 3145736 | tf_op jit(solution)/shard_map/ppermute | solution.py:171
  36.9 47.9 %collective-permute-start.2 = (bf16[256,2048]{1,0:T(8,128)(2,1)}, bf16[256,2048]{1,0:T(8,128)(2,1)}, u32[]{:S(2)}, u32[]{:S(2)}) collective-permute-start(bf16[256,2048]{1,0:T(8,128)(2,1)} %select_select_fusion.1), channel_id=1, source_target_pairs={{25,1},{26,2},{29,5},{30,6}} | collective-permute-start | bytes 3145736 | tf_op jit(solution)/shard_map/ppermute | solution.py:171
  46.3 75.0 %collective-permute-start.5 = (bf16[1024,1536]{1,0:T(8,128)(2,1)}, bf16[1024,1536]{1,0:T(8,128)(2,1)}, u32[]{:S(2)}, u32[]{:S(2)}) collective-permute-start(bf16[1024,1536]{1,0:T(8,128)(2,1)} %pad_maximum_fusion.1), channel_id=1, source_target_pairs={{0,1},{3,2},{4,5},{7,6},{8,9},{11,10},{12,13},{15,14},{16,17},{19,... | collective-permute-start | bytes 9437192 | tf_op jit(solution)/shard_map/ppermute | solution.py:171
  56.0 67.9 %collective-permute-start.6 = (bf16[1024,1536]{1,0:T(8,128)(2,1)}, bf16[1024,1536]{1,0:T(8,128)(2,1)}, u32[]{:S(2)}, u32[]{:S(2)}) collective-permute-start(bf16[1024,1536]{1,0:T(8,128)(2,1)} %pad_maximum_fusion.2), channel_id=1, source_target_pairs={{2,1},{1,2},{6,5},{5,6},{10,9},{9,10},{14,13},{13,14},{18,17},{17,... | collective-permute-start | bytes 9437192 | tf_op jit(solution)/shard_map/ppermute | solution.py:171
  60.0 128.4 %collective-permute-start.7 = (bf16[1024,1536]{1,0:T(8,128)(2,1)}, bf16[1024,1536]{1,0:T(8,128)(2,1)}, u32[]{:S(2)}, u32[]{:S(2)}) collective-permute-start(bf16[1024,1536]{1,0:T(8,128)(2,1)} %pad_maximum_fusion.3), channel_id=1, source_target_pairs={{3,1},{0,2},{7,5},{4,6},{11,9},{8,10},{15,13},{12,14},{19,17},{16,... | collective-permute-start | bytes 9437192 | tf_op jit(solution)/shard_map/ppermute | solution.py:171
  83.5 6.5 collective-permute-start.4
  87.0 4.6 collective-permute-start.3
  90.0 132.5 %collective-permute-start.28 = (bf16[256,2048]{1,0:T(8,128)(2,1)}, bf16[256,2048]{1,0:T(8,128)(2,1)}, u32[]{:S(2)}, u32[]{:S(2)}) collective-permute-start(bf16[256,2048]{1,0:T(8,128)(2,1)} %select_select_fusion), channel_id=1, source_target_pairs={{9,1},{10,2},{13,5},{14,6}} | collective-permute-start | bytes 3145736 | tf_op jit(solution)/shard_map/ppermute | solution.py:171
  91.7 130.9 %collective-permute-start.29 = (bf16[256,2048]{1,0:T(8,128)(2,1)}, bf16[256,2048]{1,0:T(8,128)(2,1)}, u32[]{:S(2)}, u32[]{:S(2)}) collective-permute-start(bf16[256,2048]{1,0:T(8,128)(2,1)} %select_select_fusion), channel_id=1, source_target_pairs={{17,1},{18,2},{21,5},{22,6}} | collective-permute-start | bytes 3145736 | tf_op jit(solution)/shard_map/ppermute | solution.py:171
  121.3 101.3 %collective-permute-start.30 = (bf16[256,2048]{1,0:T(8,128)(2,1)}, bf16[256,2048]{1,0:T(8,128)(2,1)}, u32[]{:S(2)}, u32[]{:S(2)}) collective-permute-start(bf16[256,2048]{1,0:T(8,128)(2,1)} %select_select_fusion), channel_id=1, source_target_pairs={{25,1},{26,2},{29,5},{30,6}} | collective-permute-start | bytes 3145736 | tf_op jit(solution)/shard_map/ppermute | solution.py:171
  195.8 2.0 collective-permute-start.10
  197.1 1.4 collective-permute-start.8
  197.8 0.8 collective-permute-start.9
  205.2 1.4 collective-permute-start.11
  205.9 0.7 collective-permute-start.12
  213.2 1.4 collective-permute-start.13
  213.9 1.4 collective-permute-start.14
  221.0 4.5 collective-permute-start.16
  221.8 3.7 collective-permute-start.17
  224.8 32.6 %collective-permute-start.31 = (bf16[256,2048]{1,0:T(8,128)(2,1)S(1)}, bf16[256,2048]{1,0:T(8,128)(2,1)S(1)}, u32[]{:S(2)}, u32[]{:S(2)}) collective-permute-start(bf16[256,2048]{1,0:T(8,128)(2,1)S(1)} %add_add_fusion), channel_id=1, source_target_pairs={{1,5},{2,6},{5,1},{6,2}} | collective-permute-start | bytes 3145736 | tf_op jit(solution)/shard_map/ppermute | solution.py:171
  232.1 2.0 collective-permute-start.18
  232.8 1.4 collective-permute-start.19
  233.4 0.7 collective-permute-start.20
  239.9 1.6 collective-permute-start.21
  240.6 0.9 collective-permute-start.22
  248.0 2.1 collective-permute-start.23
  248.7 1.5 collective-permute-start.24
  249.4 0.8 collective-permute-start.25
  256.0 1.5 collective-permute-start.26
  256.7 0.9 collective-permute-start.27
  264.1 2.0 collective-permute-start.32
  264.7 1.4 collective-permute-start.33
  265.4 0.7 collective-permute-start.34
  271.9 1.4 collective-permute-start.35
  272.6 0.7 collective-permute-start.36
  279.9 2.0 collective-permute-start.37
  280.5 1.4 collective-permute-start.38
  287.7 1.4 collective-permute-start.40
  288.4 0.7 collective-permute-start.41
  295.7 2.2 collective-permute-start.42
  296.3 1.6 collective-permute-start.43
  303.7 1.4 collective-permute-start.45
  304.4 0.7 collective-permute-start.46
  313.1 3.9 collective-permute-start.47
  314.4 2.6 collective-permute-start.48
  315.6 1.3 collective-permute-start.49
  324.1 1.4 collective-permute-start.50
  324.8 0.7 collective-permute-start.51
  332.1 204.8 %collective-permute-start.52 = (bf16[96,512]{1,0:T(8,128)(2,1)S(1)}, bf16[96,512]{1,0:T(8,128)(2,1)S(1)}, u32[]{:S(2)}, u32[]{:S(2)}) collective-permute-start(bf16[96,512]{1,0:T(8,128)(2,1)S(1)} %get-tuple-element.65.refs_0_), channel_id=1, source_target_pairs={{13,9},{14,10},{9,13},{10,14},{21,17},{22,18},{17,21},{18,22},{29,... | collective-permute-start | bytes 294920 | tf_op jit(solution)/shard_map/ppermute | solution.py:171
  528.3 8.6 %collective-permute-start.53 = (bf16[96,512]{1,0:T(8,128)(2,1)S(1)}, bf16[96,512]{1,0:T(8,128)(2,1)S(1)}, u32[]{:S(2)}, u32[]{:S(2)}) collective-permute-start(bf16[96,512]{1,0:T(8,128)(2,1)S(1)} %get-tuple-element.65.refs_0_), channel_id=1, source_target_pairs={{10,9},{9,10},{14,13},{13,14},{18,17},{17,18},{22,21},{21,22},{26,... | collective-permute-start | bytes 294920 | tf_op jit(solution)/shard_map/ppermute | solution.py:171
  529.0 7.9 %collective-permute-start.54 = (bf16[96,512]{1,0:T(8,128)(2,1)S(1)}, bf16[96,512]{1,0:T(8,128)(2,1)S(1)}, u32[]{:S(2)}, u32[]{:S(2)}) collective-permute-start(bf16[96,512]{1,0:T(8,128)(2,1)S(1)} %get-tuple-element.65.refs_0_), channel_id=1, source_target_pairs={{14,9},{13,10},{10,13},{9,14},{22,17},{21,18},{18,21},{17,22},{30,... | collective-permute-start | bytes 294920 | tf_op jit(solution)/shard_map/ppermute | solution.py:171
  542.7 1.4 collective-permute-start.55
  543.4 0.7 collective-permute-start.56
  550.7 2.0 collective-permute-start.57
  551.3 1.4 collective-permute-start.58
  552.0 0.7 collective-permute-start.59
  558.8 1.7 collective-permute-start.60
  559.5 1.0 collective-permute-start.61
  567.4 2.0 collective-permute-start.62
  568.1 1.4 collective-permute-start.63
  568.7 0.7 collective-permute-start.64
  650.8 10.1 %collective-permute-start.65 = (f32[8,2048]{1,0:T(8,128)}, f32[8,2048]{1,0:T(8,128)S(1)}, u32[]{:S(2)}, u32[]{:S(2)}) collective-permute-start(f32[8,2048]{1,0:T(8,128)} %all-reduce.2.cloned.1.call-done), channel_id=1, source_target_pairs={{1,0},{2,3},{5,4},{6,7},{9,8},{10,11},{13,12},{14,15},{17,16},{18,... | collective-permute-start | bytes 196616 | tf_op jit(solution)/shard_map/ppermute | solution.py:171
  (41 other events, 596.2 us)
Sparse Core Ops, SparseCore 0:
  573.9 76.8 all-reduce.1

commit v2 on v1

--- a/solution.py
+++ b/solution.py
@@ -12,7 +12,7 @@
 M = 16
 EPSILON = 1e-05
 AXES = ("section", "tp", "doc")
-VMEM_LIMIT = 48 * 1024 * 1024
+VMEM_LIMIT = 24 * 1024 * 1024
 C_FIRST, C_INIT, C_TP, C_POOL, C_LEN = 0, 1, 2, 3, 4
 
 
@@ -24,16 +24,11 @@
     tok, tok_other, mem, mem_other, gain = refs[2:7]
     weights = refs[7 : 7 + blocks]
     mixed_ref, keep_ref = refs[7 + blocks : 9 + blocks]
-    normed, acc, wbuf, sems = refs[9 + blocks :]
+    normed, acc = refs[9 + blocks :]
     rows = M + tokens
     half = halves.shape[1]
-    depth = wbuf.shape[1]
-    cols = wbuf.shape[2] // 3
-    copies = []
-    for b in range(blocks):
-        copy = pltpu.make_async_copy(weights[b], wbuf.at[b], sems.at[b])
-        copy.start()
-        copies.append(copy)
+    depth = weights[0].shape[0]
+    cols = weights[0].shape[1] // 3
     first = meta[turn, C_FIRST] == 1
     initial = meta[turn, C_INIT] == 1
     tp = meta[turn, C_TP]
@@ -61,12 +56,11 @@
 
     lax.fori_loop(0, docs, prepare, 0)
     for b in range(blocks):
-        copies[b].wait()
         at = pl.multiple_of(where[b] * depth, 128)
         left = normed[:, pl.ds(at, depth)]
         for c in range(3):
             span = pl.ds(c * cols, cols)
-            part = jnp.dot(left, wbuf[b, :, span], preferred_element_type=jnp.float32)
+            part = jnp.dot(left, weights[b][:, span], preferred_element_type=jnp.float32)
             if b == 0:
                 acc[:, span] = part
             else:
@@ -105,26 +99,21 @@
     keep, weight = refs[parts : parts + 2]
     outs = refs[parts + 2 :]
     if pool:
-        out, pooled, wbuf, sems = outs
+        out, pooled = outs
     else:
-        out, wbuf, sems = outs
+        (out,) = outs
     rows = M + tokens
     depth = mixed[0].shape[1]
     width = keep.shape[1]
-    copies = []
-    for b in range(parts):
-        at = pl.multiple_of(place[b] * depth, 128)
-        copy = pltpu.make_async_copy(weight.at[pl.ds(at, depth), :], wbuf.at[b], sems.at[b])
-        copy.start()
-        copies.append(copy)
-    for copy in copies:
-        copy.wait()
     step = min(width, 512)
     for c in range(0, width, step):
         total = keep[:, c : c + step].astype(jnp.float32)
         for b in range(parts):
+            at = pl.multiple_of(place[b] * depth, 128)
             total += jnp.dot(
-                mixed[b][...], wbuf[b, :, c : c + step], preferred_element_type=jnp.float32
+                mixed[b][...],
+                weight[pl.ds(at, depth), c : c + step],
+                preferred_element_type=jnp.float32,
             )
         out[:, c : c + step] = total.astype(jnp.bfloat16)
     if pool:
@@ -170,25 +159,39 @@
     def send(block, pairs):
         return lax.ppermute(block, AXES, [(lin(*a), lin(*b)) for a, b in pairs])
 
+    everyone = [(a, b, c) for a in range(S) for b in range(T) for c in range(D)]
+
+    def mid(move):
+        return [
+            (e, move(*e) if e[2] in planes else ((e[0] + S // 2) % S, e[1], e[2])) for e in everyone
+        ]
+
     def block_of(side):
         return jnp.concatenate(
             [lax.dynamic_slice_in_dim(w[0], side * cols, cols, 1) for w in (w_query, w_key, w_value)],
             1,
         )
 
-    weights = [block_of((z == hi).astype(jnp.int32))]
-    where = [z]
-    for source in range(D):
-        if source == lo:
-            continue
-        pairs = []
-        for a in range(S):
-            for b in range(T):
-                pairs.append(((a, b, source), (a, b, lo)))
-                pairs.append(((a, b, D - 1 - source), (a, b, hi)))
-        weights.append(send(block_of((z == D - 1 - source).astype(jnp.int32)), pairs))
-        where.append(jnp.where(z == hi, D - 1 - source, source))
-    where = jnp.stack(where).astype(jnp.int32)
+    rounds = [c for c in range(D) if c != lo]
+    blocks = [block_of((z == D - 1 - c).astype(jnp.int32)) for c in rounds]
+    own_block = block_of((z == hi).astype(jnp.int32))
+    where = jnp.stack([z] + [jnp.where(z == hi, D - 1 - c, c) for c in rounds]).astype(jnp.int32)
+
+    def relay(parity, sent):
+        moved = []
+        for c, block in zip(rounds, sent):
+            pairs = []
+            for a in range(parity, S, 2):
+                for b in range(T):
+                    pairs.append(((a, b, c), (a, b, lo)))
+                    pairs.append(((a, b, D - 1 - c), (a, b, hi)))
+            moved.append(send(block, pairs))
+        return moved
+
+    even = relay(0, blocks)
+    blocks, token_ids = lax.optimization_barrier((blocks, token_ids))
+    (blocks, even) = lax.optimization_barrier((blocks, even))
+    odd = relay(1, blocks)
 
     packed = jnp.concatenate([token_ids, seg_lengths[:, :, None]], 2)
     packed = lax.all_gather(packed, "doc", axis=0, tiled=True)
@@ -197,6 +200,8 @@
     vocab = emb_table.shape[0]
     tok, tok_other = [], []
     for seg in range(segs):
+        if seg == 1:
+            ids, even = lax.optimization_barrier((ids, even))
         local = ids[:, seg].reshape(-1) - s * vocab
         owned = (local >= 0) & (local < vocab)
         picked = jnp.take(emb_table, jnp.clip(local, 0, vocab - 1), axis=0)
@@ -231,14 +236,16 @@
 
     smem = pl.BlockSpec(memory_space=pltpu.SMEM)
     vmem = pl.BlockSpec(memory_space=pltpu.VMEM)
-    anyw = pl.BlockSpec(memory_space=pl.ANY)
     out_proj = w_out[0]
     parts = len(shifts)
 
     own = jnp.zeros((R, half), jnp.bfloat16)
     other = jnp.zeros((R, half), jnp.bfloat16)
     pools = []
+    weights = [own_block] + even
     for k in range(turns):
+        if k == 1:
+            weights = [own_block] + [a + b for a, b in zip(even, odd)]
         g, seg = k % S, k // S
         rows_of = slice(g * n * tokens, (g + 1) * n * tokens)
         tk, tko = (a[min(seg, segs - 1)][rows_of] for a in (tok, tok_other))
@@ -248,26 +255,20 @@
                 jax.ShapeDtypeStruct((R, cols), jnp.bfloat16),
                 jax.ShapeDtypeStruct((R, half), jnp.bfloat16),
             ),
-            in_specs=[smem, smem] + [vmem] * 7 + [anyw] * D,
+            in_specs=[smem, smem] + [vmem] * (7 + D),
             out_specs=(vmem, vmem),
             scratch_shapes=[
                 pltpu.VMEM((R, 2 * half), jnp.bfloat16),
                 pltpu.VMEM((R, 3 * cols), jnp.float32),
-                pltpu.VMEM((D, depth, 3 * cols), jnp.bfloat16),
-                pltpu.SemaphoreType.DMA((D,)),
             ],
             compiler_params=pltpu.CompilerParams(vmem_limit_bytes=VMEM_LIMIT),
         )(meta, where, own, other, tk, tko, mem_init, mem_other, norm_gain, *weights)
-        live = [a for a in range(S) if 0 <= k - a < segs * S]
         shared = [mixed]
         for j, i in shifts[1:]:
-            pairs = [
-                ((a, (b + j) % T, planes[(c + i) % 2]), (a, b, planes[c]))
-                for a in live
-                for b in range(T)
-                for c in range(2)
-            ]
-            shared.append(send(mixed, pairs))
+            def back(a, b, c):
+                return (a, (b - j) % T, planes[(planes.index(c) + i) % 2])
+
+            shared.append(send(mixed, mid(back)))
         pool = k >= (segs - 1) * S
         shapes = [jax.ShapeDtypeStruct((R, half), jnp.bfloat16)]
         if pool:
@@ -275,41 +276,26 @@
         result = pl.pallas_call(
             functools.partial(project_kernel, k, n, tokens, parts, pool),
             out_shape=tuple(shapes),
-            in_specs=[smem, smem, smem] + [vmem] * (parts + 1) + [anyw],
+            in_specs=[smem, smem, smem] + [vmem] * (parts + 2),
             out_specs=tuple([vmem] * len(shapes)),
-            scratch_shapes=[
-                pltpu.VMEM((parts, cols, half), jnp.bfloat16),
-                pltpu.SemaphoreType.DMA((parts,)),
-            ],
             compiler_params=pltpu.CompilerParams(vmem_limit_bytes=VMEM_LIMIT),
         )(meta, place, layer_mix, *shared, keep, out_proj)
         if pool:
             pools.append(result[1])
-        goes = [a for a in live if not (a == S - 1 and (k - a) // S == segs - 1)]
-        if goes:
-            own = send(
-                result[0],
-                [((a, b, c), ((a + 1) % S, b, c)) for a in goes for b in range(T) for c in planes],
-            )
-            other = send(
-                result[0],
-                [
-                    ((a, b, c), ((a + 1) % S, T - 1 - b, c))
-                    for a in goes
-                    for b in range(T)
-                    for c in planes
-                ],
-            )
+        if k < turns - 1:
+            own = send(result[0], [(e, ((e[0] + 1) % S, e[1], e[2])) for e in everyone])
+            other = send(result[0], [(e, ((e[0] + 1) % S, T - 1 - e[1], e[2])) for e in everyone])
 
     mine = lax.dynamic_slice_in_dim(jnp.stack(pools), s, S, 0).reshape(docs, half)
-    mine = jnp.where((z == lo) | (z == hi), mine, 0.0)
-    total = lax.psum(mine, "section")
+    total = mine
+    for a in range(1, S):
+        total = total + send(mine, [(e, ((e[0] + a) % S, e[1], e[2])) for e in everyone])
     spread = total
     for k in range(1, D // 2):
-        pairs = [
-            ((a, b, c), (a, b, c + e)) for a in range(S) for b in range(T) for c, e in ((lo, -k), (hi, k))
-        ]
-        spread = spread + send(total, pairs)
+        ends = ((lo, lo - k), (hi, hi + k))
+        pairs = [((a, b, c), (a, b, e)) for a in range(S) for b in range(T) for c, e in ends]
+        got = send(total, pairs + [(e, c) for c, e in pairs])
+        spread = jnp.where((z == lo - k) | (z == hi + k), got, spread)
     return spread
 
 

time: 680 us -> 528 us (0.78)
  starting transfers between devices: 278 us -> 124 us
  Pallas kernels: 131 us -> 74.2 us
  blocking collectives: 13.5 us -> 70.1 us
  local copies, waits for them, and re-layouts: 39.8 us -> 56.9 us
  between operations: 16.2 us -> 1.6 us
  other arithmetic: 16.8 us -> 30 us
  waiting for transfers between devices: 175 us -> 165 us
    ppermute x66 -> x72, starting transfers between devices: 278 us -> 124 us  [send(): return lax.ppermute(block, AXES, [(lin(*a), lin(*b)) for a, b in pairs])]
    psum x1 -> x0, waiting for transfers between devices: 77 us -> none  [body(): total = lax.psum(mine, 'section')]
    ppermute x66 -> x72, waiting for transfers between devices: 97.8 us -> 165 us  [send(): return lax.ppermute(block, AXES, [(lin(*a), lin(*b)) for a, b in pairs])]
    all_gather x1, blocking collectives: 13.5 us -> 70.1 us  [body(): packed = lax.all_gather(packed, 'doc', axis=0, tiled=True)]
    pallas_call x10, Pallas kernels: 58.2 us -> 22.4 us  [body(): pl.pallas_call(functools.partial(project_kernel, k, n, tokens, parts, poo...]
    pallas_call x11, Pallas kernels: 72.6 us -> 51.8 us  [body(): pl.pallas_call(functools.partial(attend_kernel, k, n, tokens, D), out_sha...]
    unnamed x82 -> x114, local copies, waits for them, and re-layouts: 3.67 us -> 17.7 us
    add x1 -> x4, other arithmetic: 1.48 us -> 12.6 us  [the longest x3 12.6 us: body(): weights = [own_block] + [a + b for a, b in zip(even, odd)]]
  transfers between devices with their start and end apart: 67 -> 72, of which waited for: 4 -> 53; matrix products, arithmetic and copies ran while one was open for 5% -> 8% of each run, Pallas kernels for 7% -> 5%
where the time goes in v2:
time: 528 us; the launch traced here: 521 us
  waiting for transfers between devices  165 us (31%)
  starting transfers between devices  124 us (23%)
  Pallas kernels  74.2 us (14%)
  blocking collectives  70.1 us (13%)
  local copies, waits for them, and re-layouts  56.9 us (11%)
  other arithmetic  30 us (6%)
    ppermute x72, waiting for transfers between devices, send(): return lax.ppermute(block, AXES, [(lin(*a), lin(*b)) for a, b in pairs])  165 us
    ppermute x72, starting transfers between devices, send(): return lax.ppermute(block, AXES, [(lin(*a), lin(*b)) for a, b in pairs])  124 us
    all_gather x1, blocking collectives, body(): packed = lax.all_gather(packed, 'doc', axis=0, tiled=True)  70.1 us
    pallas_call x11, Pallas kernels, body(): pl.pallas_call(functools.partial(attend_kernel, k, n, tokens, D), out_sha...  51.8 us
    gather x2, local copies, waits for them, and re-layouts, body(): picked = jnp.take(emb_table, jnp.clip(local, 0, vocab - 1), axis=0)  23.6 us
    pallas_call x10, Pallas kernels, body(): pl.pallas_call(functools.partial(project_kernel, k, n, tokens, parts, poo...  22.4 us
    unnamed x114, local copies, waits for them, and re-layouts  17.7 us
    add x3, other arithmetic, body(): weights = [own_block] + [a + b for a, b in zip(even, odd)]  12.6 us
  transfers between devices with their start and end apart: 72, of which 53 were waited for; matrix products, arithmetic and copies ran while one was open for 8% of the time, Pallas kernels for 5%

profile of v2, /device:TPU:0, one launch (start us, length us, event | category | flops | bytes accessed | tf_op | source)
XLA Modules:
  0.0 521.2 jit_solution(7095860447058928850)
XLA Ops:
  0.0 3.6 dynamic-slice_bitcast_fusion
  8.7 5.1 collective-permute-start.5
  15.6 2.3 collective-permute-start.6
  19.7 3.9 collective-permute-start.7
  23.7 70.1 %all_gather.3 = s32[8,2,33]{2,1,0:T(2,128)S(1)} all-gather(s32[2,2,33]{2,1,0:T(2,128)S(1)} %pad_add_fusion), channel_id=1, replica_groups=mesh['section'=4,'tp'=2,'doc'=4] {'doc'}, dimensions={0}, use_global_device_ids=true | all-gather | bytes 2640 | tf_op jit(solution)/shard_map/all_gather | solution.py:197
  94.2 12.3 %gather_fusion.1 = bf16[256,2048]{1,0:T(8,128)(2,1)} fusion(bf16[4096,2048]{1,0:T(8,128)(2,1)} %param.14, s32[1024]{0:T(1024)S(1)} %pad_clamp_fusion.1), kind=kCustom, calls=%fused_computation.clone | custom fusion | bytes 2098176 | tf_op jit(solution)/shard_map/jit(_take)/gather | solution.py:207
  111.0 2.4 collective-permute-start.13
  114.4 2.3 collective-permute-start.14
  116.7 2.4 collective-permute-start.15
  119.1 2.9 add_add_fusion.1
  127.2 11.3 %gather_fusion.2 = bf16[256,2048]{1,0:T(8,128)(2,1)} fusion(bf16[4096,2048]{1,0:T(8,128)(2,1)} %param.14, s32[1024]{0:T(1024)S(1)} %pad_clamp_fusion), kind=kCustom, calls=%fused_computation.1.clone | custom fusion | bytes 2098176 | tf_op jit(solution)/shard_map/jit(_take)/gather | solution.py:207
  138.5 2.2 fusion.26
  142.9 6.7 %shard_map.100 = (bf16[96,512]{1,0:T(8,128)(2,1)S(1)}, bf16[96,2048]{1,0:T(8,128)(2,1)S(1)}) custom-call(s32[11,6]{1,0:T(8,128)S(1)} %concatenate.26.meta, s32[4]{0:T(128)S(1)} %pad_add_fusion.2.where, bf16[96,2048]{1,0:T(8,128)(2,1)S(1)} %broadcast_15_refs_0__refs_1_.2.refs_0_.refs_1_, bf16[96,2048]{1,0:T(8,128)(2,1)S(1)} %broadcast_15_refs_0__refs_1_.2.refs_0_.refs_1_, ...), custom_call_target="tpu_custom_call" | custom-call | tf_op jit(solution)/shard_map/pallas_call | solution.py:252
  152.5 2.5 collective-permute-done.8.refs_1_
  156.4 2.4 select_select_fusion
  165.8 3.4 copy-done
  174.2 15.6 %collective-permute-start.11 = (bf16[96,2048]{1,0:T(8,128)(2,1)S(1)}, bf16[96,2048]{1,0:T(8,128)(2,1)S(1)}, u32[]{:S(2)}, u32[]{:S(2)}) collective-permute-start(bf16[96,2048]{1,0:T(8,128)(2,1)S(1)} %shard_map.101), channel_id=1, source_target_pairs={{0,8},{1,9},{2,10},{3,11},{4,12},{5,13},{6,14},{7,15},{8,16},{9,17... | collective-permute-start | bytes 1179656 | tf_op jit(solution)/shard_map/ppermute | solution.py:160
  191.2 2.9 add.155.refs_8_
  194.1 4.8 add.156.refs_9_
  199.0 4.8 add.157.refs_10_
  203.9 4.5 shard_map.102
  210.4 3.5 collective-permute-done.16.refs_1_
  215.4 3.2 collective-permute-done.18.refs_3_
  225.0 3.1 collective-permute-done.19.refs_0_
  228.0 4.3 collective-permute-done.20.refs_1_
  232.3 4.4 shard_map.104
  239.8 2.6 collective-permute-done.21.refs_1_
  250.4 5.6 %collective-permute-done.24.refs_0_ = bf16[96,2048]{1,0:T(8,128)(2,1)S(1)} collective-permute-done((bf16[96,2048]{1,0:T(8,128)(2,1)S(1)}, bf16[96,2048]{1,0:T(8,128)(2,1)S(1)}, u32[]{:S(2)}, u32[]{:S(2)}) %collective-permute-start.24) | collective-permute-done | bytes 393248 | tf_op jit(solution)/shard_map/ppermute | solution.py:160
  256.0 4.5 collective-permute-done.25.refs_1_
  260.5 4.5 shard_map.106
  268.1 2.5 collective-permute-done.26.refs_1_
  278.7 5.5 %collective-permute-done.29.refs_0_ = bf16[96,2048]{1,0:T(8,128)(2,1)S(1)} collective-permute-done((bf16[96,2048]{1,0:T(8,128)(2,1)S(1)}, bf16[96,2048]{1,0:T(8,128)(2,1)S(1)}, u32[]{:S(2)}, u32[]{:S(2)}) %collective-permute-start.29) | collective-permute-done | bytes 393248 | tf_op jit(solution)/shard_map/ppermute | solution.py:160
  284.2 4.6 collective-permute-done.30.refs_1_
  288.8 4.4 shard_map.108
  296.4 2.6 collective-permute-done.35.refs_1_
  306.9 5.6 %collective-permute-done.38.refs_0_ = bf16[96,2048]{1,0:T(8,128)(2,1)S(1)} collective-permute-done((bf16[96,2048]{1,0:T(8,128)(2,1)S(1)}, bf16[96,2048]{1,0:T(8,128)(2,1)S(1)}, u32[]{:S(2)}, u32[]{:S(2)}) %collective-permute-start.38) | collective-permute-done | bytes 393248 | tf_op jit(solution)/shard_map/ppermute | solution.py:160
  312.4 4.7 collective-permute-done.39.refs_1_
  317.1 4.4 shard_map.110
  324.7 2.6 collective-permute-done.40.refs_1_
  335.5 5.2 collective-permute-done.43.refs_0_
  340.7 4.6 collective-permute-done.44.refs_1_
  345.3 4.5 shard_map.112
  352.9 2.5 collective-permute-done.45.refs_1_
  363.7 5.4 %collective-permute-done.48.refs_0_ = bf16[96,2048]{1,0:T(8,128)(2,1)S(1)} collective-permute-done((bf16[96,2048]{1,0:T(8,128)(2,1)S(1)}, bf16[96,2048]{1,0:T(8,128)(2,1)S(1)}, u32[]{:S(2)}, u32[]{:S(2)}) %collective-permute-start.48) | collective-permute-done | bytes 393248 | tf_op jit(solution)/shard_map/ppermute | solution.py:160
  369.1 4.8 collective-permute-done.49.refs_1_
  374.0 5.1 shard_map.114
  382.9 2.9 collective-permute-done.50.refs_1_
  389.6 3.4 copy-done.1
  394.0 2.8 shard_map.115
  398.7 5.4 %collective-permute-done.53.refs_0_ = bf16[96,2048]{1,0:T(8,128)(2,1)S(1)} collective-permute-done((bf16[96,2048]{1,0:T(8,128)(2,1)S(1)}, bf16[96,2048]{1,0:T(8,128)(2,1)S(1)}, u32[]{:S(2)}, u32[]{:S(2)}) %collective-permute-start.53) | collective-permute-done | bytes 393248 | tf_op jit(solution)/shard_map/ppermute | solution.py:160
  404.1 4.8 collective-permute-done.54.refs_1_
  412.7 4.4 shard_map.116
  420.3 2.5 collective-permute-done.55.refs_1_
  430.9 5.2 %collective-permute-done.58.refs_0_ = bf16[96,2048]{1,0:T(8,128)(2,1)S(1)} collective-permute-done((bf16[96,2048]{1,0:T(8,128)(2,1)S(1)}, bf16[96,2048]{1,0:T(8,128)(2,1)S(1)}, u32[]{:S(2)}, u32[]{:S(2)}) %collective-permute-start.58) | collective-permute-done | bytes 393248 | tf_op jit(solution)/shard_map/ppermute | solution.py:160
  436.1 4.8 collective-permute-done.59.refs_1_
  441.0 4.4 shard_map.118
  448.5 2.6 collective-permute-done.60.refs_1_
  459.1 5.4 %collective-permute-done.63.refs_0_ = bf16[96,2048]{1,0:T(8,128)(2,1)S(1)} collective-permute-done((bf16[96,2048]{1,0:T(8,128)(2,1)S(1)}, bf16[96,2048]{1,0:T(8,128)(2,1)S(1)}, u32[]{:S(2)}, u32[]{:S(2)}) %collective-permute-start.63) | collective-permute-done | bytes 393248 | tf_op jit(solution)/shard_map/ppermute | solution.py:160
  464.5 4.8 collective-permute-done.64.refs_1_
  469.3 4.5 shard_map.120
  476.9 2.5 collective-permute-done.65
  483.3 3.0 shard_map.121
  489.0 2.9 collective-permute-done.69
  492.1 26.0 %collective-permute-start.71 = (f32[8,2048]{1,0:T(8,128)S(1)}, f32[8,2048]{1,0:T(8,128)S(1)}, u32[]{:S(2)}, u32[]{:S(2)}) collective-permute-start(f32[8,2048]{1,0:T(8,128)S(1)} %add_add_fusion.2), channel_id=1, source_target_pairs={{1,0},{2,3},{5,4},{6,7},{9,8},{10,11},{13,12},{14,15},{17,16},{18,... | collective-permute-start | bytes 196616 | tf_op jit(solution)/shard_map/ppermute | solution.py:160
  (269 shorter events, 154.2 us)
Async XLA Ops:
  8.7 85.3 %collective-permute-start.5 = (bf16[1024,1536]{1,0:T(8,128)(2,1)}, bf16[1024,1536]{1,0:T(8,128)(2,1)S(1)}, u32[]{:S(2)}, u32[]{:S(2)}) collective-permute-start(bf16[1024,1536]{1,0:T(8,128)(2,1)} %pad_maximum_fusion), channel_id=1, source_target_pairs={{0,1},{3,2},{4,5},{7,6},{16,17},{19,18},{20,21},{23,22}} | collective-permute-start | bytes 9437192 | tf_op jit(solution)/shard_map/ppermute | solution.py:160
  15.6 78.4 %collective-permute-start.6 = (bf16[1024,1536]{1,0:T(8,128)(2,1)}, bf16[1024,1536]{1,0:T(8,128)(2,1)}, u32[]{:S(2)}, u32[]{:S(2)}) collective-permute-start(bf16[1024,1536]{1,0:T(8,128)(2,1)} %pad_maximum_fusion.1), channel_id=1, source_target_pairs={{2,1},{1,2},{6,5},{5,6},{18,17},{17,18},{22,21},{21,22}} | collective-permute-start | bytes 9437192 | tf_op jit(solution)/shard_map/ppermute | solution.py:160
  19.7 74.3 %collective-permute-start.7 = (bf16[1024,1536]{1,0:T(8,128)(2,1)}, bf16[1024,1536]{1,0:T(8,128)(2,1)}, u32[]{:S(2)}, u32[]{:S(2)}) collective-permute-start(bf16[1024,1536]{1,0:T(8,128)(2,1)} %pad_maximum_fusion.2), channel_id=1, source_target_pairs={{3,1},{0,2},{7,5},{4,6},{19,17},{16,18},{23,21},{20,22}} | collective-permute-start | bytes 9437192 | tf_op jit(solution)/shard_map/ppermute | solution.py:160
  107.9 6.5 %collective-permute-start.2 = (bf16[256,2048]{1,0:T(8,128)(2,1)S(1)}, bf16[256,2048]{1,0:T(8,128)(2,1)S(1)}, u32[]{:S(2)}, u32[]{:S(2)}) collective-permute-start(bf16[256,2048]{1,0:T(8,128)(2,1)S(1)} %select_select_fusion.1), channel_id=1, source_target_pairs={{25,1},{26,2},{29,5},{30,6}} | collective-permute-start | bytes 3145736 | tf_op jit(solution)/shard_map/ppermute | solution.py:160
  108.7 8.1 %collective-permute-start.1 = (bf16[256,2048]{1,0:T(8,128)(2,1)S(1)}, bf16[256,2048]{1,0:T(8,128)(2,1)S(1)}, u32[]{:S(2)}, u32[]{:S(2)}) collective-permute-start(bf16[256,2048]{1,0:T(8,128)(2,1)S(1)} %select_select_fusion.1), channel_id=1, source_target_pairs={{17,1},{18,2},{21,5},{22,6}} | collective-permute-start | bytes 3145736 | tf_op jit(solution)/shard_map/ppermute | solution.py:160
  109.4 9.7 %collective-permute-start = (bf16[256,2048]{1,0:T(8,128)(2,1)S(1)}, bf16[256,2048]{1,0:T(8,128)(2,1)}, u32[]{:S(2)}, u32[]{:S(2)}) collective-permute-start(bf16[256,2048]{1,0:T(8,128)(2,1)S(1)} %select_select_fusion.1), channel_id=1, source_target_pairs={{9,1},{10,2},{13,5},{14,6}} | collective-permute-start | bytes 3145736 | tf_op jit(solution)/shard_map/ppermute | solution.py:160
  111.0 52.4 %collective-permute-start.13 = (bf16[1024,1536]{1,0:T(8,128)(2,1)}, bf16[1024,1536]{1,0:T(8,128)(2,1)}, u32[]{:S(2)}, u32[]{:S(2)}) collective-permute-start(bf16[1024,1536]{1,0:T(8,128)(2,1)} %pad_maximum_fusion), channel_id=1, source_target_pairs={{8,9},{11,10},{12,13},{15,14},{24,25},{27,26},{28,29},{31,30}} | collective-permute-start | bytes 9437192 | tf_op jit(solution)/shard_map/ppermute | solution.py:160
  113.4 29.4 %collective-permute-start.4 = (bf16[16,2048]{1,0:T(8,128)(2,1)S(1)}, bf16[16,2048]{1,0:T(8,128)(2,1)S(1)}, u32[]{:S(2)}, u32[]{:S(2)}) collective-permute-start(bf16[16,2048]{1,0:T(8,128)(2,1)S(1)} %copy-done.11), channel_id=1, source_target_pairs={{1,5},{2,6},{5,1},{6,2}} | collective-permute-start | bytes 196616 | tf_op jit(solution)/shard_map/ppermute | solution.py:160
  114.4 59.8 %collective-permute-start.14 = (bf16[1024,1536]{1,0:T(8,128)(2,1)}, bf16[1024,1536]{1,0:T(8,128)(2,1)}, u32[]{:S(2)}, u32[]{:S(2)}) collective-permute-start(bf16[1024,1536]{1,0:T(8,128)(2,1)} %pad_maximum_fusion.1), channel_id=1, source_target_pairs={{10,9},{9,10},{14,13},{13,14},{26,25},{25,26},{30,29},{29,30}} | collective-permute-start | bytes 9437192 | tf_op jit(solution)/shard_map/ppermute | solution.py:160
  116.7 73.1 %collective-permute-start.15 = (bf16[1024,1536]{1,0:T(8,128)(2,1)}, bf16[1024,1536]{1,0:T(8,128)(2,1)}, u32[]{:S(2)}, u32[]{:S(2)}) collective-permute-start(bf16[1024,1536]{1,0:T(8,128)(2,1)} %pad_maximum_fusion.2), channel_id=1, source_target_pairs={{11,9},{8,10},{15,13},{12,14},{27,25},{24,26},{31,29},{28,30}} | collective-permute-start | bytes 9437192 | tf_op jit(solution)/shard_map/ppermute | solution.py:160
  122.0 18.7 %collective-permute-start.3 = (bf16[256,2048]{1,0:T(8,128)(2,1)}, bf16[256,2048]{1,0:T(8,128)(2,1)}, u32[]{:S(2)}, u32[]{:S(2)}) collective-permute-start(bf16[256,2048]{1,0:T(8,128)(2,1)} %add_add_fusion.1), channel_id=1, source_target_pairs={{1,5},{2,6},{5,1},{6,2}} | collective-permute-start | bytes 3145736 | tf_op jit(solution)/shard_map/ppermute | solution.py:160
  151.9 6.9 %collective-permute-start.9 = (bf16[96,512]{1,0:T(8,128)(2,1)S(1)}, bf16[96,512]{1,0:T(8,128)(2,1)S(1)}, u32[]{:S(2)}, u32[]{:S(2)}) collective-permute-start(bf16[96,512]{1,0:T(8,128)(2,1)S(1)} %get-tuple-element.65.refs_0_), channel_id=1, source_target_pairs={{0,16},{1,2},{2,1},{3,19},{4,20},{5,6},{6,5},{7,23},{8,24},{9,10},... | collective-permute-start | bytes 294920 | tf_op jit(solution)/shard_map/ppermute | solution.py:160
  154.9 6.2 %collective-permute-start.10 = (bf16[96,512]{1,0:T(8,128)(2,1)S(1)}, bf16[96,512]{1,0:T(8,128)(2,1)S(1)}, u32[]{:S(2)}, u32[]{:S(2)}) collective-permute-start(bf16[96,512]{1,0:T(8,128)(2,1)S(1)} %get-tuple-element.65.refs_0_), channel_id=1, source_target_pairs={{0,16},{1,6},{2,5},{3,19},{4,20},{5,2},{6,1},{7,23},{8,24},{9,14},... | collective-permute-start | bytes 294920 | tf_op jit(solution)/shard_map/ppermute | solution.py:160
  159.5 62.5 %collective-permute-start.33 = (bf16[256,2048]{1,0:T(8,128)(2,1)}, bf16[256,2048]{1,0:T(8,128)(2,1)}, u32[]{:S(2)}, u32[]{:S(2)}) collective-permute-start(bf16[256,2048]{1,0:T(8,128)(2,1)} %select_select_fusion), channel_id=1, source_target_pairs={{25,1},{26,2},{29,5},{30,6}} | collective-permute-start | bytes 3145736 | tf_op jit(solution)/shard_map/ppermute | solution.py:160
  161.8 60.2 %collective-permute-start.32 = (bf16[256,2048]{1,0:T(8,128)(2,1)}, bf16[256,2048]{1,0:T(8,128)(2,1)}, u32[]{:S(2)}, u32[]{:S(2)}) collective-permute-start(bf16[256,2048]{1,0:T(8,128)(2,1)} %select_select_fusion), channel_id=1, source_target_pairs={{17,1},{18,2},{21,5},{22,6}} | collective-permute-start | bytes 3145736 | tf_op jit(solution)/shard_map/ppermute | solution.py:160
  163.4 58.6 %collective-permute-start.31 = (bf16[256,2048]{1,0:T(8,128)(2,1)}, bf16[256,2048]{1,0:T(8,128)(2,1)}, u32[]{:S(2)}, u32[]{:S(2)}) collective-permute-start(bf16[256,2048]{1,0:T(8,128)(2,1)} %select_select_fusion), channel_id=1, source_target_pairs={{9,1},{10,2},{13,5},{14,6}} | collective-permute-start | bytes 3145736 | tf_op jit(solution)/shard_map/ppermute | solution.py:160
  174.2 29.6 %collective-permute-start.11 = (bf16[96,2048]{1,0:T(8,128)(2,1)S(1)}, bf16[96,2048]{1,0:T(8,128)(2,1)S(1)}, u32[]{:S(2)}, u32[]{:S(2)}) collective-permute-start(bf16[96,2048]{1,0:T(8,128)(2,1)S(1)} %shard_map.101), channel_id=1, source_target_pairs={{0,8},{1,9},{2,10},{3,11},{4,12},{5,13},{6,14},{7,15},{8,16},{9,17... | collective-permute-start | bytes 1179656 | tf_op jit(solution)/shard_map/ppermute | solution.py:160
  189.8 14.0 %collective-permute-start.12 = (bf16[96,2048]{1,0:T(8,128)(2,1)S(1)}, bf16[96,2048]{1,0:T(8,128)(2,1)S(1)}, u32[]{:S(2)}, u32[]{:S(2)}) collective-permute-start(bf16[96,2048]{1,0:T(8,128)(2,1)S(1)} %shard_map.101), channel_id=1, source_target_pairs={{0,12},{1,13},{2,14},{3,15},{4,8},{5,9},{6,10},{7,11},{8,20},{9,21... | collective-permute-start | bytes 1179656 | tf_op jit(solution)/shard_map/ppermute | solution.py:160
  208.7 6.7 %collective-permute-start.17 = (bf16[96,512]{1,0:T(8,128)(2,1)S(1)}, bf16[96,512]{1,0:T(8,128)(2,1)S(1)}, u32[]{:S(2)}, u32[]{:S(2)}) collective-permute-start(bf16[96,512]{1,0:T(8,128)(2,1)S(1)} %get-tuple-element.70.refs_0_), channel_id=1, source_target_pairs={{0,16},{1,2},{2,1},{3,19},{4,20},{5,6},{6,5},{7,23},{8,24},{9,10},... | collective-permute-start | bytes 294920 | tf_op jit(solution)/shard_map/ppermute | solution.py:160
  220.8 7.3 %collective-permute-start.19 = (bf16[96,2048]{1,0:T(8,128)(2,1)S(1)}, bf16[96,2048]{1,0:T(8,128)(2,1)S(1)}, u32[]{:S(2)}, u32[]{:S(2)}) collective-permute-start(bf16[96,2048]{1,0:T(8,128)(2,1)S(1)} %shard_map.103), channel_id=1, source_target_pairs={{0,8},{1,9},{2,10},{3,11},{4,12},{5,13},{6,14},{7,15},{8,16},{9,17... | collective-permute-start | bytes 1179656 | tf_op jit(solution)/shard_map/ppermute | solution.py:160
  220.8 11.4 %collective-permute-start.20 = (bf16[96,2048]{1,0:T(8,128)(2,1)S(1)}, bf16[96,2048]{1,0:T(8,128)(2,1)S(1)}, u32[]{:S(2)}, u32[]{:S(2)}) collective-permute-start(bf16[96,2048]{1,0:T(8,128)(2,1)S(1)} %shard_map.103), channel_id=1, source_target_pairs={{0,12},{1,13},{2,14},{3,15},{4,8},{5,9},{6,10},{7,11},{8,20},{9,21... | collective-permute-start | bytes 1179656 | tf_op jit(solution)/shard_map/ppermute | solution.py:160
  224.2 54.4 %collective-permute-start.34 = (bf16[256,2048]{1,0:T(8,128)(2,1)S(1)}, bf16[256,2048]{1,0:T(8,128)(2,1)S(1)}, u32[]{:S(2)}, u32[]{:S(2)}) collective-permute-start(bf16[256,2048]{1,0:T(8,128)(2,1)S(1)} %add_add_fusion), channel_id=1, source_target_pairs={{1,5},{2,6},{5,1},{6,2}} | collective-permute-start | bytes 3145736 | tf_op jit(solution)/shard_map/ppermute | solution.py:160
  237.7 6.7 %collective-permute-start.22 = (bf16[96,512]{1,0:T(8,128)(2,1)S(1)}, bf16[96,512]{1,0:T(8,128)(2,1)S(1)}, u32[]{:S(2)}, u32[]{:S(2)}) collective-permute-start(bf16[96,512]{1,0:T(8,128)(2,1)S(1)} %get-tuple-element.72.refs_0_), channel_id=1, source_target_pairs={{0,16},{1,2},{2,1},{3,19},{4,20},{5,6},{6,5},{7,23},{8,24},{9,10},... | collective-permute-start | bytes 294920 | tf_op jit(solution)/shard_map/ppermute | solution.py:160
  238.8 7.8 %collective-permute-start.23 = (bf16[96,512]{1,0:T(8,128)(2,1)S(1)}, bf16[96,512]{1,0:T(8,128)(2,1)S(1)}, u32[]{:S(2)}, u32[]{:S(2)}) collective-permute-start(bf16[96,512]{1,0:T(8,128)(2,1)S(1)} %get-tuple-element.72.refs_0_), channel_id=1, source_target_pairs={{0,16},{1,6},{2,5},{3,19},{4,20},{5,2},{6,1},{7,23},{8,24},{9,14},... | collective-permute-start | bytes 294920 | tf_op jit(solution)/shard_map/ppermute | solution.py:160
  248.7 7.3 %collective-permute-start.24 = (bf16[96,2048]{1,0:T(8,128)(2,1)S(1)}, bf16[96,2048]{1,0:T(8,128)(2,1)S(1)}, u32[]{:S(2)}, u32[]{:S(2)}) collective-permute-start(bf16[96,2048]{1,0:T(8,128)(2,1)S(1)} %shard_map.105), channel_id=1, source_target_pairs={{0,8},{1,9},{2,10},{3,11},{4,12},{5,13},{6,14},{7,15},{8,16},{9,17... | collective-permute-start | bytes 1179656 | tf_op jit(solution)/shard_map/ppermute | solution.py:160
  248.9 11.6 %collective-permute-start.25 = (bf16[96,2048]{1,0:T(8,128)(2,1)S(1)}, bf16[96,2048]{1,0:T(8,128)(2,1)S(1)}, u32[]{:S(2)}, u32[]{:S(2)}) collective-permute-start(bf16[96,2048]{1,0:T(8,128)(2,1)S(1)} %shard_map.105), channel_id=1, source_target_pairs={{0,12},{1,13},{2,14},{3,15},{4,8},{5,9},{6,10},{7,11},{8,20},{9,21... | collective-permute-start | bytes 1179656 | tf_op jit(solution)/shard_map/ppermute | solution.py:160
  264.9 5.7 %collective-permute-start.26 = (bf16[96,512]{1,0:T(8,128)(2,1)S(1)}, bf16[96,512]{1,0:T(8,128)(2,1)S(1)}, u32[]{:S(2)}, u32[]{:S(2)}) collective-permute-start(bf16[96,512]{1,0:T(8,128)(2,1)S(1)} %get-tuple-element.74.refs_0_), channel_id=1, source_target_pairs={{0,16},{1,5},{2,6},{3,19},{4,20},{5,1},{6,2},{7,23},{8,24},{9,13},... | collective-permute-start | bytes 294920 | tf_op jit(solution)/shard_map/ppermute | solution.py:160
  266.0 6.8 %collective-permute-start.27 = (bf16[96,512]{1,0:T(8,128)(2,1)S(1)}, bf16[96,512]{1,0:T(8,128)(2,1)S(1)}, u32[]{:S(2)}, u32[]{:S(2)}) collective-permute-start(bf16[96,512]{1,0:T(8,128)(2,1)S(1)} %get-tuple-element.74.refs_0_), channel_id=1, source_target_pairs={{0,16},{1,2},{2,1},{3,19},{4,20},{5,6},{6,5},{7,23},{8,24},{9,10},... | collective-permute-start | bytes 294920 | tf_op jit(solution)/shard_map/ppermute | solution.py:160
  267.0 7.8 %collective-permute-start.28 = (bf16[96,512]{1,0:T(8,128)(2,1)S(1)}, bf16[96,512]{1,0:T(8,128)(2,1)S(1)}, u32[]{:S(2)}, u32[]{:S(2)}) collective-permute-start(bf16[96,512]{1,0:T(8,128)(2,1)S(1)} %get-tuple-element.74.refs_0_), channel_id=1, source_target_pairs={{0,16},{1,6},{2,5},{3,19},{4,20},{5,2},{6,1},{7,23},{8,24},{9,14},... | collective-permute-start | bytes 294920 | tf_op jit(solution)/shard_map/ppermute | solution.py:160
  277.0 7.3 %collective-permute-start.29 = (bf16[96,2048]{1,0:T(8,128)(2,1)S(1)}, bf16[96,2048]{1,0:T(8,128)(2,1)S(1)}, u32[]{:S(2)}, u32[]{:S(2)}) collective-permute-start(bf16[96,2048]{1,0:T(8,128)(2,1)S(1)} %shard_map.107), channel_id=1, source_target_pairs={{0,8},{1,9},{2,10},{3,11},{4,12},{5,13},{6,14},{7,15},{8,16},{9,17... | collective-permute-start | bytes 1179656 | tf_op jit(solution)/shard_map/ppermute | solution.py:160
  277.1 11.8 %collective-permute-start.30 = (bf16[96,2048]{1,0:T(8,128)(2,1)S(1)}, bf16[96,2048]{1,0:T(8,128)(2,1)S(1)}, u32[]{:S(2)}, u32[]{:S(2)}) collective-permute-start(bf16[96,2048]{1,0:T(8,128)(2,1)S(1)} %shard_map.107), channel_id=1, source_target_pairs={{0,12},{1,13},{2,14},{3,15},{4,8},{5,9},{6,10},{7,11},{8,20},{9,21... | collective-permute-start | bytes 1179656 | tf_op jit(solution)/shard_map/ppermute | solution.py:160
  293.3 5.7 %collective-permute-start.35 = (bf16[96,512]{1,0:T(8,128)(2,1)S(1)}, bf16[96,512]{1,0:T(8,128)(2,1)S(1)}, u32[]{:S(2)}, u32[]{:S(2)}) collective-permute-start(bf16[96,512]{1,0:T(8,128)(2,1)S(1)} %get-tuple-element.77.refs_0_), channel_id=1, source_target_pairs={{0,16},{1,5},{2,6},{3,19},{4,20},{5,1},{6,2},{7,23},{8,24},{9,13},... | collective-permute-start | bytes 294920 | tf_op jit(solution)/shard_map/ppermute | solution.py:160
  294.4 6.8 %collective-permute-start.36 = (bf16[96,512]{1,0:T(8,128)(2,1)S(1)}, bf16[96,512]{1,0:T(8,128)(2,1)S(1)}, u32[]{:S(2)}, u32[]{:S(2)}) collective-permute-start(bf16[96,512]{1,0:T(8,128)(2,1)S(1)} %get-tuple-element.77.refs_0_), channel_id=1, source_target_pairs={{0,16},{1,2},{2,1},{3,19},{4,20},{5,6},{6,5},{7,23},{8,24},{9,10},... | collective-permute-start | bytes 294920 | tf_op jit(solution)/shard_map/ppermute | solution.py:160
  295.4 7.6 %collective-permute-start.37 = (bf16[96,512]{1,0:T(8,128)(2,1)S(1)}, bf16[96,512]{1,0:T(8,128)(2,1)S(1)}, u32[]{:S(2)}, u32[]{:S(2)}) collective-permute-start(bf16[96,512]{1,0:T(8,128)(2,1)S(1)} %get-tuple-element.77.refs_0_), channel_id=1, source_target_pairs={{0,16},{1,6},{2,5},{3,19},{4,20},{5,2},{6,1},{7,23},{8,24},{9,14},... | collective-permute-start | bytes 294920 | tf_op jit(solution)/shard_map/ppermute | solution.py:160
  305.2 7.3 %collective-permute-start.38 = (bf16[96,2048]{1,0:T(8,128)(2,1)S(1)}, bf16[96,2048]{1,0:T(8,128)(2,1)S(1)}, u32[]{:S(2)}, u32[]{:S(2)}) collective-permute-start(bf16[96,2048]{1,0:T(8,128)(2,1)S(1)} %get-tuple-element.80), channel_id=1, source_target_pairs={{0,8},{1,9},{2,10},{3,11},{4,12},{5,13},{6,14},{7,15},{8,16},{9,17... | collective-permute-start | bytes 1179656 | tf_op jit(solution)/shard_map/ppermute | solution.py:160
  305.2 11.9 %collective-permute-start.39 = (bf16[96,2048]{1,0:T(8,128)(2,1)S(1)}, bf16[96,2048]{1,0:T(8,128)(2,1)S(1)}, u32[]{:S(2)}, u32[]{:S(2)}) collective-permute-start(bf16[96,2048]{1,0:T(8,128)(2,1)S(1)} %get-tuple-element.80), channel_id=1, source_target_pairs={{0,12},{1,13},{2,14},{3,15},{4,8},{5,9},{6,10},{7,11},{8,20},{9,21... | collective-permute-start | bytes 1179656 | tf_op jit(solution)/shard_map/ppermute | solution.py:160
  321.6 5.7 %collective-permute-start.40 = (bf16[96,512]{1,0:T(8,128)(2,1)S(1)}, bf16[96,512]{1,0:T(8,128)(2,1)S(1)}, u32[]{:S(2)}, u32[]{:S(2)}) collective-permute-start(bf16[96,512]{1,0:T(8,128)(2,1)S(1)} %get-tuple-element.81.refs_0_), channel_id=1, source_target_pairs={{0,16},{1,5},{2,6},{3,19},{4,20},{5,1},{6,2},{7,23},{8,24},{9,13},... | collective-permute-start | bytes 294920 | tf_op jit(solution)/shard_map/ppermute | solution.py:160
  322.6 6.8 %collective-permute-start.41 = (bf16[96,512]{1,0:T(8,128)(2,1)S(1)}, bf16[96,512]{1,0:T(8,128)(2,1)S(1)}, u32[]{:S(2)}, u32[]{:S(2)}) collective-permute-start(bf16[96,512]{1,0:T(8,128)(2,1)S(1)} %get-tuple-element.81.refs_0_), channel_id=1, source_target_pairs={{0,16},{1,2},{2,1},{3,19},{4,20},{5,6},{6,5},{7,23},{8,24},{9,10},... | collective-permute-start | bytes 294920 | tf_op jit(solution)/shard_map/ppermute | solution.py:160
  323.7 7.6 %collective-permute-start.42 = (bf16[96,512]{1,0:T(8,128)(2,1)S(1)}, bf16[96,512]{1,0:T(8,128)(2,1)S(1)}, u32[]{:S(2)}, u32[]{:S(2)}) collective-permute-start(bf16[96,512]{1,0:T(8,128)(2,1)S(1)} %get-tuple-element.81.refs_0_), channel_id=1, source_target_pairs={{0,16},{1,6},{2,5},{3,19},{4,20},{5,2},{6,1},{7,23},{8,24},{9,14},... | collective-permute-start | bytes 294920 | tf_op jit(solution)/shard_map/ppermute | solution.py:160
  333.5 7.3 %collective-permute-start.43 = (bf16[96,2048]{1,0:T(8,128)(2,1)S(1)}, bf16[96,2048]{1,0:T(8,128)(2,1)S(1)}, u32[]{:S(2)}, u32[]{:S(2)}) collective-permute-start(bf16[96,2048]{1,0:T(8,128)(2,1)S(1)} %get-tuple-element.84), channel_id=1, source_target_pairs={{0,8},{1,9},{2,10},{3,11},{4,12},{5,13},{6,14},{7,15},{8,16},{9,17... | collective-permute-start | bytes 1179656 | tf_op jit(solution)/shard_map/ppermute | solution.py:160
  333.5 11.8 %collective-permute-start.44 = (bf16[96,2048]{1,0:T(8,128)(2,1)S(1)}, bf16[96,2048]{1,0:T(8,128)(2,1)S(1)}, u32[]{:S(2)}, u32[]{:S(2)}) collective-permute-start(bf16[96,2048]{1,0:T(8,128)(2,1)S(1)} %get-tuple-element.84), channel_id=1, source_target_pairs={{0,12},{1,13},{2,14},{3,15},{4,8},{5,9},{6,10},{7,11},{8,20},{9,21... | collective-permute-start | bytes 1179656 | tf_op jit(solution)/shard_map/ppermute | solution.py:160
  350.9 6.7 %collective-permute-start.46 = (bf16[96,512]{1,0:T(8,128)(2,1)S(1)}, bf16[96,512]{1,0:T(8,128)(2,1)S(1)}, u32[]{:S(2)}, u32[]{:S(2)}) collective-permute-start(bf16[96,512]{1,0:T(8,128)(2,1)S(1)} %get-tuple-element.85.refs_0_), channel_id=1, source_target_pairs={{0,16},{1,2},{2,1},{3,19},{4,20},{5,6},{6,5},{7,23},{8,24},{9,10},... | collective-permute-start | bytes 294920 | tf_op jit(solution)/shard_map/ppermute | solution.py:160
  351.9 7.8 %collective-permute-start.47 = (bf16[96,512]{1,0:T(8,128)(2,1)S(1)}, bf16[96,512]{1,0:T(8,128)(2,1)S(1)}, u32[]{:S(2)}, u32[]{:S(2)}) collective-permute-start(bf16[96,512]{1,0:T(8,128)(2,1)S(1)} %get-tuple-element.85.refs_0_), channel_id=1, source_target_pairs={{0,16},{1,6},{2,5},{3,19},{4,20},{5,2},{6,1},{7,23},{8,24},{9,14},... | collective-permute-start | bytes 294920 | tf_op jit(solution)/shard_map/ppermute | solution.py:160
  361.9 7.3 %collective-permute-start.48 = (bf16[96,2048]{1,0:T(8,128)(2,1)S(1)}, bf16[96,2048]{1,0:T(8,128)(2,1)S(1)}, u32[]{:S(2)}, u32[]{:S(2)}) collective-permute-start(bf16[96,2048]{1,0:T(8,128)(2,1)S(1)} %get-tuple-element.88), channel_id=1, source_target_pairs={{0,8},{1,9},{2,10},{3,11},{4,12},{5,13},{6,14},{7,15},{8,16},{9,17... | collective-permute-start | bytes 1179656 | tf_op jit(solution)/shard_map/ppermute | solution.py:160
  362.1 11.9 %collective-permute-start.49 = (bf16[96,2048]{1,0:T(8,128)(2,1)S(1)}, bf16[96,2048]{1,0:T(8,128)(2,1)S(1)}, u32[]{:S(2)}, u32[]{:S(2)}) collective-permute-start(bf16[96,2048]{1,0:T(8,128)(2,1)S(1)} %get-tuple-element.88), channel_id=1, source_target_pairs={{0,12},{1,13},{2,14},{3,15},{4,8},{5,9},{6,10},{7,11},{8,20},{9,21... | collective-permute-start | bytes 1179656 | tf_op jit(solution)/shard_map/ppermute | solution.py:160
  379.9 5.9 %collective-permute-start.50 = (bf16[96,512]{1,0:T(8,128)(2,1)}, bf16[96,512]{1,0:T(8,128)(2,1)}, u32[]{:S(2)}, u32[]{:S(2)}) collective-permute-start(bf16[96,512]{1,0:T(8,128)(2,1)} %get-tuple-element.89.refs_0_), channel_id=1, source_target_pairs={{0,16},{1,5},{2,6},{3,19},{4,20},{5,1},{6,2},{7,23},{8,24},{9,13},... | collective-permute-start | bytes 294920 | tf_op jit(solution)/shard_map/ppermute | solution.py:160
  380.9 7.0 %collective-permute-start.51 = (bf16[96,512]{1,0:T(8,128)(2,1)}, bf16[96,512]{1,0:T(8,128)(2,1)}, u32[]{:S(2)}, u32[]{:S(2)}) collective-permute-start(bf16[96,512]{1,0:T(8,128)(2,1)} %get-tuple-element.89.refs_0_), channel_id=1, source_target_pairs={{0,16},{1,2},{2,1},{3,19},{4,20},{5,6},{6,5},{7,23},{8,24},{9,10},... | collective-permute-start | bytes 294920 | tf_op jit(solution)/shard_map/ppermute | solution.py:160
  381.9 7.7 %collective-permute-start.52 = (bf16[96,512]{1,0:T(8,128)(2,1)}, bf16[96,512]{1,0:T(8,128)(2,1)}, u32[]{:S(2)}, u32[]{:S(2)}) collective-permute-start(bf16[96,512]{1,0:T(8,128)(2,1)} %get-tuple-element.89.refs_0_), channel_id=1, source_target_pairs={{0,16},{1,6},{2,5},{3,19},{4,20},{5,2},{6,1},{7,23},{8,24},{9,14},... | collective-permute-start | bytes 294920 | tf_op jit(solution)/shard_map/ppermute | solution.py:160
  396.8 7.3 %collective-permute-start.53 = (bf16[96,2048]{1,0:T(8,128)(2,1)S(1)}, bf16[96,2048]{1,0:T(8,128)(2,1)S(1)}, u32[]{:S(2)}, u32[]{:S(2)}) collective-permute-start(bf16[96,2048]{1,0:T(8,128)(2,1)S(1)} %get-tuple-element.92), channel_id=1, source_target_pairs={{0,8},{1,9},{2,10},{3,11},{4,12},{5,13},{6,14},{7,15},{8,16},{9,17... | collective-permute-start | bytes 1179656 | tf_op jit(solution)/shard_map/ppermute | solution.py:160
  396.9 12.0 %collective-permute-start.54 = (bf16[96,2048]{1,0:T(8,128)(2,1)S(1)}, bf16[96,2048]{1,0:T(8,128)(2,1)S(1)}, u32[]{:S(2)}, u32[]{:S(2)}) collective-permute-start(bf16[96,2048]{1,0:T(8,128)(2,1)S(1)} %get-tuple-element.92), channel_id=1, source_target_pairs={{0,12},{1,13},{2,14},{3,15},{4,8},{5,9},{6,10},{7,11},{8,20},{9,21... | collective-permute-start | bytes 1179656 | tf_op jit(solution)/shard_map/ppermute | solution.py:160
  417.1 5.7 %collective-permute-start.55 = (bf16[96,512]{1,0:T(8,128)(2,1)S(1)}, bf16[96,512]{1,0:T(8,128)(2,1)S(1)}, u32[]{:S(2)}, u32[]{:S(2)}) collective-permute-start(bf16[96,512]{1,0:T(8,128)(2,1)S(1)} %get-tuple-element.93.refs_0_), channel_id=1, source_target_pairs={{0,16},{1,5},{2,6},{3,19},{4,20},{5,1},{6,2},{7,23},{8,24},{9,13},... | collective-permute-start | bytes 294920 | tf_op jit(solution)/shard_map/ppermute | solution.py:160
  418.2 6.7 %collective-permute-start.56 = (bf16[96,512]{1,0:T(8,128)(2,1)S(1)}, bf16[96,512]{1,0:T(8,128)(2,1)S(1)}, u32[]{:S(2)}, u32[]{:S(2)}) collective-permute-start(bf16[96,512]{1,0:T(8,128)(2,1)S(1)} %get-tuple-element.93.refs_0_), channel_id=1, source_target_pairs={{0,16},{1,2},{2,1},{3,19},{4,20},{5,6},{6,5},{7,23},{8,24},{9,10},... | collective-permute-start | bytes 294920 | tf_op jit(solution)/shard_map/ppermute | solution.py:160
  419.2 7.4 %collective-permute-start.57 = (bf16[96,512]{1,0:T(8,128)(2,1)S(1)}, bf16[96,512]{1,0:T(8,128)(2,1)S(1)}, u32[]{:S(2)}, u32[]{:S(2)}) collective-permute-start(bf16[96,512]{1,0:T(8,128)(2,1)S(1)} %get-tuple-element.93.refs_0_), channel_id=1, source_target_pairs={{0,16},{1,6},{2,5},{3,19},{4,20},{5,2},{6,1},{7,23},{8,24},{9,14},... | collective-permute-start | bytes 294920 | tf_op jit(solution)/shard_map/ppermute | solution.py:160
  428.9 7.3 %collective-permute-start.58 = (bf16[96,2048]{1,0:T(8,128)(2,1)S(1)}, bf16[96,2048]{1,0:T(8,128)(2,1)S(1)}, u32[]{:S(2)}, u32[]{:S(2)}) collective-permute-start(bf16[96,2048]{1,0:T(8,128)(2,1)S(1)} %get-tuple-element.96), channel_id=1, source_target_pairs={{0,8},{1,9},{2,10},{3,11},{4,12},{5,13},{6,14},{7,15},{8,16},{9,17... | collective-permute-start | bytes 1179656 | tf_op jit(solution)/shard_map/ppermute | solution.py:160
  428.9 12.0 %collective-permute-start.59 = (bf16[96,2048]{1,0:T(8,128)(2,1)S(1)}, bf16[96,2048]{1,0:T(8,128)(2,1)S(1)}, u32[]{:S(2)}, u32[]{:S(2)}) collective-permute-start(bf16[96,2048]{1,0:T(8,128)(2,1)S(1)} %get-tuple-element.96), channel_id=1, source_target_pairs={{0,12},{1,13},{2,14},{3,15},{4,8},{5,9},{6,10},{7,11},{8,20},{9,21... | collective-permute-start | bytes 1179656 | tf_op jit(solution)/shard_map/ppermute | solution.py:160
  445.4 5.7 %collective-permute-start.60 = (bf16[96,512]{1,0:T(8,128)(2,1)S(1)}, bf16[96,512]{1,0:T(8,128)(2,1)S(1)}, u32[]{:S(2)}, u32[]{:S(2)}) collective-permute-start(bf16[96,512]{1,0:T(8,128)(2,1)S(1)} %get-tuple-element.97.refs_0_), channel_id=1, source_target_pairs={{0,16},{1,5},{2,6},{3,19},{4,20},{5,1},{6,2},{7,23},{8,24},{9,13},... | collective-permute-start | bytes 294920 | tf_op jit(solution)/shard_map/ppermute | solution.py:160
  446.5 6.8 %collective-permute-start.61 = (bf16[96,512]{1,0:T(8,128)(2,1)S(1)}, bf16[96,512]{1,0:T(8,128)(2,1)S(1)}, u32[]{:S(2)}, u32[]{:S(2)}) collective-permute-start(bf16[96,512]{1,0:T(8,128)(2,1)S(1)} %get-tuple-element.97.refs_0_), channel_id=1, source_target_pairs={{0,16},{1,2},{2,1},{3,19},{4,20},{5,6},{6,5},{7,23},{8,24},{9,10},... | collective-permute-start | bytes 294920 | tf_op jit(solution)/shard_map/ppermute | solution.py:160
  447.5 7.5 %collective-permute-start.62 = (bf16[96,512]{1,0:T(8,128)(2,1)S(1)}, bf16[96,512]{1,0:T(8,128)(2,1)S(1)}, u32[]{:S(2)}, u32[]{:S(2)}) collective-permute-start(bf16[96,512]{1,0:T(8,128)(2,1)S(1)} %get-tuple-element.97.refs_0_), channel_id=1, source_target_pairs={{0,16},{1,6},{2,5},{3,19},{4,20},{5,2},{6,1},{7,23},{8,24},{9,14},... | collective-permute-start | bytes 294920 | tf_op jit(solution)/shard_map/ppermute | solution.py:160
  457.2 7.3 %collective-permute-start.63 = (bf16[96,2048]{1,0:T(8,128)(2,1)S(1)}, bf16[96,2048]{1,0:T(8,128)(2,1)S(1)}, u32[]{:S(2)}, u32[]{:S(2)}) collective-permute-start(bf16[96,2048]{1,0:T(8,128)(2,1)S(1)} %get-tuple-element.100), channel_id=1, source_target_pairs={{0,8},{1,9},{2,10},{3,11},{4,12},{5,13},{6,14},{7,15},{8,16},{9,17... | collective-permute-start | bytes 1179656 | tf_op jit(solution)/shard_map/ppermute | solution.py:160
  457.3 12.0 %collective-permute-start.64 = (bf16[96,2048]{1,0:T(8,128)(2,1)S(1)}, bf16[96,2048]{1,0:T(8,128)(2,1)S(1)}, u32[]{:S(2)}, u32[]{:S(2)}) collective-permute-start(bf16[96,2048]{1,0:T(8,128)(2,1)S(1)} %get-tuple-element.100), channel_id=1, source_target_pairs={{0,12},{1,13},{2,14},{3,15},{4,8},{5,9},{6,10},{7,11},{8,20},{9,21... | collective-permute-start | bytes 1179656 | tf_op jit(solution)/shard_map/ppermute | solution.py:160
  473.8 5.7 %collective-permute-start.65 = (bf16[96,512]{1,0:T(8,128)(2,1)S(1)}, bf16[96,512]{1,0:T(8,128)(2,1)S(1)}, u32[]{:S(2)}, u32[]{:S(2)}) collective-permute-start(bf16[96,512]{1,0:T(8,128)(2,1)S(1)} %get-tuple-element.101), channel_id=1, source_target_pairs={{0,16},{1,5},{2,6},{3,19},{4,20},{5,1},{6,2},{7,23},{8,24},{9,13},... | collective-permute-start | bytes 294920 | tf_op jit(solution)/shard_map/ppermute | solution.py:160
  474.9 6.7 %collective-permute-start.66 = (bf16[96,512]{1,0:T(8,128)(2,1)S(1)}, bf16[96,512]{1,0:T(8,128)(2,1)S(1)}, u32[]{:S(2)}, u32[]{:S(2)}) collective-permute-start(bf16[96,512]{1,0:T(8,128)(2,1)S(1)} %get-tuple-element.101), channel_id=1, source_target_pairs={{0,16},{1,2},{2,1},{3,19},{4,20},{5,6},{6,5},{7,23},{8,24},{9,10},... | collective-permute-start | bytes 294920 | tf_op jit(solution)/shard_map/ppermute | solution.py:160
  475.9 7.4 %collective-permute-start.67 = (bf16[96,512]{1,0:T(8,128)(2,1)S(1)}, bf16[96,512]{1,0:T(8,128)(2,1)S(1)}, u32[]{:S(2)}, u32[]{:S(2)}) collective-permute-start(bf16[96,512]{1,0:T(8,128)(2,1)S(1)} %get-tuple-element.101), channel_id=1, source_target_pairs={{0,16},{1,6},{2,5},{3,19},{4,20},{5,2},{6,1},{7,23},{8,24},{9,14},... | collective-permute-start | bytes 294920 | tf_op jit(solution)/shard_map/ppermute | solution.py:160
  492.1 28.2 %collective-permute-start.71 = (f32[8,2048]{1,0:T(8,128)S(1)}, f32[8,2048]{1,0:T(8,128)S(1)}, u32[]{:S(2)}, u32[]{:S(2)}) collective-permute-start(f32[8,2048]{1,0:T(8,128)S(1)} %add_add_fusion.2), channel_id=1, source_target_pairs={{1,0},{2,3},{5,4},{6,7},{9,8},{10,11},{13,12},{14,15},{17,16},{18,... | collective-permute-start | bytes 196616 | tf_op jit(solution)/shard_map/ppermute | solution.py:160
  (62 other events, 1202.3 us)

commit v3 on v2

--- a/solution.py
+++ b/solution.py
@@ -12,19 +12,17 @@
 M = 16
 EPSILON = 1e-05
 AXES = ("section", "tp", "doc")
-VMEM_LIMIT = 24 * 1024 * 1024
-C_FIRST, C_INIT, C_TP, C_POOL, C_LEN = 0, 1, 2, 3, 4
-
-
-def attend_kernel(
-    turn, docs, tokens, blocks, meta, where, *refs
-):
+C_FIRST, C_INIT, C_TP, C_POOL, C_PHASE, C_LEN = 0, 1, 2, 3, 4, 5
+
+
+def attend_kernel(turn, docs, tokens, blocks, sets, meta, where, *refs):
     halves = refs[0]
     other = refs[1]
     tok, tok_other, mem, mem_other, gain = refs[2:7]
-    weights = refs[7 : 7 + blocks]
-    mixed_ref, keep_ref = refs[7 + blocks : 9 + blocks]
-    normed, acc = refs[9 + blocks :]
+    held = 1 + sets * (blocks - 1)
+    weights = refs[7 : 7 + held]
+    mixed_ref, keep_ref = refs[7 + held : 9 + held]
+    normed, acc = refs[9 + held :]
     rows = M + tokens
     half = halves.shape[1]
     depth = weights[0].shape[0]
@@ -55,16 +53,29 @@
         return 0
 
     lax.fori_loop(0, docs, prepare, 0)
-    for b in range(blocks):
+
+    def multiply(b, weight):
         at = pl.multiple_of(where[b] * depth, 128)
         left = normed[:, pl.ds(at, depth)]
         for c in range(3):
             span = pl.ds(c * cols, cols)
-            part = jnp.dot(left, weights[b][:, span], preferred_element_type=jnp.float32)
+            part = jnp.dot(left, weight[:, span], preferred_element_type=jnp.float32)
             if b == 0:
                 acc[:, span] = part
             else:
                 acc[:, span] += part
+
+    multiply(0, weights[0])
+    for phase in range(sets):
+
+        def received(phase=phase):
+            for b in range(1, blocks):
+                multiply(b, weights[b + phase * (blocks - 1)])
+
+        if sets == 1:
+            received()
+        else:
+            pl.when(meta[turn, C_PHASE] == phase)(received)
 
     row = lax.broadcasted_iota(jnp.int32, (rows, rows), 0)
     col = lax.broadcasted_iota(jnp.int32, (rows, rows), 1)
@@ -156,6 +167,9 @@
     def lin(a, b, c):
         return (a * T + b) * D + c
 
+    limit = 24 * 2**20 + 2 * R * (4 * half + 12 * cols)
+    params = pltpu.CompilerParams(vmem_limit_bytes=limit)
+
     def send(block, pairs):
         return lax.ppermute(block, AXES, [(lin(*a), lin(*b)) for a, b in pairs])
 
@@ -165,6 +179,16 @@
         return [
             (e, move(*e) if e[2] in planes else ((e[0] + S // 2) % S, e[1], e[2])) for e in everyone
         ]
+
+    packed = jnp.concatenate([token_ids, seg_lengths[:, :, None]], 2)
+    gathered = [packed]
+    for k in range(1, D):
+        gathered.append(send(packed, [(e, (e[0], e[1], (e[2] + k) % D)) for e in everyone]))
+    source = (z - jnp.arange(D)) % D
+    chosen = (source[None, :] == jnp.arange(D)[:, None])[:, :, None, None, None]
+    gathered = jnp.sum(jnp.where(chosen, jnp.stack(gathered)[None], 0), 1)
+    packed = gathered.reshape(docs, segs, tokens + 1)
+    ids, lengths = packed[:, :, :tokens], packed[:, :, tokens]
 
     def block_of(side):
         return jnp.concatenate(
@@ -188,30 +212,29 @@
             moved.append(send(block, pairs))
         return moved
 
-    even = relay(0, blocks)
-    blocks, token_ids = lax.optimization_barrier((blocks, token_ids))
-    (blocks, even) = lax.optimization_barrier((blocks, even))
-    odd = relay(1, blocks)
-
-    packed = jnp.concatenate([token_ids, seg_lengths[:, :, None]], 2)
-    packed = lax.all_gather(packed, "doc", axis=0, tiled=True)
-    ids, lengths = packed[:, :, :tokens], packed[:, :, tokens]
-
     vocab = emb_table.shape[0]
-    tok, tok_other = [], []
-    for seg in range(segs):
-        if seg == 1:
-            ids, even = lax.optimization_barrier((ids, even))
-        local = ids[:, seg].reshape(-1) - s * vocab
+
+    def embed(index):
+        local = index.reshape(-1) - s * vocab
         owned = (local >= 0) & (local < vocab)
         picked = jnp.take(emb_table, jnp.clip(local, 0, vocab - 1), axis=0)
         picked = jnp.where(owned[:, None], picked, jnp.zeros_like(picked))
         full = picked
         for a in range(1, S):
             full = full + send(picked, [((a, b, c), (0, b, c)) for b in range(T) for c in planes])
-        tok.append(full)
-        tok_other.append(send(full, [((0, b, c), (0, T - 1 - b, c)) for b in range(T) for c in planes]))
+        return full, send(full, [((0, b, c), (0, T - 1 - b, c)) for b in range(T) for c in planes])
+
+    ids, blocks = lax.optimization_barrier((ids, blocks))
+    even = relay(0, blocks)
+    pairs = [embed(ids[:, 0])]
     mem_other = send(mem_init, [((0, b, c), (0, T - 1 - b, c)) for b in range(T) for c in planes])
+    blocks, even, pairs, mem_other, ids = lax.optimization_barrier(
+        (blocks, even, pairs, mem_other, ids)
+    )
+    odd = relay(1, blocks)
+    for seg in range(1, segs):
+        pairs.append(embed(ids[:, seg]))
+    tok, tok_other = zip(*pairs)
 
     offset = jnp.arange(turns) - s
     group = offset % S
@@ -225,6 +248,7 @@
             (s == 0) & (offset < S),
             jnp.full((turns,), t),
             active & (segment == segs - 1),
+            jnp.full((turns,), s % 2),
         ],
         1,
     ).astype(jnp.int32)
@@ -242,26 +266,25 @@
     own = jnp.zeros((R, half), jnp.bfloat16)
     other = jnp.zeros((R, half), jnp.bfloat16)
     pools = []
-    weights = [own_block] + even
     for k in range(turns):
-        if k == 1:
-            weights = [own_block] + [a + b for a, b in zip(even, odd)]
+        sets = 1 if k == 0 else 2
+        weights = [own_block] + even + (odd if k else [])
         g, seg = k % S, k // S
         rows_of = slice(g * n * tokens, (g + 1) * n * tokens)
         tk, tko = (a[min(seg, segs - 1)][rows_of] for a in (tok, tok_other))
         mixed, keep = pl.pallas_call(
-            functools.partial(attend_kernel, k, n, tokens, D),
+            functools.partial(attend_kernel, k, n, tokens, D, sets),
             out_shape=(
                 jax.ShapeDtypeStruct((R, cols), jnp.bfloat16),
                 jax.ShapeDtypeStruct((R, half), jnp.bfloat16),
             ),
-            in_specs=[smem, smem] + [vmem] * (7 + D),
+            in_specs=[smem, smem] + [vmem] * (7 + len(weights)),
             out_specs=(vmem, vmem),
             scratch_shapes=[
                 pltpu.VMEM((R, 2 * half), jnp.bfloat16),
                 pltpu.VMEM((R, 3 * cols), jnp.float32),
             ],
-            compiler_params=pltpu.CompilerParams(vmem_limit_bytes=VMEM_LIMIT),
+            compiler_params=params,
         )(meta, where, own, other, tk, tko, mem_init, mem_other, norm_gain, *weights)
         shared = [mixed]
         for j, i in shifts[1:]:
@@ -278,7 +301,7 @@
             out_shape=tuple(shapes),
             in_specs=[smem, smem, smem] + [vmem] * (parts + 2),
             out_specs=tuple([vmem] * len(shapes)),
-            compiler_params=pltpu.CompilerParams(vmem_limit_bytes=VMEM_LIMIT),
+            compiler_params=params,
         )(meta, place, layer_mix, *shared, keep, out_proj)
         if pool:
             pools.append(result[1])

time: 528 us -> 558 us (1.057)
  waiting for transfers between devices: 165 us -> 270 us
  blocking collectives: 70.1 us -> 0 us
  Pallas kernels: 74.2 us -> 126 us
  starting transfers between devices: 124 us -> 88.6 us
  other arithmetic: 30 us -> 12.8 us
  local copies, waits for them, and re-layouts: 56.9 us -> 50.5 us
    ppermute x72 -> x75, waiting for transfers between devices: 165 us -> 270 us  [send(): return lax.ppermute(block, AXES, [(lin(*a), lin(*b)) for a, b in pairs])]
    all_gather x1 -> x0, blocking collectives: 70.1 us -> none  [body(): packed = lax.all_gather(packed, 'doc', axis=0, tiled=True)]
    pallas_call x11, Pallas kernels: 51.8 us -> 103 us  [body(): pl.pallas_call(functools.partial(attend_kernel, k, n, tokens, D, sets), o...]
    ppermute x72 -> x75, starting transfers between devices: 124 us -> 88.6 us  [send(): return lax.ppermute(block, AXES, [(lin(*a), lin(*b)) for a, b in pairs])]
    add x5 -> x2, other arithmetic: 17.7 us -> 2.93 us  [embed(): full + send(picked, [((a, b, c), (0, b, c)) for b in range(T) for c in pl...]
    unnamed x114 -> x96, local copies, waits for them, and re-layouts: 17.7 us -> 13.1 us
  transfers between devices with their start and end apart: 72 -> 75, of which waited for: 53 -> 56; matrix products, arithmetic and copies ran while one was open for 8% -> 6% of each run, Pallas kernels for 5% -> 8%
where the time goes in v3:
time: 558 us; the launch traced here: 550 us
  waiting for transfers between devices  270 us (48%)
  Pallas kernels  126 us (23%)
  starting transfers between devices  88.6 us (16%)
  local copies, waits for them, and re-layouts  50.5 us (9%)
  other arithmetic  12.8 us (2%)
    ppermute x75, waiting for transfers between devices, send(): return lax.ppermute(block, AXES, [(lin(*a), lin(*b)) for a, b in pairs])  270 us
    pallas_call x11, Pallas kernels, body(): pl.pallas_call(functools.partial(attend_kernel, k, n, tokens, D, sets), o...  103 us
    ppermute x75, starting transfers between devices, send(): return lax.ppermute(block, AXES, [(lin(*a), lin(*b)) for a, b in pairs])  88.6 us
    pallas_call x10, Pallas kernels, body(): pl.pallas_call(functools.partial(project_kernel, k, n, tokens, parts, poo...  22.7 us
    gather x2, local copies, waits for them, and re-layouts, embed(): picked = jnp.take(emb_table, jnp.clip(local, 0, vocab - 1), axis=0)  21.5 us
    unnamed x96, local copies, waits for them, and re-layouts  13.1 us
  transfers between devices with their start and end apart: 75, of which 56 were waited for; matrix products, arithmetic and copies ran while one was open for 6% of the time, Pallas kernels for 8%

profile of v3, /device:TPU:0, one launch (start us, length us, event | category | flops | bytes accessed | tf_op | source)
XLA Modules:
  0.0 550.2 jit_solution(2339632739967786473)
XLA Ops:
  1.5 5.0 collective-permute-start.2
  7.7 3.9 dynamic-slice_bitcast_fusion.2
  11.6 2.5 dynamic-slice_bitcast_fusion
  20.0 10.3 %gather_fusion.1 = bf16[256,2048]{1,0:T(8,128)(2,1)S(1)} fusion(bf16[4096,2048]{1,0:T(8,128)(2,1)} %param.14, s32[1024]{0:T(1024)S(1)} %pad_clamp_fusion.1), kind=kCustom, calls=%fused_computation.clone | custom fusion | bytes 2098176 | tf_op jit(solution)/shard_map/jit(_take)/gather | solution.py:220
  32.3 5.1 collective-permute-start.3
  39.8 3.8 collective-permute-start.5
  45.1 2.6 add_add_fusion.1
  50.1 26.0 %collective-permute-done.3.refs_8_ = bf16[1024,1536]{1,0:T(8,128)(2,1)S(1)} collective-permute-done((bf16[1024,1536]{1,0:T(8,128)(2,1)}, bf16[1024,1536]{1,0:T(8,128)(2,1)S(1)}, u32[]{:S(2)}, u32[]{:S(2)}) %collective-permute-start.3) | collective-permute-done | bytes 3145760 | tf_op jit(solution)/shard_map/ppermute | solution.py:174
  77.7 65.8 %collective-permute-done.5.refs_10_ = bf16[1024,1536]{1,0:T(8,128)(2,1)} collective-permute-done((bf16[1024,1536]{1,0:T(8,128)(2,1)}, bf16[1024,1536]{1,0:T(8,128)(2,1)}, u32[]{:S(2)}, u32[]{:S(2)}) %collective-permute-start.5) | collective-permute-done | bytes 3145760 | tf_op jit(solution)/shard_map/ppermute | solution.py:174
  143.6 2.4 collective-permute-start.16
  149.9 2.5 collective-permute-start.17
  152.4 2.5 collective-permute-start.18
  159.1 6.6 %shard_map.100 = (bf16[96,512]{1,0:T(8,128)(2,1)S(1)}, bf16[96,2048]{1,0:T(8,128)(2,1)S(1)}) custom-call(s32[11,7]{1,0:T(8,128)S(1)} %concatenate.23.meta, s32[4]{0:T(128)S(1)} %pad_add_fusion.3.where, bf16[96,2048]{1,0:T(8,128)(2,1)S(1)} %broadcast_17_refs_0__refs_1_.2.refs_0_.refs_1_, bf16[96,2048]{1,0:T(8,128)(2,1)S(1)} %broadcast_17_refs_0__refs_1_.2.refs_0_.refs_1_, ...), custom_call_target="tpu_custom_call" | custom-call | tf_op jit(solution)/shard_map/pallas_call | solution.py:275
  166.6 6.1 %collective-permute-start.11 = (bf16[96,512]{1,0:T(8,128)(2,1)S(1)}, bf16[96,512]{1,0:T(8,128)(2,1)S(1)}, u32[]{:S(2)}, u32[]{:S(2)}) collective-permute-start(bf16[96,512]{1,0:T(8,128)(2,1)S(1)} %get-tuple-element.65.refs_0_), channel_id=1, source_target_pairs={{0,16},{1,5},{2,6},{3,19},{4,20},{5,1},{6,2},{7,23},{8,24},{9,13},... | collective-permute-start | bytes 294920 | tf_op jit(solution)/shard_map/ppermute | solution.py:174
  172.8 2.4 collective-permute-done.11.refs_1_
  177.3 11.3 %gather_fusion.2 = bf16[256,2048]{1,0:T(8,128)(2,1)} fusion(bf16[4096,2048]{1,0:T(8,128)(2,1)} %param.14, s32[1024]{0:T(1024)S(1)} %pad_clamp_fusion), kind=kCustom, calls=%fused_computation.1.clone | custom fusion | bytes 2098176 | tf_op jit(solution)/shard_map/jit(_take)/gather | solution.py:220
  188.7 3.4 copy-done
  193.0 2.6 shard_map.101
  197.1 5.7 %collective-permute-done.14.refs_0_ = bf16[96,2048]{1,0:T(8,128)(2,1)S(1)} collective-permute-done((bf16[96,2048]{1,0:T(8,128)(2,1)S(1)}, bf16[96,2048]{1,0:T(8,128)(2,1)S(1)}, u32[]{:S(2)}, u32[]{:S(2)}) %collective-permute-start.14) | collective-permute-done | bytes 393248 | tf_op jit(solution)/shard_map/ppermute | solution.py:174
  203.6 4.4 collective-permute-done.15.refs_1_
  209.6 10.0 %shard_map.102 = (bf16[96,512]{1,0:T(8,128)(2,1)S(1)}, bf16[96,2048]{1,0:T(8,128)(2,1)S(1)}) custom-call(s32[11,7]{1,0:T(8,128)S(1)} %concatenate.23.meta, s32[4]{0:T(128)S(1)} %pad_add_fusion.3.where, bf16[96,2048]{1,0:T(8,128)(2,1)S(1)} %collective-permute-done.14.refs_0_, bf16[96,2048]{1,0:T(8,128)(2,1)S(1)} %collective-permute-done.15.refs_1_, ...), custom_call_target="tpu_custom_call" | custom-call | tf_op jit(solution)/shard_map/pallas_call | solution.py:275
  221.7 3.6 collective-permute-done.19.refs_1_
  226.3 3.6 collective-permute-done.21.refs_3_
  234.5 4.8 collective-permute-done.22.refs_0_
  239.3 4.4 collective-permute-done.23.refs_1_
  243.7 9.5 %shard_map.104 = (bf16[96,512]{1,0:T(8,128)(2,1)S(1)}, bf16[96,2048]{1,0:T(8,128)(2,1)S(1)}) custom-call(s32[11,7]{1,0:T(8,128)S(1)} %concatenate.23.meta, s32[4]{0:T(128)S(1)} %pad_add_fusion.3.where, bf16[96,2048]{1,0:T(8,128)(2,1)S(1)} %collective-permute-done.22.refs_0_, bf16[96,2048]{1,0:T(8,128)(2,1)S(1)} %collective-permute-done.23.refs_1_, ...), custom_call_target="tpu_custom_call" | custom-call | tf_op jit(solution)/shard_map/pallas_call | solution.py:275
  256.2 2.6 collective-permute-done.24.refs_1_
  266.7 5.3 collective-permute-done.27.refs_0_
  272.0 4.8 collective-permute-done.28.refs_1_
  276.8 9.5 %shard_map.106 = (bf16[96,512]{1,0:T(8,128)(2,1)S(1)}, bf16[96,2048]{1,0:T(8,128)(2,1)S(1)}) custom-call(s32[11,7]{1,0:T(8,128)S(1)} %concatenate.23.meta, s32[4]{0:T(128)S(1)} %pad_add_fusion.3.where, bf16[96,2048]{1,0:T(8,128)(2,1)S(1)} %collective-permute-done.27.refs_0_, bf16[96,2048]{1,0:T(8,128)(2,1)S(1)} %collective-permute-done.28.refs_1_, ...), custom_call_target="tpu_custom_call" | custom-call | tf_op jit(solution)/shard_map/pallas_call | solution.py:275
  289.6 2.4 collective-permute-done.29.refs_1_
  299.9 5.7 %collective-permute-done.32.refs_0_ = bf16[96,2048]{1,0:T(8,128)(2,1)S(1)} collective-permute-done((bf16[96,2048]{1,0:T(8,128)(2,1)S(1)}, bf16[96,2048]{1,0:T(8,128)(2,1)S(1)}, u32[]{:S(2)}, u32[]{:S(2)}) %collective-permute-start.32) | collective-permute-done | bytes 393248 | tf_op jit(solution)/shard_map/ppermute | solution.py:174
  305.6 4.5 collective-permute-done.33.refs_1_
  310.1 9.6 %shard_map.108 = (bf16[96,512]{1,0:T(8,128)(2,1)S(1)}, bf16[96,2048]{1,0:T(8,128)(2,1)S(1)}) custom-call(s32[11,7]{1,0:T(8,128)S(1)} %concatenate.23.meta, s32[4]{0:T(128)S(1)} %pad_add_fusion.3.where, bf16[96,2048]{1,0:T(8,128)(2,1)S(1)} %collective-permute-done.32.refs_0_, bf16[96,2048]{1,0:T(8,128)(2,1)S(1)} %collective-permute-done.33.refs_1_, ...), custom_call_target="tpu_custom_call" | custom-call | tf_op jit(solution)/shard_map/pallas_call | solution.py:275
  322.8 2.6 collective-permute-done.38.refs_1_
  333.3 5.3 collective-permute-done.41.refs_0_
  338.6 4.8 collective-permute-done.42.refs_1_
  343.5 9.5 %shard_map.110 = (bf16[96,512]{1,0:T(8,128)(2,1)S(1)}, bf16[96,2048]{1,0:T(8,128)(2,1)S(1)}) custom-call(s32[11,7]{1,0:T(8,128)S(1)} %concatenate.23.meta, s32[4]{0:T(128)S(1)} %pad_add_fusion.3.where, bf16[96,2048]{1,0:T(8,128)(2,1)S(1)} %collective-permute-done.41.refs_0_, bf16[96,2048]{1,0:T(8,128)(2,1)S(1)} %collective-permute-done.42.refs_1_, ...), custom_call_target="tpu_custom_call" | custom-call | tf_op jit(solution)/shard_map/pallas_call | solution.py:275
  356.2 2.5 collective-permute-done.43.refs_1_
  366.5 5.8 %collective-permute-done.46.refs_0_ = bf16[96,2048]{1,0:T(8,128)(2,1)S(1)} collective-permute-done((bf16[96,2048]{1,0:T(8,128)(2,1)S(1)}, bf16[96,2048]{1,0:T(8,128)(2,1)S(1)}, u32[]{:S(2)}, u32[]{:S(2)}) %collective-permute-start.46) | collective-permute-done | bytes 393248 | tf_op jit(solution)/shard_map/ppermute | solution.py:174
  372.3 4.5 collective-permute-done.47.refs_1_
  376.8 9.7 %shard_map.112 = (bf16[96,512]{1,0:T(8,128)(2,1)S(1)}, bf16[96,2048]{1,0:T(8,128)(2,1)S(1)}) custom-call(s32[11,7]{1,0:T(8,128)S(1)} %concatenate.23.meta, s32[4]{0:T(128)S(1)} %pad_add_fusion.3.where, bf16[96,2048]{1,0:T(8,128)(2,1)S(1)} %collective-permute-done.46.refs_0_, bf16[96,2048]{1,0:T(8,128)(2,1)S(1)} %collective-permute-done.47.refs_1_, ...), custom_call_target="tpu_custom_call" | custom-call | tf_op jit(solution)/shard_map/pallas_call | solution.py:275
  389.6 2.7 collective-permute-done.48.refs_1_
  400.1 5.3 collective-permute-done.51.refs_0_
  405.4 4.8 collective-permute-done.52.refs_1_
  410.2 10.1 %shard_map.114 = (bf16[96,512]{1,0:T(8,128)(2,1)}, bf16[96,2048]{1,0:T(8,128)(2,1)S(1)}) custom-call(s32[11,7]{1,0:T(8,128)S(1)} %concatenate.23.meta, s32[4]{0:T(128)S(1)} %pad_add_fusion.3.where, bf16[96,2048]{1,0:T(8,128)(2,1)S(1)} %collective-permute-done.51.refs_0_, bf16[96,2048]{1,0:T(8,128)(2,1)S(1)} %collective-permute-done.52.refs_1_, ...), custom_call_target="tpu_custom_call" | custom-call | tf_op jit(solution)/shard_map/pallas_call | solution.py:275
  424.2 2.8 collective-permute-done.53.refs_1_
  431.2 3.4 copy-done.1
  435.6 2.7 shard_map.115
  439.9 5.8 %collective-permute-done.56.refs_0_ = bf16[96,2048]{1,0:T(8,128)(2,1)S(1)} collective-permute-done((bf16[96,2048]{1,0:T(8,128)(2,1)S(1)}, bf16[96,2048]{1,0:T(8,128)(2,1)S(1)}, u32[]{:S(2)}, u32[]{:S(2)}) %collective-permute-start.56) | collective-permute-done | bytes 393248 | tf_op jit(solution)/shard_map/ppermute | solution.py:174
  445.6 4.5 collective-permute-done.57.refs_1_
  450.2 9.5 %shard_map.116 = (bf16[96,512]{1,0:T(8,128)(2,1)S(1)}, bf16[96,2048]{1,0:T(8,128)(2,1)S(1)}) custom-call(s32[11,7]{1,0:T(8,128)S(1)} %concatenate.23.meta, s32[4]{0:T(128)S(1)} %pad_add_fusion.3.where, bf16[96,2048]{1,0:T(8,128)(2,1)S(1)} %collective-permute-done.56.refs_0_, bf16[96,2048]{1,0:T(8,128)(2,1)S(1)} %collective-permute-done.57.refs_1_, ...), custom_call_target="tpu_custom_call" | custom-call | tf_op jit(solution)/shard_map/pallas_call | solution.py:275
  462.7 2.6 collective-permute-done.58.refs_1_
  473.3 5.3 collective-permute-done.61.refs_0_
  478.6 4.8 collective-permute-done.62.refs_1_
  483.4 9.7 %shard_map.118 = (bf16[96,512]{1,0:T(8,128)(2,1)S(1)}, bf16[96,2048]{1,0:T(8,128)(2,1)S(1)}) custom-call(s32[11,7]{1,0:T(8,128)S(1)} %concatenate.23.meta, s32[4]{0:T(128)S(1)} %pad_add_fusion.3.where, bf16[96,2048]{1,0:T(8,128)(2,1)S(1)} %collective-permute-done.61.refs_0_, bf16[96,2048]{1,0:T(8,128)(2,1)S(1)} %collective-permute-done.62.refs_1_, ...), custom_call_target="tpu_custom_call" | custom-call | tf_op jit(solution)/shard_map/pallas_call | solution.py:275
  496.3 2.5 collective-permute-done.63.refs_1_
  506.7 5.8 %collective-permute-done.66.refs_0_ = bf16[96,2048]{1,0:T(8,128)(2,1)S(1)} collective-permute-done((bf16[96,2048]{1,0:T(8,128)(2,1)S(1)}, bf16[96,2048]{1,0:T(8,128)(2,1)S(1)}, u32[]{:S(2)}, u32[]{:S(2)}) %collective-permute-start.66) | collective-permute-done | bytes 393248 | tf_op jit(solution)/shard_map/ppermute | solution.py:174
  512.5 4.5 collective-permute-done.67.refs_1_
  517.0 9.5 %shard_map.120 = (bf16[96,512]{1,0:T(8,128)(2,1)S(1)}, bf16[96,2048]{1,0:T(8,128)(2,1)S(1)}) custom-call(s32[11,7]{1,0:T(8,128)S(1)} %concatenate.23.meta, s32[4]{0:T(128)S(1)} %pad_add_fusion.3.where, bf16[96,2048]{1,0:T(8,128)(2,1)S(1)} %collective-permute-done.66.refs_0_, bf16[96,2048]{1,0:T(8,128)(2,1)S(1)} %collective-permute-done.67.refs_1_, ...), custom_call_target="tpu_custom_call" | custom-call | tf_op jit(solution)/shard_map/pallas_call | solution.py:275
  529.5 2.6 collective-permute-done.68
  535.9 2.9 shard_map.121
  542.4 2.4 collective-permute-done.72
  544.9 4.2 collective-permute-done.74
  (263 shorter events, 139.4 us)
Async XLA Ops:
  1.5 18.1 %collective-permute-start.2 = (s32[2,2,33]{2,1,0:T(2,128)S(1)}, s32[2,2,33]{2,1,0:T(2,128)S(1)}, u32[]{:S(2)}, u32[]{:S(2)}) collective-permute-start(s32[2,2,33]{2,1,0:T(2,128)S(1)} %pad_add_fusion.1), channel_id=1, source_target_pairs={{0,3},{1,0},{2,1},{3,2},{4,7},{5,4},{6,5},{7,6},{8,11},{9,8},{10,9... | collective-permute-start | bytes 1592 | tf_op jit(solution)/shard_map/ppermute | solution.py:174
  6.6 13.0 %collective-permute-start.1 = (s32[2,2,33]{2,1,0:T(2,128)S(1)}, s32[2,2,33]{2,1,0:T(2,128)S(1)}, u32[]{:S(2)}, u32[]{:S(2)}) collective-permute-start(s32[2,2,33]{2,1,0:T(2,128)S(1)} %pad_add_fusion.1), channel_id=1, source_target_pairs={{0,2},{1,3},{2,0},{3,1},{4,6},{5,7},{6,4},{7,5},{8,10},{9,11},{10,... | collective-permute-start | bytes 1592 | tf_op jit(solution)/shard_map/ppermute | solution.py:174
  6.6 13.0 %collective-permute-start = (s32[2,2,33]{2,1,0:T(2,128)S(1)}, s32[2,2,33]{2,1,0:T(2,128)S(1)}, u32[]{:S(2)}, u32[]{:S(2)}) collective-permute-start(s32[2,2,33]{2,1,0:T(2,128)S(1)} %pad_add_fusion.1), channel_id=1, source_target_pairs={{0,1},{1,2},{2,3},{3,0},{4,5},{5,6},{6,7},{7,4},{8,9},{9,10},{10,1... | collective-permute-start | bytes 1592 | tf_op jit(solution)/shard_map/ppermute | solution.py:174
  31.5 12.9 %collective-permute-start.8 = (bf16[256,2048]{1,0:T(8,128)(2,1)S(1)}, bf16[256,2048]{1,0:T(8,128)(2,1)S(1)}, u32[]{:S(2)}, u32[]{:S(2)}) collective-permute-start(bf16[256,2048]{1,0:T(8,128)(2,1)S(1)} %select_select_fusion.1), channel_id=1, source_target_pairs={{25,1},{26,2},{29,5},{30,6}} | collective-permute-start | bytes 3145736 | tf_op jit(solution)/shard_map/ppermute | solution.py:174
  32.3 43.8 %collective-permute-start.3 = (bf16[1024,1536]{1,0:T(8,128)(2,1)}, bf16[1024,1536]{1,0:T(8,128)(2,1)S(1)}, u32[]{:S(2)}, u32[]{:S(2)}) collective-permute-start(bf16[1024,1536]{1,0:T(8,128)(2,1)} %pad_maximum_fusion), channel_id=1, source_target_pairs={{0,1},{3,2},{4,5},{7,6},{16,17},{19,18},{20,21},{23,22}} | collective-permute-start | bytes 9437192 | tf_op jit(solution)/shard_map/ppermute | solution.py:174
  37.5 40.2 %collective-permute-start.4 = (bf16[1024,1536]{1,0:T(8,128)(2,1)}, bf16[1024,1536]{1,0:T(8,128)(2,1)}, u32[]{:S(2)}, u32[]{:S(2)}) collective-permute-start(bf16[1024,1536]{1,0:T(8,128)(2,1)} %pad_maximum_fusion.1), channel_id=1, source_target_pairs={{2,1},{1,2},{6,5},{5,6},{18,17},{17,18},{22,21},{21,22}} | collective-permute-start | bytes 9437192 | tf_op jit(solution)/shard_map/ppermute | solution.py:174
  39.8 103.7 %collective-permute-start.5 = (bf16[1024,1536]{1,0:T(8,128)(2,1)}, bf16[1024,1536]{1,0:T(8,128)(2,1)}, u32[]{:S(2)}, u32[]{:S(2)}) collective-permute-start(bf16[1024,1536]{1,0:T(8,128)(2,1)} %pad_maximum_fusion.2), channel_id=1, source_target_pairs={{3,1},{0,2},{7,5},{4,6},{19,17},{16,18},{23,21},{20,22}} | collective-permute-start | bytes 9437192 | tf_op jit(solution)/shard_map/ppermute | solution.py:174
  143.6 65.2 %collective-permute-start.16 = (bf16[1024,1536]{1,0:T(8,128)(2,1)}, bf16[1024,1536]{1,0:T(8,128)(2,1)}, u32[]{:S(2)}, u32[]{:S(2)}) collective-permute-start(bf16[1024,1536]{1,0:T(8,128)(2,1)} %pad_maximum_fusion), channel_id=1, source_target_pairs={{8,9},{11,10},{12,13},{15,14},{24,25},{27,26},{28,29},{31,30}} | collective-permute-start | bytes 9437192 | tf_op jit(solution)/shard_map/ppermute | solution.py:174
  149.9 59.6 %collective-permute-start.17 = (bf16[1024,1536]{1,0:T(8,128)(2,1)}, bf16[1024,1536]{1,0:T(8,128)(2,1)}, u32[]{:S(2)}, u32[]{:S(2)}) collective-permute-start(bf16[1024,1536]{1,0:T(8,128)(2,1)} %pad_maximum_fusion.1), channel_id=1, source_target_pairs={{10,9},{9,10},{14,13},{13,14},{26,25},{25,26},{30,29},{29,30}} | collective-permute-start | bytes 9437192 | tf_op jit(solution)/shard_map/ppermute | solution.py:174
  152.4 57.1 %collective-permute-start.18 = (bf16[1024,1536]{1,0:T(8,128)(2,1)}, bf16[1024,1536]{1,0:T(8,128)(2,1)}, u32[]{:S(2)}, u32[]{:S(2)}) collective-permute-start(bf16[1024,1536]{1,0:T(8,128)(2,1)} %pad_maximum_fusion.2), channel_id=1, source_target_pairs={{11,9},{8,10},{15,13},{12,14},{27,25},{24,26},{31,29},{28,30}} | collective-permute-start | bytes 9437192 | tf_op jit(solution)/shard_map/ppermute | solution.py:174
  166.6 8.7 %collective-permute-start.11 = (bf16[96,512]{1,0:T(8,128)(2,1)S(1)}, bf16[96,512]{1,0:T(8,128)(2,1)S(1)}, u32[]{:S(2)}, u32[]{:S(2)}) collective-permute-start(bf16[96,512]{1,0:T(8,128)(2,1)S(1)} %get-tuple-element.65.refs_0_), channel_id=1, source_target_pairs={{0,16},{1,5},{2,6},{3,19},{4,20},{5,1},{6,2},{7,23},{8,24},{9,13},... | collective-permute-start | bytes 294920 | tf_op jit(solution)/shard_map/ppermute | solution.py:174
  172.7 16.0 %collective-permute-start.12 = (bf16[96,512]{1,0:T(8,128)(2,1)S(1)}, bf16[96,512]{1,0:T(8,128)(2,1)}, u32[]{:S(2)}, u32[]{:S(2)}) collective-permute-start(bf16[96,512]{1,0:T(8,128)(2,1)S(1)} %get-tuple-element.65.refs_0_), channel_id=1, source_target_pairs={{0,16},{1,2},{2,1},{3,19},{4,20},{5,6},{6,5},{7,23},{8,24},{9,10},... | collective-permute-start | bytes 294920 | tf_op jit(solution)/shard_map/ppermute | solution.py:174
  175.3 13.4 %collective-permute-start.13 = (bf16[96,512]{1,0:T(8,128)(2,1)S(1)}, bf16[96,512]{1,0:T(8,128)(2,1)}, u32[]{:S(2)}, u32[]{:S(2)}) collective-permute-start(bf16[96,512]{1,0:T(8,128)(2,1)S(1)} %get-tuple-element.65.refs_0_), channel_id=1, source_target_pairs={{0,16},{1,6},{2,5},{3,19},{4,20},{5,2},{6,1},{7,23},{8,24},{9,14},... | collective-permute-start | bytes 294920 | tf_op jit(solution)/shard_map/ppermute | solution.py:174
  195.6 7.3 %collective-permute-start.14 = (bf16[96,2048]{1,0:T(8,128)(2,1)S(1)}, bf16[96,2048]{1,0:T(8,128)(2,1)S(1)}, u32[]{:S(2)}, u32[]{:S(2)}) collective-permute-start(bf16[96,2048]{1,0:T(8,128)(2,1)S(1)} %shard_map.101), channel_id=1, source_target_pairs={{0,8},{1,9},{2,10},{3,11},{4,12},{5,13},{6,14},{7,15},{8,16},{9,17... | collective-permute-start | bytes 1179656 | tf_op jit(solution)/shard_map/ppermute | solution.py:174
  195.7 12.3 %collective-permute-start.15 = (bf16[96,2048]{1,0:T(8,128)(2,1)S(1)}, bf16[96,2048]{1,0:T(8,128)(2,1)S(1)}, u32[]{:S(2)}, u32[]{:S(2)}) collective-permute-start(bf16[96,2048]{1,0:T(8,128)(2,1)S(1)} %shard_map.101), channel_id=1, source_target_pairs={{0,12},{1,13},{2,14},{3,15},{4,8},{5,9},{6,10},{7,11},{8,20},{9,21... | collective-permute-start | bytes 1179656 | tf_op jit(solution)/shard_map/ppermute | solution.py:174
  202.9 30.5 %collective-permute-start.36 = (bf16[256,2048]{1,0:T(8,128)(2,1)S(1)}, bf16[256,2048]{1,0:T(8,128)(2,1)S(1)}, u32[]{:S(2)}, u32[]{:S(2)}) collective-permute-start(bf16[256,2048]{1,0:T(8,128)(2,1)S(1)} %select_select_fusion), channel_id=1, source_target_pairs={{25,1},{26,2},{29,5},{30,6}} | collective-permute-start | bytes 3145736 | tf_op jit(solution)/shard_map/ppermute | solution.py:174
  208.0 25.4 %collective-permute-start.35 = (bf16[256,2048]{1,0:T(8,128)(2,1)S(1)}, bf16[256,2048]{1,0:T(8,128)(2,1)S(1)}, u32[]{:S(2)}, u32[]{:S(2)}) collective-permute-start(bf16[256,2048]{1,0:T(8,128)(2,1)S(1)} %select_select_fusion), channel_id=1, source_target_pairs={{17,1},{18,2},{21,5},{22,6}} | collective-permute-start | bytes 3145736 | tf_op jit(solution)/shard_map/ppermute | solution.py:174
  208.8 24.6 %collective-permute-start.34 = (bf16[256,2048]{1,0:T(8,128)(2,1)S(1)}, bf16[256,2048]{1,0:T(8,128)(2,1)S(1)}, u32[]{:S(2)}, u32[]{:S(2)}) collective-permute-start(bf16[256,2048]{1,0:T(8,128)(2,1)S(1)} %select_select_fusion), channel_id=1, source_target_pairs={{9,1},{10,2},{13,5},{14,6}} | collective-permute-start | bytes 3145736 | tf_op jit(solution)/shard_map/ppermute | solution.py:174
  219.6 5.7 %collective-permute-start.19 = (bf16[96,512]{1,0:T(8,128)(2,1)S(1)}, bf16[96,512]{1,0:T(8,128)(2,1)S(1)}, u32[]{:S(2)}, u32[]{:S(2)}) collective-permute-start(bf16[96,512]{1,0:T(8,128)(2,1)S(1)} %get-tuple-element.70.refs_0_), channel_id=1, source_target_pairs={{0,16},{1,5},{2,6},{3,19},{4,20},{5,1},{6,2},{7,23},{8,24},{9,13},... | collective-permute-start | bytes 294920 | tf_op jit(solution)/shard_map/ppermute | solution.py:174
  220.1 6.3 %collective-permute-start.20 = (bf16[96,512]{1,0:T(8,128)(2,1)S(1)}, bf16[96,512]{1,0:T(8,128)(2,1)S(1)}, u32[]{:S(2)}, u32[]{:S(2)}) collective-permute-start(bf16[96,512]{1,0:T(8,128)(2,1)S(1)} %get-tuple-element.70.refs_0_), channel_id=1, source_target_pairs={{0,16},{1,2},{2,1},{3,19},{4,20},{5,6},{6,5},{7,23},{8,24},{9,10},... | collective-permute-start | bytes 294920 | tf_op jit(solution)/shard_map/ppermute | solution.py:174
  232.1 7.3 %collective-permute-start.22 = (bf16[96,2048]{1,0:T(8,128)(2,1)S(1)}, bf16[96,2048]{1,0:T(8,128)(2,1)S(1)}, u32[]{:S(2)}, u32[]{:S(2)}) collective-permute-start(bf16[96,2048]{1,0:T(8,128)(2,1)S(1)} %shard_map.103), channel_id=1, source_target_pairs={{0,8},{1,9},{2,10},{3,11},{4,12},{5,13},{6,14},{7,15},{8,16},{9,17... | collective-permute-start | bytes 1179656 | tf_op jit(solution)/shard_map/ppermute | solution.py:174
  232.1 11.6 %collective-permute-start.23 = (bf16[96,2048]{1,0:T(8,128)(2,1)S(1)}, bf16[96,2048]{1,0:T(8,128)(2,1)S(1)}, u32[]{:S(2)}, u32[]{:S(2)}) collective-permute-start(bf16[96,2048]{1,0:T(8,128)(2,1)S(1)} %shard_map.103), channel_id=1, source_target_pairs={{0,12},{1,13},{2,14},{3,15},{4,8},{5,9},{6,10},{7,11},{8,20},{9,21... | collective-permute-start | bytes 1179656 | tf_op jit(solution)/shard_map/ppermute | solution.py:174
  233.8 66.0 %collective-permute-start.37 = (bf16[256,2048]{1,0:T(8,128)(2,1)S(1)}, bf16[256,2048]{1,0:T(8,128)(2,1)S(1)}, u32[]{:S(2)}, u32[]{:S(2)}) collective-permute-start(bf16[256,2048]{1,0:T(8,128)(2,1)S(1)} %add_add_fusion), channel_id=1, source_target_pairs={{1,5},{2,6},{5,1},{6,2}} | collective-permute-start | bytes 3145736 | tf_op jit(solution)/shard_map/ppermute | solution.py:174
  253.2 5.7 %collective-permute-start.24 = (bf16[96,512]{1,0:T(8,128)(2,1)S(1)}, bf16[96,512]{1,0:T(8,128)(2,1)S(1)}, u32[]{:S(2)}, u32[]{:S(2)}) collective-permute-start(bf16[96,512]{1,0:T(8,128)(2,1)S(1)} %get-tuple-element.72.refs_0_), channel_id=1, source_target_pairs={{0,16},{1,5},{2,6},{3,19},{4,20},{5,1},{6,2},{7,23},{8,24},{9,13},... | collective-permute-start | bytes 294920 | tf_op jit(solution)/shard_map/ppermute | solution.py:174
  254.2 6.8 %collective-permute-start.25 = (bf16[96,512]{1,0:T(8,128)(2,1)S(1)}, bf16[96,512]{1,0:T(8,128)(2,1)S(1)}, u32[]{:S(2)}, u32[]{:S(2)}) collective-permute-start(bf16[96,512]{1,0:T(8,128)(2,1)S(1)} %get-tuple-element.72.refs_0_), channel_id=1, source_target_pairs={{0,16},{1,2},{2,1},{3,19},{4,20},{5,6},{6,5},{7,23},{8,24},{9,10},... | collective-permute-start | bytes 294920 | tf_op jit(solution)/shard_map/ppermute | solution.py:174
  255.3 7.3 %collective-permute-start.26 = (bf16[96,512]{1,0:T(8,128)(2,1)S(1)}, bf16[96,512]{1,0:T(8,128)(2,1)S(1)}, u32[]{:S(2)}, u32[]{:S(2)}) collective-permute-start(bf16[96,512]{1,0:T(8,128)(2,1)S(1)} %get-tuple-element.72.refs_0_), channel_id=1, source_target_pairs={{0,16},{1,6},{2,5},{3,19},{4,20},{5,2},{6,1},{7,23},{8,24},{9,14},... | collective-permute-start | bytes 294920 | tf_op jit(solution)/shard_map/ppermute | solution.py:174
  264.7 7.3 %collective-permute-start.27 = (bf16[96,2048]{1,0:T(8,128)(2,1)S(1)}, bf16[96,2048]{1,0:T(8,128)(2,1)S(1)}, u32[]{:S(2)}, u32[]{:S(2)}) collective-permute-start(bf16[96,2048]{1,0:T(8,128)(2,1)S(1)} %shard_map.105), channel_id=1, source_target_pairs={{0,8},{1,9},{2,10},{3,11},{4,12},{5,13},{6,14},{7,15},{8,16},{9,17... | collective-permute-start | bytes 1179656 | tf_op jit(solution)/shard_map/ppermute | solution.py:174
  264.8 12.0 %collective-permute-start.28 = (bf16[96,2048]{1,0:T(8,128)(2,1)S(1)}, bf16[96,2048]{1,0:T(8,128)(2,1)S(1)}, u32[]{:S(2)}, u32[]{:S(2)}) collective-permute-start(bf16[96,2048]{1,0:T(8,128)(2,1)S(1)} %shard_map.105), channel_id=1, source_target_pairs={{0,12},{1,13},{2,14},{3,15},{4,8},{5,9},{6,10},{7,11},{8,20},{9,21... | collective-permute-start | bytes 1179656 | tf_op jit(solution)/shard_map/ppermute | solution.py:174
  286.3 5.7 %collective-permute-start.29 = (bf16[96,512]{1,0:T(8,128)(2,1)S(1)}, bf16[96,512]{1,0:T(8,128)(2,1)S(1)}, u32[]{:S(2)}, u32[]{:S(2)}) collective-permute-start(bf16[96,512]{1,0:T(8,128)(2,1)S(1)} %get-tuple-element.74.refs_0_), channel_id=1, source_target_pairs={{0,16},{1,5},{2,6},{3,19},{4,20},{5,1},{6,2},{7,23},{8,24},{9,13},... | collective-permute-start | bytes 294920 | tf_op jit(solution)/shard_map/ppermute | solution.py:174
  287.5 6.7 %collective-permute-start.30 = (bf16[96,512]{1,0:T(8,128)(2,1)S(1)}, bf16[96,512]{1,0:T(8,128)(2,1)S(1)}, u32[]{:S(2)}, u32[]{:S(2)}) collective-permute-start(bf16[96,512]{1,0:T(8,128)(2,1)S(1)} %get-tuple-element.74.refs_0_), channel_id=1, source_target_pairs={{0,16},{1,2},{2,1},{3,19},{4,20},{5,6},{6,5},{7,23},{8,24},{9,10},... | collective-permute-start | bytes 294920 | tf_op jit(solution)/shard_map/ppermute | solution.py:174
  288.4 7.8 %collective-permute-start.31 = (bf16[96,512]{1,0:T(8,128)(2,1)S(1)}, bf16[96,512]{1,0:T(8,128)(2,1)S(1)}, u32[]{:S(2)}, u32[]{:S(2)}) collective-permute-start(bf16[96,512]{1,0:T(8,128)(2,1)S(1)} %get-tuple-element.74.refs_0_), channel_id=1, source_target_pairs={{0,16},{1,6},{2,5},{3,19},{4,20},{5,2},{6,1},{7,23},{8,24},{9,14},... | collective-permute-start | bytes 294920 | tf_op jit(solution)/shard_map/ppermute | solution.py:174
  298.3 7.3 %collective-permute-start.32 = (bf16[96,2048]{1,0:T(8,128)(2,1)S(1)}, bf16[96,2048]{1,0:T(8,128)(2,1)S(1)}, u32[]{:S(2)}, u32[]{:S(2)}) collective-permute-start(bf16[96,2048]{1,0:T(8,128)(2,1)S(1)} %shard_map.107), channel_id=1, source_target_pairs={{0,8},{1,9},{2,10},{3,11},{4,12},{5,13},{6,14},{7,15},{8,16},{9,17... | collective-permute-start | bytes 1179656 | tf_op jit(solution)/shard_map/ppermute | solution.py:174
  298.4 11.7 %collective-permute-start.33 = (bf16[96,2048]{1,0:T(8,128)(2,1)S(1)}, bf16[96,2048]{1,0:T(8,128)(2,1)S(1)}, u32[]{:S(2)}, u32[]{:S(2)}) collective-permute-start(bf16[96,2048]{1,0:T(8,128)(2,1)S(1)} %shard_map.107), channel_id=1, source_target_pairs={{0,12},{1,13},{2,14},{3,15},{4,8},{5,9},{6,10},{7,11},{8,20},{9,21... | collective-permute-start | bytes 1179656 | tf_op jit(solution)/shard_map/ppermute | solution.py:174
  319.8 5.7 %collective-permute-start.38 = (bf16[96,512]{1,0:T(8,128)(2,1)S(1)}, bf16[96,512]{1,0:T(8,128)(2,1)S(1)}, u32[]{:S(2)}, u32[]{:S(2)}) collective-permute-start(bf16[96,512]{1,0:T(8,128)(2,1)S(1)} %get-tuple-element.77.refs_0_), channel_id=1, source_target_pairs={{0,16},{1,5},{2,6},{3,19},{4,20},{5,1},{6,2},{7,23},{8,24},{9,13},... | collective-permute-start | bytes 294920 | tf_op jit(solution)/shard_map/ppermute | solution.py:174
  320.8 6.8 %collective-permute-start.39 = (bf16[96,512]{1,0:T(8,128)(2,1)S(1)}, bf16[96,512]{1,0:T(8,128)(2,1)S(1)}, u32[]{:S(2)}, u32[]{:S(2)}) collective-permute-start(bf16[96,512]{1,0:T(8,128)(2,1)S(1)} %get-tuple-element.77.refs_0_), channel_id=1, source_target_pairs={{0,16},{1,2},{2,1},{3,19},{4,20},{5,6},{6,5},{7,23},{8,24},{9,10},... | collective-permute-start | bytes 294920 | tf_op jit(solution)/shard_map/ppermute | solution.py:174
  321.9 7.3 %collective-permute-start.40 = (bf16[96,512]{1,0:T(8,128)(2,1)S(1)}, bf16[96,512]{1,0:T(8,128)(2,1)S(1)}, u32[]{:S(2)}, u32[]{:S(2)}) collective-permute-start(bf16[96,512]{1,0:T(8,128)(2,1)S(1)} %get-tuple-element.77.refs_0_), channel_id=1, source_target_pairs={{0,16},{1,6},{2,5},{3,19},{4,20},{5,2},{6,1},{7,23},{8,24},{9,14},... | collective-permute-start | bytes 294920 | tf_op jit(solution)/shard_map/ppermute | solution.py:174
  331.4 7.3 %collective-permute-start.41 = (bf16[96,2048]{1,0:T(8,128)(2,1)S(1)}, bf16[96,2048]{1,0:T(8,128)(2,1)S(1)}, u32[]{:S(2)}, u32[]{:S(2)}) collective-permute-start(bf16[96,2048]{1,0:T(8,128)(2,1)S(1)} %get-tuple-element.80), channel_id=1, source_target_pairs={{0,8},{1,9},{2,10},{3,11},{4,12},{5,13},{6,14},{7,15},{8,16},{9,17... | collective-permute-start | bytes 1179656 | tf_op jit(solution)/shard_map/ppermute | solution.py:174
  331.5 12.0 %collective-permute-start.42 = (bf16[96,2048]{1,0:T(8,128)(2,1)S(1)}, bf16[96,2048]{1,0:T(8,128)(2,1)S(1)}, u32[]{:S(2)}, u32[]{:S(2)}) collective-permute-start(bf16[96,2048]{1,0:T(8,128)(2,1)S(1)} %get-tuple-element.80), channel_id=1, source_target_pairs={{0,12},{1,13},{2,14},{3,15},{4,8},{5,9},{6,10},{7,11},{8,20},{9,21... | collective-permute-start | bytes 1179656 | tf_op jit(solution)/shard_map/ppermute | solution.py:174
  353.0 5.7 %collective-permute-start.43 = (bf16[96,512]{1,0:T(8,128)(2,1)S(1)}, bf16[96,512]{1,0:T(8,128)(2,1)S(1)}, u32[]{:S(2)}, u32[]{:S(2)}) collective-permute-start(bf16[96,512]{1,0:T(8,128)(2,1)S(1)} %get-tuple-element.81.refs_0_), channel_id=1, source_target_pairs={{0,16},{1,5},{2,6},{3,19},{4,20},{5,1},{6,2},{7,23},{8,24},{9,13},... | collective-permute-start | bytes 294920 | tf_op jit(solution)/shard_map/ppermute | solution.py:174
  354.1 6.7 %collective-permute-start.44 = (bf16[96,512]{1,0:T(8,128)(2,1)S(1)}, bf16[96,512]{1,0:T(8,128)(2,1)S(1)}, u32[]{:S(2)}, u32[]{:S(2)}) collective-permute-start(bf16[96,512]{1,0:T(8,128)(2,1)S(1)} %get-tuple-element.81.refs_0_), channel_id=1, source_target_pairs={{0,16},{1,2},{2,1},{3,19},{4,20},{5,6},{6,5},{7,23},{8,24},{9,10},... | collective-permute-start | bytes 294920 | tf_op jit(solution)/shard_map/ppermute | solution.py:174
  355.1 7.8 %collective-permute-start.45 = (bf16[96,512]{1,0:T(8,128)(2,1)S(1)}, bf16[96,512]{1,0:T(8,128)(2,1)S(1)}, u32[]{:S(2)}, u32[]{:S(2)}) collective-permute-start(bf16[96,512]{1,0:T(8,128)(2,1)S(1)} %get-tuple-element.81.refs_0_), channel_id=1, source_target_pairs={{0,16},{1,6},{2,5},{3,19},{4,20},{5,2},{6,1},{7,23},{8,24},{9,14},... | collective-permute-start | bytes 294920 | tf_op jit(solution)/shard_map/ppermute | solution.py:174
  365.1 7.3 %collective-permute-start.46 = (bf16[96,2048]{1,0:T(8,128)(2,1)S(1)}, bf16[96,2048]{1,0:T(8,128)(2,1)S(1)}, u32[]{:S(2)}, u32[]{:S(2)}) collective-permute-start(bf16[96,2048]{1,0:T(8,128)(2,1)S(1)} %get-tuple-element.84), channel_id=1, source_target_pairs={{0,8},{1,9},{2,10},{3,11},{4,12},{5,13},{6,14},{7,15},{8,16},{9,17... | collective-permute-start | bytes 1179656 | tf_op jit(solution)/shard_map/ppermute | solution.py:174
  365.2 11.7 %collective-permute-start.47 = (bf16[96,2048]{1,0:T(8,128)(2,1)S(1)}, bf16[96,2048]{1,0:T(8,128)(2,1)S(1)}, u32[]{:S(2)}, u32[]{:S(2)}) collective-permute-start(bf16[96,2048]{1,0:T(8,128)(2,1)S(1)} %get-tuple-element.84), channel_id=1, source_target_pairs={{0,12},{1,13},{2,14},{3,15},{4,8},{5,9},{6,10},{7,11},{8,20},{9,21... | collective-permute-start | bytes 1179656 | tf_op jit(solution)/shard_map/ppermute | solution.py:174
  386.5 5.7 %collective-permute-start.48 = (bf16[96,512]{1,0:T(8,128)(2,1)S(1)}, bf16[96,512]{1,0:T(8,128)(2,1)S(1)}, u32[]{:S(2)}, u32[]{:S(2)}) collective-permute-start(bf16[96,512]{1,0:T(8,128)(2,1)S(1)} %get-tuple-element.85.refs_0_), channel_id=1, source_target_pairs={{0,16},{1,5},{2,6},{3,19},{4,20},{5,1},{6,2},{7,23},{8,24},{9,13},... | collective-permute-start | bytes 294920 | tf_op jit(solution)/shard_map/ppermute | solution.py:174
  387.5 6.8 %collective-permute-start.49 = (bf16[96,512]{1,0:T(8,128)(2,1)S(1)}, bf16[96,512]{1,0:T(8,128)(2,1)S(1)}, u32[]{:S(2)}, u32[]{:S(2)}) collective-permute-start(bf16[96,512]{1,0:T(8,128)(2,1)S(1)} %get-tuple-element.85.refs_0_), channel_id=1, source_target_pairs={{0,16},{1,2},{2,1},{3,19},{4,20},{5,6},{6,5},{7,23},{8,24},{9,10},... | collective-permute-start | bytes 294920 | tf_op jit(solution)/shard_map/ppermute | solution.py:174
  388.6 7.3 %collective-permute-start.50 = (bf16[96,512]{1,0:T(8,128)(2,1)S(1)}, bf16[96,512]{1,0:T(8,128)(2,1)S(1)}, u32[]{:S(2)}, u32[]{:S(2)}) collective-permute-start(bf16[96,512]{1,0:T(8,128)(2,1)S(1)} %get-tuple-element.85.refs_0_), channel_id=1, source_target_pairs={{0,16},{1,6},{2,5},{3,19},{4,20},{5,2},{6,1},{7,23},{8,24},{9,14},... | collective-permute-start | bytes 294920 | tf_op jit(solution)/shard_map/ppermute | solution.py:174
  398.2 7.3 %collective-permute-start.51 = (bf16[96,2048]{1,0:T(8,128)(2,1)S(1)}, bf16[96,2048]{1,0:T(8,128)(2,1)S(1)}, u32[]{:S(2)}, u32[]{:S(2)}) collective-permute-start(bf16[96,2048]{1,0:T(8,128)(2,1)S(1)} %get-tuple-element.88), channel_id=1, source_target_pairs={{0,8},{1,9},{2,10},{3,11},{4,12},{5,13},{6,14},{7,15},{8,16},{9,17... | collective-permute-start | bytes 1179656 | tf_op jit(solution)/shard_map/ppermute | solution.py:174
  398.2 12.0 %collective-permute-start.52 = (bf16[96,2048]{1,0:T(8,128)(2,1)S(1)}, bf16[96,2048]{1,0:T(8,128)(2,1)S(1)}, u32[]{:S(2)}, u32[]{:S(2)}) collective-permute-start(bf16[96,2048]{1,0:T(8,128)(2,1)S(1)} %get-tuple-element.88), channel_id=1, source_target_pairs={{0,12},{1,13},{2,14},{3,15},{4,8},{5,9},{6,10},{7,11},{8,20},{9,21... | collective-permute-start | bytes 1179656 | tf_op jit(solution)/shard_map/ppermute | solution.py:174
  421.1 6.0 %collective-permute-start.53 = (bf16[96,512]{1,0:T(8,128)(2,1)}, bf16[96,512]{1,0:T(8,128)(2,1)}, u32[]{:S(2)}, u32[]{:S(2)}) collective-permute-start(bf16[96,512]{1,0:T(8,128)(2,1)} %get-tuple-element.89.refs_0_), channel_id=1, source_target_pairs={{0,16},{1,5},{2,6},{3,19},{4,20},{5,1},{6,2},{7,23},{8,24},{9,13},... | collective-permute-start | bytes 294920 | tf_op jit(solution)/shard_map/ppermute | solution.py:174
  422.2 7.0 %collective-permute-start.54 = (bf16[96,512]{1,0:T(8,128)(2,1)}, bf16[96,512]{1,0:T(8,128)(2,1)}, u32[]{:S(2)}, u32[]{:S(2)}) collective-permute-start(bf16[96,512]{1,0:T(8,128)(2,1)} %get-tuple-element.89.refs_0_), channel_id=1, source_target_pairs={{0,16},{1,2},{2,1},{3,19},{4,20},{5,6},{6,5},{7,23},{8,24},{9,10},... | collective-permute-start | bytes 294920 | tf_op jit(solution)/shard_map/ppermute | solution.py:174
  423.1 8.1 %collective-permute-start.55 = (bf16[96,512]{1,0:T(8,128)(2,1)}, bf16[96,512]{1,0:T(8,128)(2,1)}, u32[]{:S(2)}, u32[]{:S(2)}) collective-permute-start(bf16[96,512]{1,0:T(8,128)(2,1)} %get-tuple-element.89.refs_0_), channel_id=1, source_target_pairs={{0,16},{1,6},{2,5},{3,19},{4,20},{5,2},{6,1},{7,23},{8,24},{9,14},... | collective-permute-start | bytes 294920 | tf_op jit(solution)/shard_map/ppermute | solution.py:174
  438.4 7.3 %collective-permute-start.56 = (bf16[96,2048]{1,0:T(8,128)(2,1)S(1)}, bf16[96,2048]{1,0:T(8,128)(2,1)S(1)}, u32[]{:S(2)}, u32[]{:S(2)}) collective-permute-start(bf16[96,2048]{1,0:T(8,128)(2,1)S(1)} %get-tuple-element.92), channel_id=1, source_target_pairs={{0,8},{1,9},{2,10},{3,11},{4,12},{5,13},{6,14},{7,15},{8,16},{9,17... | collective-permute-start | bytes 1179656 | tf_op jit(solution)/shard_map/ppermute | solution.py:174
  438.5 11.7 %collective-permute-start.57 = (bf16[96,2048]{1,0:T(8,128)(2,1)S(1)}, bf16[96,2048]{1,0:T(8,128)(2,1)S(1)}, u32[]{:S(2)}, u32[]{:S(2)}) collective-permute-start(bf16[96,2048]{1,0:T(8,128)(2,1)S(1)} %get-tuple-element.92), channel_id=1, source_target_pairs={{0,12},{1,13},{2,14},{3,15},{4,8},{5,9},{6,10},{7,11},{8,20},{9,21... | collective-permute-start | bytes 1179656 | tf_op jit(solution)/shard_map/ppermute | solution.py:174
  460.7 6.8 %collective-permute-start.59 = (bf16[96,512]{1,0:T(8,128)(2,1)S(1)}, bf16[96,512]{1,0:T(8,128)(2,1)S(1)}, u32[]{:S(2)}, u32[]{:S(2)}) collective-permute-start(bf16[96,512]{1,0:T(8,128)(2,1)S(1)} %get-tuple-element.93.refs_0_), channel_id=1, source_target_pairs={{0,16},{1,2},{2,1},{3,19},{4,20},{5,6},{6,5},{7,23},{8,24},{9,10},... | collective-permute-start | bytes 294920 | tf_op jit(solution)/shard_map/ppermute | solution.py:174
  461.8 7.3 %collective-permute-start.60 = (bf16[96,512]{1,0:T(8,128)(2,1)S(1)}, bf16[96,512]{1,0:T(8,128)(2,1)S(1)}, u32[]{:S(2)}, u32[]{:S(2)}) collective-permute-start(bf16[96,512]{1,0:T(8,128)(2,1)S(1)} %get-tuple-element.93.refs_0_), channel_id=1, source_target_pairs={{0,16},{1,6},{2,5},{3,19},{4,20},{5,2},{6,1},{7,23},{8,24},{9,14},... | collective-permute-start | bytes 294920 | tf_op jit(solution)/shard_map/ppermute | solution.py:174
  471.3 7.3 %collective-permute-start.61 = (bf16[96,2048]{1,0:T(8,128)(2,1)S(1)}, bf16[96,2048]{1,0:T(8,128)(2,1)S(1)}, u32[]{:S(2)}, u32[]{:S(2)}) collective-permute-start(bf16[96,2048]{1,0:T(8,128)(2,1)S(1)} %get-tuple-element.96), channel_id=1, source_target_pairs={{0,8},{1,9},{2,10},{3,11},{4,12},{5,13},{6,14},{7,15},{8,16},{9,17... | collective-permute-start | bytes 1179656 | tf_op jit(solution)/shard_map/ppermute | solution.py:174
  471.4 12.0 %collective-permute-start.62 = (bf16[96,2048]{1,0:T(8,128)(2,1)S(1)}, bf16[96,2048]{1,0:T(8,128)(2,1)S(1)}, u32[]{:S(2)}, u32[]{:S(2)}) collective-permute-start(bf16[96,2048]{1,0:T(8,128)(2,1)S(1)} %get-tuple-element.96), channel_id=1, source_target_pairs={{0,12},{1,13},{2,14},{3,15},{4,8},{5,9},{6,10},{7,11},{8,20},{9,21... | collective-permute-start | bytes 1179656 | tf_op jit(solution)/shard_map/ppermute | solution.py:174
  493.1 5.7 %collective-permute-start.63 = (bf16[96,512]{1,0:T(8,128)(2,1)S(1)}, bf16[96,512]{1,0:T(8,128)(2,1)S(1)}, u32[]{:S(2)}, u32[]{:S(2)}) collective-permute-start(bf16[96,512]{1,0:T(8,128)(2,1)S(1)} %get-tuple-element.97.refs_0_), channel_id=1, source_target_pairs={{0,16},{1,5},{2,6},{3,19},{4,20},{5,1},{6,2},{7,23},{8,24},{9,13},... | collective-permute-start | bytes 294920 | tf_op jit(solution)/shard_map/ppermute | solution.py:174
  494.3 6.7 %collective-permute-start.64 = (bf16[96,512]{1,0:T(8,128)(2,1)S(1)}, bf16[96,512]{1,0:T(8,128)(2,1)S(1)}, u32[]{:S(2)}, u32[]{:S(2)}) collective-permute-start(bf16[96,512]{1,0:T(8,128)(2,1)S(1)} %get-tuple-element.97.refs_0_), channel_id=1, source_target_pairs={{0,16},{1,2},{2,1},{3,19},{4,20},{5,6},{6,5},{7,23},{8,24},{9,10},... | collective-permute-start | bytes 294920 | tf_op jit(solution)/shard_map/ppermute | solution.py:174
  495.2 7.8 %collective-permute-start.65 = (bf16[96,512]{1,0:T(8,128)(2,1)S(1)}, bf16[96,512]{1,0:T(8,128)(2,1)S(1)}, u32[]{:S(2)}, u32[]{:S(2)}) collective-permute-start(bf16[96,512]{1,0:T(8,128)(2,1)S(1)} %get-tuple-element.97.refs_0_), channel_id=1, source_target_pairs={{0,16},{1,6},{2,5},{3,19},{4,20},{5,2},{6,1},{7,23},{8,24},{9,14},... | collective-permute-start | bytes 294920 | tf_op jit(solution)/shard_map/ppermute | solution.py:174
  505.2 7.3 %collective-permute-start.66 = (bf16[96,2048]{1,0:T(8,128)(2,1)S(1)}, bf16[96,2048]{1,0:T(8,128)(2,1)S(1)}, u32[]{:S(2)}, u32[]{:S(2)}) collective-permute-start(bf16[96,2048]{1,0:T(8,128)(2,1)S(1)} %get-tuple-element.100), channel_id=1, source_target_pairs={{0,8},{1,9},{2,10},{3,11},{4,12},{5,13},{6,14},{7,15},{8,16},{9,17... | collective-permute-start | bytes 1179656 | tf_op jit(solution)/shard_map/ppermute | solution.py:174
  505.3 11.7 %collective-permute-start.67 = (bf16[96,2048]{1,0:T(8,128)(2,1)S(1)}, bf16[96,2048]{1,0:T(8,128)(2,1)S(1)}, u32[]{:S(2)}, u32[]{:S(2)}) collective-permute-start(bf16[96,2048]{1,0:T(8,128)(2,1)S(1)} %get-tuple-element.100), channel_id=1, source_target_pairs={{0,12},{1,13},{2,14},{3,15},{4,8},{5,9},{6,10},{7,11},{8,20},{9,21... | collective-permute-start | bytes 1179656 | tf_op jit(solution)/shard_map/ppermute | solution.py:174
  527.5 6.8 %collective-permute-start.69 = (bf16[96,512]{1,0:T(8,128)(2,1)S(1)}, bf16[96,512]{1,0:T(8,128)(2,1)S(1)}, u32[]{:S(2)}, u32[]{:S(2)}) collective-permute-start(bf16[96,512]{1,0:T(8,128)(2,1)S(1)} %get-tuple-element.101), channel_id=1, source_target_pairs={{0,16},{1,2},{2,1},{3,19},{4,20},{5,6},{6,5},{7,23},{8,24},{9,10},... | collective-permute-start | bytes 294920 | tf_op jit(solution)/shard_map/ppermute | solution.py:174
  528.5 7.3 %collective-permute-start.70 = (bf16[96,512]{1,0:T(8,128)(2,1)S(1)}, bf16[96,512]{1,0:T(8,128)(2,1)S(1)}, u32[]{:S(2)}, u32[]{:S(2)}) collective-permute-start(bf16[96,512]{1,0:T(8,128)(2,1)S(1)} %get-tuple-element.101), channel_id=1, source_target_pairs={{0,16},{1,6},{2,5},{3,19},{4,20},{5,2},{6,1},{7,23},{8,24},{9,14},... | collective-permute-start | bytes 294920 | tf_op jit(solution)/shard_map/ppermute | solution.py:174
  (56 other events, 728.7 us)

commit v4 on v3

--- a/solution.py
+++ b/solution.py
@@ -12,17 +12,16 @@
 M = 16
 EPSILON = 1e-05
 AXES = ("section", "tp", "doc")
-C_FIRST, C_INIT, C_TP, C_POOL, C_PHASE, C_LEN = 0, 1, 2, 3, 4, 5
-
-
-def attend_kernel(turn, docs, tokens, blocks, sets, meta, where, *refs):
+C_FIRST, C_INIT, C_TP, C_POOL, C_LEN = 0, 1, 2, 3, 4
+
+
+def attend_kernel(turn, docs, tokens, blocks, meta, where, *refs):
     halves = refs[0]
     other = refs[1]
     tok, tok_other, mem, mem_other, gain = refs[2:7]
-    held = 1 + sets * (blocks - 1)
-    weights = refs[7 : 7 + held]
-    mixed_ref, keep_ref = refs[7 + held : 9 + held]
-    normed, acc = refs[9 + held :]
+    weights = refs[7 : 7 + blocks]
+    mixed_ref, keep_ref = refs[7 + blocks : 9 + blocks]
+    normed, acc = refs[9 + blocks :]
     rows = M + tokens
     half = halves.shape[1]
     depth = weights[0].shape[0]
@@ -53,29 +52,16 @@
         return 0
 
     lax.fori_loop(0, docs, prepare, 0)
-
-    def multiply(b, weight):
+    for b in range(blocks):
         at = pl.multiple_of(where[b] * depth, 128)
         left = normed[:, pl.ds(at, depth)]
         for c in range(3):
             span = pl.ds(c * cols, cols)
-            part = jnp.dot(left, weight[:, span], preferred_element_type=jnp.float32)
+            part = jnp.dot(left, weights[b][:, span], preferred_element_type=jnp.float32)
             if b == 0:
                 acc[:, span] = part
             else:
                 acc[:, span] += part
-
-    multiply(0, weights[0])
-    for phase in range(sets):
-
-        def received(phase=phase):
-            for b in range(1, blocks):
-                multiply(b, weights[b + phase * (blocks - 1)])
-
-        if sets == 1:
-            received()
-        else:
-            pl.when(meta[turn, C_PHASE] == phase)(received)
 
     row = lax.broadcasted_iota(jnp.int32, (rows, rows), 0)
     col = lax.broadcasted_iota(jnp.int32, (rows, rows), 1)
@@ -103,6 +89,22 @@
         return 0
 
     lax.fori_loop(0, docs, one, 0)
+
+
+def choose_kernel(count, phase, *refs):
+    outs, sems = refs[2 * count : 3 * count], refs[3 * count]
+    for p in range(2):
+
+        @pl.when(phase[0] == p)
+        def _(p=p):
+            copies = [
+                pltpu.make_async_copy(refs[p * count + b], outs[b], sems.at[b])
+                for b in range(count)
+            ]
+            for copy in copies:
+                copy.start()
+            for copy in copies:
+                copy.wait()
 
 
 def project_kernel(turn, docs, tokens, parts, pool, meta, place, mix, *refs):
@@ -167,7 +169,7 @@
     def lin(a, b, c):
         return (a * T + b) * D + c
 
-    limit = 24 * 2**20 + 2 * R * (4 * half + 12 * cols)
+    limit = 20 * 2**20 + 2 * R * (4 * half + 12 * cols)
     params = pltpu.CompilerParams(vmem_limit_bytes=limit)
 
     def send(block, pairs):
@@ -224,17 +226,19 @@
             full = full + send(picked, [((a, b, c), (0, b, c)) for b in range(T) for c in planes])
         return full, send(full, [((0, b, c), (0, T - 1 - b, c)) for b in range(T) for c in planes])
 
-    ids, blocks = lax.optimization_barrier((ids, blocks))
+    first_ids = ids[:n, 0]
+    rest_ids = jnp.concatenate([ids[n:, 0]] + [ids[:, seg] for seg in range(1, segs)])
     even = relay(0, blocks)
-    pairs = [embed(ids[:, 0])]
+    tok_first = embed(first_ids)
     mem_other = send(mem_init, [((0, b, c), (0, T - 1 - b, c)) for b in range(T) for c in planes])
-    blocks, even, pairs, mem_other, ids = lax.optimization_barrier(
-        (blocks, even, pairs, mem_other, ids)
+    gate = sum(e[:M, :HD].astype(jnp.float32) for e in even).astype(jnp.bfloat16)
+    gate = send(gate, [(e, (e[0] ^ 1, e[1], e[2])) for e in everyone])
+    blocks, gate, even, tok_first, mem_other, rest_ids = lax.optimization_barrier(
+        (blocks, gate, even, tok_first, mem_other, rest_ids)
     )
     odd = relay(1, blocks)
-    for seg in range(1, segs):
-        pairs.append(embed(ids[:, seg]))
-    tok, tok_other = zip(*pairs)
+    zero = jnp.minimum(jnp.abs(gate[0, 0]), 0).astype(jnp.int32)
+    tok_rest = embed(rest_ids + zero)
 
     offset = jnp.arange(turns) - s
     group = offset % S
@@ -248,7 +252,6 @@
             (s == 0) & (offset < S),
             jnp.full((turns,), t),
             active & (segment == segs - 1),
-            jnp.full((turns,), s % 2),
         ],
         1,
     ).astype(jnp.int32)
@@ -267,13 +270,27 @@
     other = jnp.zeros((R, half), jnp.bfloat16)
     pools = []
     for k in range(turns):
-        sets = 1 if k == 0 else 2
-        weights = [own_block] + even + (odd if k else [])
-        g, seg = k % S, k // S
-        rows_of = slice(g * n * tokens, (g + 1) * n * tokens)
-        tk, tko = (a[min(seg, segs - 1)][rows_of] for a in (tok, tok_other))
+        if k == 0:
+            weights = [own_block] + even
+            tk, tko = tok_first
+        elif k == 1:
+            count = len(even)
+            weights = [own_block] + list(
+                pl.pallas_call(
+                    functools.partial(choose_kernel, count),
+                    out_shape=[jax.ShapeDtypeStruct(e.shape, e.dtype) for e in even],
+                    in_specs=[smem] + [pl.BlockSpec(memory_space=pl.ANY)] * (2 * count),
+                    out_specs=[vmem] * count,
+                    scratch_shapes=[pltpu.SemaphoreType.DMA((count,))],
+                    compiler_params=params,
+                )((s % 2).astype(jnp.int32).reshape(1), *even, *odd)
+            )
+        if k > 0:
+            step = n * tokens
+            at = min(k, segs * S - 1) - 1
+            tk, tko = (a[at * step : (at + 1) * step] for a in tok_rest)
         mixed, keep = pl.pallas_call(
-            functools.partial(attend_kernel, k, n, tokens, D, sets),
+            functools.partial(attend_kernel, k, n, tokens, D),
             out_shape=(
                 jax.ShapeDtypeStruct((R, cols), jnp.bfloat16),
                 jax.ShapeDtypeStruct((R, half), jnp.bfloat16),

time: 558 us -> 535 us (0.959)
  starting transfers between devices: 88.6 us -> 143 us
  Pallas kernels: 126 us -> 77.3 us
  waiting for transfers between devices: 270 us -> 231 us
  local copies, waits for them, and re-layouts: 50.5 us -> 58.3 us
    ppermute x75 -> x76, starting transfers between devices: 88.6 us -> 143 us  [send(): return lax.ppermute(block, AXES, [(lin(*a), lin(*b)) for a, b in pairs])]
    pallas_call x11 -> x12, Pallas kernels: 103 us -> 54.7 us  [the longest x11 51.8 us: body(): pl.pallas_call(functools.partial(attend_kernel, k, n, tokens, D), out_sha...]
    ppermute x75 -> x76, waiting for transfers between devices: 270 us -> 231 us  [send(): return lax.ppermute(block, AXES, [(lin(*a), lin(*b)) for a, b in pairs])]
    unnamed x96 -> x89, local copies, waits for them, and re-layouts: 13.1 us -> 19.6 us
  transfers between devices with their start and end apart: 75 -> 76, of which waited for: 56 -> 57; matrix products, arithmetic and copies ran while one was open for 6% -> 6% of each run, Pallas kernels for 8% -> 2%
where the time goes in v4:
time: 535 us; the launch traced here: 526 us
  waiting for transfers between devices  231 us (43%)
  starting transfers between devices  143 us (27%)
  Pallas kernels  77.3 us (14%)
  local copies, waits for them, and re-layouts  58.3 us (11%)
  other arithmetic  14.1 us (3%)
    ppermute x76, waiting for transfers between devices, send(): return lax.ppermute(block, AXES, [(lin(*a), lin(*b)) for a, b in pairs])  231 us
    ppermute x76, starting transfers between devices, send(): return lax.ppermute(block, AXES, [(lin(*a), lin(*b)) for a, b in pairs])  143 us
    pallas_call x11, Pallas kernels, body(): pl.pallas_call(functools.partial(attend_kernel, k, n, tokens, D), out_sha...  51.8 us
    pallas_call x10, Pallas kernels, body(): pl.pallas_call(functools.partial(project_kernel, k, n, tokens, parts, poo...  22.6 us
    gather x2, local copies, waits for them, and re-layouts, embed(): picked = jnp.take(emb_table, jnp.clip(local, 0, vocab - 1), axis=0)  22 us
    unnamed x89, local copies, waits for them, and re-layouts  19.6 us
  transfers between devices with their start and end apart: 76, of which 57 were waited for; matrix products, arithmetic and copies ran while one was open for 6% of the time, Pallas kernels for 2%

profile of v4, /device:TPU:0, one launch (start us, length us, event | category | flops | bytes accessed | tf_op | source)
XLA Modules:
  0.0 526.2 jit_solution(13395678819135735871)
XLA Ops:
  1.5 3.0 collective-permute-start
  4.6 2.6 collective-permute-start.1
  7.1 3.7 dynamic-slice_bitcast_fusion.2
  10.9 2.4 dynamic-slice_bitcast_fusion
  15.0 2.4 collective-permute-start.5
  19.3 2.3 collective-permute-start.4
  23.3 3.0 collective-permute-start.3
  28.6 57.4 %collective-permute-done.2 = s32[2,2,33]{2,1,0:T(2,128)S(1)} collective-permute-done((s32[2,2,33]{2,1,0:T(2,128)S(1)}, s32[2,2,33]{2,1,0:T(2,128)S(1)}, u32[]{:S(2)}, u32[]{:S(2)}) %collective-permute-start.2) | collective-permute-done | bytes 560 | tf_op jit(solution)/shard_map/ppermute | solution.py:176
  86.5 8.9 %gather_fusion.1 = bf16[64,2048]{1,0:T(8,128)(2,1)S(1)} fusion(bf16[4096,2048]{1,0:T(8,128)(2,1)} %param.12, s32[1024]{0:T(1024)S(1)} %pad_clamp_fusion.1), kind=kCustom, calls=%fused_computation.1 | custom fusion | bytes 524544 | tf_op jit(solution)/shard_map/jit(_take)/gather | solution.py:222
  103.2 13.1 %gather_fusion.2 = bf16[448,2048]{1,0:T(8,128)(2,1)} fusion(bf16[4096,2048]{1,0:T(8,128)(2,1)} %param.12, s32[1024]{0:T(1024)S(1)} %pad_clamp_fusion), kind=kCustom, calls=%fused_computation.2 | custom fusion | bytes 3671808 | tf_op jit(solution)/shard_map/jit(_take)/gather | solution.py:222
  121.1 2.3 collective-permute-start.21
  123.4 2.4 collective-permute-start.22
  125.8 2.4 collective-permute-start.23
  139.2 6.6 %shard_map.100 = (bf16[96,512]{1,0:T(8,128)(2,1)S(1)}, bf16[96,2048]{1,0:T(8,128)(2,1)S(1)}) custom-call(s32[11,6]{1,0:T(8,128)S(1)} %concatenate.26.meta, s32[4]{0:T(128)S(1)} %pad_add_fusion.4.where, bf16[96,2048]{1,0:T(8,128)(2,1)S(1)} %broadcast_14_refs_0__refs_1_.2.refs_0_.refs_1_, bf16[96,2048]{1,0:T(8,128)(2,1)S(1)} %broadcast_14_refs_0__refs_1_.2.refs_0_.refs_1_, ...), custom_call_target="tpu_custom_call" | custom-call | tf_op jit(solution)/shard_map/pallas_call | solution.py:292
  148.1 3.1 collective-permute-done.12.refs_1_
  153.4 2.6 collective-permute-done.13.refs_2_
  157.5 3.0 collective-permute-done.14.refs_3_
  160.6 3.4 copy-done
  164.9 2.4 shard_map.101
  167.4 21.2 %collective-permute-start.15 = (bf16[96,2048]{1,0:T(8,128)(2,1)S(1)}, bf16[96,2048]{1,0:T(8,128)(2,1)S(1)}, u32[]{:S(2)}, u32[]{:S(2)}) collective-permute-start(bf16[96,2048]{1,0:T(8,128)(2,1)S(1)} %shard_map.101), channel_id=1, source_target_pairs={{0,8},{1,9},{2,10},{3,11},{4,12},{5,13},{6,14},{7,15},{8,16},{9,17... | collective-permute-start | bytes 1179656 | tf_op jit(solution)/shard_map/ppermute | solution.py:176
  190.4 2.9 shard_map.102
  193.3 3.1 fusion.26
  196.4 3.5 collective-permute-done.16.refs_1_
  199.9 4.4 shard_map.103
  213.9 19.7 %collective-permute-start.27 = (bf16[96,2048]{1,0:T(8,128)(2,1)S(1)}, bf16[96,2048]{1,0:T(8,128)(2,1)S(1)}, u32[]{:S(2)}, u32[]{:S(2)}) collective-permute-start(bf16[96,2048]{1,0:T(8,128)(2,1)S(1)} %shard_map.104), channel_id=1, source_target_pairs={{0,8},{1,9},{2,10},{3,11},{4,12},{5,13},{6,14},{7,15},{8,16},{9,17... | collective-permute-start | bytes 1179656 | tf_op jit(solution)/shard_map/ppermute | solution.py:176
  233.7 6.4 %collective-permute-done.27.refs_0_ = bf16[96,2048]{1,0:T(8,128)(2,1)S(1)} collective-permute-done((bf16[96,2048]{1,0:T(8,128)(2,1)S(1)}, bf16[96,2048]{1,0:T(8,128)(2,1)S(1)}, u32[]{:S(2)}, u32[]{:S(2)}) %collective-permute-start.27) | collective-permute-done | bytes 393248 | tf_op jit(solution)/shard_map/ppermute | solution.py:176
  240.1 4.1 collective-permute-done.28.refs_1_
  244.2 4.4 shard_map.105
  251.4 2.9 collective-permute-done.29.refs_1_
  262.3 5.6 %collective-permute-done.32.refs_0_ = bf16[96,2048]{1,0:T(8,128)(2,1)S(1)} collective-permute-done((bf16[96,2048]{1,0:T(8,128)(2,1)S(1)}, bf16[96,2048]{1,0:T(8,128)(2,1)S(1)}, u32[]{:S(2)}, u32[]{:S(2)}) %collective-permute-start.32) | collective-permute-done | bytes 393248 | tf_op jit(solution)/shard_map/ppermute | solution.py:176
  268.0 4.1 collective-permute-done.33.refs_1_
  272.1 4.4 shard_map.107
  280.0 2.3 collective-permute-done.34.refs_1_
  290.2 5.4 %collective-permute-done.37.refs_0_ = bf16[96,2048]{1,0:T(8,128)(2,1)S(1)} collective-permute-done((bf16[96,2048]{1,0:T(8,128)(2,1)S(1)}, bf16[96,2048]{1,0:T(8,128)(2,1)S(1)}, u32[]{:S(2)}, u32[]{:S(2)}) %collective-permute-start.37) | collective-permute-done | bytes 393248 | tf_op jit(solution)/shard_map/ppermute | solution.py:176
  295.6 5.2 collective-permute-done.38.refs_1_
  300.7 4.4 shard_map.109
  308.0 2.9 collective-permute-done.39.refs_1_
  318.8 5.6 %collective-permute-done.42.refs_0_ = bf16[96,2048]{1,0:T(8,128)(2,1)S(1)} collective-permute-done((bf16[96,2048]{1,0:T(8,128)(2,1)S(1)}, bf16[96,2048]{1,0:T(8,128)(2,1)S(1)}, u32[]{:S(2)}, u32[]{:S(2)}) %collective-permute-start.42) | collective-permute-done | bytes 393248 | tf_op jit(solution)/shard_map/ppermute | solution.py:176
  324.4 4.3 collective-permute-done.43.refs_1_
  328.6 4.5 shard_map.111
  346.8 5.2 collective-permute-done.47.refs_0_
  352.0 5.2 collective-permute-done.48.refs_1_
  357.2 4.4 shard_map.113
  364.4 3.0 collective-permute-done.49.refs_1_
  375.5 5.6 %collective-permute-done.52.refs_0_ = bf16[96,2048]{1,0:T(8,128)(2,1)S(1)} collective-permute-done((bf16[96,2048]{1,0:T(8,128)(2,1)S(1)}, bf16[96,2048]{1,0:T(8,128)(2,1)S(1)}, u32[]{:S(2)}, u32[]{:S(2)}) %collective-permute-start.52) | collective-permute-done | bytes 393248 | tf_op jit(solution)/shard_map/ppermute | solution.py:176
  381.0 4.3 collective-permute-done.53.refs_1_
  385.3 5.1 shard_map.115
  394.6 2.5 collective-permute-done.54.refs_1_
  400.9 3.4 copy-done.1
  405.3 2.8 shard_map.116
  410.0 5.4 %collective-permute-done.57.refs_0_ = bf16[96,2048]{1,0:T(8,128)(2,1)S(1)} collective-permute-done((bf16[96,2048]{1,0:T(8,128)(2,1)S(1)}, bf16[96,2048]{1,0:T(8,128)(2,1)S(1)}, u32[]{:S(2)}, u32[]{:S(2)}) %collective-permute-start.57) | collective-permute-done | bytes 393248 | tf_op jit(solution)/shard_map/ppermute | solution.py:176
  415.4 5.2 collective-permute-done.58.refs_1_
  424.4 4.4 shard_map.117
  431.6 3.0 collective-permute-done.59.refs_1_
  442.6 5.3 %collective-permute-done.62.refs_0_ = bf16[96,2048]{1,0:T(8,128)(2,1)S(1)} collective-permute-done((bf16[96,2048]{1,0:T(8,128)(2,1)S(1)}, bf16[96,2048]{1,0:T(8,128)(2,1)S(1)}, u32[]{:S(2)}, u32[]{:S(2)}) %collective-permute-start.62) | collective-permute-done | bytes 393248 | tf_op jit(solution)/shard_map/ppermute | solution.py:176
  448.0 4.3 collective-permute-done.63.refs_1_
  452.3 4.5 shard_map.119
  470.5 5.4 %collective-permute-done.67.refs_0_ = bf16[96,2048]{1,0:T(8,128)(2,1)S(1)} collective-permute-done((bf16[96,2048]{1,0:T(8,128)(2,1)S(1)}, bf16[96,2048]{1,0:T(8,128)(2,1)S(1)}, u32[]{:S(2)}, u32[]{:S(2)}) %collective-permute-start.67) | collective-permute-done | bytes 393248 | tf_op jit(solution)/shard_map/ppermute | solution.py:176
  475.9 5.2 collective-permute-done.68.refs_1_
  481.1 4.5 shard_map.121
  488.3 3.0 collective-permute-done.69
  495.2 2.9 shard_map.122
  503.3 19.0 %collective-permute-start.75 = (f32[8,2048]{1,0:T(8,128)S(1)}, f32[8,2048]{1,0:T(8,128)S(1)}, u32[]{:S(2)}, u32[]{:S(2)}) collective-permute-start(f32[8,2048]{1,0:T(8,128)S(1)} %add_add_fusion.2), channel_id=1, source_target_pairs={{1,0},{2,3},{5,4},{6,7},{9,8},{10,11},{13,12},{14,15},{17,16},{18,... | collective-permute-start | bytes 196616 | tf_op jit(solution)/shard_map/ppermute | solution.py:176
  522.3 2.8 collective-permute-done.75
  (262 shorter events, 158.9 us)
Async XLA Ops:
  1.5 24.8 %collective-permute-start = (s32[2,2,33]{2,1,0:T(2,128)S(1)}, s32[2,2,33]{2,1,0:T(2,128)S(1)}, u32[]{:S(2)}, u32[]{:S(2)}) collective-permute-start(s32[2,2,33]{2,1,0:T(2,128)S(1)} %pad_add_fusion.2), channel_id=1, source_target_pairs={{0,1},{1,2},{2,3},{3,0},{4,5},{5,6},{6,7},{7,4},{8,9},{9,10},{10,1... | collective-permute-start | bytes 1592 | tf_op jit(solution)/shard_map/ppermute | solution.py:176
  4.6 24.1 %collective-permute-start.1 = (s32[2,2,33]{2,1,0:T(2,128)S(1)}, s32[2,2,33]{2,1,0:T(2,128)S(1)}, u32[]{:S(2)}, u32[]{:S(2)}) collective-permute-start(s32[2,2,33]{2,1,0:T(2,128)S(1)} %pad_add_fusion.2), channel_id=1, source_target_pairs={{0,2},{1,3},{2,0},{3,1},{4,6},{5,7},{6,4},{7,5},{8,10},{9,11},{10,... | collective-permute-start | bytes 1592 | tf_op jit(solution)/shard_map/ppermute | solution.py:176
  15.0 84.8 %collective-permute-start.5 = (bf16[1024,1536]{1,0:T(8,128)(2,1)}, bf16[1024,1536]{1,0:T(8,128)(2,1)S(1)}, u32[]{:S(2)}, u32[]{:S(2)}) collective-permute-start(bf16[1024,1536]{1,0:T(8,128)(2,1)} %pad_maximum_fusion.2), channel_id=1, source_target_pairs={{3,1},{0,2},{7,5},{4,6},{19,17},{16,18},{23,21},{20,22}} | collective-permute-start | bytes 9437192 | tf_op jit(solution)/shard_map/ppermute | solution.py:176
  19.3 80.6 %collective-permute-start.4 = (bf16[1024,1536]{1,0:T(8,128)(2,1)}, bf16[1024,1536]{1,0:T(8,128)(2,1)}, u32[]{:S(2)}, u32[]{:S(2)}) collective-permute-start(bf16[1024,1536]{1,0:T(8,128)(2,1)} %pad_maximum_fusion.1), channel_id=1, source_target_pairs={{2,1},{1,2},{6,5},{5,6},{18,17},{17,18},{22,21},{21,22}} | collective-permute-start | bytes 9437192 | tf_op jit(solution)/shard_map/ppermute | solution.py:176
  23.3 76.6 %collective-permute-start.3 = (bf16[1024,1536]{1,0:T(8,128)(2,1)}, bf16[1024,1536]{1,0:T(8,128)(2,1)}, u32[]{:S(2)}, u32[]{:S(2)}) collective-permute-start(bf16[1024,1536]{1,0:T(8,128)(2,1)} %pad_maximum_fusion), channel_id=1, source_target_pairs={{0,1},{3,2},{4,5},{7,6},{16,17},{19,18},{20,21},{23,22}} | collective-permute-start | bytes 9437192 | tf_op jit(solution)/shard_map/ppermute | solution.py:176
  26.4 59.7 %collective-permute-start.2 = (s32[2,2,33]{2,1,0:T(2,128)S(1)}, s32[2,2,33]{2,1,0:T(2,128)S(1)}, u32[]{:S(2)}, u32[]{:S(2)}) collective-permute-start(s32[2,2,33]{2,1,0:T(2,128)S(1)} %pad_add_fusion.2), channel_id=1, source_target_pairs={{0,3},{1,0},{2,1},{3,2},{4,7},{5,4},{6,5},{7,6},{8,11},{9,8},{10,9... | collective-permute-start | bytes 1592 | tf_op jit(solution)/shard_map/ppermute | solution.py:176
  118.2 7.5 %collective-permute-start.17 = (bf16[448,2048]{1,0:T(8,128)(2,1)S(1)}, bf16[448,2048]{1,0:T(8,128)(2,1)S(1)}, u32[]{:S(2)}, u32[]{:S(2)}) collective-permute-start(bf16[448,2048]{1,0:T(8,128)(2,1)S(1)} %select_select_fusion), channel_id=1, source_target_pairs={{9,1},{10,2},{13,5},{14,6}} | collective-permute-start | bytes 5505032 | tf_op jit(solution)/shard_map/ppermute | solution.py:176
  119.0 9.1 %collective-permute-start.18 = (bf16[448,2048]{1,0:T(8,128)(2,1)S(1)}, bf16[448,2048]{1,0:T(8,128)(2,1)S(1)}, u32[]{:S(2)}, u32[]{:S(2)}) collective-permute-start(bf16[448,2048]{1,0:T(8,128)(2,1)S(1)} %select_select_fusion), channel_id=1, source_target_pairs={{17,1},{18,2},{21,5},{22,6}} | collective-permute-start | bytes 5505032 | tf_op jit(solution)/shard_map/ppermute | solution.py:176
  119.8 8.4 %collective-permute-start.19 = (bf16[448,2048]{1,0:T(8,128)(2,1)S(1)}, bf16[448,2048]{1,0:T(8,128)(2,1)S(1)}, u32[]{:S(2)}, u32[]{:S(2)}) collective-permute-start(bf16[448,2048]{1,0:T(8,128)(2,1)S(1)} %select_select_fusion), channel_id=1, source_target_pairs={{25,1},{26,2},{29,5},{30,6}} | collective-permute-start | bytes 5505032 | tf_op jit(solution)/shard_map/ppermute | solution.py:176
  121.1 69.1 %collective-permute-start.21 = (bf16[1024,1536]{1,0:T(8,128)(2,1)}, bf16[1024,1536]{1,0:T(8,128)(2,1)}, u32[]{:S(2)}, u32[]{:S(2)}) collective-permute-start(bf16[1024,1536]{1,0:T(8,128)(2,1)} %pad_maximum_fusion), channel_id=1, source_target_pairs={{8,9},{11,10},{12,13},{15,14},{24,25},{27,26},{28,29},{31,30}} | collective-permute-start | bytes 9437192 | tf_op jit(solution)/shard_map/ppermute | solution.py:176
  123.4 67.0 %collective-permute-start.22 = (bf16[1024,1536]{1,0:T(8,128)(2,1)}, bf16[1024,1536]{1,0:T(8,128)(2,1)}, u32[]{:S(2)}, u32[]{:S(2)}) collective-permute-start(bf16[1024,1536]{1,0:T(8,128)(2,1)} %pad_maximum_fusion.1), channel_id=1, source_target_pairs={{10,9},{9,10},{14,13},{13,14},{26,25},{25,26},{30,29},{29,30}} | collective-permute-start | bytes 9437192 | tf_op jit(solution)/shard_map/ppermute | solution.py:176
  125.8 64.6 %collective-permute-start.23 = (bf16[1024,1536]{1,0:T(8,128)(2,1)}, bf16[1024,1536]{1,0:T(8,128)(2,1)}, u32[]{:S(2)}, u32[]{:S(2)}) collective-permute-start(bf16[1024,1536]{1,0:T(8,128)(2,1)} %pad_maximum_fusion.2), channel_id=1, source_target_pairs={{11,9},{8,10},{15,13},{12,14},{27,25},{24,26},{31,29},{28,30}} | collective-permute-start | bytes 9437192 | tf_op jit(solution)/shard_map/ppermute | solution.py:176
  130.0 63.3 %collective-permute-start.20 = (bf16[448,2048]{1,0:T(8,128)(2,1)}, bf16[448,2048]{1,0:T(8,128)(2,1)}, u32[]{:S(2)}, u32[]{:S(2)}) collective-permute-start(bf16[448,2048]{1,0:T(8,128)(2,1)} %add_add_fusion), channel_id=1, source_target_pairs={{1,5},{2,6},{5,1},{6,2}} | collective-permute-start | bytes 5505032 | tf_op jit(solution)/shard_map/ppermute | solution.py:176
  151.2 4.7 collective-permute-start.13
  167.4 29.0 %collective-permute-start.15 = (bf16[96,2048]{1,0:T(8,128)(2,1)S(1)}, bf16[96,2048]{1,0:T(8,128)(2,1)S(1)}, u32[]{:S(2)}, u32[]{:S(2)}) collective-permute-start(bf16[96,2048]{1,0:T(8,128)(2,1)S(1)} %shard_map.101), channel_id=1, source_target_pairs={{0,8},{1,9},{2,10},{3,11},{4,12},{5,13},{6,14},{7,15},{8,16},{9,17... | collective-permute-start | bytes 1179656 | tf_op jit(solution)/shard_map/ppermute | solution.py:176
  190.2 9.7 %collective-permute-start.16 = (bf16[96,2048]{1,0:T(8,128)(2,1)S(1)}, bf16[96,2048]{1,0:T(8,128)(2,1)S(1)}, u32[]{:S(2)}, u32[]{:S(2)}) collective-permute-start(bf16[96,2048]{1,0:T(8,128)(2,1)S(1)} %shard_map.101), channel_id=1, source_target_pairs={{0,12},{1,13},{2,14},{3,15},{4,8},{5,9},{6,10},{7,11},{8,20},{9,21... | collective-permute-start | bytes 1179656 | tf_op jit(solution)/shard_map/ppermute | solution.py:176
  206.4 5.4 %collective-permute-start.26 = (bf16[96,512]{1,0:T(8,128)(2,1)S(1)}, bf16[96,512]{1,0:T(8,128)(2,1)S(1)}, u32[]{:S(2)}, u32[]{:S(2)}) collective-permute-start(bf16[96,512]{1,0:T(8,128)(2,1)S(1)} %get-tuple-element.70.refs_0_), channel_id=1, source_target_pairs={{0,16},{1,6},{2,5},{3,19},{4,20},{5,2},{6,1},{7,23},{8,24},{9,14},... | collective-permute-start | bytes 294920 | tf_op jit(solution)/shard_map/ppermute | solution.py:176
  213.9 26.1 %collective-permute-start.27 = (bf16[96,2048]{1,0:T(8,128)(2,1)S(1)}, bf16[96,2048]{1,0:T(8,128)(2,1)S(1)}, u32[]{:S(2)}, u32[]{:S(2)}) collective-permute-start(bf16[96,2048]{1,0:T(8,128)(2,1)S(1)} %shard_map.104), channel_id=1, source_target_pairs={{0,8},{1,9},{2,10},{3,11},{4,12},{5,13},{6,14},{7,15},{8,16},{9,17... | collective-permute-start | bytes 1179656 | tf_op jit(solution)/shard_map/ppermute | solution.py:176
  233.7 10.5 %collective-permute-start.28 = (bf16[96,2048]{1,0:T(8,128)(2,1)S(1)}, bf16[96,2048]{1,0:T(8,128)(2,1)S(1)}, u32[]{:S(2)}, u32[]{:S(2)}) collective-permute-start(bf16[96,2048]{1,0:T(8,128)(2,1)S(1)} %shard_map.104), channel_id=1, source_target_pairs={{0,12},{1,13},{2,14},{3,15},{4,8},{5,9},{6,10},{7,11},{8,20},{9,21... | collective-permute-start | bytes 1179656 | tf_op jit(solution)/shard_map/ppermute | solution.py:176
  248.6 5.7 %collective-permute-start.29 = (bf16[96,512]{1,0:T(8,128)(2,1)S(1)}, bf16[96,512]{1,0:T(8,128)(2,1)S(1)}, u32[]{:S(2)}, u32[]{:S(2)}) collective-permute-start(bf16[96,512]{1,0:T(8,128)(2,1)S(1)} %get-tuple-element.72.refs_0_), channel_id=1, source_target_pairs={{0,16},{1,5},{2,6},{3,19},{4,20},{5,1},{6,2},{7,23},{8,24},{9,13},... | collective-permute-start | bytes 294920 | tf_op jit(solution)/shard_map/ppermute | solution.py:176
  249.4 7.1 %collective-permute-start.30 = (bf16[96,512]{1,0:T(8,128)(2,1)S(1)}, bf16[96,512]{1,0:T(8,128)(2,1)S(1)}, u32[]{:S(2)}, u32[]{:S(2)}) collective-permute-start(bf16[96,512]{1,0:T(8,128)(2,1)S(1)} %get-tuple-element.72.refs_0_), channel_id=1, source_target_pairs={{0,16},{1,2},{2,1},{3,19},{4,20},{5,6},{6,5},{7,23},{8,24},{9,10},... | collective-permute-start | bytes 294920 | tf_op jit(solution)/shard_map/ppermute | solution.py:176
  250.7 7.9 %collective-permute-start.31 = (bf16[96,512]{1,0:T(8,128)(2,1)S(1)}, bf16[96,512]{1,0:T(8,128)(2,1)S(1)}, u32[]{:S(2)}, u32[]{:S(2)}) collective-permute-start(bf16[96,512]{1,0:T(8,128)(2,1)S(1)} %get-tuple-element.72.refs_0_), channel_id=1, source_target_pairs={{0,16},{1,6},{2,5},{3,19},{4,20},{5,2},{6,1},{7,23},{8,24},{9,14},... | collective-permute-start | bytes 294920 | tf_op jit(solution)/shard_map/ppermute | solution.py:176
  260.7 7.3 %collective-permute-start.32 = (bf16[96,2048]{1,0:T(8,128)(2,1)S(1)}, bf16[96,2048]{1,0:T(8,128)(2,1)S(1)}, u32[]{:S(2)}, u32[]{:S(2)}) collective-permute-start(bf16[96,2048]{1,0:T(8,128)(2,1)S(1)} %shard_map.106), channel_id=1, source_target_pairs={{0,8},{1,9},{2,10},{3,11},{4,12},{5,13},{6,14},{7,15},{8,16},{9,17... | collective-permute-start | bytes 1179656 | tf_op jit(solution)/shard_map/ppermute | solution.py:176
  260.9 11.2 %collective-permute-start.33 = (bf16[96,2048]{1,0:T(8,128)(2,1)S(1)}, bf16[96,2048]{1,0:T(8,128)(2,1)S(1)}, u32[]{:S(2)}, u32[]{:S(2)}) collective-permute-start(bf16[96,2048]{1,0:T(8,128)(2,1)S(1)} %shard_map.106), channel_id=1, source_target_pairs={{0,12},{1,13},{2,14},{3,15},{4,8},{5,9},{6,10},{7,11},{8,20},{9,21... | collective-permute-start | bytes 1179656 | tf_op jit(solution)/shard_map/ppermute | solution.py:176
  276.5 5.7 %collective-permute-start.34 = (bf16[96,512]{1,0:T(8,128)(2,1)S(1)}, bf16[96,512]{1,0:T(8,128)(2,1)S(1)}, u32[]{:S(2)}, u32[]{:S(2)}) collective-permute-start(bf16[96,512]{1,0:T(8,128)(2,1)S(1)} %get-tuple-element.74.refs_0_), channel_id=1, source_target_pairs={{0,16},{1,5},{2,6},{3,19},{4,20},{5,1},{6,2},{7,23},{8,24},{9,13},... | collective-permute-start | bytes 294920 | tf_op jit(solution)/shard_map/ppermute | solution.py:176
  277.9 6.4 %collective-permute-start.35 = (bf16[96,512]{1,0:T(8,128)(2,1)S(1)}, bf16[96,512]{1,0:T(8,128)(2,1)S(1)}, u32[]{:S(2)}, u32[]{:S(2)}) collective-permute-start(bf16[96,512]{1,0:T(8,128)(2,1)S(1)} %get-tuple-element.74.refs_0_), channel_id=1, source_target_pairs={{0,16},{1,2},{2,1},{3,19},{4,20},{5,6},{6,5},{7,23},{8,24},{9,10},... | collective-permute-start | bytes 294920 | tf_op jit(solution)/shard_map/ppermute | solution.py:176
  278.6 7.5 %collective-permute-start.36 = (bf16[96,512]{1,0:T(8,128)(2,1)S(1)}, bf16[96,512]{1,0:T(8,128)(2,1)S(1)}, u32[]{:S(2)}, u32[]{:S(2)}) collective-permute-start(bf16[96,512]{1,0:T(8,128)(2,1)S(1)} %get-tuple-element.74.refs_0_), channel_id=1, source_target_pairs={{0,16},{1,6},{2,5},{3,19},{4,20},{5,2},{6,1},{7,23},{8,24},{9,14},... | collective-permute-start | bytes 294920 | tf_op jit(solution)/shard_map/ppermute | solution.py:176
  288.3 7.3 %collective-permute-start.37 = (bf16[96,2048]{1,0:T(8,128)(2,1)S(1)}, bf16[96,2048]{1,0:T(8,128)(2,1)S(1)}, u32[]{:S(2)}, u32[]{:S(2)}) collective-permute-start(bf16[96,2048]{1,0:T(8,128)(2,1)S(1)} %shard_map.108), channel_id=1, source_target_pairs={{0,8},{1,9},{2,10},{3,11},{4,12},{5,13},{6,14},{7,15},{8,16},{9,17... | collective-permute-start | bytes 1179656 | tf_op jit(solution)/shard_map/ppermute | solution.py:176
  288.4 12.3 %collective-permute-start.38 = (bf16[96,2048]{1,0:T(8,128)(2,1)S(1)}, bf16[96,2048]{1,0:T(8,128)(2,1)S(1)}, u32[]{:S(2)}, u32[]{:S(2)}) collective-permute-start(bf16[96,2048]{1,0:T(8,128)(2,1)S(1)} %shard_map.108), channel_id=1, source_target_pairs={{0,12},{1,13},{2,14},{3,15},{4,8},{5,9},{6,10},{7,11},{8,20},{9,21... | collective-permute-start | bytes 1179656 | tf_op jit(solution)/shard_map/ppermute | solution.py:176
  305.2 5.7 %collective-permute-start.39 = (bf16[96,512]{1,0:T(8,128)(2,1)S(1)}, bf16[96,512]{1,0:T(8,128)(2,1)S(1)}, u32[]{:S(2)}, u32[]{:S(2)}) collective-permute-start(bf16[96,512]{1,0:T(8,128)(2,1)S(1)} %get-tuple-element.76.refs_0_), channel_id=1, source_target_pairs={{0,16},{1,5},{2,6},{3,19},{4,20},{5,1},{6,2},{7,23},{8,24},{9,13},... | collective-permute-start | bytes 294920 | tf_op jit(solution)/shard_map/ppermute | solution.py:176
  305.9 7.1 %collective-permute-start.40 = (bf16[96,512]{1,0:T(8,128)(2,1)S(1)}, bf16[96,512]{1,0:T(8,128)(2,1)S(1)}, u32[]{:S(2)}, u32[]{:S(2)}) collective-permute-start(bf16[96,512]{1,0:T(8,128)(2,1)S(1)} %get-tuple-element.76.refs_0_), channel_id=1, source_target_pairs={{0,16},{1,2},{2,1},{3,19},{4,20},{5,6},{6,5},{7,23},{8,24},{9,10},... | collective-permute-start | bytes 294920 | tf_op jit(solution)/shard_map/ppermute | solution.py:176
  307.3 7.6 %collective-permute-start.41 = (bf16[96,512]{1,0:T(8,128)(2,1)S(1)}, bf16[96,512]{1,0:T(8,128)(2,1)S(1)}, u32[]{:S(2)}, u32[]{:S(2)}) collective-permute-start(bf16[96,512]{1,0:T(8,128)(2,1)S(1)} %get-tuple-element.76.refs_0_), channel_id=1, source_target_pairs={{0,16},{1,6},{2,5},{3,19},{4,20},{5,2},{6,1},{7,23},{8,24},{9,14},... | collective-permute-start | bytes 294920 | tf_op jit(solution)/shard_map/ppermute | solution.py:176
  317.1 7.3 %collective-permute-start.42 = (bf16[96,2048]{1,0:T(8,128)(2,1)S(1)}, bf16[96,2048]{1,0:T(8,128)(2,1)S(1)}, u32[]{:S(2)}, u32[]{:S(2)}) collective-permute-start(bf16[96,2048]{1,0:T(8,128)(2,1)S(1)} %get-tuple-element.79), channel_id=1, source_target_pairs={{0,8},{1,9},{2,10},{3,11},{4,12},{5,13},{6,14},{7,15},{8,16},{9,17... | collective-permute-start | bytes 1179656 | tf_op jit(solution)/shard_map/ppermute | solution.py:176
  317.2 11.5 %collective-permute-start.43 = (bf16[96,2048]{1,0:T(8,128)(2,1)S(1)}, bf16[96,2048]{1,0:T(8,128)(2,1)S(1)}, u32[]{:S(2)}, u32[]{:S(2)}) collective-permute-start(bf16[96,2048]{1,0:T(8,128)(2,1)S(1)} %get-tuple-element.79), channel_id=1, source_target_pairs={{0,12},{1,13},{2,14},{3,15},{4,8},{5,9},{6,10},{7,11},{8,20},{9,21... | collective-permute-start | bytes 1179656 | tf_op jit(solution)/shard_map/ppermute | solution.py:176
  333.1 5.7 %collective-permute-start.44 = (bf16[96,512]{1,0:T(8,128)(2,1)S(1)}, bf16[96,512]{1,0:T(8,128)(2,1)S(1)}, u32[]{:S(2)}, u32[]{:S(2)}) collective-permute-start(bf16[96,512]{1,0:T(8,128)(2,1)S(1)} %get-tuple-element.80.refs_0_), channel_id=1, source_target_pairs={{0,16},{1,5},{2,6},{3,19},{4,20},{5,1},{6,2},{7,23},{8,24},{9,13},... | collective-permute-start | bytes 294920 | tf_op jit(solution)/shard_map/ppermute | solution.py:176
  334.5 6.3 %collective-permute-start.45 = (bf16[96,512]{1,0:T(8,128)(2,1)S(1)}, bf16[96,512]{1,0:T(8,128)(2,1)S(1)}, u32[]{:S(2)}, u32[]{:S(2)}) collective-permute-start(bf16[96,512]{1,0:T(8,128)(2,1)S(1)} %get-tuple-element.80.refs_0_), channel_id=1, source_target_pairs={{0,16},{1,2},{2,1},{3,19},{4,20},{5,6},{6,5},{7,23},{8,24},{9,10},... | collective-permute-start | bytes 294920 | tf_op jit(solution)/shard_map/ppermute | solution.py:176
  335.2 7.4 %collective-permute-start.46 = (bf16[96,512]{1,0:T(8,128)(2,1)S(1)}, bf16[96,512]{1,0:T(8,128)(2,1)S(1)}, u32[]{:S(2)}, u32[]{:S(2)}) collective-permute-start(bf16[96,512]{1,0:T(8,128)(2,1)S(1)} %get-tuple-element.80.refs_0_), channel_id=1, source_target_pairs={{0,16},{1,6},{2,5},{3,19},{4,20},{5,2},{6,1},{7,23},{8,24},{9,14},... | collective-permute-start | bytes 294920 | tf_op jit(solution)/shard_map/ppermute | solution.py:176
  344.8 7.3 %collective-permute-start.47 = (bf16[96,2048]{1,0:T(8,128)(2,1)S(1)}, bf16[96,2048]{1,0:T(8,128)(2,1)S(1)}, u32[]{:S(2)}, u32[]{:S(2)}) collective-permute-start(bf16[96,2048]{1,0:T(8,128)(2,1)S(1)} %get-tuple-element.83), channel_id=1, source_target_pairs={{0,8},{1,9},{2,10},{3,11},{4,12},{5,13},{6,14},{7,15},{8,16},{9,17... | collective-permute-start | bytes 1179656 | tf_op jit(solution)/shard_map/ppermute | solution.py:176
  344.9 12.4 %collective-permute-start.48 = (bf16[96,2048]{1,0:T(8,128)(2,1)S(1)}, bf16[96,2048]{1,0:T(8,128)(2,1)S(1)}, u32[]{:S(2)}, u32[]{:S(2)}) collective-permute-start(bf16[96,2048]{1,0:T(8,128)(2,1)S(1)} %get-tuple-element.83), channel_id=1, source_target_pairs={{0,12},{1,13},{2,14},{3,15},{4,8},{5,9},{6,10},{7,11},{8,20},{9,21... | collective-permute-start | bytes 1179656 | tf_op jit(solution)/shard_map/ppermute | solution.py:176
  361.7 5.7 %collective-permute-start.49 = (bf16[96,512]{1,0:T(8,128)(2,1)S(1)}, bf16[96,512]{1,0:T(8,128)(2,1)S(1)}, u32[]{:S(2)}, u32[]{:S(2)}) collective-permute-start(bf16[96,512]{1,0:T(8,128)(2,1)S(1)} %get-tuple-element.84.refs_0_), channel_id=1, source_target_pairs={{0,16},{1,5},{2,6},{3,19},{4,20},{5,1},{6,2},{7,23},{8,24},{9,13},... | collective-permute-start | bytes 294920 | tf_op jit(solution)/shard_map/ppermute | solution.py:176
  362.4 7.1 %collective-permute-start.50 = (bf16[96,512]{1,0:T(8,128)(2,1)S(1)}, bf16[96,512]{1,0:T(8,128)(2,1)S(1)}, u32[]{:S(2)}, u32[]{:S(2)}) collective-permute-start(bf16[96,512]{1,0:T(8,128)(2,1)S(1)} %get-tuple-element.84.refs_0_), channel_id=1, source_target_pairs={{0,16},{1,2},{2,1},{3,19},{4,20},{5,6},{6,5},{7,23},{8,24},{9,10},... | collective-permute-start | bytes 294920 | tf_op jit(solution)/shard_map/ppermute | solution.py:176
  363.8 7.8 %collective-permute-start.51 = (bf16[96,512]{1,0:T(8,128)(2,1)S(1)}, bf16[96,512]{1,0:T(8,128)(2,1)S(1)}, u32[]{:S(2)}, u32[]{:S(2)}) collective-permute-start(bf16[96,512]{1,0:T(8,128)(2,1)S(1)} %get-tuple-element.84.refs_0_), channel_id=1, source_target_pairs={{0,16},{1,6},{2,5},{3,19},{4,20},{5,2},{6,1},{7,23},{8,24},{9,14},... | collective-permute-start | bytes 294920 | tf_op jit(solution)/shard_map/ppermute | solution.py:176
  373.8 7.3 %collective-permute-start.52 = (bf16[96,2048]{1,0:T(8,128)(2,1)S(1)}, bf16[96,2048]{1,0:T(8,128)(2,1)S(1)}, u32[]{:S(2)}, u32[]{:S(2)}) collective-permute-start(bf16[96,2048]{1,0:T(8,128)(2,1)S(1)} %get-tuple-element.87), channel_id=1, source_target_pairs={{0,8},{1,9},{2,10},{3,11},{4,12},{5,13},{6,14},{7,15},{8,16},{9,17... | collective-permute-start | bytes 1179656 | tf_op jit(solution)/shard_map/ppermute | solution.py:176
  373.9 11.4 %collective-permute-start.53 = (bf16[96,2048]{1,0:T(8,128)(2,1)S(1)}, bf16[96,2048]{1,0:T(8,128)(2,1)S(1)}, u32[]{:S(2)}, u32[]{:S(2)}) collective-permute-start(bf16[96,2048]{1,0:T(8,128)(2,1)S(1)} %get-tuple-element.87), channel_id=1, source_target_pairs={{0,12},{1,13},{2,14},{3,15},{4,8},{5,9},{6,10},{7,11},{8,20},{9,21... | collective-permute-start | bytes 1179656 | tf_op jit(solution)/shard_map/ppermute | solution.py:176
  391.2 5.9 %collective-permute-start.54 = (bf16[96,512]{1,0:T(8,128)(2,1)}, bf16[96,512]{1,0:T(8,128)(2,1)}, u32[]{:S(2)}, u32[]{:S(2)}) collective-permute-start(bf16[96,512]{1,0:T(8,128)(2,1)} %get-tuple-element.88.refs_0_), channel_id=1, source_target_pairs={{0,16},{1,5},{2,6},{3,19},{4,20},{5,1},{6,2},{7,23},{8,24},{9,13},... | collective-permute-start | bytes 294920 | tf_op jit(solution)/shard_map/ppermute | solution.py:176
  392.6 6.6 %collective-permute-start.55 = (bf16[96,512]{1,0:T(8,128)(2,1)}, bf16[96,512]{1,0:T(8,128)(2,1)}, u32[]{:S(2)}, u32[]{:S(2)}) collective-permute-start(bf16[96,512]{1,0:T(8,128)(2,1)} %get-tuple-element.88.refs_0_), channel_id=1, source_target_pairs={{0,16},{1,2},{2,1},{3,19},{4,20},{5,6},{6,5},{7,23},{8,24},{9,10},... | collective-permute-start | bytes 294920 | tf_op jit(solution)/shard_map/ppermute | solution.py:176
  393.2 7.7 %collective-permute-start.56 = (bf16[96,512]{1,0:T(8,128)(2,1)}, bf16[96,512]{1,0:T(8,128)(2,1)}, u32[]{:S(2)}, u32[]{:S(2)}) collective-permute-start(bf16[96,512]{1,0:T(8,128)(2,1)} %get-tuple-element.88.refs_0_), channel_id=1, source_target_pairs={{0,16},{1,6},{2,5},{3,19},{4,20},{5,2},{6,1},{7,23},{8,24},{9,14},... | collective-permute-start | bytes 294920 | tf_op jit(solution)/shard_map/ppermute | solution.py:176
  408.1 7.3 %collective-permute-start.57 = (bf16[96,2048]{1,0:T(8,128)(2,1)S(1)}, bf16[96,2048]{1,0:T(8,128)(2,1)S(1)}, u32[]{:S(2)}, u32[]{:S(2)}) collective-permute-start(bf16[96,2048]{1,0:T(8,128)(2,1)S(1)} %get-tuple-element.91), channel_id=1, source_target_pairs={{0,8},{1,9},{2,10},{3,11},{4,12},{5,13},{6,14},{7,15},{8,16},{9,17... | collective-permute-start | bytes 1179656 | tf_op jit(solution)/shard_map/ppermute | solution.py:176
  408.2 12.4 %collective-permute-start.58 = (bf16[96,2048]{1,0:T(8,128)(2,1)S(1)}, bf16[96,2048]{1,0:T(8,128)(2,1)S(1)}, u32[]{:S(2)}, u32[]{:S(2)}) collective-permute-start(bf16[96,2048]{1,0:T(8,128)(2,1)S(1)} %get-tuple-element.91), channel_id=1, source_target_pairs={{0,12},{1,13},{2,14},{3,15},{4,8},{5,9},{6,10},{7,11},{8,20},{9,21... | collective-permute-start | bytes 1179656 | tf_op jit(solution)/shard_map/ppermute | solution.py:176
  428.8 5.7 %collective-permute-start.59 = (bf16[96,512]{1,0:T(8,128)(2,1)S(1)}, bf16[96,512]{1,0:T(8,128)(2,1)S(1)}, u32[]{:S(2)}, u32[]{:S(2)}) collective-permute-start(bf16[96,512]{1,0:T(8,128)(2,1)S(1)} %get-tuple-element.92.refs_0_), channel_id=1, source_target_pairs={{0,16},{1,5},{2,6},{3,19},{4,20},{5,1},{6,2},{7,23},{8,24},{9,13},... | collective-permute-start | bytes 294920 | tf_op jit(solution)/shard_map/ppermute | solution.py:176
  429.6 7.1 %collective-permute-start.60 = (bf16[96,512]{1,0:T(8,128)(2,1)S(1)}, bf16[96,512]{1,0:T(8,128)(2,1)S(1)}, u32[]{:S(2)}, u32[]{:S(2)}) collective-permute-start(bf16[96,512]{1,0:T(8,128)(2,1)S(1)} %get-tuple-element.92.refs_0_), channel_id=1, source_target_pairs={{0,16},{1,2},{2,1},{3,19},{4,20},{5,6},{6,5},{7,23},{8,24},{9,10},... | collective-permute-start | bytes 294920 | tf_op jit(solution)/shard_map/ppermute | solution.py:176
  430.9 7.6 %collective-permute-start.61 = (bf16[96,512]{1,0:T(8,128)(2,1)S(1)}, bf16[96,512]{1,0:T(8,128)(2,1)S(1)}, u32[]{:S(2)}, u32[]{:S(2)}) collective-permute-start(bf16[96,512]{1,0:T(8,128)(2,1)S(1)} %get-tuple-element.92.refs_0_), channel_id=1, source_target_pairs={{0,16},{1,6},{2,5},{3,19},{4,20},{5,2},{6,1},{7,23},{8,24},{9,14},... | collective-permute-start | bytes 294920 | tf_op jit(solution)/shard_map/ppermute | solution.py:176
  440.7 7.3 %collective-permute-start.62 = (bf16[96,2048]{1,0:T(8,128)(2,1)S(1)}, bf16[96,2048]{1,0:T(8,128)(2,1)S(1)}, u32[]{:S(2)}, u32[]{:S(2)}) collective-permute-start(bf16[96,2048]{1,0:T(8,128)(2,1)S(1)} %get-tuple-element.95), channel_id=1, source_target_pairs={{0,8},{1,9},{2,10},{3,11},{4,12},{5,13},{6,14},{7,15},{8,16},{9,17... | collective-permute-start | bytes 1179656 | tf_op jit(solution)/shard_map/ppermute | solution.py:176
  440.8 11.5 %collective-permute-start.63 = (bf16[96,2048]{1,0:T(8,128)(2,1)S(1)}, bf16[96,2048]{1,0:T(8,128)(2,1)S(1)}, u32[]{:S(2)}, u32[]{:S(2)}) collective-permute-start(bf16[96,2048]{1,0:T(8,128)(2,1)S(1)} %get-tuple-element.95), channel_id=1, source_target_pairs={{0,12},{1,13},{2,14},{3,15},{4,8},{5,9},{6,10},{7,11},{8,20},{9,21... | collective-permute-start | bytes 1179656 | tf_op jit(solution)/shard_map/ppermute | solution.py:176
  456.7 5.7 %collective-permute-start.64 = (bf16[96,512]{1,0:T(8,128)(2,1)S(1)}, bf16[96,512]{1,0:T(8,128)(2,1)S(1)}, u32[]{:S(2)}, u32[]{:S(2)}) collective-permute-start(bf16[96,512]{1,0:T(8,128)(2,1)S(1)} %get-tuple-element.96.refs_0_), channel_id=1, source_target_pairs={{0,16},{1,5},{2,6},{3,19},{4,20},{5,1},{6,2},{7,23},{8,24},{9,13},... | collective-permute-start | bytes 294920 | tf_op jit(solution)/shard_map/ppermute | solution.py:176
  458.2 6.4 %collective-permute-start.65 = (bf16[96,512]{1,0:T(8,128)(2,1)S(1)}, bf16[96,512]{1,0:T(8,128)(2,1)S(1)}, u32[]{:S(2)}, u32[]{:S(2)}) collective-permute-start(bf16[96,512]{1,0:T(8,128)(2,1)S(1)} %get-tuple-element.96.refs_0_), channel_id=1, source_target_pairs={{0,16},{1,2},{2,1},{3,19},{4,20},{5,6},{6,5},{7,23},{8,24},{9,10},... | collective-permute-start | bytes 294920 | tf_op jit(solution)/shard_map/ppermute | solution.py:176
  458.8 7.6 %collective-permute-start.66 = (bf16[96,512]{1,0:T(8,128)(2,1)S(1)}, bf16[96,512]{1,0:T(8,128)(2,1)S(1)}, u32[]{:S(2)}, u32[]{:S(2)}) collective-permute-start(bf16[96,512]{1,0:T(8,128)(2,1)S(1)} %get-tuple-element.96.refs_0_), channel_id=1, source_target_pairs={{0,16},{1,6},{2,5},{3,19},{4,20},{5,2},{6,1},{7,23},{8,24},{9,14},... | collective-permute-start | bytes 294920 | tf_op jit(solution)/shard_map/ppermute | solution.py:176
  468.6 7.3 %collective-permute-start.67 = (bf16[96,2048]{1,0:T(8,128)(2,1)S(1)}, bf16[96,2048]{1,0:T(8,128)(2,1)S(1)}, u32[]{:S(2)}, u32[]{:S(2)}) collective-permute-start(bf16[96,2048]{1,0:T(8,128)(2,1)S(1)} %get-tuple-element.99), channel_id=1, source_target_pairs={{0,8},{1,9},{2,10},{3,11},{4,12},{5,13},{6,14},{7,15},{8,16},{9,17... | collective-permute-start | bytes 1179656 | tf_op jit(solution)/shard_map/ppermute | solution.py:176
  468.7 12.4 %collective-permute-start.68 = (bf16[96,2048]{1,0:T(8,128)(2,1)S(1)}, bf16[96,2048]{1,0:T(8,128)(2,1)S(1)}, u32[]{:S(2)}, u32[]{:S(2)}) collective-permute-start(bf16[96,2048]{1,0:T(8,128)(2,1)S(1)} %get-tuple-element.99), channel_id=1, source_target_pairs={{0,12},{1,13},{2,14},{3,15},{4,8},{5,9},{6,10},{7,11},{8,20},{9,21... | collective-permute-start | bytes 1179656 | tf_op jit(solution)/shard_map/ppermute | solution.py:176
  485.6 5.7 %collective-permute-start.69 = (bf16[96,512]{1,0:T(8,128)(2,1)S(1)}, bf16[96,512]{1,0:T(8,128)(2,1)S(1)}, u32[]{:S(2)}, u32[]{:S(2)}) collective-permute-start(bf16[96,512]{1,0:T(8,128)(2,1)S(1)} %get-tuple-element.100), channel_id=1, source_target_pairs={{0,16},{1,5},{2,6},{3,19},{4,20},{5,1},{6,2},{7,23},{8,24},{9,13},... | collective-permute-start | bytes 294920 | tf_op jit(solution)/shard_map/ppermute | solution.py:176
  486.3 7.1 %collective-permute-start.70 = (bf16[96,512]{1,0:T(8,128)(2,1)S(1)}, bf16[96,512]{1,0:T(8,128)(2,1)S(1)}, u32[]{:S(2)}, u32[]{:S(2)}) collective-permute-start(bf16[96,512]{1,0:T(8,128)(2,1)S(1)} %get-tuple-element.100), channel_id=1, source_target_pairs={{0,16},{1,2},{2,1},{3,19},{4,20},{5,6},{6,5},{7,23},{8,24},{9,10},... | collective-permute-start | bytes 294920 | tf_op jit(solution)/shard_map/ppermute | solution.py:176
  487.6 7.6 %collective-permute-start.71 = (bf16[96,512]{1,0:T(8,128)(2,1)S(1)}, bf16[96,512]{1,0:T(8,128)(2,1)S(1)}, u32[]{:S(2)}, u32[]{:S(2)}) collective-permute-start(bf16[96,512]{1,0:T(8,128)(2,1)S(1)} %get-tuple-element.100), channel_id=1, source_target_pairs={{0,16},{1,6},{2,5},{3,19},{4,20},{5,2},{6,1},{7,23},{8,24},{9,14},... | collective-permute-start | bytes 294920 | tf_op jit(solution)/shard_map/ppermute | solution.py:176
  498.3 5.0 collective-permute-start.73
  503.3 21.8 %collective-permute-start.75 = (f32[8,2048]{1,0:T(8,128)S(1)}, f32[8,2048]{1,0:T(8,128)S(1)}, u32[]{:S(2)}, u32[]{:S(2)}) collective-permute-start(f32[8,2048]{1,0:T(8,128)S(1)} %add_add_fusion.2), channel_id=1, source_target_pairs={{1,0},{2,3},{5,4},{6,7},{9,8},{10,11},{13,12},{14,15},{17,16},{18,... | collective-permute-start | bytes 196616 | tf_op jit(solution)/shard_map/ppermute | solution.py:176
  (53 other events, 1223.6 us)

commit v5 on v4

--- a/solution.py
+++ b/solution.py
@@ -226,8 +226,9 @@
             full = full + send(picked, [((a, b, c), (0, b, c)) for b in range(T) for c in planes])
         return full, send(full, [((0, b, c), (0, T - 1 - b, c)) for b in range(T) for c in planes])
 
-    first_ids = ids[:n, 0]
-    rest_ids = jnp.concatenate([ids[n:, 0]] + [ids[:, seg] for seg in range(1, segs)])
+    ids, blocks = lax.optimization_barrier((ids, blocks))
+    first_ids, rest_ids = ids[:n, 0], ids[n:, 0]
+    later_ids = jnp.concatenate([ids[:, seg] for seg in range(1, segs)])
     even = relay(0, blocks)
     tok_first = embed(first_ids)
     mem_other = send(mem_init, [((0, b, c), (0, T - 1 - b, c)) for b in range(T) for c in planes])
@@ -287,8 +288,10 @@
             )
         if k > 0:
             step = n * tokens
-            at = min(k, segs * S - 1) - 1
-            tk, tko = (a[at * step : (at + 1) * step] for a in tok_rest)
+            at = min(k, segs * S - 1) - (1 if k < S else S)
+            tk, tko = (
+                a[at * step : (at + 1) * step] for a in (tok_rest if k < S else tok_later)
+            )
         mixed, keep = pl.pallas_call(
             functools.partial(attend_kernel, k, n, tokens, D),
             out_shape=(
@@ -304,6 +307,9 @@
             compiler_params=params,
         )(meta, where, own, other, tk, tko, mem_init, mem_other, norm_gain, *weights)
         shared = [mixed]
+        if k == 0:
+            later_ids, mixed = lax.optimization_barrier((later_ids, mixed))
+            tok_later = embed(later_ids)
         for j, i in shifts[1:]:
             def back(a, b, c):
                 return (a, (b - j) % T, planes[(planes.index(c) + i) % 2])

time: 535 us -> 527 us (0.985)
  waiting for transfers between devices: 231 us -> 214 us
  other arithmetic: 14.1 us -> 22 us
  local copies, waits for them, and re-layouts: 58.3 us -> 65.5 us
  starting transfers between devices: 143 us -> 136 us
    ppermute x76 -> x80, waiting for transfers between devices: 231 us -> 214 us  [send(): return lax.ppermute(block, AXES, [(lin(*a), lin(*b)) for a, b in pairs])]
    gather x2 -> x3, local copies, waits for them, and re-layouts: 22 us -> 30.9 us  [embed(): picked = jnp.take(emb_table, jnp.clip(local, 0, vocab - 1), axis=0)]
    ppermute x76 -> x80, starting transfers between devices: 143 us -> 136 us  [send(): return lax.ppermute(block, AXES, [(lin(*a), lin(*b)) for a, b in pairs])]
    unnamed x89 -> x92, local copies, waits for them, and re-layouts: 19.6 us -> 19.4 us
  transfers between devices with their start and end apart: 76 -> 80, of which waited for: 57 -> 57; matrix products, arithmetic and copies ran while one was open for 6% -> 9% of each run, Pallas kernels for 2% -> 6%
where the time goes in v5:
time: 527 us; the launch traced here: 518 us
  waiting for transfers between devices  214 us (41%)
  starting transfers between devices  136 us (26%)
  Pallas kernels  77.4 us (15%)
  local copies, waits for them, and re-layouts  65.5 us (12%)
  other arithmetic  22 us (4%)
    ppermute x80, waiting for transfers between devices, send(): return lax.ppermute(block, AXES, [(lin(*a), lin(*b)) for a, b in pairs])  214 us
    ppermute x80, starting transfers between devices, send(): return lax.ppermute(block, AXES, [(lin(*a), lin(*b)) for a, b in pairs])  136 us
    pallas_call x11, Pallas kernels, body(): pl.pallas_call(functools.partial(attend_kernel, k, n, tokens, D), out_sha...  51.9 us
    gather x3, local copies, waits for them, and re-layouts, embed(): picked = jnp.take(emb_table, jnp.clip(local, 0, vocab - 1), axis=0)  30.9 us
    pallas_call x10, Pallas kernels, body(): pl.pallas_call(functools.partial(project_kernel, k, n, tokens, parts, poo...  22.5 us
    unnamed x92, local copies, waits for them, and re-layouts  19.4 us
  transfers between devices with their start and end apart: 80, of which 57 were waited for; matrix products, arithmetic and copies ran while one was open for 9% of the time, Pallas kernels for 6%

profile of v5, /device:TPU:0, one launch (start us, length us, event | category | flops | bytes accessed | tf_op | source)
XLA Modules:
  0.0 517.6 jit_solution(1505149049249322554)
XLA Ops:
  1.5 5.0 collective-permute-start.2
  7.7 3.9 dynamic-slice_bitcast_fusion.2
  11.6 2.4 dynamic-slice_bitcast_fusion
  19.6 4.0 collective-permute-start.5
  23.6 2.3 collective-permute-start.4
  25.9 3.0 collective-permute-start.3
  29.2 8.9 %gather_fusion.1 = bf16[64,2048]{1,0:T(8,128)(2,1)S(1)} fusion(bf16[4096,2048]{1,0:T(8,128)(2,1)} %param.12, s32[1024]{0:T(1024)S(1)} %pad_clamp_fusion.2), kind=kCustom, calls=%fused_computation.1 | custom fusion | bytes 524544 | tf_op jit(solution)/shard_map/jit(_take)/gather | solution.py:222
  46.4 12.1 %collective-permute-done.5.refs_10_.refs_2_ = bf16[1024,1536]{1,0:T(8,128)(2,1)S(1)} collective-permute-done((bf16[1024,1536]{1,0:T(8,128)(2,1)}, bf16[1024,1536]{1,0:T(8,128)(2,1)S(1)}, u32[]{:S(2)}, u32[]{:S(2)}) %collective-permute-start.5) | collective-permute-done | bytes 3145760 | tf_op jit(solution)/shard_map/ppermute | solution.py:176
  58.5 33.7 %collective-permute-done.3.refs_8_.refs_0_ = bf16[1024,1536]{1,0:T(8,128)(2,1)} collective-permute-done((bf16[1024,1536]{1,0:T(8,128)(2,1)}, bf16[1024,1536]{1,0:T(8,128)(2,1)}, u32[]{:S(2)}, u32[]{:S(2)}) %collective-permute-start.3) | collective-permute-done | bytes 3145760 | tf_op jit(solution)/shard_map/ppermute | solution.py:176
  95.5 10.7 %gather_fusion.2 = bf16[192,2048]{1,0:T(8,128)(2,1)} fusion(bf16[4096,2048]{1,0:T(8,128)(2,1)} %param.12, s32[1024]{0:T(1024)S(1)} %pad_clamp_fusion.1), kind=kCustom, calls=%fused_computation.2 | custom fusion | bytes 1573632 | tf_op jit(solution)/shard_map/jit(_take)/gather | solution.py:222
  110.1 2.4 collective-permute-start.21
  113.4 2.4 collective-permute-start.22
  115.8 2.3 collective-permute-start.23
  128.7 6.6 %shard_map.100 = (bf16[96,512]{1,0:T(8,128)(2,1)S(1)}, bf16[96,2048]{1,0:T(8,128)(2,1)S(1)}) custom-call(s32[11,6]{1,0:T(8,128)S(1)} %concatenate.23.meta, s32[4]{0:T(128)S(1)} %pad_add_fusion.3.where, bf16[96,2048]{1,0:T(8,128)(2,1)S(1)} %broadcast_14_refs_0__refs_1_.2.refs_0_.refs_1_, bf16[96,2048]{1,0:T(8,128)(2,1)S(1)} %broadcast_14_refs_0__refs_1_.2.refs_0_.refs_1_, ...), custom_call_target="tpu_custom_call" | custom-call | tf_op jit(solution)/shard_map/pallas_call | solution.py:295
  137.8 3.0 add_add_fusion.1
  143.0 11.3 %gather_fusion.3 = bf16[256,2048]{1,0:T(8,128)(2,1)} fusion(bf16[4096,2048]{1,0:T(8,128)(2,1)} %param.12, s32[1024]{0:T(1024)S(1)} %pad_clamp_fusion), kind=kCustom, calls=%fused_computation.3 | custom fusion | bytes 2098176 | tf_op jit(solution)/shard_map/jit(_take)/gather | solution.py:222
  155.9 2.4 select_select_fusion
  160.7 3.4 copy-done
  165.0 2.4 shard_map.101
  172.1 6.0 %collective-permute-start.15 = (bf16[96,2048]{1,0:T(8,128)(2,1)S(1)}, bf16[96,2048]{1,0:T(8,128)(2,1)S(1)}, u32[]{:S(2)}, u32[]{:S(2)}) collective-permute-start(bf16[96,2048]{1,0:T(8,128)(2,1)S(1)} %shard_map.101), channel_id=1, source_target_pairs={{0,8},{1,9},{2,10},{3,11},{4,12},{5,13},{6,14},{7,15},{8,16},{9,17... | collective-permute-start | bytes 1179656 | tf_op jit(solution)/shard_map/ppermute | solution.py:176
  178.0 7.2 %collective-permute-start.16 = (bf16[96,2048]{1,0:T(8,128)(2,1)S(1)}, bf16[96,2048]{1,0:T(8,128)(2,1)S(1)}, u32[]{:S(2)}, u32[]{:S(2)}) collective-permute-start(bf16[96,2048]{1,0:T(8,128)(2,1)S(1)} %shard_map.101), channel_id=1, source_target_pairs={{0,12},{1,13},{2,14},{3,15},{4,8},{5,9},{6,10},{7,11},{8,20},{9,21... | collective-permute-start | bytes 1179656 | tf_op jit(solution)/shard_map/ppermute | solution.py:176
  186.6 3.0 shard_map.102
  189.6 5.1 collective-permute-done.16.refs_1_
  194.7 4.5 shard_map.103
  201.3 3.6 collective-permute-done.24.refs_1_
  206.8 2.7 collective-permute-done.26.refs_3_
  213.4 2.2 add_add_fusion
  216.4 2.6 collective-permute-done.27.refs_0_
  219.0 4.0 collective-permute-done.28.refs_1_
  222.9 4.5 shard_map.105
  240.9 5.7 %collective-permute-done.32.refs_0_ = bf16[96,2048]{1,0:T(8,128)(2,1)S(1)} collective-permute-done((bf16[96,2048]{1,0:T(8,128)(2,1)S(1)}, bf16[96,2048]{1,0:T(8,128)(2,1)S(1)}, u32[]{:S(2)}, u32[]{:S(2)}) %collective-permute-start.32) | collective-permute-done | bytes 393248 | tf_op jit(solution)/shard_map/ppermute | solution.py:176
  246.6 5.2 %collective-permute-done.33.refs_1_ = bf16[96,2048]{1,0:T(8,128)(2,1)S(1)} collective-permute-done((bf16[96,2048]{1,0:T(8,128)(2,1)S(1)}, bf16[96,2048]{1,0:T(8,128)(2,1)S(1)}, u32[]{:S(2)}, u32[]{:S(2)}) %collective-permute-start.33) | collective-permute-done | bytes 393248 | tf_op jit(solution)/shard_map/ppermute | solution.py:176
  251.8 4.5 shard_map.107
  258.8 3.2 collective-permute-done.34.refs_1_
  269.9 5.6 %collective-permute-done.37.refs_0_ = bf16[96,2048]{1,0:T(8,128)(2,1)S(1)} collective-permute-done((bf16[96,2048]{1,0:T(8,128)(2,1)S(1)}, bf16[96,2048]{1,0:T(8,128)(2,1)S(1)}, u32[]{:S(2)}, u32[]{:S(2)}) %collective-permute-start.37) | collective-permute-done | bytes 393248 | tf_op jit(solution)/shard_map/ppermute | solution.py:176
  275.5 3.8 collective-permute-done.38.refs_1_
  279.3 4.5 shard_map.109
  297.5 5.5 %collective-permute-done.46.refs_0_ = bf16[96,2048]{1,0:T(8,128)(2,1)S(1)} collective-permute-done((bf16[96,2048]{1,0:T(8,128)(2,1)S(1)}, bf16[96,2048]{1,0:T(8,128)(2,1)S(1)}, u32[]{:S(2)}, u32[]{:S(2)}) %collective-permute-start.46) | collective-permute-done | bytes 393248 | tf_op jit(solution)/shard_map/ppermute | solution.py:176
  303.0 5.3 %collective-permute-done.47.refs_1_ = bf16[96,2048]{1,0:T(8,128)(2,1)S(1)} collective-permute-done((bf16[96,2048]{1,0:T(8,128)(2,1)S(1)}, bf16[96,2048]{1,0:T(8,128)(2,1)S(1)}, u32[]{:S(2)}, u32[]{:S(2)}) %collective-permute-start.47) | collective-permute-done | bytes 393248 | tf_op jit(solution)/shard_map/ppermute | solution.py:176
  308.2 4.5 shard_map.111
  315.3 3.1 collective-permute-done.48.refs_1_
  326.5 5.6 %collective-permute-done.51.refs_0_ = bf16[96,2048]{1,0:T(8,128)(2,1)S(1)} collective-permute-done((bf16[96,2048]{1,0:T(8,128)(2,1)S(1)}, bf16[96,2048]{1,0:T(8,128)(2,1)S(1)}, u32[]{:S(2)}, u32[]{:S(2)}) %collective-permute-start.51) | collective-permute-done | bytes 393248 | tf_op jit(solution)/shard_map/ppermute | solution.py:176
  332.1 3.9 collective-permute-done.52.refs_1_
  336.0 4.5 shard_map.113
  354.0 5.7 %collective-permute-done.56.refs_0_ = bf16[96,2048]{1,0:T(8,128)(2,1)S(1)} collective-permute-done((bf16[96,2048]{1,0:T(8,128)(2,1)S(1)}, bf16[96,2048]{1,0:T(8,128)(2,1)S(1)}, u32[]{:S(2)}, u32[]{:S(2)}) %collective-permute-start.56) | collective-permute-done | bytes 393248 | tf_op jit(solution)/shard_map/ppermute | solution.py:176
  359.7 5.2 %collective-permute-done.57.refs_1_ = bf16[96,2048]{1,0:T(8,128)(2,1)S(1)} collective-permute-done((bf16[96,2048]{1,0:T(8,128)(2,1)S(1)}, bf16[96,2048]{1,0:T(8,128)(2,1)S(1)}, u32[]{:S(2)}, u32[]{:S(2)}) %collective-permute-start.57) | collective-permute-done | bytes 393248 | tf_op jit(solution)/shard_map/ppermute | solution.py:176
  365.0 5.1 shard_map.115
  373.2 3.6 collective-permute-done.58.refs_1_
  380.8 3.4 copy-done.1
  385.2 2.7 shard_map.116
  389.8 5.4 %collective-permute-done.61.refs_0_ = bf16[96,2048]{1,0:T(8,128)(2,1)S(1)} collective-permute-done((bf16[96,2048]{1,0:T(8,128)(2,1)S(1)}, bf16[96,2048]{1,0:T(8,128)(2,1)S(1)}, u32[]{:S(2)}, u32[]{:S(2)}) %collective-permute-start.61) | collective-permute-done | bytes 393248 | tf_op jit(solution)/shard_map/ppermute | solution.py:176
  395.2 4.1 collective-permute-done.62.refs_1_
  403.1 4.5 shard_map.117
  421.1 5.7 %collective-permute-done.66.refs_0_ = bf16[96,2048]{1,0:T(8,128)(2,1)S(1)} collective-permute-done((bf16[96,2048]{1,0:T(8,128)(2,1)S(1)}, bf16[96,2048]{1,0:T(8,128)(2,1)S(1)}, u32[]{:S(2)}, u32[]{:S(2)}) %collective-permute-start.66) | collective-permute-done | bytes 393248 | tf_op jit(solution)/shard_map/ppermute | solution.py:176
  426.8 5.2 %collective-permute-done.67.refs_1_ = bf16[96,2048]{1,0:T(8,128)(2,1)S(1)} collective-permute-done((bf16[96,2048]{1,0:T(8,128)(2,1)S(1)}, bf16[96,2048]{1,0:T(8,128)(2,1)S(1)}, u32[]{:S(2)}, u32[]{:S(2)}) %collective-permute-start.67) | collective-permute-done | bytes 393248 | tf_op jit(solution)/shard_map/ppermute | solution.py:176
  432.1 4.5 shard_map.119
  439.0 3.3 collective-permute-done.68.refs_1_
  450.1 5.6 %collective-permute-done.71.refs_0_ = bf16[96,2048]{1,0:T(8,128)(2,1)S(1)} collective-permute-done((bf16[96,2048]{1,0:T(8,128)(2,1)S(1)}, bf16[96,2048]{1,0:T(8,128)(2,1)S(1)}, u32[]{:S(2)}, u32[]{:S(2)}) %collective-permute-start.71) | collective-permute-done | bytes 393248 | tf_op jit(solution)/shard_map/ppermute | solution.py:176
  455.7 3.9 collective-permute-done.72.refs_1_
  459.6 4.5 shard_map.121
  473.8 2.9 shard_map.122
  480.3 2.5 collective-permute-done.77
  482.9 31.3 %collective-permute-start.79 = (f32[8,2048]{1,0:T(8,128)S(1)}, f32[8,2048]{1,0:T(8,128)S(1)}, u32[]{:S(2)}, u32[]{:S(2)}) collective-permute-start(f32[8,2048]{1,0:T(8,128)S(1)} %add_add_fusion.3), channel_id=1, source_target_pairs={{1,0},{2,3},{5,4},{6,7},{9,8},{10,11},{13,12},{14,15},{17,16},{18,... | collective-permute-start | bytes 196616 | tf_op jit(solution)/shard_map/ppermute | solution.py:176
  514.2 2.2 collective-permute-done.79
  (285 shorter events, 171.3 us)
Async XLA Ops:
  1.5 17.9 %collective-permute-start.2 = (s32[2,2,33]{2,1,0:T(2,128)S(1)}, s32[2,2,33]{2,1,0:T(2,128)S(1)}, u32[]{:S(2)}, u32[]{:S(2)}) collective-permute-start(s32[2,2,33]{2,1,0:T(2,128)S(1)} %pad_add_fusion.1), channel_id=1, source_target_pairs={{0,3},{1,0},{2,1},{3,2},{4,7},{5,4},{6,5},{7,6},{8,11},{9,8},{10,9... | collective-permute-start | bytes 1592 | tf_op jit(solution)/shard_map/ppermute | solution.py:176
  6.6 12.9 %collective-permute-start.1 = (s32[2,2,33]{2,1,0:T(2,128)S(1)}, s32[2,2,33]{2,1,0:T(2,128)S(1)}, u32[]{:S(2)}, u32[]{:S(2)}) collective-permute-start(s32[2,2,33]{2,1,0:T(2,128)S(1)} %pad_add_fusion.1), channel_id=1, source_target_pairs={{0,2},{1,3},{2,0},{3,1},{4,6},{5,7},{6,4},{7,5},{8,10},{9,11},{10,... | collective-permute-start | bytes 1592 | tf_op jit(solution)/shard_map/ppermute | solution.py:176
  6.6 12.9 %collective-permute-start = (s32[2,2,33]{2,1,0:T(2,128)S(1)}, s32[2,2,33]{2,1,0:T(2,128)S(1)}, u32[]{:S(2)}, u32[]{:S(2)}) collective-permute-start(s32[2,2,33]{2,1,0:T(2,128)S(1)} %pad_add_fusion.1), channel_id=1, source_target_pairs={{0,1},{1,2},{2,3},{3,0},{4,5},{5,6},{6,7},{7,4},{8,9},{9,10},{10,1... | collective-permute-start | bytes 1592 | tf_op jit(solution)/shard_map/ppermute | solution.py:176
  19.6 38.9 %collective-permute-start.5 = (bf16[1024,1536]{1,0:T(8,128)(2,1)}, bf16[1024,1536]{1,0:T(8,128)(2,1)S(1)}, u32[]{:S(2)}, u32[]{:S(2)}) collective-permute-start(bf16[1024,1536]{1,0:T(8,128)(2,1)} %pad_maximum_fusion.2), channel_id=1, source_target_pairs={{3,1},{0,2},{7,5},{4,6},{19,17},{16,18},{23,21},{20,22}} | collective-permute-start | bytes 9437192 | tf_op jit(solution)/shard_map/ppermute | solution.py:176
  23.6 34.9 %collective-permute-start.4 = (bf16[1024,1536]{1,0:T(8,128)(2,1)}, bf16[1024,1536]{1,0:T(8,128)(2,1)}, u32[]{:S(2)}, u32[]{:S(2)}) collective-permute-start(bf16[1024,1536]{1,0:T(8,128)(2,1)} %pad_maximum_fusion.1), channel_id=1, source_target_pairs={{2,1},{1,2},{6,5},{5,6},{18,17},{17,18},{22,21},{21,22}} | collective-permute-start | bytes 9437192 | tf_op jit(solution)/shard_map/ppermute | solution.py:176
  25.9 66.3 %collective-permute-start.3 = (bf16[1024,1536]{1,0:T(8,128)(2,1)}, bf16[1024,1536]{1,0:T(8,128)(2,1)}, u32[]{:S(2)}, u32[]{:S(2)}) collective-permute-start(bf16[1024,1536]{1,0:T(8,128)(2,1)} %pad_maximum_fusion), channel_id=1, source_target_pairs={{0,1},{3,2},{4,5},{7,6},{16,17},{19,18},{20,21},{23,22}} | collective-permute-start | bytes 9437192 | tf_op jit(solution)/shard_map/ppermute | solution.py:176
  43.1 49.8 %collective-permute-start.11 = (bf16[16,2048]{1,0:T(8,128)(2,1)S(1)}, bf16[16,2048]{1,0:T(8,128)(2,1)S(1)}, u32[]{:S(2)}, u32[]{:S(2)}) collective-permute-start(bf16[16,2048]{1,0:T(8,128)(2,1)S(1)} %copy-done.11), channel_id=1, source_target_pairs={{1,5},{2,6},{5,1},{6,2}} | collective-permute-start | bytes 196616 | tf_op jit(solution)/shard_map/ppermute | solution.py:176
  45.1 47.9 %collective-permute-start.10 = (bf16[64,2048]{1,0:T(8,128)(2,1)S(1)}, bf16[64,2048]{1,0:T(8,128)(2,1)S(1)}, u32[]{:S(2)}, u32[]{:S(2)}) collective-permute-start(bf16[64,2048]{1,0:T(8,128)(2,1)S(1)} %add_add_fusion.2.refs_2_), channel_id=1, source_target_pairs={{1,5},{2,6},{5,1},{6,2}} | collective-permute-start | bytes 786440 | tf_op jit(solution)/shard_map/ppermute | solution.py:176
  108.5 14.3 %collective-permute-start.19 = (bf16[192,2048]{1,0:T(8,128)(2,1)}, bf16[192,2048]{1,0:T(8,128)(2,1)}, u32[]{:S(2)}, u32[]{:S(2)}) collective-permute-start(bf16[192,2048]{1,0:T(8,128)(2,1)} %select_select_fusion.1), channel_id=1, source_target_pairs={{25,1},{26,2},{29,5},{30,6}} | collective-permute-start | bytes 2359304 | tf_op jit(solution)/shard_map/ppermute | solution.py:176
  110.1 59.2 %collective-permute-start.21 = (bf16[1024,1536]{1,0:T(8,128)(2,1)}, bf16[1024,1536]{1,0:T(8,128)(2,1)}, u32[]{:S(2)}, u32[]{:S(2)}) collective-permute-start(bf16[1024,1536]{1,0:T(8,128)(2,1)} %pad_maximum_fusion), channel_id=1, source_target_pairs={{8,9},{11,10},{12,13},{15,14},{24,25},{27,26},{28,29},{31,30}} | collective-permute-start | bytes 9437192 | tf_op jit(solution)/shard_map/ppermute | solution.py:176
  113.4 58.6 %collective-permute-start.22 = (bf16[1024,1536]{1,0:T(8,128)(2,1)}, bf16[1024,1536]{1,0:T(8,128)(2,1)}, u32[]{:S(2)}, u32[]{:S(2)}) collective-permute-start(bf16[1024,1536]{1,0:T(8,128)(2,1)} %pad_maximum_fusion.1), channel_id=1, source_target_pairs={{10,9},{9,10},{14,13},{13,14},{26,25},{25,26},{30,29},{29,30}} | collective-permute-start | bytes 9437192 | tf_op jit(solution)/shard_map/ppermute | solution.py:176
  115.8 62.2 %collective-permute-start.23 = (bf16[1024,1536]{1,0:T(8,128)(2,1)}, bf16[1024,1536]{1,0:T(8,128)(2,1)}, u32[]{:S(2)}, u32[]{:S(2)}) collective-permute-start(bf16[1024,1536]{1,0:T(8,128)(2,1)} %pad_maximum_fusion.2), channel_id=1, source_target_pairs={{11,9},{8,10},{15,13},{12,14},{27,25},{24,26},{31,29},{28,30}} | collective-permute-start | bytes 9437192 | tf_op jit(solution)/shard_map/ppermute | solution.py:176
  121.3 15.0 %collective-permute-start.18 = (bf16[192,2048]{1,0:T(8,128)(2,1)}, bf16[192,2048]{1,0:T(8,128)(2,1)}, u32[]{:S(2)}, u32[]{:S(2)}) collective-permute-start(bf16[192,2048]{1,0:T(8,128)(2,1)} %select_select_fusion.1), channel_id=1, source_target_pairs={{17,1},{18,2},{21,5},{22,6}} | collective-permute-start | bytes 2359304 | tf_op jit(solution)/shard_map/ppermute | solution.py:176
  122.8 15.0 %collective-permute-start.17 = (bf16[192,2048]{1,0:T(8,128)(2,1)}, bf16[192,2048]{1,0:T(8,128)(2,1)}, u32[]{:S(2)}, u32[]{:S(2)}) collective-permute-start(bf16[192,2048]{1,0:T(8,128)(2,1)} %select_select_fusion.1), channel_id=1, source_target_pairs={{9,1},{10,2},{13,5},{14,6}} | collective-permute-start | bytes 2359304 | tf_op jit(solution)/shard_map/ppermute | solution.py:176
  136.3 6.1 %collective-permute-start.12 = (bf16[96,512]{1,0:T(8,128)(2,1)S(1)}, bf16[96,512]{1,0:T(8,128)(2,1)S(1)}, u32[]{:S(2)}, u32[]{:S(2)}) collective-permute-start(bf16[96,512]{1,0:T(8,128)(2,1)S(1)} %get-tuple-element.71.refs_0_), channel_id=1, source_target_pairs={{0,16},{1,5},{2,6},{3,19},{4,20},{5,1},{6,2},{7,23},{8,24},{9,13},... | collective-permute-start | bytes 294920 | tf_op jit(solution)/shard_map/ppermute | solution.py:176
  140.9 26.6 %collective-permute-start.20 = (bf16[192,2048]{1,0:T(8,128)(2,1)}, bf16[192,2048]{1,0:T(8,128)(2,1)}, u32[]{:S(2)}, u32[]{:S(2)}) collective-permute-start(bf16[192,2048]{1,0:T(8,128)(2,1)} %add_add_fusion.1), channel_id=1, source_target_pairs={{1,5},{2,6},{5,1},{6,2}} | collective-permute-start | bytes 2359304 | tf_op jit(solution)/shard_map/ppermute | solution.py:176
  142.4 12.0 %collective-permute-start.13 = (bf16[96,512]{1,0:T(8,128)(2,1)S(1)}, bf16[96,512]{1,0:T(8,128)(2,1)}, u32[]{:S(2)}, u32[]{:S(2)}) collective-permute-start(bf16[96,512]{1,0:T(8,128)(2,1)S(1)} %get-tuple-element.71.refs_0_), channel_id=1, source_target_pairs={{0,16},{1,2},{2,1},{3,19},{4,20},{5,6},{6,5},{7,23},{8,24},{9,10},... | collective-permute-start | bytes 294920 | tf_op jit(solution)/shard_map/ppermute | solution.py:176
  159.0 54.4 %collective-permute-start.41 = (bf16[256,2048]{1,0:T(8,128)(2,1)}, bf16[256,2048]{1,0:T(8,128)(2,1)}, u32[]{:S(2)}, u32[]{:S(2)}) collective-permute-start(bf16[256,2048]{1,0:T(8,128)(2,1)} %select_select_fusion), channel_id=1, source_target_pairs={{25,1},{26,2},{29,5},{30,6}} | collective-permute-start | bytes 3145736 | tf_op jit(solution)/shard_map/ppermute | solution.py:176
  167.4 46.0 %collective-permute-start.40 = (bf16[256,2048]{1,0:T(8,128)(2,1)}, bf16[256,2048]{1,0:T(8,128)(2,1)}, u32[]{:S(2)}, u32[]{:S(2)}) collective-permute-start(bf16[256,2048]{1,0:T(8,128)(2,1)} %select_select_fusion), channel_id=1, source_target_pairs={{17,1},{18,2},{21,5},{22,6}} | collective-permute-start | bytes 3145736 | tf_op jit(solution)/shard_map/ppermute | solution.py:176
  169.2 44.2 %collective-permute-start.39 = (bf16[256,2048]{1,0:T(8,128)(2,1)}, bf16[256,2048]{1,0:T(8,128)(2,1)}, u32[]{:S(2)}, u32[]{:S(2)}) collective-permute-start(bf16[256,2048]{1,0:T(8,128)(2,1)} %select_select_fusion), channel_id=1, source_target_pairs={{9,1},{10,2},{13,5},{14,6}} | collective-permute-start | bytes 3145736 | tf_op jit(solution)/shard_map/ppermute | solution.py:176
  172.1 17.6 %collective-permute-start.15 = (bf16[96,2048]{1,0:T(8,128)(2,1)S(1)}, bf16[96,2048]{1,0:T(8,128)(2,1)S(1)}, u32[]{:S(2)}, u32[]{:S(2)}) collective-permute-start(bf16[96,2048]{1,0:T(8,128)(2,1)S(1)} %shard_map.101), channel_id=1, source_target_pairs={{0,8},{1,9},{2,10},{3,11},{4,12},{5,13},{6,14},{7,15},{8,16},{9,17... | collective-permute-start | bytes 1179656 | tf_op jit(solution)/shard_map/ppermute | solution.py:176
  178.0 16.7 %collective-permute-start.16 = (bf16[96,2048]{1,0:T(8,128)(2,1)S(1)}, bf16[96,2048]{1,0:T(8,128)(2,1)S(1)}, u32[]{:S(2)}, u32[]{:S(2)}) collective-permute-start(bf16[96,2048]{1,0:T(8,128)(2,1)S(1)} %shard_map.101), channel_id=1, source_target_pairs={{0,12},{1,13},{2,14},{3,15},{4,8},{5,9},{6,10},{7,11},{8,20},{9,21... | collective-permute-start | bytes 1179656 | tf_op jit(solution)/shard_map/ppermute | solution.py:176
  199.3 7.6 %collective-permute-start.25 = (bf16[96,512]{1,0:T(8,128)(2,1)S(1)}, bf16[96,512]{1,0:T(8,128)(2,1)S(1)}, u32[]{:S(2)}, u32[]{:S(2)}) collective-permute-start(bf16[96,512]{1,0:T(8,128)(2,1)S(1)} %get-tuple-element.81.refs_0_), channel_id=1, source_target_pairs={{0,16},{1,2},{2,1},{3,19},{4,20},{5,6},{6,5},{7,23},{8,24},{9,10},... | collective-permute-start | bytes 294920 | tf_op jit(solution)/shard_map/ppermute | solution.py:176
  211.7 7.3 %collective-permute-start.27 = (bf16[96,2048]{1,0:T(8,128)(2,1)S(1)}, bf16[96,2048]{1,0:T(8,128)(2,1)S(1)}, u32[]{:S(2)}, u32[]{:S(2)}) collective-permute-start(bf16[96,2048]{1,0:T(8,128)(2,1)S(1)} %shard_map.104), channel_id=1, source_target_pairs={{0,8},{1,9},{2,10},{3,11},{4,12},{5,13},{6,14},{7,15},{8,16},{9,17... | collective-permute-start | bytes 1179656 | tf_op jit(solution)/shard_map/ppermute | solution.py:176
  211.8 11.2 %collective-permute-start.28 = (bf16[96,2048]{1,0:T(8,128)(2,1)S(1)}, bf16[96,2048]{1,0:T(8,128)(2,1)S(1)}, u32[]{:S(2)}, u32[]{:S(2)}) collective-permute-start(bf16[96,2048]{1,0:T(8,128)(2,1)S(1)} %shard_map.104), channel_id=1, source_target_pairs={{0,12},{1,13},{2,14},{3,15},{4,8},{5,9},{6,10},{7,11},{8,20},{9,21... | collective-permute-start | bytes 1179656 | tf_op jit(solution)/shard_map/ppermute | solution.py:176
  215.6 54.1 %collective-permute-start.42 = (bf16[256,2048]{1,0:T(8,128)(2,1)S(1)}, bf16[256,2048]{1,0:T(8,128)(2,1)S(1)}, u32[]{:S(2)}, u32[]{:S(2)}) collective-permute-start(bf16[256,2048]{1,0:T(8,128)(2,1)S(1)} %add_add_fusion), channel_id=1, source_target_pairs={{1,5},{2,6},{5,1},{6,2}} | collective-permute-start | bytes 3145736 | tf_op jit(solution)/shard_map/ppermute | solution.py:176
  227.4 5.7 %collective-permute-start.29 = (bf16[96,512]{1,0:T(8,128)(2,1)S(1)}, bf16[96,512]{1,0:T(8,128)(2,1)S(1)}, u32[]{:S(2)}, u32[]{:S(2)}) collective-permute-start(bf16[96,512]{1,0:T(8,128)(2,1)S(1)} %get-tuple-element.83.refs_0_), channel_id=1, source_target_pairs={{0,16},{1,5},{2,6},{3,19},{4,20},{5,1},{6,2},{7,23},{8,24},{9,13},... | collective-permute-start | bytes 294920 | tf_op jit(solution)/shard_map/ppermute | solution.py:176
  229.0 6.2 %collective-permute-start.30 = (bf16[96,512]{1,0:T(8,128)(2,1)S(1)}, bf16[96,512]{1,0:T(8,128)(2,1)S(1)}, u32[]{:S(2)}, u32[]{:S(2)}) collective-permute-start(bf16[96,512]{1,0:T(8,128)(2,1)S(1)} %get-tuple-element.83.refs_0_), channel_id=1, source_target_pairs={{0,16},{1,2},{2,1},{3,19},{4,20},{5,6},{6,5},{7,23},{8,24},{9,10},... | collective-permute-start | bytes 294920 | tf_op jit(solution)/shard_map/ppermute | solution.py:176
  229.5 7.7 %collective-permute-start.31 = (bf16[96,512]{1,0:T(8,128)(2,1)S(1)}, bf16[96,512]{1,0:T(8,128)(2,1)S(1)}, u32[]{:S(2)}, u32[]{:S(2)}) collective-permute-start(bf16[96,512]{1,0:T(8,128)(2,1)S(1)} %get-tuple-element.83.refs_0_), channel_id=1, source_target_pairs={{0,16},{1,6},{2,5},{3,19},{4,20},{5,2},{6,1},{7,23},{8,24},{9,14},... | collective-permute-start | bytes 294920 | tf_op jit(solution)/shard_map/ppermute | solution.py:176
  239.3 7.3 %collective-permute-start.32 = (bf16[96,2048]{1,0:T(8,128)(2,1)S(1)}, bf16[96,2048]{1,0:T(8,128)(2,1)S(1)}, u32[]{:S(2)}, u32[]{:S(2)}) collective-permute-start(bf16[96,2048]{1,0:T(8,128)(2,1)S(1)} %shard_map.106), channel_id=1, source_target_pairs={{0,8},{1,9},{2,10},{3,11},{4,12},{5,13},{6,14},{7,15},{8,16},{9,17... | collective-permute-start | bytes 1179656 | tf_op jit(solution)/shard_map/ppermute | solution.py:176
  239.4 12.4 %collective-permute-start.33 = (bf16[96,2048]{1,0:T(8,128)(2,1)S(1)}, bf16[96,2048]{1,0:T(8,128)(2,1)S(1)}, u32[]{:S(2)}, u32[]{:S(2)}) collective-permute-start(bf16[96,2048]{1,0:T(8,128)(2,1)S(1)} %shard_map.106), channel_id=1, source_target_pairs={{0,12},{1,13},{2,14},{3,15},{4,8},{5,9},{6,10},{7,11},{8,20},{9,21... | collective-permute-start | bytes 1179656 | tf_op jit(solution)/shard_map/ppermute | solution.py:176
  256.3 5.7 %collective-permute-start.34 = (bf16[96,512]{1,0:T(8,128)(2,1)S(1)}, bf16[96,512]{1,0:T(8,128)(2,1)S(1)}, u32[]{:S(2)}, u32[]{:S(2)}) collective-permute-start(bf16[96,512]{1,0:T(8,128)(2,1)S(1)} %get-tuple-element.85.refs_0_), channel_id=1, source_target_pairs={{0,16},{1,5},{2,6},{3,19},{4,20},{5,1},{6,2},{7,23},{8,24},{9,13},... | collective-permute-start | bytes 294920 | tf_op jit(solution)/shard_map/ppermute | solution.py:176
  256.7 7.4 %collective-permute-start.35 = (bf16[96,512]{1,0:T(8,128)(2,1)S(1)}, bf16[96,512]{1,0:T(8,128)(2,1)S(1)}, u32[]{:S(2)}, u32[]{:S(2)}) collective-permute-start(bf16[96,512]{1,0:T(8,128)(2,1)S(1)} %get-tuple-element.85.refs_0_), channel_id=1, source_target_pairs={{0,16},{1,2},{2,1},{3,19},{4,20},{5,6},{6,5},{7,23},{8,24},{9,10},... | collective-permute-start | bytes 294920 | tf_op jit(solution)/shard_map/ppermute | solution.py:176
  258.4 7.7 %collective-permute-start.36 = (bf16[96,512]{1,0:T(8,128)(2,1)S(1)}, bf16[96,512]{1,0:T(8,128)(2,1)S(1)}, u32[]{:S(2)}, u32[]{:S(2)}) collective-permute-start(bf16[96,512]{1,0:T(8,128)(2,1)S(1)} %get-tuple-element.85.refs_0_), channel_id=1, source_target_pairs={{0,16},{1,6},{2,5},{3,19},{4,20},{5,2},{6,1},{7,23},{8,24},{9,14},... | collective-permute-start | bytes 294920 | tf_op jit(solution)/shard_map/ppermute | solution.py:176
  268.2 7.3 %collective-permute-start.37 = (bf16[96,2048]{1,0:T(8,128)(2,1)S(1)}, bf16[96,2048]{1,0:T(8,128)(2,1)S(1)}, u32[]{:S(2)}, u32[]{:S(2)}) collective-permute-start(bf16[96,2048]{1,0:T(8,128)(2,1)S(1)} %shard_map.108), channel_id=1, source_target_pairs={{0,8},{1,9},{2,10},{3,11},{4,12},{5,13},{6,14},{7,15},{8,16},{9,17... | collective-permute-start | bytes 1179656 | tf_op jit(solution)/shard_map/ppermute | solution.py:176
  268.3 11.0 %collective-permute-start.38 = (bf16[96,2048]{1,0:T(8,128)(2,1)S(1)}, bf16[96,2048]{1,0:T(8,128)(2,1)S(1)}, u32[]{:S(2)}, u32[]{:S(2)}) collective-permute-start(bf16[96,2048]{1,0:T(8,128)(2,1)S(1)} %shard_map.108), channel_id=1, source_target_pairs={{0,12},{1,13},{2,14},{3,15},{4,8},{5,9},{6,10},{7,11},{8,20},{9,21... | collective-permute-start | bytes 1179656 | tf_op jit(solution)/shard_map/ppermute | solution.py:176
  285.5 6.1 %collective-permute-start.44 = (bf16[96,512]{1,0:T(8,128)(2,1)S(1)}, bf16[96,512]{1,0:T(8,128)(2,1)S(1)}, u32[]{:S(2)}, u32[]{:S(2)}) collective-permute-start(bf16[96,512]{1,0:T(8,128)(2,1)S(1)} %get-tuple-element.88.refs_0_), channel_id=1, source_target_pairs={{0,16},{1,2},{2,1},{3,19},{4,20},{5,6},{6,5},{7,23},{8,24},{9,10},... | collective-permute-start | bytes 294920 | tf_op jit(solution)/shard_map/ppermute | solution.py:176
  285.9 7.7 %collective-permute-start.45 = (bf16[96,512]{1,0:T(8,128)(2,1)S(1)}, bf16[96,512]{1,0:T(8,128)(2,1)S(1)}, u32[]{:S(2)}, u32[]{:S(2)}) collective-permute-start(bf16[96,512]{1,0:T(8,128)(2,1)S(1)} %get-tuple-element.88.refs_0_), channel_id=1, source_target_pairs={{0,16},{1,6},{2,5},{3,19},{4,20},{5,2},{6,1},{7,23},{8,24},{9,14},... | collective-permute-start | bytes 294920 | tf_op jit(solution)/shard_map/ppermute | solution.py:176
  295.7 7.3 %collective-permute-start.46 = (bf16[96,2048]{1,0:T(8,128)(2,1)S(1)}, bf16[96,2048]{1,0:T(8,128)(2,1)S(1)}, u32[]{:S(2)}, u32[]{:S(2)}) collective-permute-start(bf16[96,2048]{1,0:T(8,128)(2,1)S(1)} %get-tuple-element.91), channel_id=1, source_target_pairs={{0,8},{1,9},{2,10},{3,11},{4,12},{5,13},{6,14},{7,15},{8,16},{9,17... | collective-permute-start | bytes 1179656 | tf_op jit(solution)/shard_map/ppermute | solution.py:176
  295.8 12.4 %collective-permute-start.47 = (bf16[96,2048]{1,0:T(8,128)(2,1)S(1)}, bf16[96,2048]{1,0:T(8,128)(2,1)S(1)}, u32[]{:S(2)}, u32[]{:S(2)}) collective-permute-start(bf16[96,2048]{1,0:T(8,128)(2,1)S(1)} %get-tuple-element.91), channel_id=1, source_target_pairs={{0,12},{1,13},{2,14},{3,15},{4,8},{5,9},{6,10},{7,11},{8,20},{9,21... | collective-permute-start | bytes 1179656 | tf_op jit(solution)/shard_map/ppermute | solution.py:176
  313.3 7.3 %collective-permute-start.49 = (bf16[96,512]{1,0:T(8,128)(2,1)S(1)}, bf16[96,512]{1,0:T(8,128)(2,1)S(1)}, u32[]{:S(2)}, u32[]{:S(2)}) collective-permute-start(bf16[96,512]{1,0:T(8,128)(2,1)S(1)} %get-tuple-element.92.refs_0_), channel_id=1, source_target_pairs={{0,16},{1,2},{2,1},{3,19},{4,20},{5,6},{6,5},{7,23},{8,24},{9,10},... | collective-permute-start | bytes 294920 | tf_op jit(solution)/shard_map/ppermute | solution.py:176
  314.8 7.8 %collective-permute-start.50 = (bf16[96,512]{1,0:T(8,128)(2,1)S(1)}, bf16[96,512]{1,0:T(8,128)(2,1)S(1)}, u32[]{:S(2)}, u32[]{:S(2)}) collective-permute-start(bf16[96,512]{1,0:T(8,128)(2,1)S(1)} %get-tuple-element.92.refs_0_), channel_id=1, source_target_pairs={{0,16},{1,6},{2,5},{3,19},{4,20},{5,2},{6,1},{7,23},{8,24},{9,14},... | collective-permute-start | bytes 294920 | tf_op jit(solution)/shard_map/ppermute | solution.py:176
  324.8 7.3 %collective-permute-start.51 = (bf16[96,2048]{1,0:T(8,128)(2,1)S(1)}, bf16[96,2048]{1,0:T(8,128)(2,1)S(1)}, u32[]{:S(2)}, u32[]{:S(2)}) collective-permute-start(bf16[96,2048]{1,0:T(8,128)(2,1)S(1)} %get-tuple-element.95), channel_id=1, source_target_pairs={{0,8},{1,9},{2,10},{3,11},{4,12},{5,13},{6,14},{7,15},{8,16},{9,17... | collective-permute-start | bytes 1179656 | tf_op jit(solution)/shard_map/ppermute | solution.py:176
  325.0 11.0 %collective-permute-start.52 = (bf16[96,2048]{1,0:T(8,128)(2,1)S(1)}, bf16[96,2048]{1,0:T(8,128)(2,1)S(1)}, u32[]{:S(2)}, u32[]{:S(2)}) collective-permute-start(bf16[96,2048]{1,0:T(8,128)(2,1)S(1)} %get-tuple-element.95), channel_id=1, source_target_pairs={{0,12},{1,13},{2,14},{3,15},{4,8},{5,9},{6,10},{7,11},{8,20},{9,21... | collective-permute-start | bytes 1179656 | tf_op jit(solution)/shard_map/ppermute | solution.py:176
  342.2 6.1 %collective-permute-start.54 = (bf16[96,512]{1,0:T(8,128)(2,1)S(1)}, bf16[96,512]{1,0:T(8,128)(2,1)S(1)}, u32[]{:S(2)}, u32[]{:S(2)}) collective-permute-start(bf16[96,512]{1,0:T(8,128)(2,1)S(1)} %get-tuple-element.96.refs_0_), channel_id=1, source_target_pairs={{0,16},{1,2},{2,1},{3,19},{4,20},{5,6},{6,5},{7,23},{8,24},{9,10},... | collective-permute-start | bytes 294920 | tf_op jit(solution)/shard_map/ppermute | solution.py:176
  342.6 7.7 %collective-permute-start.55 = (bf16[96,512]{1,0:T(8,128)(2,1)S(1)}, bf16[96,512]{1,0:T(8,128)(2,1)S(1)}, u32[]{:S(2)}, u32[]{:S(2)}) collective-permute-start(bf16[96,512]{1,0:T(8,128)(2,1)S(1)} %get-tuple-element.96.refs_0_), channel_id=1, source_target_pairs={{0,16},{1,6},{2,5},{3,19},{4,20},{5,2},{6,1},{7,23},{8,24},{9,14},... | collective-permute-start | bytes 294920 | tf_op jit(solution)/shard_map/ppermute | solution.py:176
  352.4 7.3 %collective-permute-start.56 = (bf16[96,2048]{1,0:T(8,128)(2,1)S(1)}, bf16[96,2048]{1,0:T(8,128)(2,1)S(1)}, u32[]{:S(2)}, u32[]{:S(2)}) collective-permute-start(bf16[96,2048]{1,0:T(8,128)(2,1)S(1)} %get-tuple-element.99), channel_id=1, source_target_pairs={{0,8},{1,9},{2,10},{3,11},{4,12},{5,13},{6,14},{7,15},{8,16},{9,17... | collective-permute-start | bytes 1179656 | tf_op jit(solution)/shard_map/ppermute | solution.py:176
  352.5 12.4 %collective-permute-start.57 = (bf16[96,2048]{1,0:T(8,128)(2,1)S(1)}, bf16[96,2048]{1,0:T(8,128)(2,1)S(1)}, u32[]{:S(2)}, u32[]{:S(2)}) collective-permute-start(bf16[96,2048]{1,0:T(8,128)(2,1)S(1)} %get-tuple-element.99), channel_id=1, source_target_pairs={{0,12},{1,13},{2,14},{3,15},{4,8},{5,9},{6,10},{7,11},{8,20},{9,21... | collective-permute-start | bytes 1179656 | tf_op jit(solution)/shard_map/ppermute | solution.py:176
  370.8 6.0 %collective-permute-start.58 = (bf16[96,512]{1,0:T(8,128)(2,1)}, bf16[96,512]{1,0:T(8,128)(2,1)}, u32[]{:S(2)}, u32[]{:S(2)}) collective-permute-start(bf16[96,512]{1,0:T(8,128)(2,1)} %get-tuple-element.100.refs_0_), channel_id=1, source_target_pairs={{0,16},{1,5},{2,6},{3,19},{4,20},{5,1},{6,2},{7,23},{8,24},{9,13},... | collective-permute-start | bytes 294920 | tf_op jit(solution)/shard_map/ppermute | solution.py:176
  371.1 7.8 %collective-permute-start.59 = (bf16[96,512]{1,0:T(8,128)(2,1)}, bf16[96,512]{1,0:T(8,128)(2,1)}, u32[]{:S(2)}, u32[]{:S(2)}) collective-permute-start(bf16[96,512]{1,0:T(8,128)(2,1)} %get-tuple-element.100.refs_0_), channel_id=1, source_target_pairs={{0,16},{1,2},{2,1},{3,19},{4,20},{5,6},{6,5},{7,23},{8,24},{9,10},... | collective-permute-start | bytes 294920 | tf_op jit(solution)/shard_map/ppermute | solution.py:176
  372.8 8.0 %collective-permute-start.60 = (bf16[96,512]{1,0:T(8,128)(2,1)}, bf16[96,512]{1,0:T(8,128)(2,1)}, u32[]{:S(2)}, u32[]{:S(2)}) collective-permute-start(bf16[96,512]{1,0:T(8,128)(2,1)} %get-tuple-element.100.refs_0_), channel_id=1, source_target_pairs={{0,16},{1,6},{2,5},{3,19},{4,20},{5,2},{6,1},{7,23},{8,24},{9,14},... | collective-permute-start | bytes 294920 | tf_op jit(solution)/shard_map/ppermute | solution.py:176
  388.0 7.3 %collective-permute-start.61 = (bf16[96,2048]{1,0:T(8,128)(2,1)S(1)}, bf16[96,2048]{1,0:T(8,128)(2,1)S(1)}, u32[]{:S(2)}, u32[]{:S(2)}) collective-permute-start(bf16[96,2048]{1,0:T(8,128)(2,1)S(1)} %get-tuple-element.103), channel_id=1, source_target_pairs={{0,8},{1,9},{2,10},{3,11},{4,12},{5,13},{6,14},{7,15},{8,16},{9,17... | collective-permute-start | bytes 1179656 | tf_op jit(solution)/shard_map/ppermute | solution.py:176
  388.0 11.3 %collective-permute-start.62 = (bf16[96,2048]{1,0:T(8,128)(2,1)S(1)}, bf16[96,2048]{1,0:T(8,128)(2,1)S(1)}, u32[]{:S(2)}, u32[]{:S(2)}) collective-permute-start(bf16[96,2048]{1,0:T(8,128)(2,1)S(1)} %get-tuple-element.103), channel_id=1, source_target_pairs={{0,12},{1,13},{2,14},{3,15},{4,8},{5,9},{6,10},{7,11},{8,20},{9,21... | collective-permute-start | bytes 1179656 | tf_op jit(solution)/shard_map/ppermute | solution.py:176
  409.1 6.3 %collective-permute-start.64 = (bf16[96,512]{1,0:T(8,128)(2,1)S(1)}, bf16[96,512]{1,0:T(8,128)(2,1)S(1)}, u32[]{:S(2)}, u32[]{:S(2)}) collective-permute-start(bf16[96,512]{1,0:T(8,128)(2,1)S(1)} %get-tuple-element.104.refs_0_), channel_id=1, source_target_pairs={{0,16},{1,2},{2,1},{3,19},{4,20},{5,6},{6,5},{7,23},{8,24},{9,10},... | collective-permute-start | bytes 294920 | tf_op jit(solution)/shard_map/ppermute | solution.py:176
  409.6 7.7 %collective-permute-start.65 = (bf16[96,512]{1,0:T(8,128)(2,1)S(1)}, bf16[96,512]{1,0:T(8,128)(2,1)S(1)}, u32[]{:S(2)}, u32[]{:S(2)}) collective-permute-start(bf16[96,512]{1,0:T(8,128)(2,1)S(1)} %get-tuple-element.104.refs_0_), channel_id=1, source_target_pairs={{0,16},{1,6},{2,5},{3,19},{4,20},{5,2},{6,1},{7,23},{8,24},{9,14},... | collective-permute-start | bytes 294920 | tf_op jit(solution)/shard_map/ppermute | solution.py:176
  419.6 7.3 %collective-permute-start.66 = (bf16[96,2048]{1,0:T(8,128)(2,1)S(1)}, bf16[96,2048]{1,0:T(8,128)(2,1)S(1)}, u32[]{:S(2)}, u32[]{:S(2)}) collective-permute-start(bf16[96,2048]{1,0:T(8,128)(2,1)S(1)} %get-tuple-element.107), channel_id=1, source_target_pairs={{0,8},{1,9},{2,10},{3,11},{4,12},{5,13},{6,14},{7,15},{8,16},{9,17... | collective-permute-start | bytes 1179656 | tf_op jit(solution)/shard_map/ppermute | solution.py:176
  419.6 12.4 %collective-permute-start.67 = (bf16[96,2048]{1,0:T(8,128)(2,1)S(1)}, bf16[96,2048]{1,0:T(8,128)(2,1)S(1)}, u32[]{:S(2)}, u32[]{:S(2)}) collective-permute-start(bf16[96,2048]{1,0:T(8,128)(2,1)S(1)} %get-tuple-element.107), channel_id=1, source_target_pairs={{0,12},{1,13},{2,14},{3,15},{4,8},{5,9},{6,10},{7,11},{8,20},{9,21... | collective-permute-start | bytes 1179656 | tf_op jit(solution)/shard_map/ppermute | solution.py:176
  436.9 7.4 %collective-permute-start.69 = (bf16[96,512]{1,0:T(8,128)(2,1)S(1)}, bf16[96,512]{1,0:T(8,128)(2,1)S(1)}, u32[]{:S(2)}, u32[]{:S(2)}) collective-permute-start(bf16[96,512]{1,0:T(8,128)(2,1)S(1)} %get-tuple-element.108.refs_0_), channel_id=1, source_target_pairs={{0,16},{1,2},{2,1},{3,19},{4,20},{5,6},{6,5},{7,23},{8,24},{9,10},... | collective-permute-start | bytes 294920 | tf_op jit(solution)/shard_map/ppermute | solution.py:176
  438.6 7.6 %collective-permute-start.70 = (bf16[96,512]{1,0:T(8,128)(2,1)S(1)}, bf16[96,512]{1,0:T(8,128)(2,1)S(1)}, u32[]{:S(2)}, u32[]{:S(2)}) collective-permute-start(bf16[96,512]{1,0:T(8,128)(2,1)S(1)} %get-tuple-element.108.refs_0_), channel_id=1, source_target_pairs={{0,16},{1,6},{2,5},{3,19},{4,20},{5,2},{6,1},{7,23},{8,24},{9,14},... | collective-permute-start | bytes 294920 | tf_op jit(solution)/shard_map/ppermute | solution.py:176
  448.4 7.3 %collective-permute-start.71 = (bf16[96,2048]{1,0:T(8,128)(2,1)S(1)}, bf16[96,2048]{1,0:T(8,128)(2,1)S(1)}, u32[]{:S(2)}, u32[]{:S(2)}) collective-permute-start(bf16[96,2048]{1,0:T(8,128)(2,1)S(1)} %get-tuple-element.111), channel_id=1, source_target_pairs={{0,8},{1,9},{2,10},{3,11},{4,12},{5,13},{6,14},{7,15},{8,16},{9,17... | collective-permute-start | bytes 1179656 | tf_op jit(solution)/shard_map/ppermute | solution.py:176
  448.5 11.1 %collective-permute-start.72 = (bf16[96,2048]{1,0:T(8,128)(2,1)S(1)}, bf16[96,2048]{1,0:T(8,128)(2,1)S(1)}, u32[]{:S(2)}, u32[]{:S(2)}) collective-permute-start(bf16[96,2048]{1,0:T(8,128)(2,1)S(1)} %get-tuple-element.111), channel_id=1, source_target_pairs={{0,12},{1,13},{2,14},{3,15},{4,8},{5,9},{6,10},{7,11},{8,20},{9,21... | collective-permute-start | bytes 1179656 | tf_op jit(solution)/shard_map/ppermute | solution.py:176
  465.9 6.0 %collective-permute-start.74 = (bf16[96,512]{1,0:T(8,128)(2,1)S(1)}, bf16[96,512]{1,0:T(8,128)(2,1)S(1)}, u32[]{:S(2)}, u32[]{:S(2)}) collective-permute-start(bf16[96,512]{1,0:T(8,128)(2,1)S(1)} %get-tuple-element.112), channel_id=1, source_target_pairs={{0,16},{1,2},{2,1},{3,19},{4,20},{5,6},{6,5},{7,23},{8,24},{9,10},... | collective-permute-start | bytes 294920 | tf_op jit(solution)/shard_map/ppermute | solution.py:176
  466.2 7.7 %collective-permute-start.75 = (bf16[96,512]{1,0:T(8,128)(2,1)S(1)}, bf16[96,512]{1,0:T(8,128)(2,1)S(1)}, u32[]{:S(2)}, u32[]{:S(2)}) collective-permute-start(bf16[96,512]{1,0:T(8,128)(2,1)S(1)} %get-tuple-element.112), channel_id=1, source_target_pairs={{0,16},{1,6},{2,5},{3,19},{4,20},{5,2},{6,1},{7,23},{8,24},{9,14},... | collective-permute-start | bytes 294920 | tf_op jit(solution)/shard_map/ppermute | solution.py:176
  482.9 33.6 %collective-permute-start.79 = (f32[8,2048]{1,0:T(8,128)S(1)}, f32[8,2048]{1,0:T(8,128)S(1)}, u32[]{:S(2)}, u32[]{:S(2)}) collective-permute-start(f32[8,2048]{1,0:T(8,128)S(1)} %add_add_fusion.3), channel_id=1, source_target_pairs={{1,0},{2,3},{5,4},{6,7},{9,8},{10,11},{13,12},{14,15},{17,16},{18,... | collective-permute-start | bytes 196616 | tf_op jit(solution)/shard_map/ppermute | solution.py:176
  (59 other events, 1178.7 us)

commit v6 on v3

--- a/solution.py
+++ b/solution.py
@@ -12,17 +12,16 @@
 M = 16
 EPSILON = 1e-05
 AXES = ("section", "tp", "doc")
-C_FIRST, C_INIT, C_TP, C_POOL, C_PHASE, C_LEN = 0, 1, 2, 3, 4, 5
-
-
-def attend_kernel(turn, docs, tokens, blocks, sets, meta, where, *refs):
+C_FIRST, C_INIT, C_TP, C_POOL, C_LEN = 0, 1, 2, 3, 4
+
+
+def attend_kernel(turn, docs, tokens, blocks, meta, where, *refs):
     halves = refs[0]
     other = refs[1]
     tok, tok_other, mem, mem_other, gain = refs[2:7]
-    held = 1 + sets * (blocks - 1)
-    weights = refs[7 : 7 + held]
-    mixed_ref, keep_ref = refs[7 + held : 9 + held]
-    normed, acc = refs[9 + held :]
+    weights = refs[7 : 7 + blocks]
+    mixed_ref, keep_ref = refs[7 + blocks : 9 + blocks]
+    normed, acc = refs[9 + blocks :]
     rows = M + tokens
     half = halves.shape[1]
     depth = weights[0].shape[0]
@@ -53,29 +52,16 @@
         return 0
 
     lax.fori_loop(0, docs, prepare, 0)
-
-    def multiply(b, weight):
+    for b in range(blocks):
         at = pl.multiple_of(where[b] * depth, 128)
         left = normed[:, pl.ds(at, depth)]
         for c in range(3):
             span = pl.ds(c * cols, cols)
-            part = jnp.dot(left, weight[:, span], preferred_element_type=jnp.float32)
+            part = jnp.dot(left, weights[b][:, span], preferred_element_type=jnp.float32)
             if b == 0:
                 acc[:, span] = part
             else:
                 acc[:, span] += part
-
-    multiply(0, weights[0])
-    for phase in range(sets):
-
-        def received(phase=phase):
-            for b in range(1, blocks):
-                multiply(b, weights[b + phase * (blocks - 1)])
-
-        if sets == 1:
-            received()
-        else:
-            pl.when(meta[turn, C_PHASE] == phase)(received)
 
     row = lax.broadcasted_iota(jnp.int32, (rows, rows), 0)
     col = lax.broadcasted_iota(jnp.int32, (rows, rows), 1)
@@ -167,7 +153,7 @@
     def lin(a, b, c):
         return (a * T + b) * D + c
 
-    limit = 24 * 2**20 + 2 * R * (4 * half + 12 * cols)
+    limit = 20 * 2**20 + 2 * R * (4 * half + 12 * cols)
     params = pltpu.CompilerParams(vmem_limit_bytes=limit)
 
     def send(block, pairs):
@@ -201,16 +187,13 @@
     own_block = block_of((z == hi).astype(jnp.int32))
     where = jnp.stack([z] + [jnp.where(z == hi, D - 1 - c, c) for c in rounds]).astype(jnp.int32)
 
-    def relay(parity, sent):
-        moved = []
-        for c, block in zip(rounds, sent):
-            pairs = []
-            for a in range(parity, S, 2):
-                for b in range(T):
-                    pairs.append(((a, b, c), (a, b, lo)))
-                    pairs.append(((a, b, D - 1 - c), (a, b, hi)))
-            moved.append(send(block, pairs))
-        return moved
+    def relay(c, block):
+        pairs = []
+        for a in range(S):
+            for b in range(T):
+                pairs.append(((a, b, c), (a, b, lo)))
+                pairs.append(((a, b, D - 1 - c), (a, b, hi)))
+        return send(block, pairs)
 
     vocab = emb_table.shape[0]
 
@@ -225,16 +208,11 @@
         return full, send(full, [((0, b, c), (0, T - 1 - b, c)) for b in range(T) for c in planes])
 
     ids, blocks = lax.optimization_barrier((ids, blocks))
-    even = relay(0, blocks)
-    pairs = [embed(ids[:, 0])]
+    early = [relay(c, block) for c, block in zip(rounds[:-1], blocks[:-1])]
+    last, early = lax.optimization_barrier((blocks[-1], early))
+    weights = [own_block] + early + [relay(rounds[-1], last)]
+    tok, tok_other = embed(jnp.concatenate([ids[:, seg] for seg in range(segs)]))
     mem_other = send(mem_init, [((0, b, c), (0, T - 1 - b, c)) for b in range(T) for c in planes])
-    blocks, even, pairs, mem_other, ids = lax.optimization_barrier(
-        (blocks, even, pairs, mem_other, ids)
-    )
-    odd = relay(1, blocks)
-    for seg in range(1, segs):
-        pairs.append(embed(ids[:, seg]))
-    tok, tok_other = zip(*pairs)
 
     offset = jnp.arange(turns) - s
     group = offset % S
@@ -248,7 +226,6 @@
             (s == 0) & (offset < S),
             jnp.full((turns,), t),
             active & (segment == segs - 1),
-            jnp.full((turns,), s % 2),
         ],
         1,
     ).astype(jnp.int32)
@@ -267,13 +244,11 @@
     other = jnp.zeros((R, half), jnp.bfloat16)
     pools = []
     for k in range(turns):
-        sets = 1 if k == 0 else 2
-        weights = [own_block] + even + (odd if k else [])
-        g, seg = k % S, k // S
-        rows_of = slice(g * n * tokens, (g + 1) * n * tokens)
-        tk, tko = (a[min(seg, segs - 1)][rows_of] for a in (tok, tok_other))
+        step = n * tokens
+        at = min(k, segs * S - 1) * step
+        tk, tko = tok[at : at + step], tok_other[at : at + step]
         mixed, keep = pl.pallas_call(
-            functools.partial(attend_kernel, k, n, tokens, D, sets),
+            functools.partial(attend_kernel, k, n, tokens, D),
             out_shape=(
                 jax.ShapeDtypeStruct((R, cols), jnp.bfloat16),
                 jax.ShapeDtypeStruct((R, half), jnp.bfloat16),

time: 558 us -> 508 us (0.910)
  Pallas kernels: 126 us -> 96.1 us
  local copies, waits for them, and re-layouts: 50.5 us -> 33.2 us
  starting transfers between devices: 88.6 us -> 82.5 us
    pallas_call x11, Pallas kernels: 103 us -> 73.8 us  [body(): pl.pallas_call(functools.partial(attend_kernel, k, n, tokens, D), out_sha...]
    gather x2 -> x1, local copies, waits for them, and re-layouts: 21.5 us -> 13.2 us  [embed(): picked = jnp.take(emb_table, jnp.clip(local, 0, vocab - 1), axis=0)]
    unnamed x96 -> x56, local copies, waits for them, and re-layouts: 13.1 us -> 5.27 us
    ppermute x75 -> x68, starting transfers between devices: 88.6 us -> 82.5 us  [send(): return lax.ppermute(block, AXES, [(lin(*a), lin(*b)) for a, b in pairs])]
    ppermute x75 -> x68, waiting for transfers between devices: 270 us -> 274 us  [send(): return lax.ppermute(block, AXES, [(lin(*a), lin(*b)) for a, b in pairs])]
  transfers between devices with their start and end apart: 75 -> 68, of which waited for: 56 -> 58; matrix products, arithmetic and copies ran while one was open for 6% -> 7% of each run, Pallas kernels for 8% -> 0%
where the time goes in v6:
time: 508 us; the launch traced here: 500 us
  waiting for transfers between devices  274 us (54%)
  Pallas kernels  96.1 us (19%)
  starting transfers between devices  82.5 us (16%)
  local copies, waits for them, and re-layouts  33.2 us (7%)
  other arithmetic  13.5 us (3%)
    ppermute x68, waiting for transfers between devices, send(): return lax.ppermute(block, AXES, [(lin(*a), lin(*b)) for a, b in pairs])  274 us
    ppermute x68, starting transfers between devices, send(): return lax.ppermute(block, AXES, [(lin(*a), lin(*b)) for a, b in pairs])  82.5 us
    pallas_call x11, Pallas kernels, body(): pl.pallas_call(functools.partial(attend_kernel, k, n, tokens, D), out_sha...  73.8 us
    pallas_call x10, Pallas kernels, body(): pl.pallas_call(functools.partial(project_kernel, k, n, tokens, parts, poo...  22.2 us
    gather x1, local copies, waits for them, and re-layouts, embed(): picked = jnp.take(emb_table, jnp.clip(local, 0, vocab - 1), axis=0)  13.2 us
  transfers between devices with their start and end apart: 68, of which 58 were waited for; matrix products, arithmetic and copies ran while one was open for 7% of the time, Pallas kernels for 0%

profile of v6, /device:TPU:0, one launch (start us, length us, event | category | flops | bytes accessed | tf_op | source)
XLA Modules:
  0.0 500.4 jit_solution(14836944794513314403)
XLA Ops:
  1.5 3.0 collective-permute-start
  4.6 2.6 collective-permute-start.1
  8.5 3.7 dynamic-slice_bitcast_fusion.2
  12.3 2.4 dynamic-slice_bitcast_fusion
  20.5 2.8 collective-permute-start.8
  23.3 2.3 collective-permute-start.9
  25.7 13.2 %gather_fusion.1 = bf16[512,2048]{1,0:T(8,128)(2,1)} fusion(bf16[4096,2048]{1,0:T(8,128)(2,1)} %param.12, s32[1024]{0:T(1024)S(1)} %pad_clamp_fusion), kind=kCustom, calls=%fused_computation.1 | custom fusion | bytes 4196352 | tf_op jit(solution)/shard_map/jit(_take)/gather | solution.py:203
  43.4 46.5 %collective-permute-done.8.refs_8_ = bf16[1024,1536]{1,0:T(8,128)(2,1)S(1)} collective-permute-done((bf16[1024,1536]{1,0:T(8,128)(2,1)}, bf16[1024,1536]{1,0:T(8,128)(2,1)S(1)}, u32[]{:S(2)}, u32[]{:S(2)}) %collective-permute-start.8) | collective-permute-done | bytes 3145760 | tf_op jit(solution)/shard_map/ppermute | solution.py:160
  89.9 7.1 %collective-permute-start.10 = (bf16[1024,1536]{1,0:T(8,128)(2,1)}, bf16[1024,1536]{1,0:T(8,128)(2,1)}, u32[]{:S(2)}, u32[]{:S(2)}) collective-permute-start(bf16[1024,1536]{1,0:T(8,128)(2,1)} %pad_maximum_fusion.2), channel_id=1, source_target_pairs={{3,1},{0,2},{7,5},{4,6},{11,9},{8,10},{15,13},{12,14},{19,17},{16,... | collective-permute-start | bytes 9437192 | tf_op jit(solution)/shard_map/ppermute | solution.py:160
  109.8 51.8 %collective-permute-done.10.refs_10_ = bf16[1024,1536]{1,0:T(8,128)(2,1)} collective-permute-done((bf16[1024,1536]{1,0:T(8,128)(2,1)}, bf16[1024,1536]{1,0:T(8,128)(2,1)}, u32[]{:S(2)}, u32[]{:S(2)}) %collective-permute-start.10) | collective-permute-done | bytes 3145760 | tf_op jit(solution)/shard_map/ppermute | solution.py:160
  161.6 6.8 %shard_map.100 = (bf16[96,512]{1,0:T(8,128)(2,1)S(1)}, bf16[96,2048]{1,0:T(8,128)(2,1)S(1)}) custom-call(s32[11,6]{1,0:T(8,128)S(1)} %concatenate.26.meta, s32[4]{0:T(128)S(1)} %pad_add_fusion.3.where, bf16[96,2048]{1,0:T(8,128)(2,1)S(1)} %broadcast_14_refs_0__refs_1_.2.refs_0_.refs_1_, bf16[96,2048]{1,0:T(8,128)(2,1)S(1)} %broadcast_14_refs_0__refs_1_.2.refs_0_.refs_1_, ...), custom_call_target="tpu_custom_call" | custom-call | tf_op jit(solution)/shard_map/pallas_call | solution.py:250
  175.5 2.1 shard_map.101
  177.7 2.3 collective-permute-start.15
  180.0 4.9 collective-permute-done.14.refs_0_
  184.9 5.3 %collective-permute-done.15.refs_1_ = bf16[96,2048]{1,0:T(8,128)(2,1)S(1)} collective-permute-done((bf16[96,2048]{1,0:T(8,128)(2,1)S(1)}, bf16[96,2048]{1,0:T(8,128)(2,1)S(1)}, u32[]{:S(2)}, u32[]{:S(2)}) %collective-permute-start.15) | collective-permute-done | bytes 393248 | tf_op jit(solution)/shard_map/ppermute | solution.py:160
  190.2 6.6 %shard_map.102 = (bf16[96,512]{1,0:T(8,128)(2,1)S(1)}, bf16[96,2048]{1,0:T(8,128)(2,1)S(1)}) custom-call(s32[11,6]{1,0:T(8,128)S(1)} %concatenate.26.meta, s32[4]{0:T(128)S(1)} %pad_add_fusion.3.where, bf16[96,2048]{1,0:T(8,128)(2,1)S(1)} %collective-permute-done.14.refs_0_, bf16[96,2048]{1,0:T(8,128)(2,1)S(1)} %collective-permute-done.15.refs_1_, ...), custom_call_target="tpu_custom_call" | custom-call | tf_op jit(solution)/shard_map/pallas_call | solution.py:250
  200.0 2.6 collective-permute-done.16.refs_1_
  210.2 5.1 %collective-permute-done.19.refs_0_ = bf16[96,2048]{1,0:T(8,128)(2,1)S(1)} collective-permute-done((bf16[96,2048]{1,0:T(8,128)(2,1)S(1)}, bf16[96,2048]{1,0:T(8,128)(2,1)S(1)}, u32[]{:S(2)}, u32[]{:S(2)}) %collective-permute-start.19) | collective-permute-done | bytes 393248 | tf_op jit(solution)/shard_map/ppermute | solution.py:160
  215.3 5.0 collective-permute-done.20.refs_1_
  220.3 6.6 %shard_map.104 = (bf16[96,512]{1,0:T(8,128)(2,1)S(1)}, bf16[96,2048]{1,0:T(8,128)(2,1)S(1)}) custom-call(s32[11,6]{1,0:T(8,128)S(1)} %concatenate.26.meta, s32[4]{0:T(128)S(1)} %pad_add_fusion.3.where, bf16[96,2048]{1,0:T(8,128)(2,1)S(1)} %collective-permute-done.19.refs_0_, bf16[96,2048]{1,0:T(8,128)(2,1)S(1)} %collective-permute-done.20.refs_1_, ...), custom_call_target="tpu_custom_call" | custom-call | tf_op jit(solution)/shard_map/pallas_call | solution.py:250
  230.1 2.4 collective-permute-done.21.refs_1_
  240.5 5.1 %collective-permute-done.24.refs_0_ = bf16[96,2048]{1,0:T(8,128)(2,1)S(1)} collective-permute-done((bf16[96,2048]{1,0:T(8,128)(2,1)S(1)}, bf16[96,2048]{1,0:T(8,128)(2,1)S(1)}, u32[]{:S(2)}, u32[]{:S(2)}) %collective-permute-start.24) | collective-permute-done | bytes 393248 | tf_op jit(solution)/shard_map/ppermute | solution.py:160
  245.6 5.1 %collective-permute-done.25.refs_1_ = bf16[96,2048]{1,0:T(8,128)(2,1)S(1)} collective-permute-done((bf16[96,2048]{1,0:T(8,128)(2,1)S(1)}, bf16[96,2048]{1,0:T(8,128)(2,1)S(1)}, u32[]{:S(2)}, u32[]{:S(2)}) %collective-permute-start.25) | collective-permute-done | bytes 393248 | tf_op jit(solution)/shard_map/ppermute | solution.py:160
  250.7 6.6 %shard_map.106 = (bf16[96,512]{1,0:T(8,128)(2,1)S(1)}, bf16[96,2048]{1,0:T(8,128)(2,1)S(1)}) custom-call(s32[11,6]{1,0:T(8,128)S(1)} %concatenate.26.meta, s32[4]{0:T(128)S(1)} %pad_add_fusion.3.where, bf16[96,2048]{1,0:T(8,128)(2,1)S(1)} %collective-permute-done.24.refs_0_, bf16[96,2048]{1,0:T(8,128)(2,1)S(1)} %collective-permute-done.25.refs_1_, ...), custom_call_target="tpu_custom_call" | custom-call | tf_op jit(solution)/shard_map/pallas_call | solution.py:250
  260.4 2.7 collective-permute-done.26.refs_1_
  266.8 2.1 shard_map.107
  270.9 5.3 %collective-permute-done.29.refs_0_ = bf16[96,2048]{1,0:T(8,128)(2,1)S(1)} collective-permute-done((bf16[96,2048]{1,0:T(8,128)(2,1)S(1)}, bf16[96,2048]{1,0:T(8,128)(2,1)S(1)}, u32[]{:S(2)}, u32[]{:S(2)}) %collective-permute-start.29) | collective-permute-done | bytes 393248 | tf_op jit(solution)/shard_map/ppermute | solution.py:160
  276.1 5.0 collective-permute-done.30.refs_1_
  281.1 6.6 %shard_map.108 = (bf16[96,512]{1,0:T(8,128)(2,1)S(1)}, bf16[96,2048]{1,0:T(8,128)(2,1)S(1)}) custom-call(s32[11,6]{1,0:T(8,128)S(1)} %concatenate.26.meta, s32[4]{0:T(128)S(1)} %pad_add_fusion.3.where, bf16[96,2048]{1,0:T(8,128)(2,1)S(1)} %collective-permute-done.29.refs_0_, bf16[96,2048]{1,0:T(8,128)(2,1)S(1)} %collective-permute-done.30.refs_1_, ...), custom_call_target="tpu_custom_call" | custom-call | tf_op jit(solution)/shard_map/pallas_call | solution.py:250
  290.8 2.6 collective-permute-done.31.refs_1_
  297.1 2.2 shard_map.109
  301.3 5.2 %collective-permute-done.34.refs_0_ = bf16[96,2048]{1,0:T(8,128)(2,1)S(1)} collective-permute-done((bf16[96,2048]{1,0:T(8,128)(2,1)S(1)}, bf16[96,2048]{1,0:T(8,128)(2,1)S(1)}, u32[]{:S(2)}, u32[]{:S(2)}) %collective-permute-start.34) | collective-permute-done | bytes 393248 | tf_op jit(solution)/shard_map/ppermute | solution.py:160
  306.6 5.0 collective-permute-done.35.refs_1_
  311.5 6.6 %shard_map.110 = (bf16[96,512]{1,0:T(8,128)(2,1)S(1)}, bf16[96,2048]{1,0:T(8,128)(2,1)S(1)}) custom-call(s32[11,6]{1,0:T(8,128)S(1)} %concatenate.26.meta, s32[4]{0:T(128)S(1)} %pad_add_fusion.3.where, bf16[96,2048]{1,0:T(8,128)(2,1)S(1)} %collective-permute-done.34.refs_0_, bf16[96,2048]{1,0:T(8,128)(2,1)S(1)} %collective-permute-done.35.refs_1_, ...), custom_call_target="tpu_custom_call" | custom-call | tf_op jit(solution)/shard_map/pallas_call | solution.py:250
  321.3 2.5 collective-permute-done.36.refs_1_
  327.6 2.2 shard_map.111
  331.9 5.1 %collective-permute-done.39.refs_0_ = bf16[96,2048]{1,0:T(8,128)(2,1)S(1)} collective-permute-done((bf16[96,2048]{1,0:T(8,128)(2,1)S(1)}, bf16[96,2048]{1,0:T(8,128)(2,1)S(1)}, u32[]{:S(2)}, u32[]{:S(2)}) %collective-permute-start.39) | collective-permute-done | bytes 393248 | tf_op jit(solution)/shard_map/ppermute | solution.py:160
  337.0 4.9 collective-permute-done.40.refs_1_
  342.0 6.6 %shard_map.112 = (bf16[96,512]{1,0:T(8,128)(2,1)S(1)}, bf16[96,2048]{1,0:T(8,128)(2,1)S(1)}) custom-call(s32[11,6]{1,0:T(8,128)S(1)} %concatenate.26.meta, s32[4]{0:T(128)S(1)} %pad_add_fusion.3.where, bf16[96,2048]{1,0:T(8,128)(2,1)S(1)} %collective-permute-done.39.refs_0_, bf16[96,2048]{1,0:T(8,128)(2,1)S(1)} %collective-permute-done.40.refs_1_, ...), custom_call_target="tpu_custom_call" | custom-call | tf_op jit(solution)/shard_map/pallas_call | solution.py:250
  351.7 2.6 collective-permute-done.41.refs_1_
  358.2 2.2 shard_map.113
  362.4 5.3 %collective-permute-done.44.refs_0_ = bf16[96,2048]{1,0:T(8,128)(2,1)S(1)} collective-permute-done((bf16[96,2048]{1,0:T(8,128)(2,1)S(1)}, bf16[96,2048]{1,0:T(8,128)(2,1)S(1)}, u32[]{:S(2)}, u32[]{:S(2)}) %collective-permute-start.44) | collective-permute-done | bytes 393248 | tf_op jit(solution)/shard_map/ppermute | solution.py:160
  367.6 5.0 collective-permute-done.45.refs_1_
  372.6 7.3 %shard_map.114 = (bf16[96,512]{1,0:T(8,128)(2,1)}, bf16[96,2048]{1,0:T(8,128)(2,1)S(1)}) custom-call(s32[11,6]{1,0:T(8,128)S(1)} %concatenate.26.meta, s32[4]{0:T(128)S(1)} %pad_add_fusion.3.where, bf16[96,2048]{1,0:T(8,128)(2,1)S(1)} %collective-permute-done.44.refs_0_, bf16[96,2048]{1,0:T(8,128)(2,1)S(1)} %collective-permute-done.45.refs_1_, ...), custom_call_target="tpu_custom_call" | custom-call | tf_op jit(solution)/shard_map/pallas_call | solution.py:250
  383.7 2.9 collective-permute-done.46.refs_1_
  390.3 3.4 copy-done
  394.7 2.7 shard_map.115
  399.4 5.3 %collective-permute-done.49.refs_0_ = bf16[96,2048]{1,0:T(8,128)(2,1)S(1)} collective-permute-done((bf16[96,2048]{1,0:T(8,128)(2,1)S(1)}, bf16[96,2048]{1,0:T(8,128)(2,1)S(1)}, u32[]{:S(2)}, u32[]{:S(2)}) %collective-permute-start.49) | collective-permute-done | bytes 393248 | tf_op jit(solution)/shard_map/ppermute | solution.py:160
  404.7 4.9 collective-permute-done.50.refs_1_
  409.6 6.6 %shard_map.116 = (bf16[96,512]{1,0:T(8,128)(2,1)S(1)}, bf16[96,2048]{1,0:T(8,128)(2,1)S(1)}) custom-call(s32[11,6]{1,0:T(8,128)S(1)} %concatenate.26.meta, s32[4]{0:T(128)S(1)} %pad_add_fusion.3.where, bf16[96,2048]{1,0:T(8,128)(2,1)S(1)} %collective-permute-done.49.refs_0_, bf16[96,2048]{1,0:T(8,128)(2,1)S(1)} %collective-permute-done.50.refs_1_, ...), custom_call_target="tpu_custom_call" | custom-call | tf_op jit(solution)/shard_map/pallas_call | solution.py:250
  419.4 2.6 collective-permute-done.51.refs_1_
  425.6 2.2 shard_map.117
  427.9 2.2 collective-permute-start.55
  430.0 5.0 %collective-permute-done.54.refs_0_ = bf16[96,2048]{1,0:T(8,128)(2,1)S(1)} collective-permute-done((bf16[96,2048]{1,0:T(8,128)(2,1)S(1)}, bf16[96,2048]{1,0:T(8,128)(2,1)S(1)}, u32[]{:S(2)}, u32[]{:S(2)}) %collective-permute-start.54) | collective-permute-done | bytes 393248 | tf_op jit(solution)/shard_map/ppermute | solution.py:160
  435.1 5.0 collective-permute-done.55.refs_1_
  440.0 6.6 %shard_map.118 = (bf16[96,512]{1,0:T(8,128)(2,1)S(1)}, bf16[96,2048]{1,0:T(8,128)(2,1)S(1)}) custom-call(s32[11,6]{1,0:T(8,128)S(1)} %concatenate.26.meta, s32[4]{0:T(128)S(1)} %pad_add_fusion.3.where, bf16[96,2048]{1,0:T(8,128)(2,1)S(1)} %collective-permute-done.54.refs_0_, bf16[96,2048]{1,0:T(8,128)(2,1)S(1)} %collective-permute-done.55.refs_1_, ...), custom_call_target="tpu_custom_call" | custom-call | tf_op jit(solution)/shard_map/pallas_call | solution.py:250
  449.8 2.6 collective-permute-done.56.refs_1_
  456.3 2.2 shard_map.119
  460.5 5.3 %collective-permute-done.59.refs_0_ = bf16[96,2048]{1,0:T(8,128)(2,1)S(1)} collective-permute-done((bf16[96,2048]{1,0:T(8,128)(2,1)S(1)}, bf16[96,2048]{1,0:T(8,128)(2,1)S(1)}, u32[]{:S(2)}, u32[]{:S(2)}) %collective-permute-start.59) | collective-permute-done | bytes 393248 | tf_op jit(solution)/shard_map/ppermute | solution.py:160
  465.8 4.8 collective-permute-done.60.refs_1_
  470.6 6.6 %shard_map.120 = (bf16[96,512]{1,0:T(8,128)(2,1)S(1)}, bf16[96,2048]{1,0:T(8,128)(2,1)S(1)}) custom-call(s32[11,6]{1,0:T(8,128)S(1)} %concatenate.26.meta, s32[4]{0:T(128)S(1)} %pad_add_fusion.3.where, bf16[96,2048]{1,0:T(8,128)(2,1)S(1)} %collective-permute-done.59.refs_0_, bf16[96,2048]{1,0:T(8,128)(2,1)S(1)} %collective-permute-done.60.refs_1_, ...), custom_call_target="tpu_custom_call" | custom-call | tf_op jit(solution)/shard_map/pallas_call | solution.py:250
  480.4 2.5 collective-permute-done.61
  486.7 3.0 shard_map.121
  494.9 4.6 collective-permute-done.67
  (198 shorter events, 128.7 us)
Async XLA Ops:
  1.5 18.6 %collective-permute-start = (s32[2,2,33]{2,1,0:T(2,128)S(1)}, s32[2,2,33]{2,1,0:T(2,128)S(1)}, u32[]{:S(2)}, u32[]{:S(2)}) collective-permute-start(s32[2,2,33]{2,1,0:T(2,128)S(1)} %pad_add_fusion.1), channel_id=1, source_target_pairs={{0,1},{1,2},{2,3},{3,0},{4,5},{5,6},{6,7},{7,4},{8,9},{9,10},{10,1... | collective-permute-start | bytes 1592 | tf_op jit(solution)/shard_map/ppermute | solution.py:160
  4.6 15.6 %collective-permute-start.1 = (s32[2,2,33]{2,1,0:T(2,128)S(1)}, s32[2,2,33]{2,1,0:T(2,128)S(1)}, u32[]{:S(2)}, u32[]{:S(2)}) collective-permute-start(s32[2,2,33]{2,1,0:T(2,128)S(1)} %pad_add_fusion.1), channel_id=1, source_target_pairs={{0,2},{1,3},{2,0},{3,1},{4,6},{5,7},{6,4},{7,5},{8,10},{9,11},{10,... | collective-permute-start | bytes 1592 | tf_op jit(solution)/shard_map/ppermute | solution.py:160
  7.1 13.0 %collective-permute-start.2 = (s32[2,2,33]{2,1,0:T(2,128)S(1)}, s32[2,2,33]{2,1,0:T(2,128)S(1)}, u32[]{:S(2)}, u32[]{:S(2)}) collective-permute-start(s32[2,2,33]{2,1,0:T(2,128)S(1)} %pad_add_fusion.1), channel_id=1, source_target_pairs={{0,3},{1,0},{2,1},{3,2},{4,7},{5,4},{6,5},{7,6},{8,11},{9,8},{10,9... | collective-permute-start | bytes 1592 | tf_op jit(solution)/shard_map/ppermute | solution.py:160
  20.5 69.4 %collective-permute-start.8 = (bf16[1024,1536]{1,0:T(8,128)(2,1)}, bf16[1024,1536]{1,0:T(8,128)(2,1)S(1)}, u32[]{:S(2)}, u32[]{:S(2)}) collective-permute-start(bf16[1024,1536]{1,0:T(8,128)(2,1)} %pad_maximum_fusion), channel_id=1, source_target_pairs={{0,1},{3,2},{4,5},{7,6},{8,9},{11,10},{12,13},{15,14},{16,17},{19,... | collective-permute-start | bytes 9437192 | tf_op jit(solution)/shard_map/ppermute | solution.py:160
  23.3 66.6 %collective-permute-start.9 = (bf16[1024,1536]{1,0:T(8,128)(2,1)}, bf16[1024,1536]{1,0:T(8,128)(2,1)}, u32[]{:S(2)}, u32[]{:S(2)}) collective-permute-start(bf16[1024,1536]{1,0:T(8,128)(2,1)} %pad_maximum_fusion.1), channel_id=1, source_target_pairs={{2,1},{1,2},{6,5},{5,6},{10,9},{9,10},{14,13},{13,14},{18,17},{17,... | collective-permute-start | bytes 9437192 | tf_op jit(solution)/shard_map/ppermute | solution.py:160
  41.0 56.0 %collective-permute-start.3 = (bf16[512,2048]{1,0:T(8,128)(2,1)S(1)}, bf16[512,2048]{1,0:T(8,128)(2,1)S(1)}, u32[]{:S(2)}, u32[]{:S(2)}) collective-permute-start(bf16[512,2048]{1,0:T(8,128)(2,1)S(1)} %select_select_fusion), channel_id=1, source_target_pairs={{9,1},{10,2},{13,5},{14,6}} | collective-permute-start | bytes 6291464 | tf_op jit(solution)/shard_map/ppermute | solution.py:160
  41.8 55.2 %collective-permute-start.4 = (bf16[512,2048]{1,0:T(8,128)(2,1)S(1)}, bf16[512,2048]{1,0:T(8,128)(2,1)S(1)}, u32[]{:S(2)}, u32[]{:S(2)}) collective-permute-start(bf16[512,2048]{1,0:T(8,128)(2,1)S(1)} %select_select_fusion), channel_id=1, source_target_pairs={{17,1},{18,2},{21,5},{22,6}} | collective-permute-start | bytes 6291464 | tf_op jit(solution)/shard_map/ppermute | solution.py:160
  42.6 54.4 %collective-permute-start.5 = (bf16[512,2048]{1,0:T(8,128)(2,1)S(1)}, bf16[512,2048]{1,0:T(8,128)(2,1)S(1)}, u32[]{:S(2)}, u32[]{:S(2)}) collective-permute-start(bf16[512,2048]{1,0:T(8,128)(2,1)S(1)} %select_select_fusion), channel_id=1, source_target_pairs={{25,1},{26,2},{29,5},{30,6}} | collective-permute-start | bytes 6291464 | tf_op jit(solution)/shard_map/ppermute | solution.py:160
  89.9 71.6 %collective-permute-start.10 = (bf16[1024,1536]{1,0:T(8,128)(2,1)}, bf16[1024,1536]{1,0:T(8,128)(2,1)}, u32[]{:S(2)}, u32[]{:S(2)}) collective-permute-start(bf16[1024,1536]{1,0:T(8,128)(2,1)} %pad_maximum_fusion.2), channel_id=1, source_target_pairs={{3,1},{0,2},{7,5},{4,6},{11,9},{8,10},{15,13},{12,14},{19,17},{16,... | collective-permute-start | bytes 9437192 | tf_op jit(solution)/shard_map/ppermute | solution.py:160
  99.1 8.8 %collective-permute-start.6 = (bf16[512,2048]{1,0:T(8,128)(2,1)}, bf16[512,2048]{1,0:T(8,128)(2,1)}, u32[]{:S(2)}, u32[]{:S(2)}) collective-permute-start(bf16[512,2048]{1,0:T(8,128)(2,1)} %add_add_fusion), channel_id=1, source_target_pairs={{1,5},{2,6},{5,1},{6,2}} | collective-permute-start | bytes 6291464 | tf_op jit(solution)/shard_map/ppermute | solution.py:160
  101.1 8.6 %collective-permute-start.7 = (bf16[16,2048]{1,0:T(8,128)(2,1)S(1)}, bf16[16,2048]{1,0:T(8,128)(2,1)S(1)}, u32[]{:S(2)}, u32[]{:S(2)}) collective-permute-start(bf16[16,2048]{1,0:T(8,128)(2,1)S(1)} %copy-done.4), channel_id=1, source_target_pairs={{1,5},{2,6},{5,1},{6,2}} | collective-permute-start | bytes 196616 | tf_op jit(solution)/shard_map/ppermute | solution.py:160
  168.4 4.7 collective-permute-start.11
  170.5 5.0 collective-permute-start.13
  177.6 7.3 %collective-permute-start.14 = (bf16[96,2048]{1,0:T(8,128)(2,1)S(1)}, bf16[96,2048]{1,0:T(8,128)(2,1)S(1)}, u32[]{:S(2)}, u32[]{:S(2)}) collective-permute-start(bf16[96,2048]{1,0:T(8,128)(2,1)S(1)} %shard_map.101), channel_id=1, source_target_pairs={{0,8},{1,9},{2,10},{3,11},{4,12},{5,13},{6,14},{7,15},{8,16},{9,17... | collective-permute-start | bytes 1179656 | tf_op jit(solution)/shard_map/ppermute | solution.py:160
  177.7 12.5 %collective-permute-start.15 = (bf16[96,2048]{1,0:T(8,128)(2,1)S(1)}, bf16[96,2048]{1,0:T(8,128)(2,1)S(1)}, u32[]{:S(2)}, u32[]{:S(2)}) collective-permute-start(bf16[96,2048]{1,0:T(8,128)(2,1)S(1)} %shard_map.101), channel_id=1, source_target_pairs={{0,12},{1,13},{2,14},{3,15},{4,8},{5,9},{6,10},{7,11},{8,20},{9,21... | collective-permute-start | bytes 1179656 | tf_op jit(solution)/shard_map/ppermute | solution.py:160
  196.8 5.7 %collective-permute-start.16 = (bf16[96,512]{1,0:T(8,128)(2,1)S(1)}, bf16[96,512]{1,0:T(8,128)(2,1)S(1)}, u32[]{:S(2)}, u32[]{:S(2)}) collective-permute-start(bf16[96,512]{1,0:T(8,128)(2,1)S(1)} %get-tuple-element.56.refs_0_), channel_id=1, source_target_pairs={{0,16},{1,5},{2,6},{3,19},{4,20},{5,1},{6,2},{7,23},{8,24},{9,13},... | collective-permute-start | bytes 294920 | tf_op jit(solution)/shard_map/ppermute | solution.py:160
  197.9 6.7 %collective-permute-start.17 = (bf16[96,512]{1,0:T(8,128)(2,1)S(1)}, bf16[96,512]{1,0:T(8,128)(2,1)S(1)}, u32[]{:S(2)}, u32[]{:S(2)}) collective-permute-start(bf16[96,512]{1,0:T(8,128)(2,1)S(1)} %get-tuple-element.56.refs_0_), channel_id=1, source_target_pairs={{0,16},{1,2},{2,1},{3,19},{4,20},{5,6},{6,5},{7,23},{8,24},{9,10},... | collective-permute-start | bytes 294920 | tf_op jit(solution)/shard_map/ppermute | solution.py:160
  198.9 7.0 %collective-permute-start.18 = (bf16[96,512]{1,0:T(8,128)(2,1)S(1)}, bf16[96,512]{1,0:T(8,128)(2,1)S(1)}, u32[]{:S(2)}, u32[]{:S(2)}) collective-permute-start(bf16[96,512]{1,0:T(8,128)(2,1)S(1)} %get-tuple-element.56.refs_0_), channel_id=1, source_target_pairs={{0,16},{1,6},{2,5},{3,19},{4,20},{5,2},{6,1},{7,23},{8,24},{9,14},... | collective-permute-start | bytes 294920 | tf_op jit(solution)/shard_map/ppermute | solution.py:160
  208.0 7.3 %collective-permute-start.19 = (bf16[96,2048]{1,0:T(8,128)(2,1)S(1)}, bf16[96,2048]{1,0:T(8,128)(2,1)S(1)}, u32[]{:S(2)}, u32[]{:S(2)}) collective-permute-start(bf16[96,2048]{1,0:T(8,128)(2,1)S(1)} %shard_map.103), channel_id=1, source_target_pairs={{0,8},{1,9},{2,10},{3,11},{4,12},{5,13},{6,14},{7,15},{8,16},{9,17... | collective-permute-start | bytes 1179656 | tf_op jit(solution)/shard_map/ppermute | solution.py:160
  208.1 12.2 %collective-permute-start.20 = (bf16[96,2048]{1,0:T(8,128)(2,1)S(1)}, bf16[96,2048]{1,0:T(8,128)(2,1)S(1)}, u32[]{:S(2)}, u32[]{:S(2)}) collective-permute-start(bf16[96,2048]{1,0:T(8,128)(2,1)S(1)} %shard_map.103), channel_id=1, source_target_pairs={{0,12},{1,13},{2,14},{3,15},{4,8},{5,9},{6,10},{7,11},{8,20},{9,21... | collective-permute-start | bytes 1179656 | tf_op jit(solution)/shard_map/ppermute | solution.py:160
  226.9 5.7 %collective-permute-start.21 = (bf16[96,512]{1,0:T(8,128)(2,1)S(1)}, bf16[96,512]{1,0:T(8,128)(2,1)S(1)}, u32[]{:S(2)}, u32[]{:S(2)}) collective-permute-start(bf16[96,512]{1,0:T(8,128)(2,1)S(1)} %get-tuple-element.58.refs_0_), channel_id=1, source_target_pairs={{0,16},{1,5},{2,6},{3,19},{4,20},{5,1},{6,2},{7,23},{8,24},{9,13},... | collective-permute-start | bytes 294920 | tf_op jit(solution)/shard_map/ppermute | solution.py:160
  228.1 6.6 %collective-permute-start.22 = (bf16[96,512]{1,0:T(8,128)(2,1)S(1)}, bf16[96,512]{1,0:T(8,128)(2,1)S(1)}, u32[]{:S(2)}, u32[]{:S(2)}) collective-permute-start(bf16[96,512]{1,0:T(8,128)(2,1)S(1)} %get-tuple-element.58.refs_0_), channel_id=1, source_target_pairs={{0,16},{1,2},{2,1},{3,19},{4,20},{5,6},{6,5},{7,23},{8,24},{9,10},... | collective-permute-start | bytes 294920 | tf_op jit(solution)/shard_map/ppermute | solution.py:160
  229.0 7.2 %collective-permute-start.23 = (bf16[96,512]{1,0:T(8,128)(2,1)S(1)}, bf16[96,512]{1,0:T(8,128)(2,1)S(1)}, u32[]{:S(2)}, u32[]{:S(2)}) collective-permute-start(bf16[96,512]{1,0:T(8,128)(2,1)S(1)} %get-tuple-element.58.refs_0_), channel_id=1, source_target_pairs={{0,16},{1,6},{2,5},{3,19},{4,20},{5,2},{6,1},{7,23},{8,24},{9,14},... | collective-permute-start | bytes 294920 | tf_op jit(solution)/shard_map/ppermute | solution.py:160
  238.4 7.3 %collective-permute-start.24 = (bf16[96,2048]{1,0:T(8,128)(2,1)S(1)}, bf16[96,2048]{1,0:T(8,128)(2,1)S(1)}, u32[]{:S(2)}, u32[]{:S(2)}) collective-permute-start(bf16[96,2048]{1,0:T(8,128)(2,1)S(1)} %shard_map.105), channel_id=1, source_target_pairs={{0,8},{1,9},{2,10},{3,11},{4,12},{5,13},{6,14},{7,15},{8,16},{9,17... | collective-permute-start | bytes 1179656 | tf_op jit(solution)/shard_map/ppermute | solution.py:160
  238.4 12.3 %collective-permute-start.25 = (bf16[96,2048]{1,0:T(8,128)(2,1)S(1)}, bf16[96,2048]{1,0:T(8,128)(2,1)S(1)}, u32[]{:S(2)}, u32[]{:S(2)}) collective-permute-start(bf16[96,2048]{1,0:T(8,128)(2,1)S(1)} %shard_map.105), channel_id=1, source_target_pairs={{0,12},{1,13},{2,14},{3,15},{4,8},{5,9},{6,10},{7,11},{8,20},{9,21... | collective-permute-start | bytes 1179656 | tf_op jit(solution)/shard_map/ppermute | solution.py:160
  257.4 5.7 %collective-permute-start.26 = (bf16[96,512]{1,0:T(8,128)(2,1)S(1)}, bf16[96,512]{1,0:T(8,128)(2,1)S(1)}, u32[]{:S(2)}, u32[]{:S(2)}) collective-permute-start(bf16[96,512]{1,0:T(8,128)(2,1)S(1)} %get-tuple-element.60.refs_0_), channel_id=1, source_target_pairs={{0,16},{1,5},{2,6},{3,19},{4,20},{5,1},{6,2},{7,23},{8,24},{9,13},... | collective-permute-start | bytes 294920 | tf_op jit(solution)/shard_map/ppermute | solution.py:160
  258.3 6.9 %collective-permute-start.27 = (bf16[96,512]{1,0:T(8,128)(2,1)S(1)}, bf16[96,512]{1,0:T(8,128)(2,1)S(1)}, u32[]{:S(2)}, u32[]{:S(2)}) collective-permute-start(bf16[96,512]{1,0:T(8,128)(2,1)S(1)} %get-tuple-element.60.refs_0_), channel_id=1, source_target_pairs={{0,16},{1,2},{2,1},{3,19},{4,20},{5,6},{6,5},{7,23},{8,24},{9,10},... | collective-permute-start | bytes 294920 | tf_op jit(solution)/shard_map/ppermute | solution.py:160
  259.5 7.2 %collective-permute-start.28 = (bf16[96,512]{1,0:T(8,128)(2,1)S(1)}, bf16[96,512]{1,0:T(8,128)(2,1)S(1)}, u32[]{:S(2)}, u32[]{:S(2)}) collective-permute-start(bf16[96,512]{1,0:T(8,128)(2,1)S(1)} %get-tuple-element.60.refs_0_), channel_id=1, source_target_pairs={{0,16},{1,6},{2,5},{3,19},{4,20},{5,2},{6,1},{7,23},{8,24},{9,14},... | collective-permute-start | bytes 294920 | tf_op jit(solution)/shard_map/ppermute | solution.py:160
  268.9 7.3 %collective-permute-start.29 = (bf16[96,2048]{1,0:T(8,128)(2,1)S(1)}, bf16[96,2048]{1,0:T(8,128)(2,1)S(1)}, u32[]{:S(2)}, u32[]{:S(2)}) collective-permute-start(bf16[96,2048]{1,0:T(8,128)(2,1)S(1)} %shard_map.107), channel_id=1, source_target_pairs={{0,8},{1,9},{2,10},{3,11},{4,12},{5,13},{6,14},{7,15},{8,16},{9,17... | collective-permute-start | bytes 1179656 | tf_op jit(solution)/shard_map/ppermute | solution.py:160
  269.0 12.2 %collective-permute-start.30 = (bf16[96,2048]{1,0:T(8,128)(2,1)S(1)}, bf16[96,2048]{1,0:T(8,128)(2,1)S(1)}, u32[]{:S(2)}, u32[]{:S(2)}) collective-permute-start(bf16[96,2048]{1,0:T(8,128)(2,1)S(1)} %shard_map.107), channel_id=1, source_target_pairs={{0,12},{1,13},{2,14},{3,15},{4,8},{5,9},{6,10},{7,11},{8,20},{9,21... | collective-permute-start | bytes 1179656 | tf_op jit(solution)/shard_map/ppermute | solution.py:160
  287.8 5.7 %collective-permute-start.31 = (bf16[96,512]{1,0:T(8,128)(2,1)S(1)}, bf16[96,512]{1,0:T(8,128)(2,1)S(1)}, u32[]{:S(2)}, u32[]{:S(2)}) collective-permute-start(bf16[96,512]{1,0:T(8,128)(2,1)S(1)} %get-tuple-element.62.refs_0_), channel_id=1, source_target_pairs={{0,16},{1,5},{2,6},{3,19},{4,20},{5,1},{6,2},{7,23},{8,24},{9,13},... | collective-permute-start | bytes 294920 | tf_op jit(solution)/shard_map/ppermute | solution.py:160
  288.8 6.8 %collective-permute-start.32 = (bf16[96,512]{1,0:T(8,128)(2,1)S(1)}, bf16[96,512]{1,0:T(8,128)(2,1)S(1)}, u32[]{:S(2)}, u32[]{:S(2)}) collective-permute-start(bf16[96,512]{1,0:T(8,128)(2,1)S(1)} %get-tuple-element.62.refs_0_), channel_id=1, source_target_pairs={{0,16},{1,2},{2,1},{3,19},{4,20},{5,6},{6,5},{7,23},{8,24},{9,10},... | collective-permute-start | bytes 294920 | tf_op jit(solution)/shard_map/ppermute | solution.py:160
  289.9 7.2 %collective-permute-start.33 = (bf16[96,512]{1,0:T(8,128)(2,1)S(1)}, bf16[96,512]{1,0:T(8,128)(2,1)S(1)}, u32[]{:S(2)}, u32[]{:S(2)}) collective-permute-start(bf16[96,512]{1,0:T(8,128)(2,1)S(1)} %get-tuple-element.62.refs_0_), channel_id=1, source_target_pairs={{0,16},{1,6},{2,5},{3,19},{4,20},{5,2},{6,1},{7,23},{8,24},{9,14},... | collective-permute-start | bytes 294920 | tf_op jit(solution)/shard_map/ppermute | solution.py:160
  299.3 7.3 %collective-permute-start.34 = (bf16[96,2048]{1,0:T(8,128)(2,1)S(1)}, bf16[96,2048]{1,0:T(8,128)(2,1)S(1)}, u32[]{:S(2)}, u32[]{:S(2)}) collective-permute-start(bf16[96,2048]{1,0:T(8,128)(2,1)S(1)} %get-tuple-element.65), channel_id=1, source_target_pairs={{0,8},{1,9},{2,10},{3,11},{4,12},{5,13},{6,14},{7,15},{8,16},{9,17... | collective-permute-start | bytes 1179656 | tf_op jit(solution)/shard_map/ppermute | solution.py:160
  299.4 12.1 %collective-permute-start.35 = (bf16[96,2048]{1,0:T(8,128)(2,1)S(1)}, bf16[96,2048]{1,0:T(8,128)(2,1)S(1)}, u32[]{:S(2)}, u32[]{:S(2)}) collective-permute-start(bf16[96,2048]{1,0:T(8,128)(2,1)S(1)} %get-tuple-element.65), channel_id=1, source_target_pairs={{0,12},{1,13},{2,14},{3,15},{4,8},{5,9},{6,10},{7,11},{8,20},{9,21... | collective-permute-start | bytes 1179656 | tf_op jit(solution)/shard_map/ppermute | solution.py:160
  318.2 5.7 %collective-permute-start.36 = (bf16[96,512]{1,0:T(8,128)(2,1)S(1)}, bf16[96,512]{1,0:T(8,128)(2,1)S(1)}, u32[]{:S(2)}, u32[]{:S(2)}) collective-permute-start(bf16[96,512]{1,0:T(8,128)(2,1)S(1)} %get-tuple-element.66.refs_0_), channel_id=1, source_target_pairs={{0,16},{1,5},{2,6},{3,19},{4,20},{5,1},{6,2},{7,23},{8,24},{9,13},... | collective-permute-start | bytes 294920 | tf_op jit(solution)/shard_map/ppermute | solution.py:160
  319.3 6.7 %collective-permute-start.37 = (bf16[96,512]{1,0:T(8,128)(2,1)S(1)}, bf16[96,512]{1,0:T(8,128)(2,1)S(1)}, u32[]{:S(2)}, u32[]{:S(2)}) collective-permute-start(bf16[96,512]{1,0:T(8,128)(2,1)S(1)} %get-tuple-element.66.refs_0_), channel_id=1, source_target_pairs={{0,16},{1,2},{2,1},{3,19},{4,20},{5,6},{6,5},{7,23},{8,24},{9,10},... | collective-permute-start | bytes 294920 | tf_op jit(solution)/shard_map/ppermute | solution.py:160
  320.3 7.3 %collective-permute-start.38 = (bf16[96,512]{1,0:T(8,128)(2,1)S(1)}, bf16[96,512]{1,0:T(8,128)(2,1)S(1)}, u32[]{:S(2)}, u32[]{:S(2)}) collective-permute-start(bf16[96,512]{1,0:T(8,128)(2,1)S(1)} %get-tuple-element.66.refs_0_), channel_id=1, source_target_pairs={{0,16},{1,6},{2,5},{3,19},{4,20},{5,2},{6,1},{7,23},{8,24},{9,14},... | collective-permute-start | bytes 294920 | tf_op jit(solution)/shard_map/ppermute | solution.py:160
  329.8 7.3 %collective-permute-start.39 = (bf16[96,2048]{1,0:T(8,128)(2,1)S(1)}, bf16[96,2048]{1,0:T(8,128)(2,1)S(1)}, u32[]{:S(2)}, u32[]{:S(2)}) collective-permute-start(bf16[96,2048]{1,0:T(8,128)(2,1)S(1)} %get-tuple-element.69), channel_id=1, source_target_pairs={{0,8},{1,9},{2,10},{3,11},{4,12},{5,13},{6,14},{7,15},{8,16},{9,17... | collective-permute-start | bytes 1179656 | tf_op jit(solution)/shard_map/ppermute | solution.py:160
  329.9 12.1 %collective-permute-start.40 = (bf16[96,2048]{1,0:T(8,128)(2,1)S(1)}, bf16[96,2048]{1,0:T(8,128)(2,1)S(1)}, u32[]{:S(2)}, u32[]{:S(2)}) collective-permute-start(bf16[96,2048]{1,0:T(8,128)(2,1)S(1)} %get-tuple-element.69), channel_id=1, source_target_pairs={{0,12},{1,13},{2,14},{3,15},{4,8},{5,9},{6,10},{7,11},{8,20},{9,21... | collective-permute-start | bytes 1179656 | tf_op jit(solution)/shard_map/ppermute | solution.py:160
  348.6 5.6 %collective-permute-start.41 = (bf16[96,512]{1,0:T(8,128)(2,1)S(1)}, bf16[96,512]{1,0:T(8,128)(2,1)S(1)}, u32[]{:S(2)}, u32[]{:S(2)}) collective-permute-start(bf16[96,512]{1,0:T(8,128)(2,1)S(1)} %get-tuple-element.70.refs_0_), channel_id=1, source_target_pairs={{0,16},{1,5},{2,6},{3,19},{4,20},{5,1},{6,2},{7,23},{8,24},{9,13},... | collective-permute-start | bytes 294920 | tf_op jit(solution)/shard_map/ppermute | solution.py:160
  349.7 6.7 %collective-permute-start.42 = (bf16[96,512]{1,0:T(8,128)(2,1)S(1)}, bf16[96,512]{1,0:T(8,128)(2,1)S(1)}, u32[]{:S(2)}, u32[]{:S(2)}) collective-permute-start(bf16[96,512]{1,0:T(8,128)(2,1)S(1)} %get-tuple-element.70.refs_0_), channel_id=1, source_target_pairs={{0,16},{1,2},{2,1},{3,19},{4,20},{5,6},{6,5},{7,23},{8,24},{9,10},... | collective-permute-start | bytes 294920 | tf_op jit(solution)/shard_map/ppermute | solution.py:160
  350.7 7.4 %collective-permute-start.43 = (bf16[96,512]{1,0:T(8,128)(2,1)S(1)}, bf16[96,512]{1,0:T(8,128)(2,1)S(1)}, u32[]{:S(2)}, u32[]{:S(2)}) collective-permute-start(bf16[96,512]{1,0:T(8,128)(2,1)S(1)} %get-tuple-element.70.refs_0_), channel_id=1, source_target_pairs={{0,16},{1,6},{2,5},{3,19},{4,20},{5,2},{6,1},{7,23},{8,24},{9,14},... | collective-permute-start | bytes 294920 | tf_op jit(solution)/shard_map/ppermute | solution.py:160
  360.4 7.3 %collective-permute-start.44 = (bf16[96,2048]{1,0:T(8,128)(2,1)S(1)}, bf16[96,2048]{1,0:T(8,128)(2,1)S(1)}, u32[]{:S(2)}, u32[]{:S(2)}) collective-permute-start(bf16[96,2048]{1,0:T(8,128)(2,1)S(1)} %get-tuple-element.73), channel_id=1, source_target_pairs={{0,8},{1,9},{2,10},{3,11},{4,12},{5,13},{6,14},{7,15},{8,16},{9,17... | collective-permute-start | bytes 1179656 | tf_op jit(solution)/shard_map/ppermute | solution.py:160
  360.4 12.2 %collective-permute-start.45 = (bf16[96,2048]{1,0:T(8,128)(2,1)S(1)}, bf16[96,2048]{1,0:T(8,128)(2,1)S(1)}, u32[]{:S(2)}, u32[]{:S(2)}) collective-permute-start(bf16[96,2048]{1,0:T(8,128)(2,1)S(1)} %get-tuple-element.73), channel_id=1, source_target_pairs={{0,12},{1,13},{2,14},{3,15},{4,8},{5,9},{6,10},{7,11},{8,20},{9,21... | collective-permute-start | bytes 1179656 | tf_op jit(solution)/shard_map/ppermute | solution.py:160
  380.6 5.9 %collective-permute-start.46 = (bf16[96,512]{1,0:T(8,128)(2,1)}, bf16[96,512]{1,0:T(8,128)(2,1)}, u32[]{:S(2)}, u32[]{:S(2)}) collective-permute-start(bf16[96,512]{1,0:T(8,128)(2,1)} %get-tuple-element.74.refs_0_), channel_id=1, source_target_pairs={{0,16},{1,5},{2,6},{3,19},{4,20},{5,1},{6,2},{7,23},{8,24},{9,13},... | collective-permute-start | bytes 294920 | tf_op jit(solution)/shard_map/ppermute | solution.py:160
  381.6 7.0 %collective-permute-start.47 = (bf16[96,512]{1,0:T(8,128)(2,1)}, bf16[96,512]{1,0:T(8,128)(2,1)}, u32[]{:S(2)}, u32[]{:S(2)}) collective-permute-start(bf16[96,512]{1,0:T(8,128)(2,1)} %get-tuple-element.74.refs_0_), channel_id=1, source_target_pairs={{0,16},{1,2},{2,1},{3,19},{4,20},{5,6},{6,5},{7,23},{8,24},{9,10},... | collective-permute-start | bytes 294920 | tf_op jit(solution)/shard_map/ppermute | solution.py:160
  382.6 7.7 %collective-permute-start.48 = (bf16[96,512]{1,0:T(8,128)(2,1)}, bf16[96,512]{1,0:T(8,128)(2,1)}, u32[]{:S(2)}, u32[]{:S(2)}) collective-permute-start(bf16[96,512]{1,0:T(8,128)(2,1)} %get-tuple-element.74.refs_0_), channel_id=1, source_target_pairs={{0,16},{1,6},{2,5},{3,19},{4,20},{5,2},{6,1},{7,23},{8,24},{9,14},... | collective-permute-start | bytes 294920 | tf_op jit(solution)/shard_map/ppermute | solution.py:160
  397.4 7.3 %collective-permute-start.49 = (bf16[96,2048]{1,0:T(8,128)(2,1)S(1)}, bf16[96,2048]{1,0:T(8,128)(2,1)S(1)}, u32[]{:S(2)}, u32[]{:S(2)}) collective-permute-start(bf16[96,2048]{1,0:T(8,128)(2,1)S(1)} %get-tuple-element.77), channel_id=1, source_target_pairs={{0,8},{1,9},{2,10},{3,11},{4,12},{5,13},{6,14},{7,15},{8,16},{9,17... | collective-permute-start | bytes 1179656 | tf_op jit(solution)/shard_map/ppermute | solution.py:160
  397.5 12.1 %collective-permute-start.50 = (bf16[96,2048]{1,0:T(8,128)(2,1)S(1)}, bf16[96,2048]{1,0:T(8,128)(2,1)S(1)}, u32[]{:S(2)}, u32[]{:S(2)}) collective-permute-start(bf16[96,2048]{1,0:T(8,128)(2,1)S(1)} %get-tuple-element.77), channel_id=1, source_target_pairs={{0,12},{1,13},{2,14},{3,15},{4,8},{5,9},{6,10},{7,11},{8,20},{9,21... | collective-permute-start | bytes 1179656 | tf_op jit(solution)/shard_map/ppermute | solution.py:160
  416.2 5.7 %collective-permute-start.51 = (bf16[96,512]{1,0:T(8,128)(2,1)S(1)}, bf16[96,512]{1,0:T(8,128)(2,1)S(1)}, u32[]{:S(2)}, u32[]{:S(2)}) collective-permute-start(bf16[96,512]{1,0:T(8,128)(2,1)S(1)} %get-tuple-element.78.refs_0_), channel_id=1, source_target_pairs={{0,16},{1,5},{2,6},{3,19},{4,20},{5,1},{6,2},{7,23},{8,24},{9,13},... | collective-permute-start | bytes 294920 | tf_op jit(solution)/shard_map/ppermute | solution.py:160
  417.3 6.7 %collective-permute-start.52 = (bf16[96,512]{1,0:T(8,128)(2,1)S(1)}, bf16[96,512]{1,0:T(8,128)(2,1)S(1)}, u32[]{:S(2)}, u32[]{:S(2)}) collective-permute-start(bf16[96,512]{1,0:T(8,128)(2,1)S(1)} %get-tuple-element.78.refs_0_), channel_id=1, source_target_pairs={{0,16},{1,2},{2,1},{3,19},{4,20},{5,6},{6,5},{7,23},{8,24},{9,10},... | collective-permute-start | bytes 294920 | tf_op jit(solution)/shard_map/ppermute | solution.py:160
  418.4 7.2 %collective-permute-start.53 = (bf16[96,512]{1,0:T(8,128)(2,1)S(1)}, bf16[96,512]{1,0:T(8,128)(2,1)S(1)}, u32[]{:S(2)}, u32[]{:S(2)}) collective-permute-start(bf16[96,512]{1,0:T(8,128)(2,1)S(1)} %get-tuple-element.78.refs_0_), channel_id=1, source_target_pairs={{0,16},{1,6},{2,5},{3,19},{4,20},{5,2},{6,1},{7,23},{8,24},{9,14},... | collective-permute-start | bytes 294920 | tf_op jit(solution)/shard_map/ppermute | solution.py:160
  427.8 7.3 %collective-permute-start.54 = (bf16[96,2048]{1,0:T(8,128)(2,1)S(1)}, bf16[96,2048]{1,0:T(8,128)(2,1)S(1)}, u32[]{:S(2)}, u32[]{:S(2)}) collective-permute-start(bf16[96,2048]{1,0:T(8,128)(2,1)S(1)} %get-tuple-element.81), channel_id=1, source_target_pairs={{0,8},{1,9},{2,10},{3,11},{4,12},{5,13},{6,14},{7,15},{8,16},{9,17... | collective-permute-start | bytes 1179656 | tf_op jit(solution)/shard_map/ppermute | solution.py:160
  427.9 12.1 %collective-permute-start.55 = (bf16[96,2048]{1,0:T(8,128)(2,1)S(1)}, bf16[96,2048]{1,0:T(8,128)(2,1)S(1)}, u32[]{:S(2)}, u32[]{:S(2)}) collective-permute-start(bf16[96,2048]{1,0:T(8,128)(2,1)S(1)} %get-tuple-element.81), channel_id=1, source_target_pairs={{0,12},{1,13},{2,14},{3,15},{4,8},{5,9},{6,10},{7,11},{8,20},{9,21... | collective-permute-start | bytes 1179656 | tf_op jit(solution)/shard_map/ppermute | solution.py:160
  446.7 5.7 %collective-permute-start.56 = (bf16[96,512]{1,0:T(8,128)(2,1)S(1)}, bf16[96,512]{1,0:T(8,128)(2,1)S(1)}, u32[]{:S(2)}, u32[]{:S(2)}) collective-permute-start(bf16[96,512]{1,0:T(8,128)(2,1)S(1)} %get-tuple-element.82.refs_0_), channel_id=1, source_target_pairs={{0,16},{1,5},{2,6},{3,19},{4,20},{5,1},{6,2},{7,23},{8,24},{9,13},... | collective-permute-start | bytes 294920 | tf_op jit(solution)/shard_map/ppermute | solution.py:160
  447.8 6.8 %collective-permute-start.57 = (bf16[96,512]{1,0:T(8,128)(2,1)S(1)}, bf16[96,512]{1,0:T(8,128)(2,1)S(1)}, u32[]{:S(2)}, u32[]{:S(2)}) collective-permute-start(bf16[96,512]{1,0:T(8,128)(2,1)S(1)} %get-tuple-element.82.refs_0_), channel_id=1, source_target_pairs={{0,16},{1,2},{2,1},{3,19},{4,20},{5,6},{6,5},{7,23},{8,24},{9,10},... | collective-permute-start | bytes 294920 | tf_op jit(solution)/shard_map/ppermute | solution.py:160
  448.8 7.6 %collective-permute-start.58 = (bf16[96,512]{1,0:T(8,128)(2,1)S(1)}, bf16[96,512]{1,0:T(8,128)(2,1)S(1)}, u32[]{:S(2)}, u32[]{:S(2)}) collective-permute-start(bf16[96,512]{1,0:T(8,128)(2,1)S(1)} %get-tuple-element.82.refs_0_), channel_id=1, source_target_pairs={{0,16},{1,6},{2,5},{3,19},{4,20},{5,2},{6,1},{7,23},{8,24},{9,14},... | collective-permute-start | bytes 294920 | tf_op jit(solution)/shard_map/ppermute | solution.py:160
  458.5 7.3 %collective-permute-start.59 = (bf16[96,2048]{1,0:T(8,128)(2,1)S(1)}, bf16[96,2048]{1,0:T(8,128)(2,1)S(1)}, u32[]{:S(2)}, u32[]{:S(2)}) collective-permute-start(bf16[96,2048]{1,0:T(8,128)(2,1)S(1)} %get-tuple-element.85), channel_id=1, source_target_pairs={{0,8},{1,9},{2,10},{3,11},{4,12},{5,13},{6,14},{7,15},{8,16},{9,17... | collective-permute-start | bytes 1179656 | tf_op jit(solution)/shard_map/ppermute | solution.py:160
  458.6 12.0 %collective-permute-start.60 = (bf16[96,2048]{1,0:T(8,128)(2,1)S(1)}, bf16[96,2048]{1,0:T(8,128)(2,1)S(1)}, u32[]{:S(2)}, u32[]{:S(2)}) collective-permute-start(bf16[96,2048]{1,0:T(8,128)(2,1)S(1)} %get-tuple-element.85), channel_id=1, source_target_pairs={{0,12},{1,13},{2,14},{3,15},{4,8},{5,9},{6,10},{7,11},{8,20},{9,21... | collective-permute-start | bytes 1179656 | tf_op jit(solution)/shard_map/ppermute | solution.py:160
  477.3 5.7 %collective-permute-start.61 = (bf16[96,512]{1,0:T(8,128)(2,1)S(1)}, bf16[96,512]{1,0:T(8,128)(2,1)S(1)}, u32[]{:S(2)}, u32[]{:S(2)}) collective-permute-start(bf16[96,512]{1,0:T(8,128)(2,1)S(1)} %get-tuple-element.86), channel_id=1, source_target_pairs={{0,16},{1,5},{2,6},{3,19},{4,20},{5,1},{6,2},{7,23},{8,24},{9,13},... | collective-permute-start | bytes 294920 | tf_op jit(solution)/shard_map/ppermute | solution.py:160
  478.4 6.6 %collective-permute-start.62 = (bf16[96,512]{1,0:T(8,128)(2,1)S(1)}, bf16[96,512]{1,0:T(8,128)(2,1)S(1)}, u32[]{:S(2)}, u32[]{:S(2)}) collective-permute-start(bf16[96,512]{1,0:T(8,128)(2,1)S(1)} %get-tuple-element.86), channel_id=1, source_target_pairs={{0,16},{1,2},{2,1},{3,19},{4,20},{5,6},{6,5},{7,23},{8,24},{9,10},... | collective-permute-start | bytes 294920 | tf_op jit(solution)/shard_map/ppermute | solution.py:160
  479.4 7.3 %collective-permute-start.63 = (bf16[96,512]{1,0:T(8,128)(2,1)S(1)}, bf16[96,512]{1,0:T(8,128)(2,1)S(1)}, u32[]{:S(2)}, u32[]{:S(2)}) collective-permute-start(bf16[96,512]{1,0:T(8,128)(2,1)S(1)} %get-tuple-element.86), channel_id=1, source_target_pairs={{0,16},{1,6},{2,5},{3,19},{4,20},{5,2},{6,1},{7,23},{8,24},{9,14},... | collective-permute-start | bytes 294920 | tf_op jit(solution)/shard_map/ppermute | solution.py:160
  489.8 5.0 collective-permute-start.65
  (29 other events, 798.8 us)

commit v7 on v6

--- a/solution.py
+++ b/solution.py
@@ -51,7 +51,8 @@
             ).astype(jnp.bfloat16)
         return 0
 
-    lax.fori_loop(0, docs, prepare, 0)
+    together = docs if docs <= 4 else 1
+    lax.fori_loop(0, docs, prepare, 0, unroll=together)
     for b in range(blocks):
         at = pl.multiple_of(where[b] * depth, 128)
         left = normed[:, pl.ds(at, depth)]
@@ -88,7 +89,16 @@
             ).astype(jnp.bfloat16)
         return 0
 
-    lax.fori_loop(0, docs, one, 0)
+    lax.fori_loop(0, docs, one, 0, unroll=together)
+
+
+def hold_kernel(count, *refs):
+    outs, sems = refs[count : 2 * count], refs[2 * count]
+    copies = [pltpu.make_async_copy(refs[b], outs[b], sems.at[b]) for b in range(count)]
+    for copy in copies:
+        copy.start()
+    for copy in copies:
+        copy.wait()
 
 
 def project_kernel(turn, docs, tokens, parts, pool, meta, place, mix, *refs):
@@ -207,10 +217,10 @@
             full = full + send(picked, [((a, b, c), (0, b, c)) for b in range(T) for c in planes])
         return full, send(full, [((0, b, c), (0, T - 1 - b, c)) for b in range(T) for c in planes])
 
-    ids, blocks = lax.optimization_barrier((ids, blocks))
+    blocks = [lax.optimization_barrier((block, ids))[0] for block in blocks]
     early = [relay(c, block) for c, block in zip(rounds[:-1], blocks[:-1])]
     last, early = lax.optimization_barrier((blocks[-1], early))
-    weights = [own_block] + early + [relay(rounds[-1], last)]
+    received = early + [relay(rounds[-1], last)]
     tok, tok_other = embed(jnp.concatenate([ids[:, seg] for seg in range(segs)]))
     mem_other = send(mem_init, [((0, b, c), (0, T - 1 - b, c)) for b in range(T) for c in planes])
 
@@ -239,6 +249,16 @@
     vmem = pl.BlockSpec(memory_space=pltpu.VMEM)
     out_proj = w_out[0]
     parts = len(shifts)
+
+    held = pl.pallas_call(
+        functools.partial(hold_kernel, len(received)),
+        out_shape=[jax.ShapeDtypeStruct(w.shape, w.dtype) for w in received],
+        in_specs=[pl.BlockSpec(memory_space=pl.ANY)] * len(received),
+        out_specs=[vmem] * len(received),
+        scratch_shapes=[pltpu.SemaphoreType.DMA((len(received),))],
+        compiler_params=params,
+    )(*received)
+    weights = [own_block, *held]
 
     own = jnp.zeros((R, half), jnp.bfloat16)
     other = jnp.zeros((R, half), jnp.bfloat16)
@@ -281,8 +301,10 @@
         if pool:
             pools.append(result[1])
         if k < turns - 1:
-            own = send(result[0], [(e, ((e[0] + 1) % S, e[1], e[2])) for e in everyone])
-            other = send(result[0], [(e, ((e[0] + 1) % S, T - 1 - e[1], e[2])) for e in everyone])
+            paired = S % 2 == 0 and k in (0, turns - 2)
+            after = [e[0] ^ 1 if paired else (e[0] + 1) % S for e in everyone]
+            own = send(result[0], [(e, (a, e[1], e[2])) for e, a in zip(everyone, after)])
+            other = send(result[0], [(e, (a, T - 1 - e[1], e[2])) for e, a in zip(everyone, after)])
 
     mine = lax.dynamic_slice_in_dim(jnp.stack(pools), s, S, 0).reshape(docs, half)
     total = mine

time: 508 us -> 477 us (0.939)
  Pallas kernels: 96.1 us -> 64.9 us
    pallas_call x11, Pallas kernels: 73.8 us -> 39.4 us  [body(): pl.pallas_call(functools.partial(attend_kernel, k, n, tokens, D), out_sha...]
  transfers between devices with their start and end apart: 68 -> 68, of which waited for: 58 -> 58; matrix products, arithmetic and copies ran while one was open for 7% -> 8% of each run, Pallas kernels for 0% -> 1%
where the time goes in v7:
time: 477 us; the launch traced here: 470 us
  waiting for transfers between devices  270 us (57%)
  starting transfers between devices  81.6 us (17%)
  Pallas kernels  64.9 us (14%)
  local copies, waits for them, and re-layouts  38 us (8%)
  other arithmetic  13.6 us (3%)
    ppermute x68, waiting for transfers between devices, send(): return lax.ppermute(block, AXES, [(lin(*a), lin(*b)) for a, b in pairs])  270 us
    ppermute x68, starting transfers between devices, send(): return lax.ppermute(block, AXES, [(lin(*a), lin(*b)) for a, b in pairs])  81.6 us
    pallas_call x11, Pallas kernels, body(): pl.pallas_call(functools.partial(attend_kernel, k, n, tokens, D), out_sha...  39.4 us
    pallas_call x10, Pallas kernels, body(): pl.pallas_call(functools.partial(project_kernel, k, n, tokens, parts, poo...  22.3 us
    gather x1, local copies, waits for them, and re-layouts, embed(): picked = jnp.take(emb_table, jnp.clip(local, 0, vocab - 1), axis=0)  13.2 us
    unnamed x74, local copies, waits for them, and re-layouts  9.65 us
  transfers between devices with their start and end apart: 68, of which 58 were waited for; matrix products, arithmetic and copies ran while one was open for 8% of the time, Pallas kernels for 1%

profile of v7, /device:TPU:0, one launch (start us, length us, event | category | flops | bytes accessed | tf_op | source)
XLA Modules:
  0.0 470.1 jit_solution(586077602050712872)
XLA Ops:
  1.5 3.0 collective-permute-start
  4.6 2.6 collective-permute-start.1
  8.5 4.0 dynamic-slice_bitcast_fusion.2
  12.5 2.6 dynamic-slice_bitcast_fusion
  19.3 2.8 collective-permute-start.8
  22.1 2.3 collective-permute-start.9
  24.5 13.2 %gather_fusion.1 = bf16[512,2048]{1,0:T(8,128)(2,1)} fusion(bf16[4096,2048]{1,0:T(8,128)(2,1)} %param.12, s32[1024]{0:T(1024)S(1)} %pad_clamp_fusion), kind=kCustom, calls=%fused_computation.1 | custom fusion | bytes 4196352 | tf_op jit(solution)/shard_map/jit(_take)/gather | solution.py:213
  44.0 44.7 %collective-permute-done.8.refs_0_ = bf16[1024,1536]{1,0:T(8,128)(2,1)S(1)} collective-permute-done((bf16[1024,1536]{1,0:T(8,128)(2,1)}, bf16[1024,1536]{1,0:T(8,128)(2,1)S(1)}, u32[]{:S(2)}, u32[]{:S(2)}) %collective-permute-start.8) | collective-permute-done | bytes 3145760 | tf_op jit(solution)/shard_map/ppermute | solution.py:170
  88.7 7.2 %collective-permute-start.10 = (bf16[1024,1536]{1,0:T(8,128)(2,1)}, bf16[1024,1536]{1,0:T(8,128)(2,1)}, u32[]{:S(2)}, u32[]{:S(2)}) collective-permute-start(bf16[1024,1536]{1,0:T(8,128)(2,1)} %pad_maximum_fusion.1), channel_id=1, source_target_pairs={{3,1},{0,2},{7,5},{4,6},{11,9},{8,10},{15,13},{12,14},{19,17},{16,... | collective-permute-start | bytes 9437192 | tf_op jit(solution)/shard_map/ppermute | solution.py:170
  108.6 51.7 %collective-permute-done.10.refs_2_ = bf16[1024,1536]{1,0:T(8,128)(2,1)} collective-permute-done((bf16[1024,1536]{1,0:T(8,128)(2,1)}, bf16[1024,1536]{1,0:T(8,128)(2,1)}, u32[]{:S(2)}, u32[]{:S(2)}) %collective-permute-start.10) | collective-permute-done | bytes 3145760 | tf_op jit(solution)/shard_map/ppermute | solution.py:170
  160.3 3.2 shard_map.100
  163.7 3.5 shard_map.101
  174.3 2.1 shard_map.102
  178.2 9.2 %collective-permute-done.15.refs_1_ = bf16[96,2048]{1,0:T(8,128)(2,1)S(1)} collective-permute-done((bf16[96,2048]{1,0:T(8,128)(2,1)S(1)}, bf16[96,2048]{1,0:T(8,128)(2,1)S(1)}, u32[]{:S(2)}, u32[]{:S(2)}) %collective-permute-start.15) | collective-permute-done | bytes 393248 | tf_op jit(solution)/shard_map/ppermute | solution.py:170
  187.4 3.5 shard_map.103
  194.1 2.5 collective-permute-done.16.refs_1_
  200.3 2.1 shard_map.104
  202.5 2.3 collective-permute-start.20
  204.8 4.9 %collective-permute-done.19.refs_0_ = bf16[96,2048]{1,0:T(8,128)(2,1)S(1)} collective-permute-done((bf16[96,2048]{1,0:T(8,128)(2,1)S(1)}, bf16[96,2048]{1,0:T(8,128)(2,1)S(1)}, u32[]{:S(2)}, u32[]{:S(2)}) %collective-permute-start.19) | collective-permute-done | bytes 393248 | tf_op jit(solution)/shard_map/ppermute | solution.py:170
  209.7 5.3 %collective-permute-done.20.refs_1_ = bf16[96,2048]{1,0:T(8,128)(2,1)S(1)} collective-permute-done((bf16[96,2048]{1,0:T(8,128)(2,1)S(1)}, bf16[96,2048]{1,0:T(8,128)(2,1)S(1)}, u32[]{:S(2)}, u32[]{:S(2)}) %collective-permute-start.20) | collective-permute-done | bytes 393248 | tf_op jit(solution)/shard_map/ppermute | solution.py:170
  215.0 3.5 shard_map.105
  221.6 2.6 collective-permute-done.21.refs_1_
  232.0 5.1 %collective-permute-done.24.refs_0_ = bf16[96,2048]{1,0:T(8,128)(2,1)S(1)} collective-permute-done((bf16[96,2048]{1,0:T(8,128)(2,1)S(1)}, bf16[96,2048]{1,0:T(8,128)(2,1)S(1)}, u32[]{:S(2)}, u32[]{:S(2)}) %collective-permute-start.24) | collective-permute-done | bytes 393248 | tf_op jit(solution)/shard_map/ppermute | solution.py:170
  237.1 5.0 %collective-permute-done.25.refs_1_ = bf16[96,2048]{1,0:T(8,128)(2,1)S(1)} collective-permute-done((bf16[96,2048]{1,0:T(8,128)(2,1)S(1)}, bf16[96,2048]{1,0:T(8,128)(2,1)S(1)}, u32[]{:S(2)}, u32[]{:S(2)}) %collective-permute-start.25) | collective-permute-done | bytes 393248 | tf_op jit(solution)/shard_map/ppermute | solution.py:170
  242.1 3.5 shard_map.107
  248.9 2.5 collective-permute-done.26.refs_1_
  255.0 2.1 shard_map.108
  259.1 5.2 %collective-permute-done.29.refs_0_ = bf16[96,2048]{1,0:T(8,128)(2,1)S(1)} collective-permute-done((bf16[96,2048]{1,0:T(8,128)(2,1)S(1)}, bf16[96,2048]{1,0:T(8,128)(2,1)S(1)}, u32[]{:S(2)}, u32[]{:S(2)}) %collective-permute-start.29) | collective-permute-done | bytes 393248 | tf_op jit(solution)/shard_map/ppermute | solution.py:170
  264.4 5.1 %collective-permute-done.30.refs_1_ = bf16[96,2048]{1,0:T(8,128)(2,1)S(1)} collective-permute-done((bf16[96,2048]{1,0:T(8,128)(2,1)S(1)}, bf16[96,2048]{1,0:T(8,128)(2,1)S(1)}, u32[]{:S(2)}, u32[]{:S(2)}) %collective-permute-start.30) | collective-permute-done | bytes 393248 | tf_op jit(solution)/shard_map/ppermute | solution.py:170
  269.5 3.5 shard_map.109
  276.0 2.7 collective-permute-done.31.refs_1_
  282.2 2.2 shard_map.110
  286.6 5.1 %collective-permute-done.34.refs_0_ = bf16[96,2048]{1,0:T(8,128)(2,1)S(1)} collective-permute-done((bf16[96,2048]{1,0:T(8,128)(2,1)S(1)}, bf16[96,2048]{1,0:T(8,128)(2,1)S(1)}, u32[]{:S(2)}, u32[]{:S(2)}) %collective-permute-start.34) | collective-permute-done | bytes 393248 | tf_op jit(solution)/shard_map/ppermute | solution.py:170
  291.7 5.0 %collective-permute-done.35.refs_1_ = bf16[96,2048]{1,0:T(8,128)(2,1)S(1)} collective-permute-done((bf16[96,2048]{1,0:T(8,128)(2,1)S(1)}, bf16[96,2048]{1,0:T(8,128)(2,1)S(1)}, u32[]{:S(2)}, u32[]{:S(2)}) %collective-permute-start.35) | collective-permute-done | bytes 393248 | tf_op jit(solution)/shard_map/ppermute | solution.py:170
  296.7 3.5 shard_map.111
  303.4 2.4 collective-permute-done.36.refs_1_
  309.5 2.2 shard_map.112
  311.8 2.2 collective-permute-start.40
  313.9 5.0 %collective-permute-done.39.refs_0_ = bf16[96,2048]{1,0:T(8,128)(2,1)S(1)} collective-permute-done((bf16[96,2048]{1,0:T(8,128)(2,1)S(1)}, bf16[96,2048]{1,0:T(8,128)(2,1)S(1)}, u32[]{:S(2)}, u32[]{:S(2)}) %collective-permute-start.39) | collective-permute-done | bytes 393248 | tf_op jit(solution)/shard_map/ppermute | solution.py:170
  319.0 5.1 %collective-permute-done.40.refs_1_ = bf16[96,2048]{1,0:T(8,128)(2,1)S(1)} collective-permute-done((bf16[96,2048]{1,0:T(8,128)(2,1)S(1)}, bf16[96,2048]{1,0:T(8,128)(2,1)S(1)}, u32[]{:S(2)}, u32[]{:S(2)}) %collective-permute-start.40) | collective-permute-done | bytes 393248 | tf_op jit(solution)/shard_map/ppermute | solution.py:170
  324.1 3.5 shard_map.113
  330.6 2.7 collective-permute-done.41.refs_1_
  337.1 2.2 shard_map.114
  341.7 5.4 %collective-permute-done.44.refs_0_ = bf16[96,2048]{1,0:T(8,128)(2,1)S(1)} collective-permute-done((bf16[96,2048]{1,0:T(8,128)(2,1)S(1)}, bf16[96,2048]{1,0:T(8,128)(2,1)S(1)}, u32[]{:S(2)}, u32[]{:S(2)}) %collective-permute-start.44) | collective-permute-done | bytes 393248 | tf_op jit(solution)/shard_map/ppermute | solution.py:170
  347.1 4.9 %collective-permute-done.45.refs_1_ = bf16[96,2048]{1,0:T(8,128)(2,1)S(1)} collective-permute-done((bf16[96,2048]{1,0:T(8,128)(2,1)S(1)}, bf16[96,2048]{1,0:T(8,128)(2,1)S(1)}, u32[]{:S(2)}, u32[]{:S(2)}) %collective-permute-start.45) | collective-permute-done | bytes 393248 | tf_op jit(solution)/shard_map/ppermute | solution.py:170
  352.0 4.2 shard_map.115
  359.9 2.9 collective-permute-done.46.refs_1_
  366.6 3.4 copy-done
  371.0 2.7 shard_map.116
  375.7 5.3 %collective-permute-done.49.refs_0_ = bf16[96,2048]{1,0:T(8,128)(2,1)S(1)} collective-permute-done((bf16[96,2048]{1,0:T(8,128)(2,1)S(1)}, bf16[96,2048]{1,0:T(8,128)(2,1)S(1)}, u32[]{:S(2)}, u32[]{:S(2)}) %collective-permute-start.49) | collective-permute-done | bytes 393248 | tf_op jit(solution)/shard_map/ppermute | solution.py:170
  381.0 4.8 %collective-permute-done.50.refs_1_ = bf16[96,2048]{1,0:T(8,128)(2,1)S(1)} collective-permute-done((bf16[96,2048]{1,0:T(8,128)(2,1)S(1)}, bf16[96,2048]{1,0:T(8,128)(2,1)S(1)}, u32[]{:S(2)}, u32[]{:S(2)}) %collective-permute-start.50) | collective-permute-done | bytes 393248 | tf_op jit(solution)/shard_map/ppermute | solution.py:170
  389.6 3.5 shard_map.117
  396.3 2.5 collective-permute-done.51.refs_1_
  402.6 2.2 shard_map.118
  406.9 5.1 %collective-permute-done.54.refs_0_ = bf16[96,2048]{1,0:T(8,128)(2,1)S(1)} collective-permute-done((bf16[96,2048]{1,0:T(8,128)(2,1)S(1)}, bf16[96,2048]{1,0:T(8,128)(2,1)S(1)}, u32[]{:S(2)}, u32[]{:S(2)}) %collective-permute-start.54) | collective-permute-done | bytes 393248 | tf_op jit(solution)/shard_map/ppermute | solution.py:170
  412.1 4.9 %collective-permute-done.55.refs_1_ = bf16[96,2048]{1,0:T(8,128)(2,1)S(1)} collective-permute-done((bf16[96,2048]{1,0:T(8,128)(2,1)S(1)}, bf16[96,2048]{1,0:T(8,128)(2,1)S(1)}, u32[]{:S(2)}, u32[]{:S(2)}) %collective-permute-start.55) | collective-permute-done | bytes 393248 | tf_op jit(solution)/shard_map/ppermute | solution.py:170
  417.0 3.5 shard_map.119
  423.6 2.7 collective-permute-done.56.refs_1_
  430.2 2.2 shard_map.120
  434.2 9.2 %collective-permute-done.60.refs_1_ = bf16[96,2048]{1,0:T(8,128)(2,1)S(1)} collective-permute-done((bf16[96,2048]{1,0:T(8,128)(2,1)S(1)}, bf16[96,2048]{1,0:T(8,128)(2,1)S(1)}, u32[]{:S(2)}, u32[]{:S(2)}) %collective-permute-start.60) | collective-permute-done | bytes 393248 | tf_op jit(solution)/shard_map/ppermute | solution.py:170
  443.4 3.5 shard_map.121
  450.0 2.6 collective-permute-done.61
  456.3 3.0 shard_map.122
  464.4 4.6 collective-permute-done.67
  (217 shorter events, 130.3 us)
Async XLA Ops:
  1.5 17.4 %collective-permute-start = (s32[2,2,33]{2,1,0:T(2,128)S(1)}, s32[2,2,33]{2,1,0:T(2,128)S(1)}, u32[]{:S(2)}, u32[]{:S(2)}) collective-permute-start(s32[2,2,33]{2,1,0:T(2,128)S(1)} %pad_add_fusion.1), channel_id=1, source_target_pairs={{0,1},{1,2},{2,3},{3,0},{4,5},{5,6},{6,7},{7,4},{8,9},{9,10},{10,1... | collective-permute-start | bytes 1592 | tf_op jit(solution)/shard_map/ppermute | solution.py:170
  4.6 14.4 %collective-permute-start.1 = (s32[2,2,33]{2,1,0:T(2,128)S(1)}, s32[2,2,33]{2,1,0:T(2,128)S(1)}, u32[]{:S(2)}, u32[]{:S(2)}) collective-permute-start(s32[2,2,33]{2,1,0:T(2,128)S(1)} %pad_add_fusion.1), channel_id=1, source_target_pairs={{0,2},{1,3},{2,0},{3,1},{4,6},{5,7},{6,4},{7,5},{8,10},{9,11},{10,... | collective-permute-start | bytes 1592 | tf_op jit(solution)/shard_map/ppermute | solution.py:170
  7.1 11.8 %collective-permute-start.2 = (s32[2,2,33]{2,1,0:T(2,128)S(1)}, s32[2,2,33]{2,1,0:T(2,128)S(1)}, u32[]{:S(2)}, u32[]{:S(2)}) collective-permute-start(s32[2,2,33]{2,1,0:T(2,128)S(1)} %pad_add_fusion.1), channel_id=1, source_target_pairs={{0,3},{1,0},{2,1},{3,2},{4,7},{5,4},{6,5},{7,6},{8,11},{9,8},{10,9... | collective-permute-start | bytes 1592 | tf_op jit(solution)/shard_map/ppermute | solution.py:170
  19.3 69.4 %collective-permute-start.8 = (bf16[1024,1536]{1,0:T(8,128)(2,1)}, bf16[1024,1536]{1,0:T(8,128)(2,1)S(1)}, u32[]{:S(2)}, u32[]{:S(2)}) collective-permute-start(bf16[1024,1536]{1,0:T(8,128)(2,1)} %pad_maximum_fusion.2), channel_id=1, source_target_pairs={{0,1},{3,2},{4,5},{7,6},{8,9},{11,10},{12,13},{15,14},{16,17},{19,... | collective-permute-start | bytes 9437192 | tf_op jit(solution)/shard_map/ppermute | solution.py:170
  22.1 66.6 %collective-permute-start.9 = (bf16[1024,1536]{1,0:T(8,128)(2,1)}, bf16[1024,1536]{1,0:T(8,128)(2,1)}, u32[]{:S(2)}, u32[]{:S(2)}) collective-permute-start(bf16[1024,1536]{1,0:T(8,128)(2,1)} %pad_maximum_fusion.3), channel_id=1, source_target_pairs={{2,1},{1,2},{6,5},{5,6},{10,9},{9,10},{14,13},{13,14},{18,17},{17,... | collective-permute-start | bytes 9437192 | tf_op jit(solution)/shard_map/ppermute | solution.py:170
  39.8 56.1 %collective-permute-start.3 = (bf16[512,2048]{1,0:T(8,128)(2,1)S(1)}, bf16[512,2048]{1,0:T(8,128)(2,1)S(1)}, u32[]{:S(2)}, u32[]{:S(2)}) collective-permute-start(bf16[512,2048]{1,0:T(8,128)(2,1)S(1)} %select_select_fusion), channel_id=1, source_target_pairs={{9,1},{10,2},{13,5},{14,6}} | collective-permute-start | bytes 6291464 | tf_op jit(solution)/shard_map/ppermute | solution.py:170
  40.6 55.3 %collective-permute-start.4 = (bf16[512,2048]{1,0:T(8,128)(2,1)S(1)}, bf16[512,2048]{1,0:T(8,128)(2,1)S(1)}, u32[]{:S(2)}, u32[]{:S(2)}) collective-permute-start(bf16[512,2048]{1,0:T(8,128)(2,1)S(1)} %select_select_fusion), channel_id=1, source_target_pairs={{17,1},{18,2},{21,5},{22,6}} | collective-permute-start | bytes 6291464 | tf_op jit(solution)/shard_map/ppermute | solution.py:170
  41.4 54.5 %collective-permute-start.5 = (bf16[512,2048]{1,0:T(8,128)(2,1)S(1)}, bf16[512,2048]{1,0:T(8,128)(2,1)S(1)}, u32[]{:S(2)}, u32[]{:S(2)}) collective-permute-start(bf16[512,2048]{1,0:T(8,128)(2,1)S(1)} %select_select_fusion), channel_id=1, source_target_pairs={{25,1},{26,2},{29,5},{30,6}} | collective-permute-start | bytes 6291464 | tf_op jit(solution)/shard_map/ppermute | solution.py:170
  88.7 71.6 %collective-permute-start.10 = (bf16[1024,1536]{1,0:T(8,128)(2,1)}, bf16[1024,1536]{1,0:T(8,128)(2,1)}, u32[]{:S(2)}, u32[]{:S(2)}) collective-permute-start(bf16[1024,1536]{1,0:T(8,128)(2,1)} %pad_maximum_fusion.1), channel_id=1, source_target_pairs={{3,1},{0,2},{7,5},{4,6},{11,9},{8,10},{15,13},{12,14},{19,17},{16,... | collective-permute-start | bytes 9437192 | tf_op jit(solution)/shard_map/ppermute | solution.py:170
  98.0 8.8 %collective-permute-start.6 = (bf16[512,2048]{1,0:T(8,128)(2,1)}, bf16[512,2048]{1,0:T(8,128)(2,1)}, u32[]{:S(2)}, u32[]{:S(2)}) collective-permute-start(bf16[512,2048]{1,0:T(8,128)(2,1)} %add_add_fusion), channel_id=1, source_target_pairs={{1,5},{2,6},{5,1},{6,2}} | collective-permute-start | bytes 6291464 | tf_op jit(solution)/shard_map/ppermute | solution.py:170
  100.0 63.6 %collective-permute-start.7 = (bf16[16,2048]{1,0:T(8,128)(2,1)S(1)}, bf16[16,2048]{1,0:T(8,128)(2,1)S(1)}, u32[]{:S(2)}, u32[]{:S(2)}) collective-permute-start(bf16[16,2048]{1,0:T(8,128)(2,1)S(1)} %copy-done.8), channel_id=1, source_target_pairs={{1,5},{2,6},{5,1},{6,2}} | collective-permute-start | bytes 196616 | tf_op jit(solution)/shard_map/ppermute | solution.py:170
  167.2 4.7 collective-permute-start.11
  168.6 4.6 collective-permute-start.12
  169.3 5.0 %collective-permute-start.13 = (bf16[96,512]{1,0:T(8,128)(2,1)S(1)}, bf16[96,512]{1,0:T(8,128)(2,1)S(1)}, u32[]{:S(2)}, u32[]{:S(2)}) collective-permute-start(bf16[96,512]{1,0:T(8,128)(2,1)S(1)} %get-tuple-element.58.refs_0_), channel_id=1, source_target_pairs={{0,16},{1,6},{2,5},{3,19},{4,20},{5,2},{6,1},{7,23},{8,24},{9,14},... | collective-permute-start | bytes 294920 | tf_op jit(solution)/shard_map/ppermute | solution.py:170
  176.5 10.9 %collective-permute-start.15 = (bf16[96,2048]{1,0:T(8,128)(2,1)S(1)}, bf16[96,2048]{1,0:T(8,128)(2,1)S(1)}, u32[]{:S(2)}, u32[]{:S(2)}) collective-permute-start(bf16[96,2048]{1,0:T(8,128)(2,1)S(1)} %shard_map.102), channel_id=1, source_target_pairs={{0,12},{1,13},{2,14},{3,15},{4,8},{5,9},{6,10},{7,11},{8,4},{9,5},... | collective-permute-start | bytes 1179656 | tf_op jit(solution)/shard_map/ppermute | solution.py:170
  190.9 5.7 %collective-permute-start.16 = (bf16[96,512]{1,0:T(8,128)(2,1)S(1)}, bf16[96,512]{1,0:T(8,128)(2,1)S(1)}, u32[]{:S(2)}, u32[]{:S(2)}) collective-permute-start(bf16[96,512]{1,0:T(8,128)(2,1)S(1)} %get-tuple-element.60.refs_0_), channel_id=1, source_target_pairs={{0,16},{1,5},{2,6},{3,19},{4,20},{5,1},{6,2},{7,23},{8,24},{9,13},... | collective-permute-start | bytes 294920 | tf_op jit(solution)/shard_map/ppermute | solution.py:170
  192.1 6.7 %collective-permute-start.17 = (bf16[96,512]{1,0:T(8,128)(2,1)S(1)}, bf16[96,512]{1,0:T(8,128)(2,1)S(1)}, u32[]{:S(2)}, u32[]{:S(2)}) collective-permute-start(bf16[96,512]{1,0:T(8,128)(2,1)S(1)} %get-tuple-element.60.refs_0_), channel_id=1, source_target_pairs={{0,16},{1,2},{2,1},{3,19},{4,20},{5,6},{6,5},{7,23},{8,24},{9,10},... | collective-permute-start | bytes 294920 | tf_op jit(solution)/shard_map/ppermute | solution.py:170
  193.0 7.2 %collective-permute-start.18 = (bf16[96,512]{1,0:T(8,128)(2,1)S(1)}, bf16[96,512]{1,0:T(8,128)(2,1)S(1)}, u32[]{:S(2)}, u32[]{:S(2)}) collective-permute-start(bf16[96,512]{1,0:T(8,128)(2,1)S(1)} %get-tuple-element.60.refs_0_), channel_id=1, source_target_pairs={{0,16},{1,6},{2,5},{3,19},{4,20},{5,2},{6,1},{7,23},{8,24},{9,14},... | collective-permute-start | bytes 294920 | tf_op jit(solution)/shard_map/ppermute | solution.py:170
  202.4 7.3 %collective-permute-start.19 = (bf16[96,2048]{1,0:T(8,128)(2,1)S(1)}, bf16[96,2048]{1,0:T(8,128)(2,1)S(1)}, u32[]{:S(2)}, u32[]{:S(2)}) collective-permute-start(bf16[96,2048]{1,0:T(8,128)(2,1)S(1)} %shard_map.104), channel_id=1, source_target_pairs={{0,8},{1,9},{2,10},{3,11},{4,12},{5,13},{6,14},{7,15},{8,16},{9,17... | collective-permute-start | bytes 1179656 | tf_op jit(solution)/shard_map/ppermute | solution.py:170
  202.5 12.5 %collective-permute-start.20 = (bf16[96,2048]{1,0:T(8,128)(2,1)S(1)}, bf16[96,2048]{1,0:T(8,128)(2,1)S(1)}, u32[]{:S(2)}, u32[]{:S(2)}) collective-permute-start(bf16[96,2048]{1,0:T(8,128)(2,1)S(1)} %shard_map.104), channel_id=1, source_target_pairs={{0,12},{1,13},{2,14},{3,15},{4,8},{5,9},{6,10},{7,11},{8,20},{9,21... | collective-permute-start | bytes 1179656 | tf_op jit(solution)/shard_map/ppermute | solution.py:170
  218.5 5.7 %collective-permute-start.21 = (bf16[96,512]{1,0:T(8,128)(2,1)S(1)}, bf16[96,512]{1,0:T(8,128)(2,1)S(1)}, u32[]{:S(2)}, u32[]{:S(2)}) collective-permute-start(bf16[96,512]{1,0:T(8,128)(2,1)S(1)} %get-tuple-element.62.refs_0_), channel_id=1, source_target_pairs={{0,16},{1,5},{2,6},{3,19},{4,20},{5,1},{6,2},{7,23},{8,24},{9,13},... | collective-permute-start | bytes 294920 | tf_op jit(solution)/shard_map/ppermute | solution.py:170
  219.6 6.7 %collective-permute-start.22 = (bf16[96,512]{1,0:T(8,128)(2,1)S(1)}, bf16[96,512]{1,0:T(8,128)(2,1)S(1)}, u32[]{:S(2)}, u32[]{:S(2)}) collective-permute-start(bf16[96,512]{1,0:T(8,128)(2,1)S(1)} %get-tuple-element.62.refs_0_), channel_id=1, source_target_pairs={{0,16},{1,2},{2,1},{3,19},{4,20},{5,6},{6,5},{7,23},{8,24},{9,10},... | collective-permute-start | bytes 294920 | tf_op jit(solution)/shard_map/ppermute | solution.py:170
  220.6 7.0 %collective-permute-start.23 = (bf16[96,512]{1,0:T(8,128)(2,1)S(1)}, bf16[96,512]{1,0:T(8,128)(2,1)S(1)}, u32[]{:S(2)}, u32[]{:S(2)}) collective-permute-start(bf16[96,512]{1,0:T(8,128)(2,1)S(1)} %get-tuple-element.62.refs_0_), channel_id=1, source_target_pairs={{0,16},{1,6},{2,5},{3,19},{4,20},{5,2},{6,1},{7,23},{8,24},{9,14},... | collective-permute-start | bytes 294920 | tf_op jit(solution)/shard_map/ppermute | solution.py:170
  229.7 7.4 %collective-permute-start.24 = (bf16[96,2048]{1,0:T(8,128)(2,1)S(1)}, bf16[96,2048]{1,0:T(8,128)(2,1)S(1)}, u32[]{:S(2)}, u32[]{:S(2)}) collective-permute-start(bf16[96,2048]{1,0:T(8,128)(2,1)S(1)} %shard_map.106), channel_id=1, source_target_pairs={{0,8},{1,9},{2,10},{3,11},{4,12},{5,13},{6,14},{7,15},{8,16},{9,17... | collective-permute-start | bytes 1179656 | tf_op jit(solution)/shard_map/ppermute | solution.py:170
  229.9 12.2 %collective-permute-start.25 = (bf16[96,2048]{1,0:T(8,128)(2,1)S(1)}, bf16[96,2048]{1,0:T(8,128)(2,1)S(1)}, u32[]{:S(2)}, u32[]{:S(2)}) collective-permute-start(bf16[96,2048]{1,0:T(8,128)(2,1)S(1)} %shard_map.106), channel_id=1, source_target_pairs={{0,12},{1,13},{2,14},{3,15},{4,8},{5,9},{6,10},{7,11},{8,20},{9,21... | collective-permute-start | bytes 1179656 | tf_op jit(solution)/shard_map/ppermute | solution.py:170
  245.6 5.7 %collective-permute-start.26 = (bf16[96,512]{1,0:T(8,128)(2,1)S(1)}, bf16[96,512]{1,0:T(8,128)(2,1)S(1)}, u32[]{:S(2)}, u32[]{:S(2)}) collective-permute-start(bf16[96,512]{1,0:T(8,128)(2,1)S(1)} %get-tuple-element.64.refs_0_), channel_id=1, source_target_pairs={{0,16},{1,5},{2,6},{3,19},{4,20},{5,1},{6,2},{7,23},{8,24},{9,13},... | collective-permute-start | bytes 294920 | tf_op jit(solution)/shard_map/ppermute | solution.py:170
  246.8 6.6 %collective-permute-start.27 = (bf16[96,512]{1,0:T(8,128)(2,1)S(1)}, bf16[96,512]{1,0:T(8,128)(2,1)S(1)}, u32[]{:S(2)}, u32[]{:S(2)}) collective-permute-start(bf16[96,512]{1,0:T(8,128)(2,1)S(1)} %get-tuple-element.64.refs_0_), channel_id=1, source_target_pairs={{0,16},{1,2},{2,1},{3,19},{4,20},{5,6},{6,5},{7,23},{8,24},{9,10},... | collective-permute-start | bytes 294920 | tf_op jit(solution)/shard_map/ppermute | solution.py:170
  247.7 7.2 %collective-permute-start.28 = (bf16[96,512]{1,0:T(8,128)(2,1)S(1)}, bf16[96,512]{1,0:T(8,128)(2,1)S(1)}, u32[]{:S(2)}, u32[]{:S(2)}) collective-permute-start(bf16[96,512]{1,0:T(8,128)(2,1)S(1)} %get-tuple-element.64.refs_0_), channel_id=1, source_target_pairs={{0,16},{1,6},{2,5},{3,19},{4,20},{5,2},{6,1},{7,23},{8,24},{9,14},... | collective-permute-start | bytes 294920 | tf_op jit(solution)/shard_map/ppermute | solution.py:170
  257.1 7.3 %collective-permute-start.29 = (bf16[96,2048]{1,0:T(8,128)(2,1)S(1)}, bf16[96,2048]{1,0:T(8,128)(2,1)S(1)}, u32[]{:S(2)}, u32[]{:S(2)}) collective-permute-start(bf16[96,2048]{1,0:T(8,128)(2,1)S(1)} %shard_map.108), channel_id=1, source_target_pairs={{0,8},{1,9},{2,10},{3,11},{4,12},{5,13},{6,14},{7,15},{8,16},{9,17... | collective-permute-start | bytes 1179656 | tf_op jit(solution)/shard_map/ppermute | solution.py:170
  257.2 12.3 %collective-permute-start.30 = (bf16[96,2048]{1,0:T(8,128)(2,1)S(1)}, bf16[96,2048]{1,0:T(8,128)(2,1)S(1)}, u32[]{:S(2)}, u32[]{:S(2)}) collective-permute-start(bf16[96,2048]{1,0:T(8,128)(2,1)S(1)} %shard_map.108), channel_id=1, source_target_pairs={{0,12},{1,13},{2,14},{3,15},{4,8},{5,9},{6,10},{7,11},{8,20},{9,21... | collective-permute-start | bytes 1179656 | tf_op jit(solution)/shard_map/ppermute | solution.py:170
  273.0 5.7 %collective-permute-start.31 = (bf16[96,512]{1,0:T(8,128)(2,1)S(1)}, bf16[96,512]{1,0:T(8,128)(2,1)S(1)}, u32[]{:S(2)}, u32[]{:S(2)}) collective-permute-start(bf16[96,512]{1,0:T(8,128)(2,1)S(1)} %get-tuple-element.66.refs_0_), channel_id=1, source_target_pairs={{0,16},{1,5},{2,6},{3,19},{4,20},{5,1},{6,2},{7,23},{8,24},{9,13},... | collective-permute-start | bytes 294920 | tf_op jit(solution)/shard_map/ppermute | solution.py:170
  274.0 6.8 %collective-permute-start.32 = (bf16[96,512]{1,0:T(8,128)(2,1)S(1)}, bf16[96,512]{1,0:T(8,128)(2,1)S(1)}, u32[]{:S(2)}, u32[]{:S(2)}) collective-permute-start(bf16[96,512]{1,0:T(8,128)(2,1)S(1)} %get-tuple-element.66.refs_0_), channel_id=1, source_target_pairs={{0,16},{1,2},{2,1},{3,19},{4,20},{5,6},{6,5},{7,23},{8,24},{9,10},... | collective-permute-start | bytes 294920 | tf_op jit(solution)/shard_map/ppermute | solution.py:170
  275.1 7.1 %collective-permute-start.33 = (bf16[96,512]{1,0:T(8,128)(2,1)S(1)}, bf16[96,512]{1,0:T(8,128)(2,1)S(1)}, u32[]{:S(2)}, u32[]{:S(2)}) collective-permute-start(bf16[96,512]{1,0:T(8,128)(2,1)S(1)} %get-tuple-element.66.refs_0_), channel_id=1, source_target_pairs={{0,16},{1,6},{2,5},{3,19},{4,20},{5,2},{6,1},{7,23},{8,24},{9,14},... | collective-permute-start | bytes 294920 | tf_op jit(solution)/shard_map/ppermute | solution.py:170
  284.4 7.3 %collective-permute-start.34 = (bf16[96,2048]{1,0:T(8,128)(2,1)S(1)}, bf16[96,2048]{1,0:T(8,128)(2,1)S(1)}, u32[]{:S(2)}, u32[]{:S(2)}) collective-permute-start(bf16[96,2048]{1,0:T(8,128)(2,1)S(1)} %get-tuple-element.69), channel_id=1, source_target_pairs={{0,8},{1,9},{2,10},{3,11},{4,12},{5,13},{6,14},{7,15},{8,16},{9,17... | collective-permute-start | bytes 1179656 | tf_op jit(solution)/shard_map/ppermute | solution.py:170
  284.5 12.2 %collective-permute-start.35 = (bf16[96,2048]{1,0:T(8,128)(2,1)S(1)}, bf16[96,2048]{1,0:T(8,128)(2,1)S(1)}, u32[]{:S(2)}, u32[]{:S(2)}) collective-permute-start(bf16[96,2048]{1,0:T(8,128)(2,1)S(1)} %get-tuple-element.69), channel_id=1, source_target_pairs={{0,12},{1,13},{2,14},{3,15},{4,8},{5,9},{6,10},{7,11},{8,20},{9,21... | collective-permute-start | bytes 1179656 | tf_op jit(solution)/shard_map/ppermute | solution.py:170
  300.2 5.7 %collective-permute-start.36 = (bf16[96,512]{1,0:T(8,128)(2,1)S(1)}, bf16[96,512]{1,0:T(8,128)(2,1)S(1)}, u32[]{:S(2)}, u32[]{:S(2)}) collective-permute-start(bf16[96,512]{1,0:T(8,128)(2,1)S(1)} %get-tuple-element.70.refs_0_), channel_id=1, source_target_pairs={{0,16},{1,5},{2,6},{3,19},{4,20},{5,1},{6,2},{7,23},{8,24},{9,13},... | collective-permute-start | bytes 294920 | tf_op jit(solution)/shard_map/ppermute | solution.py:170
  301.4 6.6 %collective-permute-start.37 = (bf16[96,512]{1,0:T(8,128)(2,1)S(1)}, bf16[96,512]{1,0:T(8,128)(2,1)S(1)}, u32[]{:S(2)}, u32[]{:S(2)}) collective-permute-start(bf16[96,512]{1,0:T(8,128)(2,1)S(1)} %get-tuple-element.70.refs_0_), channel_id=1, source_target_pairs={{0,16},{1,2},{2,1},{3,19},{4,20},{5,6},{6,5},{7,23},{8,24},{9,10},... | collective-permute-start | bytes 294920 | tf_op jit(solution)/shard_map/ppermute | solution.py:170
  302.3 7.2 %collective-permute-start.38 = (bf16[96,512]{1,0:T(8,128)(2,1)S(1)}, bf16[96,512]{1,0:T(8,128)(2,1)S(1)}, u32[]{:S(2)}, u32[]{:S(2)}) collective-permute-start(bf16[96,512]{1,0:T(8,128)(2,1)S(1)} %get-tuple-element.70.refs_0_), channel_id=1, source_target_pairs={{0,16},{1,6},{2,5},{3,19},{4,20},{5,2},{6,1},{7,23},{8,24},{9,14},... | collective-permute-start | bytes 294920 | tf_op jit(solution)/shard_map/ppermute | solution.py:170
  311.7 7.3 %collective-permute-start.39 = (bf16[96,2048]{1,0:T(8,128)(2,1)S(1)}, bf16[96,2048]{1,0:T(8,128)(2,1)S(1)}, u32[]{:S(2)}, u32[]{:S(2)}) collective-permute-start(bf16[96,2048]{1,0:T(8,128)(2,1)S(1)} %get-tuple-element.73), channel_id=1, source_target_pairs={{0,8},{1,9},{2,10},{3,11},{4,12},{5,13},{6,14},{7,15},{8,16},{9,17... | collective-permute-start | bytes 1179656 | tf_op jit(solution)/shard_map/ppermute | solution.py:170
  311.8 12.3 %collective-permute-start.40 = (bf16[96,2048]{1,0:T(8,128)(2,1)S(1)}, bf16[96,2048]{1,0:T(8,128)(2,1)S(1)}, u32[]{:S(2)}, u32[]{:S(2)}) collective-permute-start(bf16[96,2048]{1,0:T(8,128)(2,1)S(1)} %get-tuple-element.73), channel_id=1, source_target_pairs={{0,12},{1,13},{2,14},{3,15},{4,8},{5,9},{6,10},{7,11},{8,20},{9,21... | collective-permute-start | bytes 1179656 | tf_op jit(solution)/shard_map/ppermute | solution.py:170
  327.6 5.7 %collective-permute-start.41 = (bf16[96,512]{1,0:T(8,128)(2,1)S(1)}, bf16[96,512]{1,0:T(8,128)(2,1)S(1)}, u32[]{:S(2)}, u32[]{:S(2)}) collective-permute-start(bf16[96,512]{1,0:T(8,128)(2,1)S(1)} %get-tuple-element.74.refs_0_), channel_id=1, source_target_pairs={{0,16},{1,5},{2,6},{3,19},{4,20},{5,1},{6,2},{7,23},{8,24},{9,13},... | collective-permute-start | bytes 294920 | tf_op jit(solution)/shard_map/ppermute | solution.py:170
  328.6 6.8 %collective-permute-start.42 = (bf16[96,512]{1,0:T(8,128)(2,1)S(1)}, bf16[96,512]{1,0:T(8,128)(2,1)S(1)}, u32[]{:S(2)}, u32[]{:S(2)}) collective-permute-start(bf16[96,512]{1,0:T(8,128)(2,1)S(1)} %get-tuple-element.74.refs_0_), channel_id=1, source_target_pairs={{0,16},{1,2},{2,1},{3,19},{4,20},{5,6},{6,5},{7,23},{8,24},{9,10},... | collective-permute-start | bytes 294920 | tf_op jit(solution)/shard_map/ppermute | solution.py:170
  329.7 7.3 %collective-permute-start.43 = (bf16[96,512]{1,0:T(8,128)(2,1)S(1)}, bf16[96,512]{1,0:T(8,128)(2,1)S(1)}, u32[]{:S(2)}, u32[]{:S(2)}) collective-permute-start(bf16[96,512]{1,0:T(8,128)(2,1)S(1)} %get-tuple-element.74.refs_0_), channel_id=1, source_target_pairs={{0,16},{1,6},{2,5},{3,19},{4,20},{5,2},{6,1},{7,23},{8,24},{9,14},... | collective-permute-start | bytes 294920 | tf_op jit(solution)/shard_map/ppermute | solution.py:170
  339.9 7.2 %collective-permute-start.44 = (bf16[96,2048]{1,0:T(8,128)(2,1)S(1)}, bf16[96,2048]{1,0:T(8,128)(2,1)S(1)}, u32[]{:S(2)}, u32[]{:S(2)}) collective-permute-start(bf16[96,2048]{1,0:T(8,128)(2,1)S(1)} %get-tuple-element.77), channel_id=1, source_target_pairs={{0,8},{1,9},{2,10},{3,11},{4,12},{5,13},{6,14},{7,15},{8,16},{9,17... | collective-permute-start | bytes 1179656 | tf_op jit(solution)/shard_map/ppermute | solution.py:170
  339.9 12.1 %collective-permute-start.45 = (bf16[96,2048]{1,0:T(8,128)(2,1)S(1)}, bf16[96,2048]{1,0:T(8,128)(2,1)S(1)}, u32[]{:S(2)}, u32[]{:S(2)}) collective-permute-start(bf16[96,2048]{1,0:T(8,128)(2,1)S(1)} %get-tuple-element.77), channel_id=1, source_target_pairs={{0,12},{1,13},{2,14},{3,15},{4,8},{5,9},{6,10},{7,11},{8,20},{9,21... | collective-permute-start | bytes 1179656 | tf_op jit(solution)/shard_map/ppermute | solution.py:170
  356.9 5.9 %collective-permute-start.46 = (bf16[96,512]{1,0:T(8,128)(2,1)}, bf16[96,512]{1,0:T(8,128)(2,1)}, u32[]{:S(2)}, u32[]{:S(2)}) collective-permute-start(bf16[96,512]{1,0:T(8,128)(2,1)} %get-tuple-element.78.refs_0_), channel_id=1, source_target_pairs={{0,16},{1,5},{2,6},{3,19},{4,20},{5,1},{6,2},{7,23},{8,24},{9,13},... | collective-permute-start | bytes 294920 | tf_op jit(solution)/shard_map/ppermute | solution.py:170
  357.9 7.1 %collective-permute-start.47 = (bf16[96,512]{1,0:T(8,128)(2,1)}, bf16[96,512]{1,0:T(8,128)(2,1)}, u32[]{:S(2)}, u32[]{:S(2)}) collective-permute-start(bf16[96,512]{1,0:T(8,128)(2,1)} %get-tuple-element.78.refs_0_), channel_id=1, source_target_pairs={{0,16},{1,2},{2,1},{3,19},{4,20},{5,6},{6,5},{7,23},{8,24},{9,10},... | collective-permute-start | bytes 294920 | tf_op jit(solution)/shard_map/ppermute | solution.py:170
  358.9 7.6 %collective-permute-start.48 = (bf16[96,512]{1,0:T(8,128)(2,1)}, bf16[96,512]{1,0:T(8,128)(2,1)}, u32[]{:S(2)}, u32[]{:S(2)}) collective-permute-start(bf16[96,512]{1,0:T(8,128)(2,1)} %get-tuple-element.78.refs_0_), channel_id=1, source_target_pairs={{0,16},{1,6},{2,5},{3,19},{4,20},{5,2},{6,1},{7,23},{8,24},{9,14},... | collective-permute-start | bytes 294920 | tf_op jit(solution)/shard_map/ppermute | solution.py:170
  373.7 7.3 %collective-permute-start.49 = (bf16[96,2048]{1,0:T(8,128)(2,1)S(1)}, bf16[96,2048]{1,0:T(8,128)(2,1)S(1)}, u32[]{:S(2)}, u32[]{:S(2)}) collective-permute-start(bf16[96,2048]{1,0:T(8,128)(2,1)S(1)} %get-tuple-element.81), channel_id=1, source_target_pairs={{0,8},{1,9},{2,10},{3,11},{4,12},{5,13},{6,14},{7,15},{8,16},{9,17... | collective-permute-start | bytes 1179656 | tf_op jit(solution)/shard_map/ppermute | solution.py:170
  373.8 12.0 %collective-permute-start.50 = (bf16[96,2048]{1,0:T(8,128)(2,1)S(1)}, bf16[96,2048]{1,0:T(8,128)(2,1)S(1)}, u32[]{:S(2)}, u32[]{:S(2)}) collective-permute-start(bf16[96,2048]{1,0:T(8,128)(2,1)S(1)} %get-tuple-element.81), channel_id=1, source_target_pairs={{0,12},{1,13},{2,14},{3,15},{4,8},{5,9},{6,10},{7,11},{8,20},{9,21... | collective-permute-start | bytes 1179656 | tf_op jit(solution)/shard_map/ppermute | solution.py:170
  393.1 5.7 %collective-permute-start.51 = (bf16[96,512]{1,0:T(8,128)(2,1)S(1)}, bf16[96,512]{1,0:T(8,128)(2,1)S(1)}, u32[]{:S(2)}, u32[]{:S(2)}) collective-permute-start(bf16[96,512]{1,0:T(8,128)(2,1)S(1)} %get-tuple-element.82.refs_0_), channel_id=1, source_target_pairs={{0,16},{1,5},{2,6},{3,19},{4,20},{5,1},{6,2},{7,23},{8,24},{9,13},... | collective-permute-start | bytes 294920 | tf_op jit(solution)/shard_map/ppermute | solution.py:170
  394.3 6.6 %collective-permute-start.52 = (bf16[96,512]{1,0:T(8,128)(2,1)S(1)}, bf16[96,512]{1,0:T(8,128)(2,1)S(1)}, u32[]{:S(2)}, u32[]{:S(2)}) collective-permute-start(bf16[96,512]{1,0:T(8,128)(2,1)S(1)} %get-tuple-element.82.refs_0_), channel_id=1, source_target_pairs={{0,16},{1,2},{2,1},{3,19},{4,20},{5,6},{6,5},{7,23},{8,24},{9,10},... | collective-permute-start | bytes 294920 | tf_op jit(solution)/shard_map/ppermute | solution.py:170
  395.2 7.4 %collective-permute-start.53 = (bf16[96,512]{1,0:T(8,128)(2,1)S(1)}, bf16[96,512]{1,0:T(8,128)(2,1)S(1)}, u32[]{:S(2)}, u32[]{:S(2)}) collective-permute-start(bf16[96,512]{1,0:T(8,128)(2,1)S(1)} %get-tuple-element.82.refs_0_), channel_id=1, source_target_pairs={{0,16},{1,6},{2,5},{3,19},{4,20},{5,2},{6,1},{7,23},{8,24},{9,14},... | collective-permute-start | bytes 294920 | tf_op jit(solution)/shard_map/ppermute | solution.py:170
  404.8 7.3 %collective-permute-start.54 = (bf16[96,2048]{1,0:T(8,128)(2,1)S(1)}, bf16[96,2048]{1,0:T(8,128)(2,1)S(1)}, u32[]{:S(2)}, u32[]{:S(2)}) collective-permute-start(bf16[96,2048]{1,0:T(8,128)(2,1)S(1)} %get-tuple-element.85), channel_id=1, source_target_pairs={{0,8},{1,9},{2,10},{3,11},{4,12},{5,13},{6,14},{7,15},{8,16},{9,17... | collective-permute-start | bytes 1179656 | tf_op jit(solution)/shard_map/ppermute | solution.py:170
  404.9 12.1 %collective-permute-start.55 = (bf16[96,2048]{1,0:T(8,128)(2,1)S(1)}, bf16[96,2048]{1,0:T(8,128)(2,1)S(1)}, u32[]{:S(2)}, u32[]{:S(2)}) collective-permute-start(bf16[96,2048]{1,0:T(8,128)(2,1)S(1)} %get-tuple-element.85), channel_id=1, source_target_pairs={{0,12},{1,13},{2,14},{3,15},{4,8},{5,9},{6,10},{7,11},{8,20},{9,21... | collective-permute-start | bytes 1179656 | tf_op jit(solution)/shard_map/ppermute | solution.py:170
  420.5 5.7 %collective-permute-start.56 = (bf16[96,512]{1,0:T(8,128)(2,1)S(1)}, bf16[96,512]{1,0:T(8,128)(2,1)S(1)}, u32[]{:S(2)}, u32[]{:S(2)}) collective-permute-start(bf16[96,512]{1,0:T(8,128)(2,1)S(1)} %get-tuple-element.86.refs_0_), channel_id=1, source_target_pairs={{0,16},{1,5},{2,6},{3,19},{4,20},{5,1},{6,2},{7,23},{8,24},{9,13},... | collective-permute-start | bytes 294920 | tf_op jit(solution)/shard_map/ppermute | solution.py:170
  421.5 6.8 %collective-permute-start.57 = (bf16[96,512]{1,0:T(8,128)(2,1)S(1)}, bf16[96,512]{1,0:T(8,128)(2,1)S(1)}, u32[]{:S(2)}, u32[]{:S(2)}) collective-permute-start(bf16[96,512]{1,0:T(8,128)(2,1)S(1)} %get-tuple-element.86.refs_0_), channel_id=1, source_target_pairs={{0,16},{1,2},{2,1},{3,19},{4,20},{5,6},{6,5},{7,23},{8,24},{9,10},... | collective-permute-start | bytes 294920 | tf_op jit(solution)/shard_map/ppermute | solution.py:170
  422.6 7.5 %collective-permute-start.58 = (bf16[96,512]{1,0:T(8,128)(2,1)S(1)}, bf16[96,512]{1,0:T(8,128)(2,1)S(1)}, u32[]{:S(2)}, u32[]{:S(2)}) collective-permute-start(bf16[96,512]{1,0:T(8,128)(2,1)S(1)} %get-tuple-element.86.refs_0_), channel_id=1, source_target_pairs={{0,16},{1,6},{2,5},{3,19},{4,20},{5,2},{6,1},{7,23},{8,24},{9,14},... | collective-permute-start | bytes 294920 | tf_op jit(solution)/shard_map/ppermute | solution.py:170
  432.4 10.9 %collective-permute-start.60 = (bf16[96,2048]{1,0:T(8,128)(2,1)S(1)}, bf16[96,2048]{1,0:T(8,128)(2,1)S(1)}, u32[]{:S(2)}, u32[]{:S(2)}) collective-permute-start(bf16[96,2048]{1,0:T(8,128)(2,1)S(1)} %get-tuple-element.89), channel_id=1, source_target_pairs={{0,12},{1,13},{2,14},{3,15},{4,8},{5,9},{6,10},{7,11},{8,4},{9,5},... | collective-permute-start | bytes 1179656 | tf_op jit(solution)/shard_map/ppermute | solution.py:170
  446.9 5.7 %collective-permute-start.61 = (bf16[96,512]{1,0:T(8,128)(2,1)S(1)}, bf16[96,512]{1,0:T(8,128)(2,1)S(1)}, u32[]{:S(2)}, u32[]{:S(2)}) collective-permute-start(bf16[96,512]{1,0:T(8,128)(2,1)S(1)} %get-tuple-element.90), channel_id=1, source_target_pairs={{0,16},{1,5},{2,6},{3,19},{4,20},{5,1},{6,2},{7,23},{8,24},{9,13},... | collective-permute-start | bytes 294920 | tf_op jit(solution)/shard_map/ppermute | solution.py:170
  448.0 6.7 %collective-permute-start.62 = (bf16[96,512]{1,0:T(8,128)(2,1)S(1)}, bf16[96,512]{1,0:T(8,128)(2,1)S(1)}, u32[]{:S(2)}, u32[]{:S(2)}) collective-permute-start(bf16[96,512]{1,0:T(8,128)(2,1)S(1)} %get-tuple-element.90), channel_id=1, source_target_pairs={{0,16},{1,2},{2,1},{3,19},{4,20},{5,6},{6,5},{7,23},{8,24},{9,10},... | collective-permute-start | bytes 294920 | tf_op jit(solution)/shard_map/ppermute | solution.py:170
  449.0 7.2 %collective-permute-start.63 = (bf16[96,512]{1,0:T(8,128)(2,1)S(1)}, bf16[96,512]{1,0:T(8,128)(2,1)S(1)}, u32[]{:S(2)}, u32[]{:S(2)}) collective-permute-start(bf16[96,512]{1,0:T(8,128)(2,1)S(1)} %get-tuple-element.90), channel_id=1, source_target_pairs={{0,16},{1,6},{2,5},{3,19},{4,20},{5,2},{6,1},{7,23},{8,24},{9,14},... | collective-permute-start | bytes 294920 | tf_op jit(solution)/shard_map/ppermute | solution.py:170
  459.3 5.0 %collective-permute-start.65 = (f32[8,2048]{1,0:T(8,128)S(1)}, f32[8,2048]{1,0:T(8,128)S(1)}, u32[]{:S(2)}, u32[]{:S(2)}) collective-permute-start(f32[8,2048]{1,0:T(8,128)S(1)} %reshape.226), channel_id=1, source_target_pairs={{0,16},{1,17},{2,18},{3,19},{4,20},{5,21},{6,22},{7,23},{8,24},{9,... | collective-permute-start | bytes 196616 | tf_op jit(solution)/shard_map/ppermute | solution.py:170
  464.4 4.7 collective-permute-start.67
  (38 other events, 1283.8 us)

commit v8 on v7

--- a/solution.py
+++ b/solution.py
@@ -95,6 +95,26 @@
 def hold_kernel(count, *refs):
     outs, sems = refs[count : 2 * count], refs[2 * count]
     copies = [pltpu.make_async_copy(refs[b], outs[b], sems.at[b]) for b in range(count)]
+    for copy in copies:
+        copy.start()
+    for copy in copies:
+        copy.wait()
+
+
+def cut_kernel(count, sides, *refs):
+    outs, sems = refs[3 : 3 + count], refs[3 + count]
+    cols = outs[0].shape[1] // 3
+    copies = []
+    for b in range(count):
+        at = pl.multiple_of(sides[b] * cols, 128)
+        for c in range(3):
+            copies.append(
+                pltpu.make_async_copy(
+                    refs[c].at[0, :, pl.ds(at, cols)],
+                    outs[b].at[:, pl.ds(c * cols, cols)],
+                    sems.at[3 * b + c],
+                )
+            )
     for copy in copies:
         copy.start()
     for copy in copies:
@@ -186,15 +206,26 @@
     packed = gathered.reshape(docs, segs, tokens + 1)
     ids, lengths = packed[:, :, :tokens], packed[:, :, tokens]
 
-    def block_of(side):
-        return jnp.concatenate(
-            [lax.dynamic_slice_in_dim(w[0], side * cols, cols, 1) for w in (w_query, w_key, w_value)],
-            1,
-        )
+    smem = pl.BlockSpec(memory_space=pltpu.SMEM)
+    vmem = pl.BlockSpec(memory_space=pltpu.VMEM)
+    hbm = pl.BlockSpec(memory_space=pl.ANY)
+
+    def cut(sides):
+        count = len(sides)
+        size = count * depth * 3 * cols * 4
+        return pl.pallas_call(
+            functools.partial(cut_kernel, count),
+            out_shape=[jax.ShapeDtypeStruct((depth, 3 * cols), jnp.bfloat16)] * count,
+            in_specs=[smem] + [hbm] * 3,
+            out_specs=[hbm] * count,
+            scratch_shapes=[pltpu.SemaphoreType.DMA((3 * count,))],
+            cost_estimate=pl.CostEstimate(flops=0, bytes_accessed=size, transcendentals=0),
+        )(jnp.stack(sides).astype(jnp.int32), w_query, w_key, w_value)
 
     rounds = [c for c in range(D) if c != lo]
-    blocks = [block_of((z == D - 1 - c).astype(jnp.int32)) for c in rounds]
-    own_block = block_of((z == hi).astype(jnp.int32))
+    blocks = list(cut([z == D - 1 - c for c in rounds[:-1]]))
+    last, own_block = cut([z == D - 1 - rounds[-1], z == hi])
+    blocks.append(last)
     where = jnp.stack([z] + [jnp.where(z == hi, D - 1 - c, c) for c in rounds]).astype(jnp.int32)
 
     def relay(c, block):
@@ -220,7 +251,7 @@
     blocks = [lax.optimization_barrier((block, ids))[0] for block in blocks]
     early = [relay(c, block) for c, block in zip(rounds[:-1], blocks[:-1])]
     last, early = lax.optimization_barrier((blocks[-1], early))
-    received = early + [relay(rounds[-1], last)]
+    received = [own_block] + early + [relay(rounds[-1], last)]
     tok, tok_other = embed(jnp.concatenate([ids[:, seg] for seg in range(segs)]))
     mem_other = send(mem_init, [((0, b, c), (0, T - 1 - b, c)) for b in range(T) for c in planes])
 
@@ -245,12 +276,10 @@
     side = (z == hi).astype(jnp.int32)
     place = jnp.stack([((t + j) % T) * 2 + (side + i) % 2 for j, i in shifts]).astype(jnp.int32)
 
-    smem = pl.BlockSpec(memory_space=pltpu.SMEM)
-    vmem = pl.BlockSpec(memory_space=pltpu.VMEM)
     out_proj = w_out[0]
     parts = len(shifts)
 
-    held = pl.pallas_call(
+    weights = pl.pallas_call(
         functools.partial(hold_kernel, len(received)),
         out_shape=[jax.ShapeDtypeStruct(w.shape, w.dtype) for w in received],
         in_specs=[pl.BlockSpec(memory_space=pl.ANY)] * len(received),
@@ -258,7 +287,6 @@
         scratch_shapes=[pltpu.SemaphoreType.DMA((len(received),))],
         compiler_params=params,
     )(*received)
-    weights = [own_block, *held]
 
     own = jnp.zeros((R, half), jnp.bfloat16)
     other = jnp.zeros((R, half), jnp.bfloat16)
@@ -304,7 +332,14 @@
             paired = S % 2 == 0 and k in (0, turns - 2)
             after = [e[0] ^ 1 if paired else (e[0] + 1) % S for e in everyone]
             own = send(result[0], [(e, (a, e[1], e[2])) for e, a in zip(everyone, after)])
-            other = send(result[0], [(e, (a, T - 1 - e[1], e[2])) for e, a in zip(everyone, after)])
+            counts = {0: (0,), turns - 2: (S - 2,)}.get(k, range(S)) if paired else range(S)
+            other = send(
+                result[0],
+                [
+                    (e, (a, T - 1 - e[1] if e[0] in counts else e[1], e[2]))
+                    for e, a in zip(everyone, after)
+                ],
+            )
 
     mine = lax.dynamic_slice_in_dim(jnp.stack(pools), s, S, 0).reshape(docs, half)
     total = mine

time: 477 us -> 804 us (1.69)
  Pallas kernels: 64.9 us -> 450 us
  waiting for transfers between devices: 270 us -> 218 us
    pallas_call x0 -> x2, Pallas kernels: none -> 385 us  [cut(): pl.pallas_call(functools.partial(cut_kernel, count), out_shape=[jax.Shape...]
    ppermute x68, waiting for transfers between devices: 270 us -> 218 us  [send(): return lax.ppermute(block, AXES, [(lin(*a), lin(*b)) for a, b in pairs])]
  transfers between devices with their start and end apart: 68 -> 68, of which waited for: 58 -> 57; matrix products, arithmetic and copies ran while one was open for 8% -> 4% of each run, Pallas kernels for 1% -> 49%
where the time goes in v8:
time: 804 us; the launch traced here: 795 us
  Pallas kernels  450 us (56%)
  waiting for transfers between devices  218 us (27%)
  starting transfers between devices  82.2 us (10%)
  local copies, waits for them, and re-layouts  30.9 us (4%)
  other arithmetic  12 us (1%)
    pallas_call x2, Pallas kernels, cut(): pl.pallas_call(functools.partial(cut_kernel, count), out_shape=[jax.Shape...  385 us
    ppermute x68, waiting for transfers between devices, send(): return lax.ppermute(block, AXES, [(lin(*a), lin(*b)) for a, b in pairs])  218 us
    ppermute x68, starting transfers between devices, send(): return lax.ppermute(block, AXES, [(lin(*a), lin(*b)) for a, b in pairs])  82.2 us
    pallas_call x11, Pallas kernels, body(): pl.pallas_call(functools.partial(attend_kernel, k, n, tokens, D), out_sha...  39.5 us
    pallas_call x10, Pallas kernels, body(): pl.pallas_call(functools.partial(project_kernel, k, n, tokens, parts, poo...  22.3 us
  transfers between devices with their start and end apart: 68, of which 57 were waited for; matrix products, arithmetic and copies ran while one was open for 4% of the time, Pallas kernels for 49%

profile of v8, /device:TPU:0, one launch (start us, length us, event | category | flops | bytes accessed | tf_op | source)
XLA Modules:
  0.0 795.4 jit_solution(15746184772113461328)
XLA Ops:
  1.5 3.0 collective-permute-start
  4.6 2.6 collective-permute-start.1
  9.9 192.4 %shard_map.101 = (bf16[1024,1536]{1,0:T(8,128)(2,1)}, bf16[1024,1536]{1,0:T(8,128)(2,1)}) custom-call(s32[2]{0:T(128)} %add_convert_fusion.1.sides, bf16[1,1024,1024]{2,1,0:T(8,128)(2,1)} %refs_0_.3, bf16[1,1024,1024]{2,1,0:T(8,128)(2,1)} %refs_1_.3, bf16[1,1024,1024]{2,1,0:T(8,128)(2,1)} %refs_2_.3), custom_call_target="tpu_custom_call" | custom-call | bytes 12582912 | tf_op jit(solution)/shard_map/pallas_call | solution.py:216
  202.7 2.8 collective-permute-start.8
  205.5 2.3 collective-permute-start.9
  207.9 13.2 %gather_fusion.1 = bf16[512,2048]{1,0:T(8,128)(2,1)} fusion(bf16[4096,2048]{1,0:T(8,128)(2,1)} %param.12, s32[1024]{0:T(1024)S(1)} %pad_clamp_fusion), kind=kCustom, calls=%fused_computation.1 | custom fusion | bytes 4196352 | tf_op jit(solution)/shard_map/jit(_take)/gather | solution.py:244
  221.0 3.2 select_select_fusion
  231.0 192.4 %shard_map.100 = (bf16[1024,1536]{1,0:T(8,128)(2,1)}, bf16[1024,1536]{1,0:T(8,128)(2,1)}) custom-call(s32[2]{0:T(128)} %add_convert_fusion.sides, bf16[1,1024,1024]{2,1,0:T(8,128)(2,1)} %refs_0_.3, bf16[1,1024,1024]{2,1,0:T(8,128)(2,1)} %refs_1_.3, bf16[1,1024,1024]{2,1,0:T(8,128)(2,1)} %refs_2_.3), custom_call_target="tpu_custom_call" | custom-call | bytes 12582912 | tf_op jit(solution)/shard_map/pallas_call | solution.py:216
  423.5 2.9 collective-permute-start.10
  426.4 4.9 add_add_fusion
  439.6 52.2 %collective-permute-done.10.refs_3_ = bf16[1024,1536]{1,0:T(8,128)(2,1)} collective-permute-done((bf16[1024,1536]{1,0:T(8,128)(2,1)}, bf16[1024,1536]{1,0:T(8,128)(2,1)}, u32[]{:S(2)}, u32[]{:S(2)}) %collective-permute-start.10) | collective-permute-done | bytes 3145760 | tf_op jit(solution)/shard_map/ppermute | solution.py:190
  491.9 3.5 shard_map.102
  495.5 3.5 shard_map.103
  499.0 3.6 collective-permute-start.11
  509.8 2.1 shard_map.104
  514.1 5.3 collective-permute-done.15.refs_1_
  519.4 3.5 shard_map.105
  525.1 3.6 collective-permute-done.16.refs_1_
  532.7 2.1 shard_map.106
  535.1 7.0 collective-permute-done.19.refs_0_
  542.1 3.6 collective-permute-done.20.refs_1_
  545.8 3.5 shard_map.107
  551.9 3.1 collective-permute-done.21.refs_1_
  559.2 2.1 shard_map.108
  562.8 5.8 collective-permute-done.24.refs_0_
  568.6 4.1 collective-permute-done.25.refs_1_
  572.7 3.5 shard_map.109
  579.6 2.2 collective-permute-done.26.refs_1_
  589.8 5.3 collective-permute-done.29.refs_0_
  595.1 5.1 collective-permute-done.30.refs_1_
  600.2 3.5 shard_map.111
  606.6 2.8 collective-permute-done.31.refs_1_
  613.6 2.2 shard_map.112
  617.5 5.5 collective-permute-done.34.refs_0_
  623.0 4.4 collective-permute-done.35.refs_1_
  627.4 3.5 shard_map.113
  634.4 2.2 collective-permute-done.36.refs_1_
  640.5 2.2 shard_map.114
  644.5 5.4 collective-permute-done.39.refs_0_
  649.9 5.1 collective-permute-done.40.refs_1_
  655.0 3.5 shard_map.115
  661.4 3.0 collective-permute-done.41.refs_1_
  668.2 2.2 shard_map.116
  672.3 5.4 collective-permute-done.44.refs_0_
  677.7 4.4 collective-permute-done.45.refs_1_
  682.1 4.2 shard_map.117
  690.3 2.6 collective-permute-done.46.refs_1_
  697.0 3.4 copy-done
  701.3 2.8 shard_map.118
  706.0 5.4 collective-permute-done.49.refs_0_
  711.4 5.1 collective-permute-done.50.refs_1_
  720.3 3.5 shard_map.119
  726.6 2.9 collective-permute-done.51.refs_1_
  733.5 2.2 shard_map.120
  737.4 5.5 collective-permute-done.54.refs_0_
  743.0 4.4 collective-permute-done.55.refs_1_
  747.3 3.5 shard_map.121
  754.3 2.2 collective-permute-done.56.refs_1_
  760.4 2.2 shard_map.122
  765.0 3.5 shard_map.123
  768.5 5.5 collective-permute-start.61
  776.6 2.8 collective-permute-done.62
  781.5 3.0 shard_map.124
  789.7 4.6 collective-permute-done.67
  (204 shorter events, 124.2 us)
Async XLA Ops:
  1.5 200.8 %collective-permute-start = (s32[2,2,33]{2,1,0:T(2,128)S(1)}, s32[2,2,33]{2,1,0:T(2,128)S(1)}, u32[]{:S(2)}, u32[]{:S(2)}) collective-permute-start(s32[2,2,33]{2,1,0:T(2,128)S(1)} %pad_add_fusion.1), channel_id=1, source_target_pairs={{0,1},{1,2},{2,3},{3,0},{4,5},{5,6},{6,7},{7,4},{8,9},{9,10},{10,1... | collective-permute-start | bytes 1592 | tf_op jit(solution)/shard_map/ppermute | solution.py:190
  4.6 197.7 %collective-permute-start.1 = (s32[2,2,33]{2,1,0:T(2,128)S(1)}, s32[2,2,33]{2,1,0:T(2,128)S(1)}, u32[]{:S(2)}, u32[]{:S(2)}) collective-permute-start(s32[2,2,33]{2,1,0:T(2,128)S(1)} %pad_add_fusion.1), channel_id=1, source_target_pairs={{0,2},{1,3},{2,0},{3,1},{4,6},{5,7},{6,4},{7,5},{8,10},{9,11},{10,... | collective-permute-start | bytes 1592 | tf_op jit(solution)/shard_map/ppermute | solution.py:190
  7.1 195.2 %collective-permute-start.2 = (s32[2,2,33]{2,1,0:T(2,128)S(1)}, s32[2,2,33]{2,1,0:T(2,128)S(1)}, u32[]{:S(2)}, u32[]{:S(2)}) collective-permute-start(s32[2,2,33]{2,1,0:T(2,128)S(1)} %pad_add_fusion.1), channel_id=1, source_target_pairs={{0,3},{1,0},{2,1},{3,2},{4,7},{5,4},{6,5},{7,6},{8,11},{9,8},{10,9... | collective-permute-start | bytes 1592 | tf_op jit(solution)/shard_map/ppermute | solution.py:190
  202.7 220.7 %collective-permute-start.8 = (bf16[1024,1536]{1,0:T(8,128)(2,1)}, bf16[1024,1536]{1,0:T(8,128)(2,1)S(1)}, u32[]{:S(2)}, u32[]{:S(2)}) collective-permute-start(bf16[1024,1536]{1,0:T(8,128)(2,1)} %get-tuple-element.58), channel_id=1, source_target_pairs={{0,1},{3,2},{4,5},{7,6},{8,9},{11,10},{12,13},{15,14},{16,17},{19,... | collective-permute-start | bytes 9437192 | tf_op jit(solution)/shard_map/ppermute | solution.py:190
  205.5 217.9 %collective-permute-start.9 = (bf16[1024,1536]{1,0:T(8,128)(2,1)}, bf16[1024,1536]{1,0:T(8,128)(2,1)}, u32[]{:S(2)}, u32[]{:S(2)}) collective-permute-start(bf16[1024,1536]{1,0:T(8,128)(2,1)} %get-tuple-element.60), channel_id=1, source_target_pairs={{2,1},{1,2},{6,5},{5,6},{10,9},{9,10},{14,13},{13,14},{18,17},{17,... | collective-permute-start | bytes 9437192 | tf_op jit(solution)/shard_map/ppermute | solution.py:190
  224.3 202.1 %collective-permute-start.3 = (bf16[512,2048]{1,0:T(8,128)(2,1)}, bf16[512,2048]{1,0:T(8,128)(2,1)}, u32[]{:S(2)}, u32[]{:S(2)}) collective-permute-start(bf16[512,2048]{1,0:T(8,128)(2,1)} %select_select_fusion), channel_id=1, source_target_pairs={{9,1},{10,2},{13,5},{14,6}} | collective-permute-start | bytes 6291464 | tf_op jit(solution)/shard_map/ppermute | solution.py:190
  226.3 200.0 %collective-permute-start.4 = (bf16[512,2048]{1,0:T(8,128)(2,1)}, bf16[512,2048]{1,0:T(8,128)(2,1)}, u32[]{:S(2)}, u32[]{:S(2)}) collective-permute-start(bf16[512,2048]{1,0:T(8,128)(2,1)} %select_select_fusion), channel_id=1, source_target_pairs={{17,1},{18,2},{21,5},{22,6}} | collective-permute-start | bytes 6291464 | tf_op jit(solution)/shard_map/ppermute | solution.py:190
  228.4 198.0 %collective-permute-start.5 = (bf16[512,2048]{1,0:T(8,128)(2,1)}, bf16[512,2048]{1,0:T(8,128)(2,1)}, u32[]{:S(2)}, u32[]{:S(2)}) collective-permute-start(bf16[512,2048]{1,0:T(8,128)(2,1)} %select_select_fusion), channel_id=1, source_target_pairs={{25,1},{26,2},{29,5},{30,6}} | collective-permute-start | bytes 6291464 | tf_op jit(solution)/shard_map/ppermute | solution.py:190
  423.5 68.4 %collective-permute-start.10 = (bf16[1024,1536]{1,0:T(8,128)(2,1)}, bf16[1024,1536]{1,0:T(8,128)(2,1)}, u32[]{:S(2)}, u32[]{:S(2)}) collective-permute-start(bf16[1024,1536]{1,0:T(8,128)(2,1)} %get-tuple-element.63), channel_id=1, source_target_pairs={{3,1},{0,2},{7,5},{4,6},{11,9},{8,10},{15,13},{12,14},{19,17},{16,... | collective-permute-start | bytes 9437192 | tf_op jit(solution)/shard_map/ppermute | solution.py:190
  431.3 6.5 collective-permute-start.6
  433.3 62.1 %collective-permute-start.7 = (bf16[16,2048]{1,0:T(8,128)(2,1)S(1)}, bf16[16,2048]{1,0:T(8,128)(2,1)S(1)}, u32[]{:S(2)}, u32[]{:S(2)}) collective-permute-start(bf16[16,2048]{1,0:T(8,128)(2,1)S(1)} %copy-done.9), channel_id=1, source_target_pairs={{1,5},{2,6},{5,1},{6,2}} | collective-permute-start | bytes 196616 | tf_op jit(solution)/shard_map/ppermute | solution.py:190
  499.0 7.2 collective-permute-start.11
  502.6 5.7 collective-permute-start.12
  502.7 7.1 collective-permute-start.13
  512.1 7.4 collective-permute-start.15
  523.0 5.7 collective-permute-start.16
  523.0 7.8 collective-permute-start.17
  525.0 7.7 collective-permute-start.18
  534.9 7.3 collective-permute-start.19
  534.9 10.8 %collective-permute-start.20 = (bf16[96,2048]{1,0:T(8,128)(2,1)S(1)}, bf16[96,2048]{1,0:T(8,128)(2,1)S(1)}, u32[]{:S(2)}, u32[]{:S(2)}) collective-permute-start(bf16[96,2048]{1,0:T(8,128)(2,1)S(1)} %shard_map.106), channel_id=1, source_target_pairs={{0,12},{1,13},{2,14},{3,15},{4,8},{5,9},{6,10},{7,11},{8,20},{9,21... | collective-permute-start | bytes 1179656 | tf_op jit(solution)/shard_map/ppermute | solution.py:190
  549.3 5.7 collective-permute-start.21
  549.9 7.3 collective-permute-start.22
  551.4 7.9 collective-permute-start.23
  561.4 7.3 collective-permute-start.24
  561.5 11.1 %collective-permute-start.25 = (bf16[96,2048]{1,0:T(8,128)(2,1)S(1)}, bf16[96,2048]{1,0:T(8,128)(2,1)S(1)}, u32[]{:S(2)}, u32[]{:S(2)}) collective-permute-start(bf16[96,2048]{1,0:T(8,128)(2,1)S(1)} %shard_map.108), channel_id=1, source_target_pairs={{0,12},{1,13},{2,14},{3,15},{4,8},{5,9},{6,10},{7,11},{8,20},{9,21... | collective-permute-start | bytes 1179656 | tf_op jit(solution)/shard_map/ppermute | solution.py:190
  576.2 5.6 collective-permute-start.26
  577.6 6.4 collective-permute-start.27
  578.3 7.4 collective-permute-start.28
  587.9 7.3 collective-permute-start.29
  588.0 12.3 %collective-permute-start.30 = (bf16[96,2048]{1,0:T(8,128)(2,1)S(1)}, bf16[96,2048]{1,0:T(8,128)(2,1)S(1)}, u32[]{:S(2)}, u32[]{:S(2)}) collective-permute-start(bf16[96,2048]{1,0:T(8,128)(2,1)S(1)} %shard_map.110), channel_id=1, source_target_pairs={{0,12},{1,13},{2,14},{3,15},{4,8},{5,9},{6,10},{7,11},{8,20},{9,21... | collective-permute-start | bytes 1179656 | tf_op jit(solution)/shard_map/ppermute | solution.py:190
  603.8 5.6 collective-permute-start.31
  604.5 6.9 collective-permute-start.32
  605.9 7.7 collective-permute-start.33
  615.8 7.3 collective-permute-start.34
  615.9 11.5 %collective-permute-start.35 = (bf16[96,2048]{1,0:T(8,128)(2,1)S(1)}, bf16[96,2048]{1,0:T(8,128)(2,1)S(1)}, u32[]{:S(2)}, u32[]{:S(2)}) collective-permute-start(bf16[96,2048]{1,0:T(8,128)(2,1)S(1)} %get-tuple-element.79), channel_id=1, source_target_pairs={{0,12},{1,13},{2,14},{3,15},{4,8},{5,9},{6,10},{7,11},{8,20},{9,21... | collective-permute-start | bytes 1179656 | tf_op jit(solution)/shard_map/ppermute | solution.py:190
  630.9 5.6 collective-permute-start.36
  632.3 6.4 collective-permute-start.37
  633.0 7.4 collective-permute-start.38
  642.7 7.3 collective-permute-start.39
  642.8 12.3 %collective-permute-start.40 = (bf16[96,2048]{1,0:T(8,128)(2,1)S(1)}, bf16[96,2048]{1,0:T(8,128)(2,1)S(1)}, u32[]{:S(2)}, u32[]{:S(2)}) collective-permute-start(bf16[96,2048]{1,0:T(8,128)(2,1)S(1)} %get-tuple-element.83), channel_id=1, source_target_pairs={{0,12},{1,13},{2,14},{3,15},{4,8},{5,9},{6,10},{7,11},{8,20},{9,21... | collective-permute-start | bytes 1179656 | tf_op jit(solution)/shard_map/ppermute | solution.py:190
  658.6 5.7 collective-permute-start.41
  659.3 7.1 collective-permute-start.42
  660.7 7.5 collective-permute-start.43
  670.4 7.3 collective-permute-start.44
  670.5 11.6 %collective-permute-start.45 = (bf16[96,2048]{1,0:T(8,128)(2,1)S(1)}, bf16[96,2048]{1,0:T(8,128)(2,1)S(1)}, u32[]{:S(2)}, u32[]{:S(2)}) collective-permute-start(bf16[96,2048]{1,0:T(8,128)(2,1)S(1)} %get-tuple-element.87), channel_id=1, source_target_pairs={{0,12},{1,13},{2,14},{3,15},{4,8},{5,9},{6,10},{7,11},{8,20},{9,21... | collective-permute-start | bytes 1179656 | tf_op jit(solution)/shard_map/ppermute | solution.py:190
  687.0 6.0 collective-permute-start.46
  688.3 6.8 collective-permute-start.47
  689.0 7.9 collective-permute-start.48
  704.1 7.3 collective-permute-start.49
  704.2 12.3 %collective-permute-start.50 = (bf16[96,2048]{1,0:T(8,128)(2,1)S(1)}, bf16[96,2048]{1,0:T(8,128)(2,1)S(1)}, u32[]{:S(2)}, u32[]{:S(2)}) collective-permute-start(bf16[96,2048]{1,0:T(8,128)(2,1)S(1)} %get-tuple-element.91), channel_id=1, source_target_pairs={{0,12},{1,13},{2,14},{3,15},{4,8},{5,9},{6,10},{7,11},{8,20},{9,21... | collective-permute-start | bytes 1179656 | tf_op jit(solution)/shard_map/ppermute | solution.py:190
  723.8 5.7 collective-permute-start.51
  724.6 7.1 collective-permute-start.52
  725.9 7.6 collective-permute-start.53
  735.7 7.3 collective-permute-start.54
  735.8 11.6 %collective-permute-start.55 = (bf16[96,2048]{1,0:T(8,128)(2,1)S(1)}, bf16[96,2048]{1,0:T(8,128)(2,1)S(1)}, u32[]{:S(2)}, u32[]{:S(2)}) collective-permute-start(bf16[96,2048]{1,0:T(8,128)(2,1)S(1)} %get-tuple-element.95), channel_id=1, source_target_pairs={{0,12},{1,13},{2,14},{3,15},{4,8},{5,9},{6,10},{7,11},{8,20},{9,21... | collective-permute-start | bytes 1179656 | tf_op jit(solution)/shard_map/ppermute | solution.py:190
  750.9 5.7 collective-permute-start.56
  752.3 6.4 collective-permute-start.57
  753.0 7.4 collective-permute-start.58
  768.5 8.1 %collective-permute-start.61 = (bf16[96,512]{1,0:T(8,128)(2,1)S(1)}, bf16[96,512]{1,0:T(8,128)(2,1)S(1)}, u32[]{:S(2)}, u32[]{:S(2)}) collective-permute-start(bf16[96,512]{1,0:T(8,128)(2,1)S(1)} %get-tuple-element.100), channel_id=1, source_target_pairs={{0,16},{1,5},{2,6},{3,19},{4,20},{5,1},{6,2},{7,23},{8,24},{9,13},... | collective-permute-start | bytes 294920 | tf_op jit(solution)/shard_map/ppermute | solution.py:190
  774.0 5.5 collective-permute-start.62
  774.0 7.5 collective-permute-start.63
  784.6 3.8 collective-permute-start.64
  784.7 4.4 collective-permute-start.65
  789.6 4.7 collective-permute-start.67
  (33 other events, 1193.1 us)

commit v9 on v7

--- a/solution.py
+++ b/solution.py
@@ -304,7 +304,14 @@
             paired = S % 2 == 0 and k in (0, turns - 2)
             after = [e[0] ^ 1 if paired else (e[0] + 1) % S for e in everyone]
             own = send(result[0], [(e, (a, e[1], e[2])) for e, a in zip(everyone, after)])
-            other = send(result[0], [(e, (a, T - 1 - e[1], e[2])) for e, a in zip(everyone, after)])
+            counts = {0: (0,), turns - 2: (S - 2,)}.get(k, range(S)) if paired else range(S)
+            other = send(
+                result[0],
+                [
+                    (e, (a, T - 1 - e[1] if e[0] in counts else e[1], e[2]))
+                    for e, a in zip(everyone, after)
+                ],
+            )
 
     mine = lax.dynamic_slice_in_dim(jnp.stack(pools), s, S, 0).reshape(docs, half)
     total = mine

time: 477 us -> 467 us (0.979)
  waiting for transfers between devices: 270 us -> 261 us
    ppermute x68, waiting for transfers between devices: 270 us -> 261 us  [send(): return lax.ppermute(block, AXES, [(lin(*a), lin(*b)) for a, b in pairs])]
  transfers between devices with their start and end apart: 68 -> 68, of which waited for: 58 -> 59; matrix products, arithmetic and copies ran while one was open for 8% -> 8% of each run, Pallas kernels for 1% -> 1%
where the time goes in v9:
time: 467 us; the launch traced here: 460 us
  waiting for transfers between devices  261 us (56%)
  starting transfers between devices  80.3 us (17%)
  Pallas kernels  64.9 us (14%)
  local copies, waits for them, and re-layouts  38 us (8%)
  other arithmetic  13.6 us (3%)
    ppermute x68, waiting for transfers between devices, send(): return lax.ppermute(block, AXES, [(lin(*a), lin(*b)) for a, b in pairs])  261 us
    ppermute x68, starting transfers between devices, send(): return lax.ppermute(block, AXES, [(lin(*a), lin(*b)) for a, b in pairs])  80.3 us
    pallas_call x11, Pallas kernels, body(): pl.pallas_call(functools.partial(attend_kernel, k, n, tokens, D), out_sha...  39.4 us
    pallas_call x10, Pallas kernels, body(): pl.pallas_call(functools.partial(project_kernel, k, n, tokens, parts, poo...  22.3 us
    gather x1, local copies, waits for them, and re-layouts, embed(): picked = jnp.take(emb_table, jnp.clip(local, 0, vocab - 1), axis=0)  13.2 us
    unnamed x74, local copies, waits for them, and re-layouts  9.65 us
  transfers between devices with their start and end apart: 68, of which 59 were waited for; matrix products, arithmetic and copies ran while one was open for 8% of the time, Pallas kernels for 1%

profile of v9, /device:TPU:0, one launch (start us, length us, event | category | flops | bytes accessed | tf_op | source)
XLA Modules:
  0.0 459.8 jit_solution(12315854495909031673)
XLA Ops:
  1.5 3.0 collective-permute-start
  4.6 2.6 collective-permute-start.1
  8.5 4.0 dynamic-slice_bitcast_fusion.2
  12.5 2.6 dynamic-slice_bitcast_fusion
  19.3 2.8 collective-permute-start.8
  22.1 2.3 collective-permute-start.9
  24.5 13.2 %gather_fusion.1 = bf16[512,2048]{1,0:T(8,128)(2,1)} fusion(bf16[4096,2048]{1,0:T(8,128)(2,1)} %param.12, s32[1024]{0:T(1024)S(1)} %pad_clamp_fusion), kind=kCustom, calls=%fused_computation.1 | custom fusion | bytes 4196352 | tf_op jit(solution)/shard_map/jit(_take)/gather | solution.py:213
  44.0 44.7 %collective-permute-done.8.refs_0_ = bf16[1024,1536]{1,0:T(8,128)(2,1)S(1)} collective-permute-done((bf16[1024,1536]{1,0:T(8,128)(2,1)}, bf16[1024,1536]{1,0:T(8,128)(2,1)S(1)}, u32[]{:S(2)}, u32[]{:S(2)}) %collective-permute-start.8) | collective-permute-done | bytes 3145760 | tf_op jit(solution)/shard_map/ppermute | solution.py:170
  88.7 7.2 %collective-permute-start.10 = (bf16[1024,1536]{1,0:T(8,128)(2,1)}, bf16[1024,1536]{1,0:T(8,128)(2,1)}, u32[]{:S(2)}, u32[]{:S(2)}) collective-permute-start(bf16[1024,1536]{1,0:T(8,128)(2,1)} %pad_maximum_fusion.1), channel_id=1, source_target_pairs={{3,1},{0,2},{7,5},{4,6},{11,9},{8,10},{15,13},{12,14},{19,17},{16,... | collective-permute-start | bytes 9437192 | tf_op jit(solution)/shard_map/ppermute | solution.py:170
  108.6 51.7 %collective-permute-done.10.refs_2_ = bf16[1024,1536]{1,0:T(8,128)(2,1)} collective-permute-done((bf16[1024,1536]{1,0:T(8,128)(2,1)}, bf16[1024,1536]{1,0:T(8,128)(2,1)}, u32[]{:S(2)}, u32[]{:S(2)}) %collective-permute-start.10) | collective-permute-done | bytes 3145760 | tf_op jit(solution)/shard_map/ppermute | solution.py:170
  160.3 3.2 shard_map.100
  163.7 3.5 shard_map.101
  174.3 2.1 shard_map.102
  178.2 5.2 %collective-permute-done.15.refs_1_ = bf16[96,2048]{1,0:T(8,128)(2,1)S(1)} collective-permute-done((bf16[96,2048]{1,0:T(8,128)(2,1)S(1)}, bf16[96,2048]{1,0:T(8,128)(2,1)S(1)}, u32[]{:S(2)}, u32[]{:S(2)}) %collective-permute-start.15) | collective-permute-done | bytes 393248 | tf_op jit(solution)/shard_map/ppermute | solution.py:170
  183.4 3.5 shard_map.103
  189.1 3.6 collective-permute-done.16.refs_1_
  196.7 2.1 shard_map.104
  199.1 7.0 %collective-permute-done.19.refs_0_ = bf16[96,2048]{1,0:T(8,128)(2,1)S(1)} collective-permute-done((bf16[96,2048]{1,0:T(8,128)(2,1)S(1)}, bf16[96,2048]{1,0:T(8,128)(2,1)S(1)}, u32[]{:S(2)}, u32[]{:S(2)}) %collective-permute-start.19) | collective-permute-done | bytes 393248 | tf_op jit(solution)/shard_map/ppermute | solution.py:170
  206.1 3.6 collective-permute-done.20.refs_1_
  209.7 3.5 shard_map.105
  215.9 3.1 collective-permute-done.21.refs_1_
  223.2 2.1 shard_map.106
  226.9 5.8 %collective-permute-done.24.refs_0_ = bf16[96,2048]{1,0:T(8,128)(2,1)S(1)} collective-permute-done((bf16[96,2048]{1,0:T(8,128)(2,1)S(1)}, bf16[96,2048]{1,0:T(8,128)(2,1)S(1)}, u32[]{:S(2)}, u32[]{:S(2)}) %collective-permute-start.24) | collective-permute-done | bytes 393248 | tf_op jit(solution)/shard_map/ppermute | solution.py:170
  232.8 4.1 collective-permute-done.25.refs_1_
  236.8 3.5 shard_map.107
  243.8 2.2 collective-permute-done.26.refs_1_
  249.9 2.1 shard_map.108
  253.8 5.4 %collective-permute-done.29.refs_0_ = bf16[96,2048]{1,0:T(8,128)(2,1)S(1)} collective-permute-done((bf16[96,2048]{1,0:T(8,128)(2,1)S(1)}, bf16[96,2048]{1,0:T(8,128)(2,1)S(1)}, u32[]{:S(2)}, u32[]{:S(2)}) %collective-permute-start.29) | collective-permute-done | bytes 393248 | tf_op jit(solution)/shard_map/ppermute | solution.py:170
  259.3 5.1 %collective-permute-done.30.refs_1_ = bf16[96,2048]{1,0:T(8,128)(2,1)S(1)} collective-permute-done((bf16[96,2048]{1,0:T(8,128)(2,1)S(1)}, bf16[96,2048]{1,0:T(8,128)(2,1)S(1)}, u32[]{:S(2)}, u32[]{:S(2)}) %collective-permute-start.30) | collective-permute-done | bytes 393248 | tf_op jit(solution)/shard_map/ppermute | solution.py:170
  264.4 3.5 shard_map.109
  270.7 2.9 collective-permute-done.31.refs_1_
  277.8 2.2 shard_map.110
  281.5 5.8 %collective-permute-done.34.refs_0_ = bf16[96,2048]{1,0:T(8,128)(2,1)S(1)} collective-permute-done((bf16[96,2048]{1,0:T(8,128)(2,1)S(1)}, bf16[96,2048]{1,0:T(8,128)(2,1)S(1)}, u32[]{:S(2)}, u32[]{:S(2)}) %collective-permute-start.34) | collective-permute-done | bytes 393248 | tf_op jit(solution)/shard_map/ppermute | solution.py:170
  287.3 4.1 collective-permute-done.35.refs_1_
  291.4 3.5 shard_map.111
  298.3 2.2 collective-permute-done.36.refs_1_
  304.4 2.2 shard_map.112
  308.6 5.3 %collective-permute-done.39.refs_0_ = bf16[96,2048]{1,0:T(8,128)(2,1)S(1)} collective-permute-done((bf16[96,2048]{1,0:T(8,128)(2,1)S(1)}, bf16[96,2048]{1,0:T(8,128)(2,1)S(1)}, u32[]{:S(2)}, u32[]{:S(2)}) %collective-permute-start.39) | collective-permute-done | bytes 393248 | tf_op jit(solution)/shard_map/ppermute | solution.py:170
  313.9 5.1 %collective-permute-done.40.refs_1_ = bf16[96,2048]{1,0:T(8,128)(2,1)S(1)} collective-permute-done((bf16[96,2048]{1,0:T(8,128)(2,1)S(1)}, bf16[96,2048]{1,0:T(8,128)(2,1)S(1)}, u32[]{:S(2)}, u32[]{:S(2)}) %collective-permute-start.40) | collective-permute-done | bytes 393248 | tf_op jit(solution)/shard_map/ppermute | solution.py:170
  319.0 3.5 shard_map.113
  325.3 2.8 collective-permute-done.41.refs_1_
  328.1 2.1 collective-permute-done.42.refs_2_
  332.3 2.2 shard_map.114
  336.8 5.5 %collective-permute-done.44.refs_0_ = bf16[96,2048]{1,0:T(8,128)(2,1)S(1)} collective-permute-done((bf16[96,2048]{1,0:T(8,128)(2,1)S(1)}, bf16[96,2048]{1,0:T(8,128)(2,1)S(1)}, u32[]{:S(2)}, u32[]{:S(2)}) %collective-permute-start.44) | collective-permute-done | bytes 393248 | tf_op jit(solution)/shard_map/ppermute | solution.py:170
  342.3 4.4 collective-permute-done.45.refs_1_
  346.7 4.2 shard_map.115
  355.0 2.5 collective-permute-done.46.refs_1_
  361.5 3.4 copy-done
  365.9 2.7 shard_map.116
  370.4 5.4 %collective-permute-done.49.refs_0_ = bf16[96,2048]{1,0:T(8,128)(2,1)S(1)} collective-permute-done((bf16[96,2048]{1,0:T(8,128)(2,1)S(1)}, bf16[96,2048]{1,0:T(8,128)(2,1)S(1)}, u32[]{:S(2)}, u32[]{:S(2)}) %collective-permute-start.49) | collective-permute-done | bytes 393248 | tf_op jit(solution)/shard_map/ppermute | solution.py:170
  375.8 5.1 %collective-permute-done.50.refs_1_ = bf16[96,2048]{1,0:T(8,128)(2,1)S(1)} collective-permute-done((bf16[96,2048]{1,0:T(8,128)(2,1)S(1)}, bf16[96,2048]{1,0:T(8,128)(2,1)S(1)}, u32[]{:S(2)}, u32[]{:S(2)}) %collective-permute-start.50) | collective-permute-done | bytes 393248 | tf_op jit(solution)/shard_map/ppermute | solution.py:170
  384.7 3.5 shard_map.117
  391.1 2.8 collective-permute-done.51.refs_1_
  397.9 2.2 shard_map.118
  402.1 5.2 %collective-permute-done.54.refs_0_ = bf16[96,2048]{1,0:T(8,128)(2,1)S(1)} collective-permute-done((bf16[96,2048]{1,0:T(8,128)(2,1)S(1)}, bf16[96,2048]{1,0:T(8,128)(2,1)S(1)}, u32[]{:S(2)}, u32[]{:S(2)}) %collective-permute-start.54) | collective-permute-done | bytes 393248 | tf_op jit(solution)/shard_map/ppermute | solution.py:170
  407.3 4.4 collective-permute-done.55.refs_1_
  411.8 3.5 shard_map.119
  418.7 2.3 collective-permute-done.56.refs_1_
  425.1 2.2 shard_map.120
  429.6 3.5 shard_map.121
  433.1 5.2 %collective-permute-start.61 = (bf16[96,512]{1,0:T(8,128)(2,1)S(1)}, bf16[96,512]{1,0:T(8,128)(2,1)S(1)}, u32[]{:S(2)}, u32[]{:S(2)}) collective-permute-start(bf16[96,512]{1,0:T(8,128)(2,1)S(1)} %get-tuple-element.90), channel_id=1, source_target_pairs={{0,16},{1,5},{2,6},{3,19},{4,20},{5,1},{6,2},{7,23},{8,24},{9,13},... | collective-permute-start | bytes 294920 | tf_op jit(solution)/shard_map/ppermute | solution.py:170
  441.1 2.7 collective-permute-done.62
  445.9 3.0 shard_map.122
  454.2 4.5 collective-permute-done.67
  (217 shorter events, 126.9 us)
Async XLA Ops:
  1.5 17.4 %collective-permute-start = (s32[2,2,33]{2,1,0:T(2,128)S(1)}, s32[2,2,33]{2,1,0:T(2,128)S(1)}, u32[]{:S(2)}, u32[]{:S(2)}) collective-permute-start(s32[2,2,33]{2,1,0:T(2,128)S(1)} %pad_add_fusion.1), channel_id=1, source_target_pairs={{0,1},{1,2},{2,3},{3,0},{4,5},{5,6},{6,7},{7,4},{8,9},{9,10},{10,1... | collective-permute-start | bytes 1592 | tf_op jit(solution)/shard_map/ppermute | solution.py:170
  4.6 14.4 %collective-permute-start.1 = (s32[2,2,33]{2,1,0:T(2,128)S(1)}, s32[2,2,33]{2,1,0:T(2,128)S(1)}, u32[]{:S(2)}, u32[]{:S(2)}) collective-permute-start(s32[2,2,33]{2,1,0:T(2,128)S(1)} %pad_add_fusion.1), channel_id=1, source_target_pairs={{0,2},{1,3},{2,0},{3,1},{4,6},{5,7},{6,4},{7,5},{8,10},{9,11},{10,... | collective-permute-start | bytes 1592 | tf_op jit(solution)/shard_map/ppermute | solution.py:170
  7.1 11.8 %collective-permute-start.2 = (s32[2,2,33]{2,1,0:T(2,128)S(1)}, s32[2,2,33]{2,1,0:T(2,128)S(1)}, u32[]{:S(2)}, u32[]{:S(2)}) collective-permute-start(s32[2,2,33]{2,1,0:T(2,128)S(1)} %pad_add_fusion.1), channel_id=1, source_target_pairs={{0,3},{1,0},{2,1},{3,2},{4,7},{5,4},{6,5},{7,6},{8,11},{9,8},{10,9... | collective-permute-start | bytes 1592 | tf_op jit(solution)/shard_map/ppermute | solution.py:170
  19.3 69.4 %collective-permute-start.8 = (bf16[1024,1536]{1,0:T(8,128)(2,1)}, bf16[1024,1536]{1,0:T(8,128)(2,1)S(1)}, u32[]{:S(2)}, u32[]{:S(2)}) collective-permute-start(bf16[1024,1536]{1,0:T(8,128)(2,1)} %pad_maximum_fusion.2), channel_id=1, source_target_pairs={{0,1},{3,2},{4,5},{7,6},{8,9},{11,10},{12,13},{15,14},{16,17},{19,... | collective-permute-start | bytes 9437192 | tf_op jit(solution)/shard_map/ppermute | solution.py:170
  22.1 66.6 %collective-permute-start.9 = (bf16[1024,1536]{1,0:T(8,128)(2,1)}, bf16[1024,1536]{1,0:T(8,128)(2,1)}, u32[]{:S(2)}, u32[]{:S(2)}) collective-permute-start(bf16[1024,1536]{1,0:T(8,128)(2,1)} %pad_maximum_fusion.3), channel_id=1, source_target_pairs={{2,1},{1,2},{6,5},{5,6},{10,9},{9,10},{14,13},{13,14},{18,17},{17,... | collective-permute-start | bytes 9437192 | tf_op jit(solution)/shard_map/ppermute | solution.py:170
  39.8 56.1 %collective-permute-start.3 = (bf16[512,2048]{1,0:T(8,128)(2,1)S(1)}, bf16[512,2048]{1,0:T(8,128)(2,1)S(1)}, u32[]{:S(2)}, u32[]{:S(2)}) collective-permute-start(bf16[512,2048]{1,0:T(8,128)(2,1)S(1)} %select_select_fusion), channel_id=1, source_target_pairs={{9,1},{10,2},{13,5},{14,6}} | collective-permute-start | bytes 6291464 | tf_op jit(solution)/shard_map/ppermute | solution.py:170
  40.6 55.3 %collective-permute-start.4 = (bf16[512,2048]{1,0:T(8,128)(2,1)S(1)}, bf16[512,2048]{1,0:T(8,128)(2,1)S(1)}, u32[]{:S(2)}, u32[]{:S(2)}) collective-permute-start(bf16[512,2048]{1,0:T(8,128)(2,1)S(1)} %select_select_fusion), channel_id=1, source_target_pairs={{17,1},{18,2},{21,5},{22,6}} | collective-permute-start | bytes 6291464 | tf_op jit(solution)/shard_map/ppermute | solution.py:170
  41.4 54.5 %collective-permute-start.5 = (bf16[512,2048]{1,0:T(8,128)(2,1)S(1)}, bf16[512,2048]{1,0:T(8,128)(2,1)S(1)}, u32[]{:S(2)}, u32[]{:S(2)}) collective-permute-start(bf16[512,2048]{1,0:T(8,128)(2,1)S(1)} %select_select_fusion), channel_id=1, source_target_pairs={{25,1},{26,2},{29,5},{30,6}} | collective-permute-start | bytes 6291464 | tf_op jit(solution)/shard_map/ppermute | solution.py:170
  88.7 71.6 %collective-permute-start.10 = (bf16[1024,1536]{1,0:T(8,128)(2,1)}, bf16[1024,1536]{1,0:T(8,128)(2,1)}, u32[]{:S(2)}, u32[]{:S(2)}) collective-permute-start(bf16[1024,1536]{1,0:T(8,128)(2,1)} %pad_maximum_fusion.1), channel_id=1, source_target_pairs={{3,1},{0,2},{7,5},{4,6},{11,9},{8,10},{15,13},{12,14},{19,17},{16,... | collective-permute-start | bytes 9437192 | tf_op jit(solution)/shard_map/ppermute | solution.py:170
  98.0 8.8 %collective-permute-start.6 = (bf16[512,2048]{1,0:T(8,128)(2,1)}, bf16[512,2048]{1,0:T(8,128)(2,1)}, u32[]{:S(2)}, u32[]{:S(2)}) collective-permute-start(bf16[512,2048]{1,0:T(8,128)(2,1)} %add_add_fusion), channel_id=1, source_target_pairs={{1,5},{2,6},{5,1},{6,2}} | collective-permute-start | bytes 6291464 | tf_op jit(solution)/shard_map/ppermute | solution.py:170
  100.0 63.6 %collective-permute-start.7 = (bf16[16,2048]{1,0:T(8,128)(2,1)S(1)}, bf16[16,2048]{1,0:T(8,128)(2,1)S(1)}, u32[]{:S(2)}, u32[]{:S(2)}) collective-permute-start(bf16[16,2048]{1,0:T(8,128)(2,1)S(1)} %copy-done.8), channel_id=1, source_target_pairs={{1,5},{2,6},{5,1},{6,2}} | collective-permute-start | bytes 196616 | tf_op jit(solution)/shard_map/ppermute | solution.py:170
  167.2 4.7 %collective-permute-start.11 = (bf16[96,512]{1,0:T(8,128)(2,1)S(1)}, bf16[96,512]{1,0:T(8,128)(2,1)S(1)}, u32[]{:S(2)}, u32[]{:S(2)}) collective-permute-start(bf16[96,512]{1,0:T(8,128)(2,1)S(1)} %get-tuple-element.58.refs_0_), channel_id=1, source_target_pairs={{0,16},{1,5},{2,6},{3,19},{4,20},{5,1},{6,2},{7,23},{8,24},{9,13},... | collective-permute-start | bytes 294920 | tf_op jit(solution)/shard_map/ppermute | solution.py:170
  168.6 4.6 %collective-permute-start.12 = (bf16[96,512]{1,0:T(8,128)(2,1)S(1)}, bf16[96,512]{1,0:T(8,128)(2,1)S(1)}, u32[]{:S(2)}, u32[]{:S(2)}) collective-permute-start(bf16[96,512]{1,0:T(8,128)(2,1)S(1)} %get-tuple-element.58.refs_0_), channel_id=1, source_target_pairs={{0,16},{1,2},{2,1},{3,19},{4,20},{5,6},{6,5},{7,23},{8,24},{9,10},... | collective-permute-start | bytes 294920 | tf_op jit(solution)/shard_map/ppermute | solution.py:170
  169.3 5.0 %collective-permute-start.13 = (bf16[96,512]{1,0:T(8,128)(2,1)S(1)}, bf16[96,512]{1,0:T(8,128)(2,1)S(1)}, u32[]{:S(2)}, u32[]{:S(2)}) collective-permute-start(bf16[96,512]{1,0:T(8,128)(2,1)S(1)} %get-tuple-element.58.refs_0_), channel_id=1, source_target_pairs={{0,16},{1,6},{2,5},{3,19},{4,20},{5,2},{6,1},{7,23},{8,24},{9,14},... | collective-permute-start | bytes 294920 | tf_op jit(solution)/shard_map/ppermute | solution.py:170
  176.5 6.9 %collective-permute-start.15 = (bf16[96,2048]{1,0:T(8,128)(2,1)S(1)}, bf16[96,2048]{1,0:T(8,128)(2,1)S(1)}, u32[]{:S(2)}, u32[]{:S(2)}) collective-permute-start(bf16[96,2048]{1,0:T(8,128)(2,1)S(1)} %shard_map.102), channel_id=1, source_target_pairs={{0,12},{1,13},{2,14},{3,15},{4,8},{5,9},{6,10},{7,11},{8,0},{9,1},... | collective-permute-start | bytes 1179656 | tf_op jit(solution)/shard_map/ppermute | solution.py:170
  186.9 5.7 %collective-permute-start.16 = (bf16[96,512]{1,0:T(8,128)(2,1)S(1)}, bf16[96,512]{1,0:T(8,128)(2,1)S(1)}, u32[]{:S(2)}, u32[]{:S(2)}) collective-permute-start(bf16[96,512]{1,0:T(8,128)(2,1)S(1)} %get-tuple-element.60.refs_0_), channel_id=1, source_target_pairs={{0,16},{1,5},{2,6},{3,19},{4,20},{5,1},{6,2},{7,23},{8,24},{9,13},... | collective-permute-start | bytes 294920 | tf_op jit(solution)/shard_map/ppermute | solution.py:170
  187.0 7.8 %collective-permute-start.17 = (bf16[96,512]{1,0:T(8,128)(2,1)S(1)}, bf16[96,512]{1,0:T(8,128)(2,1)S(1)}, u32[]{:S(2)}, u32[]{:S(2)}) collective-permute-start(bf16[96,512]{1,0:T(8,128)(2,1)S(1)} %get-tuple-element.60.refs_0_), channel_id=1, source_target_pairs={{0,16},{1,2},{2,1},{3,19},{4,20},{5,6},{6,5},{7,23},{8,24},{9,10},... | collective-permute-start | bytes 294920 | tf_op jit(solution)/shard_map/ppermute | solution.py:170
  189.0 7.7 %collective-permute-start.18 = (bf16[96,512]{1,0:T(8,128)(2,1)S(1)}, bf16[96,512]{1,0:T(8,128)(2,1)S(1)}, u32[]{:S(2)}, u32[]{:S(2)}) collective-permute-start(bf16[96,512]{1,0:T(8,128)(2,1)S(1)} %get-tuple-element.60.refs_0_), channel_id=1, source_target_pairs={{0,16},{1,6},{2,5},{3,19},{4,20},{5,2},{6,1},{7,23},{8,24},{9,14},... | collective-permute-start | bytes 294920 | tf_op jit(solution)/shard_map/ppermute | solution.py:170
  198.8 7.3 %collective-permute-start.19 = (bf16[96,2048]{1,0:T(8,128)(2,1)S(1)}, bf16[96,2048]{1,0:T(8,128)(2,1)S(1)}, u32[]{:S(2)}, u32[]{:S(2)}) collective-permute-start(bf16[96,2048]{1,0:T(8,128)(2,1)S(1)} %shard_map.104), channel_id=1, source_target_pairs={{0,8},{1,9},{2,10},{3,11},{4,12},{5,13},{6,14},{7,15},{8,16},{9,17... | collective-permute-start | bytes 1179656 | tf_op jit(solution)/shard_map/ppermute | solution.py:170
  198.9 10.8 %collective-permute-start.20 = (bf16[96,2048]{1,0:T(8,128)(2,1)S(1)}, bf16[96,2048]{1,0:T(8,128)(2,1)S(1)}, u32[]{:S(2)}, u32[]{:S(2)}) collective-permute-start(bf16[96,2048]{1,0:T(8,128)(2,1)S(1)} %shard_map.104), channel_id=1, source_target_pairs={{0,12},{1,13},{2,14},{3,15},{4,8},{5,9},{6,10},{7,11},{8,20},{9,21... | collective-permute-start | bytes 1179656 | tf_op jit(solution)/shard_map/ppermute | solution.py:170
  213.3 5.7 %collective-permute-start.21 = (bf16[96,512]{1,0:T(8,128)(2,1)S(1)}, bf16[96,512]{1,0:T(8,128)(2,1)S(1)}, u32[]{:S(2)}, u32[]{:S(2)}) collective-permute-start(bf16[96,512]{1,0:T(8,128)(2,1)S(1)} %get-tuple-element.62.refs_0_), channel_id=1, source_target_pairs={{0,16},{1,5},{2,6},{3,19},{4,20},{5,1},{6,2},{7,23},{8,24},{9,13},... | collective-permute-start | bytes 294920 | tf_op jit(solution)/shard_map/ppermute | solution.py:170
  213.8 7.3 %collective-permute-start.22 = (bf16[96,512]{1,0:T(8,128)(2,1)S(1)}, bf16[96,512]{1,0:T(8,128)(2,1)S(1)}, u32[]{:S(2)}, u32[]{:S(2)}) collective-permute-start(bf16[96,512]{1,0:T(8,128)(2,1)S(1)} %get-tuple-element.62.refs_0_), channel_id=1, source_target_pairs={{0,16},{1,2},{2,1},{3,19},{4,20},{5,6},{6,5},{7,23},{8,24},{9,10},... | collective-permute-start | bytes 294920 | tf_op jit(solution)/shard_map/ppermute | solution.py:170
  215.3 7.8 %collective-permute-start.23 = (bf16[96,512]{1,0:T(8,128)(2,1)S(1)}, bf16[96,512]{1,0:T(8,128)(2,1)S(1)}, u32[]{:S(2)}, u32[]{:S(2)}) collective-permute-start(bf16[96,512]{1,0:T(8,128)(2,1)S(1)} %get-tuple-element.62.refs_0_), channel_id=1, source_target_pairs={{0,16},{1,6},{2,5},{3,19},{4,20},{5,2},{6,1},{7,23},{8,24},{9,14},... | collective-permute-start | bytes 294920 | tf_op jit(solution)/shard_map/ppermute | solution.py:170
  225.3 7.4 %collective-permute-start.24 = (bf16[96,2048]{1,0:T(8,128)(2,1)S(1)}, bf16[96,2048]{1,0:T(8,128)(2,1)S(1)}, u32[]{:S(2)}, u32[]{:S(2)}) collective-permute-start(bf16[96,2048]{1,0:T(8,128)(2,1)S(1)} %shard_map.106), channel_id=1, source_target_pairs={{0,8},{1,9},{2,10},{3,11},{4,12},{5,13},{6,14},{7,15},{8,16},{9,17... | collective-permute-start | bytes 1179656 | tf_op jit(solution)/shard_map/ppermute | solution.py:170
  225.7 11.2 %collective-permute-start.25 = (bf16[96,2048]{1,0:T(8,128)(2,1)S(1)}, bf16[96,2048]{1,0:T(8,128)(2,1)S(1)}, u32[]{:S(2)}, u32[]{:S(2)}) collective-permute-start(bf16[96,2048]{1,0:T(8,128)(2,1)S(1)} %shard_map.106), channel_id=1, source_target_pairs={{0,12},{1,13},{2,14},{3,15},{4,8},{5,9},{6,10},{7,11},{8,20},{9,21... | collective-permute-start | bytes 1179656 | tf_op jit(solution)/shard_map/ppermute | solution.py:170
  240.3 5.7 %collective-permute-start.26 = (bf16[96,512]{1,0:T(8,128)(2,1)S(1)}, bf16[96,512]{1,0:T(8,128)(2,1)S(1)}, u32[]{:S(2)}, u32[]{:S(2)}) collective-permute-start(bf16[96,512]{1,0:T(8,128)(2,1)S(1)} %get-tuple-element.64.refs_0_), channel_id=1, source_target_pairs={{0,16},{1,5},{2,6},{3,19},{4,20},{5,1},{6,2},{7,23},{8,24},{9,13},... | collective-permute-start | bytes 294920 | tf_op jit(solution)/shard_map/ppermute | solution.py:170
  241.7 6.4 %collective-permute-start.27 = (bf16[96,512]{1,0:T(8,128)(2,1)S(1)}, bf16[96,512]{1,0:T(8,128)(2,1)S(1)}, u32[]{:S(2)}, u32[]{:S(2)}) collective-permute-start(bf16[96,512]{1,0:T(8,128)(2,1)S(1)} %get-tuple-element.64.refs_0_), channel_id=1, source_target_pairs={{0,16},{1,2},{2,1},{3,19},{4,20},{5,6},{6,5},{7,23},{8,24},{9,10},... | collective-permute-start | bytes 294920 | tf_op jit(solution)/shard_map/ppermute | solution.py:170
  242.4 7.4 %collective-permute-start.28 = (bf16[96,512]{1,0:T(8,128)(2,1)S(1)}, bf16[96,512]{1,0:T(8,128)(2,1)S(1)}, u32[]{:S(2)}, u32[]{:S(2)}) collective-permute-start(bf16[96,512]{1,0:T(8,128)(2,1)S(1)} %get-tuple-element.64.refs_0_), channel_id=1, source_target_pairs={{0,16},{1,6},{2,5},{3,19},{4,20},{5,2},{6,1},{7,23},{8,24},{9,14},... | collective-permute-start | bytes 294920 | tf_op jit(solution)/shard_map/ppermute | solution.py:170
  252.0 7.3 %collective-permute-start.29 = (bf16[96,2048]{1,0:T(8,128)(2,1)S(1)}, bf16[96,2048]{1,0:T(8,128)(2,1)S(1)}, u32[]{:S(2)}, u32[]{:S(2)}) collective-permute-start(bf16[96,2048]{1,0:T(8,128)(2,1)S(1)} %shard_map.108), channel_id=1, source_target_pairs={{0,8},{1,9},{2,10},{3,11},{4,12},{5,13},{6,14},{7,15},{8,16},{9,17... | collective-permute-start | bytes 1179656 | tf_op jit(solution)/shard_map/ppermute | solution.py:170
  252.1 12.3 %collective-permute-start.30 = (bf16[96,2048]{1,0:T(8,128)(2,1)S(1)}, bf16[96,2048]{1,0:T(8,128)(2,1)S(1)}, u32[]{:S(2)}, u32[]{:S(2)}) collective-permute-start(bf16[96,2048]{1,0:T(8,128)(2,1)S(1)} %shard_map.108), channel_id=1, source_target_pairs={{0,12},{1,13},{2,14},{3,15},{4,8},{5,9},{6,10},{7,11},{8,20},{9,21... | collective-permute-start | bytes 1179656 | tf_op jit(solution)/shard_map/ppermute | solution.py:170
  267.9 5.7 %collective-permute-start.31 = (bf16[96,512]{1,0:T(8,128)(2,1)S(1)}, bf16[96,512]{1,0:T(8,128)(2,1)S(1)}, u32[]{:S(2)}, u32[]{:S(2)}) collective-permute-start(bf16[96,512]{1,0:T(8,128)(2,1)S(1)} %get-tuple-element.66.refs_0_), channel_id=1, source_target_pairs={{0,16},{1,5},{2,6},{3,19},{4,20},{5,1},{6,2},{7,23},{8,24},{9,13},... | collective-permute-start | bytes 294920 | tf_op jit(solution)/shard_map/ppermute | solution.py:170
  268.7 7.1 %collective-permute-start.32 = (bf16[96,512]{1,0:T(8,128)(2,1)S(1)}, bf16[96,512]{1,0:T(8,128)(2,1)S(1)}, u32[]{:S(2)}, u32[]{:S(2)}) collective-permute-start(bf16[96,512]{1,0:T(8,128)(2,1)S(1)} %get-tuple-element.66.refs_0_), channel_id=1, source_target_pairs={{0,16},{1,2},{2,1},{3,19},{4,20},{5,6},{6,5},{7,23},{8,24},{9,10},... | collective-permute-start | bytes 294920 | tf_op jit(solution)/shard_map/ppermute | solution.py:170
  270.0 7.8 %collective-permute-start.33 = (bf16[96,512]{1,0:T(8,128)(2,1)S(1)}, bf16[96,512]{1,0:T(8,128)(2,1)S(1)}, u32[]{:S(2)}, u32[]{:S(2)}) collective-permute-start(bf16[96,512]{1,0:T(8,128)(2,1)S(1)} %get-tuple-element.66.refs_0_), channel_id=1, source_target_pairs={{0,16},{1,6},{2,5},{3,19},{4,20},{5,2},{6,1},{7,23},{8,24},{9,14},... | collective-permute-start | bytes 294920 | tf_op jit(solution)/shard_map/ppermute | solution.py:170
  280.1 7.3 %collective-permute-start.34 = (bf16[96,2048]{1,0:T(8,128)(2,1)S(1)}, bf16[96,2048]{1,0:T(8,128)(2,1)S(1)}, u32[]{:S(2)}, u32[]{:S(2)}) collective-permute-start(bf16[96,2048]{1,0:T(8,128)(2,1)S(1)} %get-tuple-element.69), channel_id=1, source_target_pairs={{0,8},{1,9},{2,10},{3,11},{4,12},{5,13},{6,14},{7,15},{8,16},{9,17... | collective-permute-start | bytes 1179656 | tf_op jit(solution)/shard_map/ppermute | solution.py:170
  280.2 11.1 %collective-permute-start.35 = (bf16[96,2048]{1,0:T(8,128)(2,1)S(1)}, bf16[96,2048]{1,0:T(8,128)(2,1)S(1)}, u32[]{:S(2)}, u32[]{:S(2)}) collective-permute-start(bf16[96,2048]{1,0:T(8,128)(2,1)S(1)} %get-tuple-element.69), channel_id=1, source_target_pairs={{0,12},{1,13},{2,14},{3,15},{4,8},{5,9},{6,10},{7,11},{8,20},{9,21... | collective-permute-start | bytes 1179656 | tf_op jit(solution)/shard_map/ppermute | solution.py:170
  294.9 5.6 %collective-permute-start.36 = (bf16[96,512]{1,0:T(8,128)(2,1)S(1)}, bf16[96,512]{1,0:T(8,128)(2,1)S(1)}, u32[]{:S(2)}, u32[]{:S(2)}) collective-permute-start(bf16[96,512]{1,0:T(8,128)(2,1)S(1)} %get-tuple-element.70.refs_0_), channel_id=1, source_target_pairs={{0,16},{1,5},{2,6},{3,19},{4,20},{5,1},{6,2},{7,23},{8,24},{9,13},... | collective-permute-start | bytes 294920 | tf_op jit(solution)/shard_map/ppermute | solution.py:170
  296.3 6.4 %collective-permute-start.37 = (bf16[96,512]{1,0:T(8,128)(2,1)S(1)}, bf16[96,512]{1,0:T(8,128)(2,1)S(1)}, u32[]{:S(2)}, u32[]{:S(2)}) collective-permute-start(bf16[96,512]{1,0:T(8,128)(2,1)S(1)} %get-tuple-element.70.refs_0_), channel_id=1, source_target_pairs={{0,16},{1,2},{2,1},{3,19},{4,20},{5,6},{6,5},{7,23},{8,24},{9,10},... | collective-permute-start | bytes 294920 | tf_op jit(solution)/shard_map/ppermute | solution.py:170
  297.0 7.4 %collective-permute-start.38 = (bf16[96,512]{1,0:T(8,128)(2,1)S(1)}, bf16[96,512]{1,0:T(8,128)(2,1)S(1)}, u32[]{:S(2)}, u32[]{:S(2)}) collective-permute-start(bf16[96,512]{1,0:T(8,128)(2,1)S(1)} %get-tuple-element.70.refs_0_), channel_id=1, source_target_pairs={{0,16},{1,6},{2,5},{3,19},{4,20},{5,2},{6,1},{7,23},{8,24},{9,14},... | collective-permute-start | bytes 294920 | tf_op jit(solution)/shard_map/ppermute | solution.py:170
  306.6 7.3 %collective-permute-start.39 = (bf16[96,2048]{1,0:T(8,128)(2,1)S(1)}, bf16[96,2048]{1,0:T(8,128)(2,1)S(1)}, u32[]{:S(2)}, u32[]{:S(2)}) collective-permute-start(bf16[96,2048]{1,0:T(8,128)(2,1)S(1)} %get-tuple-element.73), channel_id=1, source_target_pairs={{0,8},{1,9},{2,10},{3,11},{4,12},{5,13},{6,14},{7,15},{8,16},{9,17... | collective-permute-start | bytes 1179656 | tf_op jit(solution)/shard_map/ppermute | solution.py:170
  306.7 12.3 %collective-permute-start.40 = (bf16[96,2048]{1,0:T(8,128)(2,1)S(1)}, bf16[96,2048]{1,0:T(8,128)(2,1)S(1)}, u32[]{:S(2)}, u32[]{:S(2)}) collective-permute-start(bf16[96,2048]{1,0:T(8,128)(2,1)S(1)} %get-tuple-element.73), channel_id=1, source_target_pairs={{0,12},{1,13},{2,14},{3,15},{4,8},{5,9},{6,10},{7,11},{8,20},{9,21... | collective-permute-start | bytes 1179656 | tf_op jit(solution)/shard_map/ppermute | solution.py:170
  322.5 5.5 %collective-permute-start.41 = (bf16[96,512]{1,0:T(8,128)(2,1)S(1)}, bf16[96,512]{1,0:T(8,128)(2,1)S(1)}, u32[]{:S(2)}, u32[]{:S(2)}) collective-permute-start(bf16[96,512]{1,0:T(8,128)(2,1)S(1)} %get-tuple-element.74.refs_0_), channel_id=1, source_target_pairs={{0,16},{1,5},{2,6},{3,19},{4,20},{5,1},{6,2},{7,23},{8,24},{9,13},... | collective-permute-start | bytes 294920 | tf_op jit(solution)/shard_map/ppermute | solution.py:170
  323.3 6.9 %collective-permute-start.42 = (bf16[96,512]{1,0:T(8,128)(2,1)S(1)}, bf16[96,512]{1,0:T(8,128)(2,1)S(1)}, u32[]{:S(2)}, u32[]{:S(2)}) collective-permute-start(bf16[96,512]{1,0:T(8,128)(2,1)S(1)} %get-tuple-element.74.refs_0_), channel_id=1, source_target_pairs={{0,16},{1,2},{2,1},{3,19},{4,20},{5,6},{6,5},{7,23},{8,24},{9,10},... | collective-permute-start | bytes 294920 | tf_op jit(solution)/shard_map/ppermute | solution.py:170
  324.6 7.7 %collective-permute-start.43 = (bf16[96,512]{1,0:T(8,128)(2,1)S(1)}, bf16[96,512]{1,0:T(8,128)(2,1)S(1)}, u32[]{:S(2)}, u32[]{:S(2)}) collective-permute-start(bf16[96,512]{1,0:T(8,128)(2,1)S(1)} %get-tuple-element.74.refs_0_), channel_id=1, source_target_pairs={{0,16},{1,6},{2,5},{3,19},{4,20},{5,2},{6,1},{7,23},{8,24},{9,14},... | collective-permute-start | bytes 294920 | tf_op jit(solution)/shard_map/ppermute | solution.py:170
  335.1 7.2 %collective-permute-start.44 = (bf16[96,2048]{1,0:T(8,128)(2,1)S(1)}, bf16[96,2048]{1,0:T(8,128)(2,1)S(1)}, u32[]{:S(2)}, u32[]{:S(2)}) collective-permute-start(bf16[96,2048]{1,0:T(8,128)(2,1)S(1)} %get-tuple-element.77), channel_id=1, source_target_pairs={{0,8},{1,9},{2,10},{3,11},{4,12},{5,13},{6,14},{7,15},{8,16},{9,17... | collective-permute-start | bytes 1179656 | tf_op jit(solution)/shard_map/ppermute | solution.py:170
  335.2 11.5 %collective-permute-start.45 = (bf16[96,2048]{1,0:T(8,128)(2,1)S(1)}, bf16[96,2048]{1,0:T(8,128)(2,1)S(1)}, u32[]{:S(2)}, u32[]{:S(2)}) collective-permute-start(bf16[96,2048]{1,0:T(8,128)(2,1)S(1)} %get-tuple-element.77), channel_id=1, source_target_pairs={{0,12},{1,13},{2,14},{3,15},{4,8},{5,9},{6,10},{7,11},{8,20},{9,21... | collective-permute-start | bytes 1179656 | tf_op jit(solution)/shard_map/ppermute | solution.py:170
  351.7 5.9 %collective-permute-start.46 = (bf16[96,512]{1,0:T(8,128)(2,1)}, bf16[96,512]{1,0:T(8,128)(2,1)}, u32[]{:S(2)}, u32[]{:S(2)}) collective-permute-start(bf16[96,512]{1,0:T(8,128)(2,1)} %get-tuple-element.78.refs_0_), channel_id=1, source_target_pairs={{0,16},{1,5},{2,6},{3,19},{4,20},{5,1},{6,2},{7,23},{8,24},{9,13},... | collective-permute-start | bytes 294920 | tf_op jit(solution)/shard_map/ppermute | solution.py:170
  353.0 6.7 %collective-permute-start.47 = (bf16[96,512]{1,0:T(8,128)(2,1)}, bf16[96,512]{1,0:T(8,128)(2,1)}, u32[]{:S(2)}, u32[]{:S(2)}) collective-permute-start(bf16[96,512]{1,0:T(8,128)(2,1)} %get-tuple-element.78.refs_0_), channel_id=1, source_target_pairs={{0,16},{1,2},{2,1},{3,19},{4,20},{5,6},{6,5},{7,23},{8,24},{9,10},... | collective-permute-start | bytes 294920 | tf_op jit(solution)/shard_map/ppermute | solution.py:170
  353.7 7.8 %collective-permute-start.48 = (bf16[96,512]{1,0:T(8,128)(2,1)}, bf16[96,512]{1,0:T(8,128)(2,1)}, u32[]{:S(2)}, u32[]{:S(2)}) collective-permute-start(bf16[96,512]{1,0:T(8,128)(2,1)} %get-tuple-element.78.refs_0_), channel_id=1, source_target_pairs={{0,16},{1,6},{2,5},{3,19},{4,20},{5,2},{6,1},{7,23},{8,24},{9,14},... | collective-permute-start | bytes 294920 | tf_op jit(solution)/shard_map/ppermute | solution.py:170
  368.6 7.3 %collective-permute-start.49 = (bf16[96,2048]{1,0:T(8,128)(2,1)S(1)}, bf16[96,2048]{1,0:T(8,128)(2,1)S(1)}, u32[]{:S(2)}, u32[]{:S(2)}) collective-permute-start(bf16[96,2048]{1,0:T(8,128)(2,1)S(1)} %get-tuple-element.81), channel_id=1, source_target_pairs={{0,8},{1,9},{2,10},{3,11},{4,12},{5,13},{6,14},{7,15},{8,16},{9,17... | collective-permute-start | bytes 1179656 | tf_op jit(solution)/shard_map/ppermute | solution.py:170
  368.7 12.3 %collective-permute-start.50 = (bf16[96,2048]{1,0:T(8,128)(2,1)S(1)}, bf16[96,2048]{1,0:T(8,128)(2,1)S(1)}, u32[]{:S(2)}, u32[]{:S(2)}) collective-permute-start(bf16[96,2048]{1,0:T(8,128)(2,1)S(1)} %get-tuple-element.81), channel_id=1, source_target_pairs={{0,12},{1,13},{2,14},{3,15},{4,8},{5,9},{6,10},{7,11},{8,20},{9,21... | collective-permute-start | bytes 1179656 | tf_op jit(solution)/shard_map/ppermute | solution.py:170
  388.3 5.6 %collective-permute-start.51 = (bf16[96,512]{1,0:T(8,128)(2,1)S(1)}, bf16[96,512]{1,0:T(8,128)(2,1)S(1)}, u32[]{:S(2)}, u32[]{:S(2)}) collective-permute-start(bf16[96,512]{1,0:T(8,128)(2,1)S(1)} %get-tuple-element.82.refs_0_), channel_id=1, source_target_pairs={{0,16},{1,5},{2,6},{3,19},{4,20},{5,1},{6,2},{7,23},{8,24},{9,13},... | collective-permute-start | bytes 294920 | tf_op jit(solution)/shard_map/ppermute | solution.py:170
  389.0 7.0 %collective-permute-start.52 = (bf16[96,512]{1,0:T(8,128)(2,1)S(1)}, bf16[96,512]{1,0:T(8,128)(2,1)S(1)}, u32[]{:S(2)}, u32[]{:S(2)}) collective-permute-start(bf16[96,512]{1,0:T(8,128)(2,1)S(1)} %get-tuple-element.82.refs_0_), channel_id=1, source_target_pairs={{0,16},{1,2},{2,1},{3,19},{4,20},{5,6},{6,5},{7,23},{8,24},{9,10},... | collective-permute-start | bytes 294920 | tf_op jit(solution)/shard_map/ppermute | solution.py:170
  390.4 7.5 %collective-permute-start.53 = (bf16[96,512]{1,0:T(8,128)(2,1)S(1)}, bf16[96,512]{1,0:T(8,128)(2,1)S(1)}, u32[]{:S(2)}, u32[]{:S(2)}) collective-permute-start(bf16[96,512]{1,0:T(8,128)(2,1)S(1)} %get-tuple-element.82.refs_0_), channel_id=1, source_target_pairs={{0,16},{1,6},{2,5},{3,19},{4,20},{5,2},{6,1},{7,23},{8,24},{9,14},... | collective-permute-start | bytes 294920 | tf_op jit(solution)/shard_map/ppermute | solution.py:170
  400.1 7.3 %collective-permute-start.54 = (bf16[96,2048]{1,0:T(8,128)(2,1)S(1)}, bf16[96,2048]{1,0:T(8,128)(2,1)S(1)}, u32[]{:S(2)}, u32[]{:S(2)}) collective-permute-start(bf16[96,2048]{1,0:T(8,128)(2,1)S(1)} %get-tuple-element.85), channel_id=1, source_target_pairs={{0,8},{1,9},{2,10},{3,11},{4,12},{5,13},{6,14},{7,15},{8,16},{9,17... | collective-permute-start | bytes 1179656 | tf_op jit(solution)/shard_map/ppermute | solution.py:170
  400.1 11.6 %collective-permute-start.55 = (bf16[96,2048]{1,0:T(8,128)(2,1)S(1)}, bf16[96,2048]{1,0:T(8,128)(2,1)S(1)}, u32[]{:S(2)}, u32[]{:S(2)}) collective-permute-start(bf16[96,2048]{1,0:T(8,128)(2,1)S(1)} %get-tuple-element.85), channel_id=1, source_target_pairs={{0,12},{1,13},{2,14},{3,15},{4,8},{5,9},{6,10},{7,11},{8,20},{9,21... | collective-permute-start | bytes 1179656 | tf_op jit(solution)/shard_map/ppermute | solution.py:170
  415.3 5.7 %collective-permute-start.56 = (bf16[96,512]{1,0:T(8,128)(2,1)S(1)}, bf16[96,512]{1,0:T(8,128)(2,1)S(1)}, u32[]{:S(2)}, u32[]{:S(2)}) collective-permute-start(bf16[96,512]{1,0:T(8,128)(2,1)S(1)} %get-tuple-element.86.refs_0_), channel_id=1, source_target_pairs={{0,16},{1,5},{2,6},{3,19},{4,20},{5,1},{6,2},{7,23},{8,24},{9,13},... | collective-permute-start | bytes 294920 | tf_op jit(solution)/shard_map/ppermute | solution.py:170
  416.7 6.4 %collective-permute-start.57 = (bf16[96,512]{1,0:T(8,128)(2,1)S(1)}, bf16[96,512]{1,0:T(8,128)(2,1)S(1)}, u32[]{:S(2)}, u32[]{:S(2)}) collective-permute-start(bf16[96,512]{1,0:T(8,128)(2,1)S(1)} %get-tuple-element.86.refs_0_), channel_id=1, source_target_pairs={{0,16},{1,2},{2,1},{3,19},{4,20},{5,6},{6,5},{7,23},{8,24},{9,10},... | collective-permute-start | bytes 294920 | tf_op jit(solution)/shard_map/ppermute | solution.py:170
  417.4 7.7 %collective-permute-start.58 = (bf16[96,512]{1,0:T(8,128)(2,1)S(1)}, bf16[96,512]{1,0:T(8,128)(2,1)S(1)}, u32[]{:S(2)}, u32[]{:S(2)}) collective-permute-start(bf16[96,512]{1,0:T(8,128)(2,1)S(1)} %get-tuple-element.86.refs_0_), channel_id=1, source_target_pairs={{0,16},{1,6},{2,5},{3,19},{4,20},{5,2},{6,1},{7,23},{8,24},{9,14},... | collective-permute-start | bytes 294920 | tf_op jit(solution)/shard_map/ppermute | solution.py:170
  433.1 7.9 %collective-permute-start.61 = (bf16[96,512]{1,0:T(8,128)(2,1)S(1)}, bf16[96,512]{1,0:T(8,128)(2,1)S(1)}, u32[]{:S(2)}, u32[]{:S(2)}) collective-permute-start(bf16[96,512]{1,0:T(8,128)(2,1)S(1)} %get-tuple-element.90), channel_id=1, source_target_pairs={{0,16},{1,5},{2,6},{3,19},{4,20},{5,1},{6,2},{7,23},{8,24},{9,13},... | collective-permute-start | bytes 294920 | tf_op jit(solution)/shard_map/ppermute | solution.py:170
  438.4 5.5 %collective-permute-start.62 = (bf16[96,512]{1,0:T(8,128)(2,1)S(1)}, bf16[96,512]{1,0:T(8,128)(2,1)S(1)}, u32[]{:S(2)}, u32[]{:S(2)}) collective-permute-start(bf16[96,512]{1,0:T(8,128)(2,1)S(1)} %get-tuple-element.90), channel_id=1, source_target_pairs={{0,16},{1,2},{2,1},{3,19},{4,20},{5,6},{6,5},{7,23},{8,24},{9,10},... | collective-permute-start | bytes 294920 | tf_op jit(solution)/shard_map/ppermute | solution.py:170
  438.4 7.5 %collective-permute-start.63 = (bf16[96,512]{1,0:T(8,128)(2,1)S(1)}, bf16[96,512]{1,0:T(8,128)(2,1)S(1)}, u32[]{:S(2)}, u32[]{:S(2)}) collective-permute-start(bf16[96,512]{1,0:T(8,128)(2,1)S(1)} %get-tuple-element.90), channel_id=1, source_target_pairs={{0,16},{1,6},{2,5},{3,19},{4,20},{5,2},{6,1},{7,23},{8,24},{9,14},... | collective-permute-start | bytes 294920 | tf_op jit(solution)/shard_map/ppermute | solution.py:170
  449.0 3.8 collective-permute-start.64
  449.1 4.3 collective-permute-start.65
  454.1 4.6 %collective-permute-start.67 = (f32[8,2048]{1,0:T(8,128)S(1)}, f32[8,2048]{1,0:T(8,128)S(1)}, u32[]{:S(2)}, u32[]{:S(2)}) collective-permute-start(f32[8,2048]{1,0:T(8,128)S(1)} %add_add_fusion.1), channel_id=1, source_target_pairs={{1,0},{2,3},{5,4},{6,7},{9,8},{10,11},{13,12},{14,15},{17,16},{18,... | collective-permute-start | bytes 196616 | tf_op jit(solution)/shard_map/ppermute | solution.py:170
  (38 other events, 1260.3 us)

commit v10 on v9

--- a/solution.py
+++ b/solution.py
@@ -304,7 +304,9 @@
             paired = S % 2 == 0 and k in (0, turns - 2)
             after = [e[0] ^ 1 if paired else (e[0] + 1) % S for e in everyone]
             own = send(result[0], [(e, (a, e[1], e[2])) for e, a in zip(everyone, after)])
-            counts = {0: (0,), turns - 2: (S - 2,)}.get(k, range(S)) if paired else range(S)
+            counts = [
+                a for a in range(S) if 0 <= k - a < segs * S - (S if a == S - 1 else 0)
+            ]
             other = send(
                 result[0],
                 [

time: 467 us -> 462 us (0.989)
    ppermute x68, waiting for transfers between devices: 261 us -> 257 us  [send(): return lax.ppermute(block, AXES, [(lin(*a), lin(*b)) for a, b in pairs])]
where the time goes in v10:
time: 462 us; the launch traced here: 455 us
  waiting for transfers between devices  257 us (56%)
  starting transfers between devices  79.7 us (17%)
  Pallas kernels  64.9 us (14%)
  local copies, waits for them, and re-layouts  38 us (8%)
  other arithmetic  13.6 us (3%)
    ppermute x68, waiting for transfers between devices, send(): return lax.ppermute(block, AXES, [(lin(*a), lin(*b)) for a, b in pairs])  257 us
    ppermute x68, starting transfers between devices, send(): return lax.ppermute(block, AXES, [(lin(*a), lin(*b)) for a, b in pairs])  79.7 us
    pallas_call x11, Pallas kernels, body(): pl.pallas_call(functools.partial(attend_kernel, k, n, tokens, D), out_sha...  39.4 us
    pallas_call x10, Pallas kernels, body(): pl.pallas_call(functools.partial(project_kernel, k, n, tokens, parts, poo...  22.3 us
    gather x1, local copies, waits for them, and re-layouts, embed(): picked = jnp.take(emb_table, jnp.clip(local, 0, vocab - 1), axis=0)  13.2 us
    unnamed x74, local copies, waits for them, and re-layouts  9.65 us
  transfers between devices with their start and end apart: 68, of which 59 were waited for; matrix products, arithmetic and copies ran while one was open for 8% of the time, Pallas kernels for 1%

profile of v10, /device:TPU:0, one launch (start us, length us, event | category | flops | bytes accessed | tf_op | source)
XLA Modules:
  0.0 454.5 jit_solution(11544550914099437159)
XLA Ops:
  1.5 3.0 collective-permute-start
  4.6 2.6 collective-permute-start.1
  8.5 4.0 dynamic-slice_bitcast_fusion.2
  12.5 2.6 dynamic-slice_bitcast_fusion
  19.3 2.8 collective-permute-start.8
  22.1 2.3 collective-permute-start.9
  24.5 13.2 %gather_fusion.1 = bf16[512,2048]{1,0:T(8,128)(2,1)} fusion(bf16[4096,2048]{1,0:T(8,128)(2,1)} %param.12, s32[1024]{0:T(1024)S(1)} %pad_clamp_fusion), kind=kCustom, calls=%fused_computation.1 | custom fusion | bytes 4196352 | tf_op jit(solution)/shard_map/jit(_take)/gather | solution.py:213
  44.0 44.7 %collective-permute-done.8.refs_0_ = bf16[1024,1536]{1,0:T(8,128)(2,1)S(1)} collective-permute-done((bf16[1024,1536]{1,0:T(8,128)(2,1)}, bf16[1024,1536]{1,0:T(8,128)(2,1)S(1)}, u32[]{:S(2)}, u32[]{:S(2)}) %collective-permute-start.8) | collective-permute-done | bytes 3145760 | tf_op jit(solution)/shard_map/ppermute | solution.py:170
  88.7 7.2 %collective-permute-start.10 = (bf16[1024,1536]{1,0:T(8,128)(2,1)}, bf16[1024,1536]{1,0:T(8,128)(2,1)}, u32[]{:S(2)}, u32[]{:S(2)}) collective-permute-start(bf16[1024,1536]{1,0:T(8,128)(2,1)} %pad_maximum_fusion.1), channel_id=1, source_target_pairs={{3,1},{0,2},{7,5},{4,6},{11,9},{8,10},{15,13},{12,14},{19,17},{16,... | collective-permute-start | bytes 9437192 | tf_op jit(solution)/shard_map/ppermute | solution.py:170
  108.6 51.7 %collective-permute-done.10.refs_2_ = bf16[1024,1536]{1,0:T(8,128)(2,1)} collective-permute-done((bf16[1024,1536]{1,0:T(8,128)(2,1)}, bf16[1024,1536]{1,0:T(8,128)(2,1)}, u32[]{:S(2)}, u32[]{:S(2)}) %collective-permute-start.10) | collective-permute-done | bytes 3145760 | tf_op jit(solution)/shard_map/ppermute | solution.py:170
  160.3 3.2 shard_map.100
  163.7 3.5 shard_map.101
  174.3 2.1 shard_map.102
  178.2 5.2 %collective-permute-done.15.refs_1_ = bf16[96,2048]{1,0:T(8,128)(2,1)S(1)} collective-permute-done((bf16[96,2048]{1,0:T(8,128)(2,1)S(1)}, bf16[96,2048]{1,0:T(8,128)(2,1)S(1)}, u32[]{:S(2)}, u32[]{:S(2)}) %collective-permute-start.15) | collective-permute-done | bytes 393248 | tf_op jit(solution)/shard_map/ppermute | solution.py:170
  183.4 3.5 shard_map.103
  189.1 3.6 collective-permute-done.16.refs_1_
  196.7 2.1 shard_map.104
  199.1 7.0 %collective-permute-done.19.refs_0_ = bf16[96,2048]{1,0:T(8,128)(2,1)S(1)} collective-permute-done((bf16[96,2048]{1,0:T(8,128)(2,1)S(1)}, bf16[96,2048]{1,0:T(8,128)(2,1)S(1)}, u32[]{:S(2)}, u32[]{:S(2)}) %collective-permute-start.19) | collective-permute-done | bytes 393248 | tf_op jit(solution)/shard_map/ppermute | solution.py:170
  206.1 4.2 collective-permute-done.20.refs_1_
  210.3 3.5 shard_map.105
  216.0 3.0 collective-permute-done.21.refs_1_
  221.1 2.1 shard_map.106
  224.4 6.3 %collective-permute-done.24.refs_0_ = bf16[96,2048]{1,0:T(8,128)(2,1)S(1)} collective-permute-done((bf16[96,2048]{1,0:T(8,128)(2,1)S(1)}, bf16[96,2048]{1,0:T(8,128)(2,1)S(1)}, u32[]{:S(2)}, u32[]{:S(2)}) %collective-permute-start.24) | collective-permute-done | bytes 393248 | tf_op jit(solution)/shard_map/ppermute | solution.py:170
  230.7 4.2 collective-permute-done.25.refs_1_
  234.9 3.5 shard_map.107
  241.3 2.8 collective-permute-done.26.refs_1_
  244.1 2.1 collective-permute-done.27.refs_2_
  247.8 2.1 shard_map.108
  250.1 7.1 %collective-permute-done.29.refs_0_ = bf16[96,2048]{1,0:T(8,128)(2,1)S(1)} collective-permute-done((bf16[96,2048]{1,0:T(8,128)(2,1)S(1)}, bf16[96,2048]{1,0:T(8,128)(2,1)S(1)}, u32[]{:S(2)}, u32[]{:S(2)}) %collective-permute-start.29) | collective-permute-done | bytes 393248 | tf_op jit(solution)/shard_map/ppermute | solution.py:170
  257.2 2.9 collective-permute-done.30.refs_1_
  260.1 3.5 shard_map.109
  272.0 2.2 shard_map.110
  276.2 5.6 %collective-permute-done.34.refs_0_ = bf16[96,2048]{1,0:T(8,128)(2,1)S(1)} collective-permute-done((bf16[96,2048]{1,0:T(8,128)(2,1)S(1)}, bf16[96,2048]{1,0:T(8,128)(2,1)S(1)}, u32[]{:S(2)}, u32[]{:S(2)}) %collective-permute-start.34) | collective-permute-done | bytes 393248 | tf_op jit(solution)/shard_map/ppermute | solution.py:170
  281.8 4.6 %collective-permute-done.35.refs_1_ = bf16[96,2048]{1,0:T(8,128)(2,1)S(1)} collective-permute-done((bf16[96,2048]{1,0:T(8,128)(2,1)S(1)}, bf16[96,2048]{1,0:T(8,128)(2,1)S(1)}, u32[]{:S(2)}, u32[]{:S(2)}) %collective-permute-start.35) | collective-permute-done | bytes 393248 | tf_op jit(solution)/shard_map/ppermute | solution.py:170
  286.4 3.5 shard_map.111
  293.1 2.6 collective-permute-done.36.refs_1_
  299.7 2.2 shard_map.112
  303.7 5.4 %collective-permute-done.39.refs_0_ = bf16[96,2048]{1,0:T(8,128)(2,1)S(1)} collective-permute-done((bf16[96,2048]{1,0:T(8,128)(2,1)S(1)}, bf16[96,2048]{1,0:T(8,128)(2,1)S(1)}, u32[]{:S(2)}, u32[]{:S(2)}) %collective-permute-start.39) | collective-permute-done | bytes 393248 | tf_op jit(solution)/shard_map/ppermute | solution.py:170
  309.1 4.6 %collective-permute-done.40.refs_1_ = bf16[96,2048]{1,0:T(8,128)(2,1)S(1)} collective-permute-done((bf16[96,2048]{1,0:T(8,128)(2,1)S(1)}, bf16[96,2048]{1,0:T(8,128)(2,1)S(1)}, u32[]{:S(2)}, u32[]{:S(2)}) %collective-permute-start.40) | collective-permute-done | bytes 393248 | tf_op jit(solution)/shard_map/ppermute | solution.py:170
  313.8 3.5 shard_map.113
  320.4 2.6 collective-permute-done.41.refs_1_
  327.2 2.2 shard_map.114
  331.6 5.6 %collective-permute-done.44.refs_0_ = bf16[96,2048]{1,0:T(8,128)(2,1)S(1)} collective-permute-done((bf16[96,2048]{1,0:T(8,128)(2,1)S(1)}, bf16[96,2048]{1,0:T(8,128)(2,1)S(1)}, u32[]{:S(2)}, u32[]{:S(2)}) %collective-permute-start.44) | collective-permute-done | bytes 393248 | tf_op jit(solution)/shard_map/ppermute | solution.py:170
  337.2 4.6 %collective-permute-done.45.refs_1_ = bf16[96,2048]{1,0:T(8,128)(2,1)S(1)} collective-permute-done((bf16[96,2048]{1,0:T(8,128)(2,1)S(1)}, bf16[96,2048]{1,0:T(8,128)(2,1)S(1)}, u32[]{:S(2)}, u32[]{:S(2)}) %collective-permute-start.45) | collective-permute-done | bytes 393248 | tf_op jit(solution)/shard_map/ppermute | solution.py:170
  341.8 4.2 shard_map.115
  349.8 2.9 collective-permute-done.46.refs_1_
  356.7 3.4 copy-done
  361.1 2.7 shard_map.116
  365.5 5.6 %collective-permute-done.49.refs_0_ = bf16[96,2048]{1,0:T(8,128)(2,1)S(1)} collective-permute-done((bf16[96,2048]{1,0:T(8,128)(2,1)S(1)}, bf16[96,2048]{1,0:T(8,128)(2,1)S(1)}, u32[]{:S(2)}, u32[]{:S(2)}) %collective-permute-start.49) | collective-permute-done | bytes 393248 | tf_op jit(solution)/shard_map/ppermute | solution.py:170
  371.1 4.2 collective-permute-done.50.refs_1_
  379.1 3.5 shard_map.117
  386.1 2.1 collective-permute-done.51.refs_1_
  388.3 2.1 collective-permute-done.52.refs_2_
  392.0 2.2 shard_map.118
  396.4 5.1 %collective-permute-done.54.refs_0_ = bf16[96,2048]{1,0:T(8,128)(2,1)S(1)} collective-permute-done((bf16[96,2048]{1,0:T(8,128)(2,1)S(1)}, bf16[96,2048]{1,0:T(8,128)(2,1)S(1)}, u32[]{:S(2)}, u32[]{:S(2)}) %collective-permute-start.54) | collective-permute-done | bytes 393248 | tf_op jit(solution)/shard_map/ppermute | solution.py:170
  401.5 4.2 collective-permute-done.55.refs_1_
  405.7 3.5 shard_map.119
  409.2 2.3 collective-permute-start.56
  418.8 2.2 shard_map.120
  423.4 3.5 shard_map.121
  426.9 5.9 %collective-permute-start.61 = (bf16[96,512]{1,0:T(8,128)(2,1)S(1)}, bf16[96,512]{1,0:T(8,128)(2,1)S(1)}, u32[]{:S(2)}, u32[]{:S(2)}) collective-permute-start(bf16[96,512]{1,0:T(8,128)(2,1)S(1)} %get-tuple-element.90), channel_id=1, source_target_pairs={{0,16},{1,5},{2,6},{3,19},{4,20},{5,1},{6,2},{7,23},{8,24},{9,13},... | collective-permute-start | bytes 294920 | tf_op jit(solution)/shard_map/ppermute | solution.py:170
  435.9 2.6 collective-permute-done.62
  440.7 3.0 shard_map.122
  448.9 4.5 collective-permute-done.67
  (217 shorter events, 121.6 us)
Async XLA Ops:
  1.5 17.4 %collective-permute-start = (s32[2,2,33]{2,1,0:T(2,128)S(1)}, s32[2,2,33]{2,1,0:T(2,128)S(1)}, u32[]{:S(2)}, u32[]{:S(2)}) collective-permute-start(s32[2,2,33]{2,1,0:T(2,128)S(1)} %pad_add_fusion.1), channel_id=1, source_target_pairs={{0,1},{1,2},{2,3},{3,0},{4,5},{5,6},{6,7},{7,4},{8,9},{9,10},{10,1... | collective-permute-start | bytes 1592 | tf_op jit(solution)/shard_map/ppermute | solution.py:170
  4.6 14.4 %collective-permute-start.1 = (s32[2,2,33]{2,1,0:T(2,128)S(1)}, s32[2,2,33]{2,1,0:T(2,128)S(1)}, u32[]{:S(2)}, u32[]{:S(2)}) collective-permute-start(s32[2,2,33]{2,1,0:T(2,128)S(1)} %pad_add_fusion.1), channel_id=1, source_target_pairs={{0,2},{1,3},{2,0},{3,1},{4,6},{5,7},{6,4},{7,5},{8,10},{9,11},{10,... | collective-permute-start | bytes 1592 | tf_op jit(solution)/shard_map/ppermute | solution.py:170
  7.1 11.8 %collective-permute-start.2 = (s32[2,2,33]{2,1,0:T(2,128)S(1)}, s32[2,2,33]{2,1,0:T(2,128)S(1)}, u32[]{:S(2)}, u32[]{:S(2)}) collective-permute-start(s32[2,2,33]{2,1,0:T(2,128)S(1)} %pad_add_fusion.1), channel_id=1, source_target_pairs={{0,3},{1,0},{2,1},{3,2},{4,7},{5,4},{6,5},{7,6},{8,11},{9,8},{10,9... | collective-permute-start | bytes 1592 | tf_op jit(solution)/shard_map/ppermute | solution.py:170
  19.3 69.4 %collective-permute-start.8 = (bf16[1024,1536]{1,0:T(8,128)(2,1)}, bf16[1024,1536]{1,0:T(8,128)(2,1)S(1)}, u32[]{:S(2)}, u32[]{:S(2)}) collective-permute-start(bf16[1024,1536]{1,0:T(8,128)(2,1)} %pad_maximum_fusion.2), channel_id=1, source_target_pairs={{0,1},{3,2},{4,5},{7,6},{8,9},{11,10},{12,13},{15,14},{16,17},{19,... | collective-permute-start | bytes 9437192 | tf_op jit(solution)/shard_map/ppermute | solution.py:170
  22.1 66.6 %collective-permute-start.9 = (bf16[1024,1536]{1,0:T(8,128)(2,1)}, bf16[1024,1536]{1,0:T(8,128)(2,1)}, u32[]{:S(2)}, u32[]{:S(2)}) collective-permute-start(bf16[1024,1536]{1,0:T(8,128)(2,1)} %pad_maximum_fusion.3), channel_id=1, source_target_pairs={{2,1},{1,2},{6,5},{5,6},{10,9},{9,10},{14,13},{13,14},{18,17},{17,... | collective-permute-start | bytes 9437192 | tf_op jit(solution)/shard_map/ppermute | solution.py:170
  39.8 56.1 %collective-permute-start.3 = (bf16[512,2048]{1,0:T(8,128)(2,1)S(1)}, bf16[512,2048]{1,0:T(8,128)(2,1)S(1)}, u32[]{:S(2)}, u32[]{:S(2)}) collective-permute-start(bf16[512,2048]{1,0:T(8,128)(2,1)S(1)} %select_select_fusion), channel_id=1, source_target_pairs={{9,1},{10,2},{13,5},{14,6}} | collective-permute-start | bytes 6291464 | tf_op jit(solution)/shard_map/ppermute | solution.py:170
  40.6 55.3 %collective-permute-start.4 = (bf16[512,2048]{1,0:T(8,128)(2,1)S(1)}, bf16[512,2048]{1,0:T(8,128)(2,1)S(1)}, u32[]{:S(2)}, u32[]{:S(2)}) collective-permute-start(bf16[512,2048]{1,0:T(8,128)(2,1)S(1)} %select_select_fusion), channel_id=1, source_target_pairs={{17,1},{18,2},{21,5},{22,6}} | collective-permute-start | bytes 6291464 | tf_op jit(solution)/shard_map/ppermute | solution.py:170
  41.4 54.5 %collective-permute-start.5 = (bf16[512,2048]{1,0:T(8,128)(2,1)S(1)}, bf16[512,2048]{1,0:T(8,128)(2,1)S(1)}, u32[]{:S(2)}, u32[]{:S(2)}) collective-permute-start(bf16[512,2048]{1,0:T(8,128)(2,1)S(1)} %select_select_fusion), channel_id=1, source_target_pairs={{25,1},{26,2},{29,5},{30,6}} | collective-permute-start | bytes 6291464 | tf_op jit(solution)/shard_map/ppermute | solution.py:170
  88.7 71.6 %collective-permute-start.10 = (bf16[1024,1536]{1,0:T(8,128)(2,1)}, bf16[1024,1536]{1,0:T(8,128)(2,1)}, u32[]{:S(2)}, u32[]{:S(2)}) collective-permute-start(bf16[1024,1536]{1,0:T(8,128)(2,1)} %pad_maximum_fusion.1), channel_id=1, source_target_pairs={{3,1},{0,2},{7,5},{4,6},{11,9},{8,10},{15,13},{12,14},{19,17},{16,... | collective-permute-start | bytes 9437192 | tf_op jit(solution)/shard_map/ppermute | solution.py:170
  98.0 8.8 %collective-permute-start.6 = (bf16[512,2048]{1,0:T(8,128)(2,1)}, bf16[512,2048]{1,0:T(8,128)(2,1)}, u32[]{:S(2)}, u32[]{:S(2)}) collective-permute-start(bf16[512,2048]{1,0:T(8,128)(2,1)} %add_add_fusion), channel_id=1, source_target_pairs={{1,5},{2,6},{5,1},{6,2}} | collective-permute-start | bytes 6291464 | tf_op jit(solution)/shard_map/ppermute | solution.py:170
  100.0 63.6 %collective-permute-start.7 = (bf16[16,2048]{1,0:T(8,128)(2,1)S(1)}, bf16[16,2048]{1,0:T(8,128)(2,1)S(1)}, u32[]{:S(2)}, u32[]{:S(2)}) collective-permute-start(bf16[16,2048]{1,0:T(8,128)(2,1)S(1)} %copy-done.8), channel_id=1, source_target_pairs={{1,5},{2,6},{5,1},{6,2}} | collective-permute-start | bytes 196616 | tf_op jit(solution)/shard_map/ppermute | solution.py:170
  167.2 4.7 %collective-permute-start.11 = (bf16[96,512]{1,0:T(8,128)(2,1)S(1)}, bf16[96,512]{1,0:T(8,128)(2,1)S(1)}, u32[]{:S(2)}, u32[]{:S(2)}) collective-permute-start(bf16[96,512]{1,0:T(8,128)(2,1)S(1)} %get-tuple-element.58.refs_0_), channel_id=1, source_target_pairs={{0,16},{1,5},{2,6},{3,19},{4,20},{5,1},{6,2},{7,23},{8,24},{9,13},... | collective-permute-start | bytes 294920 | tf_op jit(solution)/shard_map/ppermute | solution.py:170
  168.6 4.6 %collective-permute-start.12 = (bf16[96,512]{1,0:T(8,128)(2,1)S(1)}, bf16[96,512]{1,0:T(8,128)(2,1)S(1)}, u32[]{:S(2)}, u32[]{:S(2)}) collective-permute-start(bf16[96,512]{1,0:T(8,128)(2,1)S(1)} %get-tuple-element.58.refs_0_), channel_id=1, source_target_pairs={{0,16},{1,2},{2,1},{3,19},{4,20},{5,6},{6,5},{7,23},{8,24},{9,10},... | collective-permute-start | bytes 294920 | tf_op jit(solution)/shard_map/ppermute | solution.py:170
  169.3 5.0 %collective-permute-start.13 = (bf16[96,512]{1,0:T(8,128)(2,1)S(1)}, bf16[96,512]{1,0:T(8,128)(2,1)S(1)}, u32[]{:S(2)}, u32[]{:S(2)}) collective-permute-start(bf16[96,512]{1,0:T(8,128)(2,1)S(1)} %get-tuple-element.58.refs_0_), channel_id=1, source_target_pairs={{0,16},{1,6},{2,5},{3,19},{4,20},{5,2},{6,1},{7,23},{8,24},{9,14},... | collective-permute-start | bytes 294920 | tf_op jit(solution)/shard_map/ppermute | solution.py:170
  176.5 6.9 %collective-permute-start.15 = (bf16[96,2048]{1,0:T(8,128)(2,1)S(1)}, bf16[96,2048]{1,0:T(8,128)(2,1)S(1)}, u32[]{:S(2)}, u32[]{:S(2)}) collective-permute-start(bf16[96,2048]{1,0:T(8,128)(2,1)S(1)} %shard_map.102), channel_id=1, source_target_pairs={{0,12},{1,13},{2,14},{3,15},{4,8},{5,9},{6,10},{7,11},{8,0},{9,1},... | collective-permute-start | bytes 1179656 | tf_op jit(solution)/shard_map/ppermute | solution.py:170
  186.9 5.7 %collective-permute-start.16 = (bf16[96,512]{1,0:T(8,128)(2,1)S(1)}, bf16[96,512]{1,0:T(8,128)(2,1)S(1)}, u32[]{:S(2)}, u32[]{:S(2)}) collective-permute-start(bf16[96,512]{1,0:T(8,128)(2,1)S(1)} %get-tuple-element.60.refs_0_), channel_id=1, source_target_pairs={{0,16},{1,5},{2,6},{3,19},{4,20},{5,1},{6,2},{7,23},{8,24},{9,13},... | collective-permute-start | bytes 294920 | tf_op jit(solution)/shard_map/ppermute | solution.py:170
  187.0 7.8 %collective-permute-start.17 = (bf16[96,512]{1,0:T(8,128)(2,1)S(1)}, bf16[96,512]{1,0:T(8,128)(2,1)S(1)}, u32[]{:S(2)}, u32[]{:S(2)}) collective-permute-start(bf16[96,512]{1,0:T(8,128)(2,1)S(1)} %get-tuple-element.60.refs_0_), channel_id=1, source_target_pairs={{0,16},{1,2},{2,1},{3,19},{4,20},{5,6},{6,5},{7,23},{8,24},{9,10},... | collective-permute-start | bytes 294920 | tf_op jit(solution)/shard_map/ppermute | solution.py:170
  189.0 7.7 %collective-permute-start.18 = (bf16[96,512]{1,0:T(8,128)(2,1)S(1)}, bf16[96,512]{1,0:T(8,128)(2,1)S(1)}, u32[]{:S(2)}, u32[]{:S(2)}) collective-permute-start(bf16[96,512]{1,0:T(8,128)(2,1)S(1)} %get-tuple-element.60.refs_0_), channel_id=1, source_target_pairs={{0,16},{1,6},{2,5},{3,19},{4,20},{5,2},{6,1},{7,23},{8,24},{9,14},... | collective-permute-start | bytes 294920 | tf_op jit(solution)/shard_map/ppermute | solution.py:170
  198.8 7.3 %collective-permute-start.19 = (bf16[96,2048]{1,0:T(8,128)(2,1)S(1)}, bf16[96,2048]{1,0:T(8,128)(2,1)S(1)}, u32[]{:S(2)}, u32[]{:S(2)}) collective-permute-start(bf16[96,2048]{1,0:T(8,128)(2,1)S(1)} %shard_map.104), channel_id=1, source_target_pairs={{0,8},{1,9},{2,10},{3,11},{4,12},{5,13},{6,14},{7,15},{8,16},{9,17... | collective-permute-start | bytes 1179656 | tf_op jit(solution)/shard_map/ppermute | solution.py:170
  198.9 11.4 %collective-permute-start.20 = (bf16[96,2048]{1,0:T(8,128)(2,1)S(1)}, bf16[96,2048]{1,0:T(8,128)(2,1)S(1)}, u32[]{:S(2)}, u32[]{:S(2)}) collective-permute-start(bf16[96,2048]{1,0:T(8,128)(2,1)S(1)} %shard_map.104), channel_id=1, source_target_pairs={{0,12},{1,13},{2,14},{3,15},{4,8},{5,9},{6,10},{7,11},{8,20},{9,21... | collective-permute-start | bytes 1179656 | tf_op jit(solution)/shard_map/ppermute | solution.py:170
  213.8 5.2 %collective-permute-start.21 = (bf16[96,512]{1,0:T(8,128)(2,1)S(1)}, bf16[96,512]{1,0:T(8,128)(2,1)S(1)}, u32[]{:S(2)}, u32[]{:S(2)}) collective-permute-start(bf16[96,512]{1,0:T(8,128)(2,1)S(1)} %get-tuple-element.62.refs_0_), channel_id=1, source_target_pairs={{0,16},{1,5},{2,6},{3,19},{4,20},{5,1},{6,2},{7,23},{8,24},{9,13},... | collective-permute-start | bytes 294920 | tf_op jit(solution)/shard_map/ppermute | solution.py:170
  213.9 6.2 %collective-permute-start.22 = (bf16[96,512]{1,0:T(8,128)(2,1)S(1)}, bf16[96,512]{1,0:T(8,128)(2,1)S(1)}, u32[]{:S(2)}, u32[]{:S(2)}) collective-permute-start(bf16[96,512]{1,0:T(8,128)(2,1)S(1)} %get-tuple-element.62.refs_0_), channel_id=1, source_target_pairs={{0,16},{1,2},{2,1},{3,19},{4,20},{5,6},{6,5},{7,23},{8,24},{9,10},... | collective-permute-start | bytes 294920 | tf_op jit(solution)/shard_map/ppermute | solution.py:170
  215.9 5.2 %collective-permute-start.23 = (bf16[96,512]{1,0:T(8,128)(2,1)S(1)}, bf16[96,512]{1,0:T(8,128)(2,1)S(1)}, u32[]{:S(2)}, u32[]{:S(2)}) collective-permute-start(bf16[96,512]{1,0:T(8,128)(2,1)S(1)} %get-tuple-element.62.refs_0_), channel_id=1, source_target_pairs={{0,16},{1,6},{2,5},{3,19},{4,20},{5,2},{6,1},{7,23},{8,24},{9,14},... | collective-permute-start | bytes 294920 | tf_op jit(solution)/shard_map/ppermute | solution.py:170
  223.3 7.4 %collective-permute-start.24 = (bf16[96,2048]{1,0:T(8,128)(2,1)S(1)}, bf16[96,2048]{1,0:T(8,128)(2,1)S(1)}, u32[]{:S(2)}, u32[]{:S(2)}) collective-permute-start(bf16[96,2048]{1,0:T(8,128)(2,1)S(1)} %shard_map.106), channel_id=1, source_target_pairs={{0,8},{1,9},{2,10},{3,11},{4,12},{5,13},{6,14},{7,15},{8,16},{9,17... | collective-permute-start | bytes 1179656 | tf_op jit(solution)/shard_map/ppermute | solution.py:170
  223.5 11.4 %collective-permute-start.25 = (bf16[96,2048]{1,0:T(8,128)(2,1)S(1)}, bf16[96,2048]{1,0:T(8,128)(2,1)S(1)}, u32[]{:S(2)}, u32[]{:S(2)}) collective-permute-start(bf16[96,2048]{1,0:T(8,128)(2,1)S(1)} %shard_map.106), channel_id=1, source_target_pairs={{0,12},{1,13},{2,14},{3,15},{4,8},{5,9},{6,10},{7,11},{8,20},{9,21... | collective-permute-start | bytes 1179656 | tf_op jit(solution)/shard_map/ppermute | solution.py:170
  238.4 5.7 %collective-permute-start.26 = (bf16[96,512]{1,0:T(8,128)(2,1)S(1)}, bf16[96,512]{1,0:T(8,128)(2,1)S(1)}, u32[]{:S(2)}, u32[]{:S(2)}) collective-permute-start(bf16[96,512]{1,0:T(8,128)(2,1)S(1)} %get-tuple-element.64.refs_0_), channel_id=1, source_target_pairs={{0,16},{1,5},{2,6},{3,19},{4,20},{5,1},{6,2},{7,23},{8,24},{9,13},... | collective-permute-start | bytes 294920 | tf_op jit(solution)/shard_map/ppermute | solution.py:170
  239.3 6.9 %collective-permute-start.27 = (bf16[96,512]{1,0:T(8,128)(2,1)S(1)}, bf16[96,512]{1,0:T(8,128)(2,1)S(1)}, u32[]{:S(2)}, u32[]{:S(2)}) collective-permute-start(bf16[96,512]{1,0:T(8,128)(2,1)S(1)} %get-tuple-element.64.refs_0_), channel_id=1, source_target_pairs={{0,16},{1,2},{2,1},{3,19},{4,20},{5,6},{6,5},{7,23},{8,24},{9,10},... | collective-permute-start | bytes 294920 | tf_op jit(solution)/shard_map/ppermute | solution.py:170
  240.5 7.3 %collective-permute-start.28 = (bf16[96,512]{1,0:T(8,128)(2,1)S(1)}, bf16[96,512]{1,0:T(8,128)(2,1)S(1)}, u32[]{:S(2)}, u32[]{:S(2)}) collective-permute-start(bf16[96,512]{1,0:T(8,128)(2,1)S(1)} %get-tuple-element.64.refs_0_), channel_id=1, source_target_pairs={{0,16},{1,6},{2,5},{3,19},{4,20},{5,2},{6,1},{7,23},{8,24},{9,14},... | collective-permute-start | bytes 294920 | tf_op jit(solution)/shard_map/ppermute | solution.py:170
  249.9 7.3 %collective-permute-start.29 = (bf16[96,2048]{1,0:T(8,128)(2,1)S(1)}, bf16[96,2048]{1,0:T(8,128)(2,1)S(1)}, u32[]{:S(2)}, u32[]{:S(2)}) collective-permute-start(bf16[96,2048]{1,0:T(8,128)(2,1)S(1)} %shard_map.108), channel_id=1, source_target_pairs={{0,8},{1,9},{2,10},{3,11},{4,12},{5,13},{6,14},{7,15},{8,16},{9,17... | collective-permute-start | bytes 1179656 | tf_op jit(solution)/shard_map/ppermute | solution.py:170
  250.0 10.1 %collective-permute-start.30 = (bf16[96,2048]{1,0:T(8,128)(2,1)S(1)}, bf16[96,2048]{1,0:T(8,128)(2,1)S(1)}, u32[]{:S(2)}, u32[]{:S(2)}) collective-permute-start(bf16[96,2048]{1,0:T(8,128)(2,1)S(1)} %shard_map.108), channel_id=1, source_target_pairs={{0,12},{1,13},{2,14},{3,15},{4,8},{5,9},{6,10},{7,11},{8,20},{9,21... | collective-permute-start | bytes 1179656 | tf_op jit(solution)/shard_map/ppermute | solution.py:170
  263.6 4.7 %collective-permute-start.31 = (bf16[96,512]{1,0:T(8,128)(2,1)S(1)}, bf16[96,512]{1,0:T(8,128)(2,1)S(1)}, u32[]{:S(2)}, u32[]{:S(2)}) collective-permute-start(bf16[96,512]{1,0:T(8,128)(2,1)S(1)} %get-tuple-element.66.refs_0_), channel_id=1, source_target_pairs={{0,16},{1,5},{2,6},{3,19},{4,20},{5,1},{6,2},{7,23},{8,24},{9,13},... | collective-permute-start | bytes 294920 | tf_op jit(solution)/shard_map/ppermute | solution.py:170
  264.7 5.2 %collective-permute-start.32 = (bf16[96,512]{1,0:T(8,128)(2,1)S(1)}, bf16[96,512]{1,0:T(8,128)(2,1)S(1)}, u32[]{:S(2)}, u32[]{:S(2)}) collective-permute-start(bf16[96,512]{1,0:T(8,128)(2,1)S(1)} %get-tuple-element.66.refs_0_), channel_id=1, source_target_pairs={{0,16},{1,2},{2,1},{3,19},{4,20},{5,6},{6,5},{7,23},{8,24},{9,10},... | collective-permute-start | bytes 294920 | tf_op jit(solution)/shard_map/ppermute | solution.py:170
  265.7 6.3 %collective-permute-start.33 = (bf16[96,512]{1,0:T(8,128)(2,1)S(1)}, bf16[96,512]{1,0:T(8,128)(2,1)S(1)}, u32[]{:S(2)}, u32[]{:S(2)}) collective-permute-start(bf16[96,512]{1,0:T(8,128)(2,1)S(1)} %get-tuple-element.66.refs_0_), channel_id=1, source_target_pairs={{0,16},{1,6},{2,5},{3,19},{4,20},{5,2},{6,1},{7,23},{8,24},{9,14},... | collective-permute-start | bytes 294920 | tf_op jit(solution)/shard_map/ppermute | solution.py:170
  274.2 7.5 %collective-permute-start.34 = (bf16[96,2048]{1,0:T(8,128)(2,1)S(1)}, bf16[96,2048]{1,0:T(8,128)(2,1)S(1)}, u32[]{:S(2)}, u32[]{:S(2)}) collective-permute-start(bf16[96,2048]{1,0:T(8,128)(2,1)S(1)} %get-tuple-element.69), channel_id=1, source_target_pairs={{0,8},{1,9},{2,10},{3,11},{4,12},{5,13},{6,14},{7,15},{8,16},{9,17... | collective-permute-start | bytes 1179656 | tf_op jit(solution)/shard_map/ppermute | solution.py:170
  275.7 10.7 %collective-permute-start.35 = (bf16[96,2048]{1,0:T(8,128)(2,1)S(1)}, bf16[96,2048]{1,0:T(8,128)(2,1)S(1)}, u32[]{:S(2)}, u32[]{:S(2)}) collective-permute-start(bf16[96,2048]{1,0:T(8,128)(2,1)S(1)} %get-tuple-element.69), channel_id=1, source_target_pairs={{0,12},{1,13},{2,14},{3,15},{4,8},{5,9},{6,10},{7,11},{8,20},{9,21... | collective-permute-start | bytes 1179656 | tf_op jit(solution)/shard_map/ppermute | solution.py:170
  289.9 5.7 %collective-permute-start.36 = (bf16[96,512]{1,0:T(8,128)(2,1)S(1)}, bf16[96,512]{1,0:T(8,128)(2,1)S(1)}, u32[]{:S(2)}, u32[]{:S(2)}) collective-permute-start(bf16[96,512]{1,0:T(8,128)(2,1)S(1)} %get-tuple-element.70.refs_0_), channel_id=1, source_target_pairs={{0,16},{1,5},{2,6},{3,19},{4,20},{5,1},{6,2},{7,23},{8,24},{9,13},... | collective-permute-start | bytes 294920 | tf_op jit(solution)/shard_map/ppermute | solution.py:170
  291.0 6.7 %collective-permute-start.37 = (bf16[96,512]{1,0:T(8,128)(2,1)S(1)}, bf16[96,512]{1,0:T(8,128)(2,1)S(1)}, u32[]{:S(2)}, u32[]{:S(2)}) collective-permute-start(bf16[96,512]{1,0:T(8,128)(2,1)S(1)} %get-tuple-element.70.refs_0_), channel_id=1, source_target_pairs={{0,16},{1,2},{2,1},{3,19},{4,20},{5,6},{6,5},{7,23},{8,24},{9,10},... | collective-permute-start | bytes 294920 | tf_op jit(solution)/shard_map/ppermute | solution.py:170
  292.0 7.6 %collective-permute-start.38 = (bf16[96,512]{1,0:T(8,128)(2,1)S(1)}, bf16[96,512]{1,0:T(8,128)(2,1)S(1)}, u32[]{:S(2)}, u32[]{:S(2)}) collective-permute-start(bf16[96,512]{1,0:T(8,128)(2,1)S(1)} %get-tuple-element.70.refs_0_), channel_id=1, source_target_pairs={{0,16},{1,6},{2,5},{3,19},{4,20},{5,2},{6,1},{7,23},{8,24},{9,14},... | collective-permute-start | bytes 294920 | tf_op jit(solution)/shard_map/ppermute | solution.py:170
  301.9 7.3 %collective-permute-start.39 = (bf16[96,2048]{1,0:T(8,128)(2,1)S(1)}, bf16[96,2048]{1,0:T(8,128)(2,1)S(1)}, u32[]{:S(2)}, u32[]{:S(2)}) collective-permute-start(bf16[96,2048]{1,0:T(8,128)(2,1)S(1)} %get-tuple-element.73), channel_id=1, source_target_pairs={{0,8},{1,9},{2,10},{3,11},{4,12},{5,13},{6,14},{7,15},{8,16},{9,17... | collective-permute-start | bytes 1179656 | tf_op jit(solution)/shard_map/ppermute | solution.py:170
  301.9 11.8 %collective-permute-start.40 = (bf16[96,2048]{1,0:T(8,128)(2,1)S(1)}, bf16[96,2048]{1,0:T(8,128)(2,1)S(1)}, u32[]{:S(2)}, u32[]{:S(2)}) collective-permute-start(bf16[96,2048]{1,0:T(8,128)(2,1)S(1)} %get-tuple-element.73), channel_id=1, source_target_pairs={{0,12},{1,13},{2,14},{3,15},{4,8},{5,9},{6,10},{7,11},{8,20},{9,21... | collective-permute-start | bytes 1179656 | tf_op jit(solution)/shard_map/ppermute | solution.py:170
  317.3 5.7 %collective-permute-start.41 = (bf16[96,512]{1,0:T(8,128)(2,1)S(1)}, bf16[96,512]{1,0:T(8,128)(2,1)S(1)}, u32[]{:S(2)}, u32[]{:S(2)}) collective-permute-start(bf16[96,512]{1,0:T(8,128)(2,1)S(1)} %get-tuple-element.74.refs_0_), channel_id=1, source_target_pairs={{0,16},{1,5},{2,6},{3,19},{4,20},{5,1},{6,2},{7,23},{8,24},{9,13},... | collective-permute-start | bytes 294920 | tf_op jit(solution)/shard_map/ppermute | solution.py:170
  318.3 6.8 %collective-permute-start.42 = (bf16[96,512]{1,0:T(8,128)(2,1)S(1)}, bf16[96,512]{1,0:T(8,128)(2,1)S(1)}, u32[]{:S(2)}, u32[]{:S(2)}) collective-permute-start(bf16[96,512]{1,0:T(8,128)(2,1)S(1)} %get-tuple-element.74.refs_0_), channel_id=1, source_target_pairs={{0,16},{1,2},{2,1},{3,19},{4,20},{5,6},{6,5},{7,23},{8,24},{9,10},... | collective-permute-start | bytes 294920 | tf_op jit(solution)/shard_map/ppermute | solution.py:170
  319.4 7.8 %collective-permute-start.43 = (bf16[96,512]{1,0:T(8,128)(2,1)S(1)}, bf16[96,512]{1,0:T(8,128)(2,1)S(1)}, u32[]{:S(2)}, u32[]{:S(2)}) collective-permute-start(bf16[96,512]{1,0:T(8,128)(2,1)S(1)} %get-tuple-element.74.refs_0_), channel_id=1, source_target_pairs={{0,16},{1,6},{2,5},{3,19},{4,20},{5,2},{6,1},{7,23},{8,24},{9,14},... | collective-permute-start | bytes 294920 | tf_op jit(solution)/shard_map/ppermute | solution.py:170
  330.0 7.2 %collective-permute-start.44 = (bf16[96,2048]{1,0:T(8,128)(2,1)S(1)}, bf16[96,2048]{1,0:T(8,128)(2,1)S(1)}, u32[]{:S(2)}, u32[]{:S(2)}) collective-permute-start(bf16[96,2048]{1,0:T(8,128)(2,1)S(1)} %get-tuple-element.77), channel_id=1, source_target_pairs={{0,8},{1,9},{2,10},{3,11},{4,12},{5,13},{6,14},{7,15},{8,16},{9,17... | collective-permute-start | bytes 1179656 | tf_op jit(solution)/shard_map/ppermute | solution.py:170
  330.1 11.7 %collective-permute-start.45 = (bf16[96,2048]{1,0:T(8,128)(2,1)S(1)}, bf16[96,2048]{1,0:T(8,128)(2,1)S(1)}, u32[]{:S(2)}, u32[]{:S(2)}) collective-permute-start(bf16[96,2048]{1,0:T(8,128)(2,1)S(1)} %get-tuple-element.77), channel_id=1, source_target_pairs={{0,12},{1,13},{2,14},{3,15},{4,8},{5,9},{6,10},{7,11},{8,20},{9,21... | collective-permute-start | bytes 1179656 | tf_op jit(solution)/shard_map/ppermute | solution.py:170
  346.7 6.0 %collective-permute-start.46 = (bf16[96,512]{1,0:T(8,128)(2,1)}, bf16[96,512]{1,0:T(8,128)(2,1)}, u32[]{:S(2)}, u32[]{:S(2)}) collective-permute-start(bf16[96,512]{1,0:T(8,128)(2,1)} %get-tuple-element.78.refs_0_), channel_id=1, source_target_pairs={{0,16},{1,5},{2,6},{3,19},{4,20},{5,1},{6,2},{7,23},{8,24},{9,13},... | collective-permute-start | bytes 294920 | tf_op jit(solution)/shard_map/ppermute | solution.py:170
  347.7 7.1 %collective-permute-start.47 = (bf16[96,512]{1,0:T(8,128)(2,1)}, bf16[96,512]{1,0:T(8,128)(2,1)}, u32[]{:S(2)}, u32[]{:S(2)}) collective-permute-start(bf16[96,512]{1,0:T(8,128)(2,1)} %get-tuple-element.78.refs_0_), channel_id=1, source_target_pairs={{0,16},{1,2},{2,1},{3,19},{4,20},{5,6},{6,5},{7,23},{8,24},{9,10},... | collective-permute-start | bytes 294920 | tf_op jit(solution)/shard_map/ppermute | solution.py:170
  348.7 7.9 %collective-permute-start.48 = (bf16[96,512]{1,0:T(8,128)(2,1)}, bf16[96,512]{1,0:T(8,128)(2,1)}, u32[]{:S(2)}, u32[]{:S(2)}) collective-permute-start(bf16[96,512]{1,0:T(8,128)(2,1)} %get-tuple-element.78.refs_0_), channel_id=1, source_target_pairs={{0,16},{1,6},{2,5},{3,19},{4,20},{5,2},{6,1},{7,23},{8,24},{9,14},... | collective-permute-start | bytes 294920 | tf_op jit(solution)/shard_map/ppermute | solution.py:170
  363.8 7.3 %collective-permute-start.49 = (bf16[96,2048]{1,0:T(8,128)(2,1)S(1)}, bf16[96,2048]{1,0:T(8,128)(2,1)S(1)}, u32[]{:S(2)}, u32[]{:S(2)}) collective-permute-start(bf16[96,2048]{1,0:T(8,128)(2,1)S(1)} %get-tuple-element.81), channel_id=1, source_target_pairs={{0,8},{1,9},{2,10},{3,11},{4,12},{5,13},{6,14},{7,15},{8,16},{9,17... | collective-permute-start | bytes 1179656 | tf_op jit(solution)/shard_map/ppermute | solution.py:170
  363.9 11.4 %collective-permute-start.50 = (bf16[96,2048]{1,0:T(8,128)(2,1)S(1)}, bf16[96,2048]{1,0:T(8,128)(2,1)S(1)}, u32[]{:S(2)}, u32[]{:S(2)}) collective-permute-start(bf16[96,2048]{1,0:T(8,128)(2,1)S(1)} %get-tuple-element.81), channel_id=1, source_target_pairs={{0,12},{1,13},{2,14},{3,15},{4,8},{5,9},{6,10},{7,11},{8,20},{9,21... | collective-permute-start | bytes 1179656 | tf_op jit(solution)/shard_map/ppermute | solution.py:170
  382.6 5.7 %collective-permute-start.51 = (bf16[96,512]{1,0:T(8,128)(2,1)S(1)}, bf16[96,512]{1,0:T(8,128)(2,1)S(1)}, u32[]{:S(2)}, u32[]{:S(2)}) collective-permute-start(bf16[96,512]{1,0:T(8,128)(2,1)S(1)} %get-tuple-element.82.refs_0_), channel_id=1, source_target_pairs={{0,16},{1,5},{2,6},{3,19},{4,20},{5,1},{6,2},{7,23},{8,24},{9,13},... | collective-permute-start | bytes 294920 | tf_op jit(solution)/shard_map/ppermute | solution.py:170
  384.1 6.3 %collective-permute-start.52 = (bf16[96,512]{1,0:T(8,128)(2,1)S(1)}, bf16[96,512]{1,0:T(8,128)(2,1)S(1)}, u32[]{:S(2)}, u32[]{:S(2)}) collective-permute-start(bf16[96,512]{1,0:T(8,128)(2,1)S(1)} %get-tuple-element.82.refs_0_), channel_id=1, source_target_pairs={{0,16},{1,2},{2,1},{3,19},{4,20},{5,6},{6,5},{7,23},{8,24},{9,10},... | collective-permute-start | bytes 294920 | tf_op jit(solution)/shard_map/ppermute | solution.py:170
  384.7 7.3 %collective-permute-start.53 = (bf16[96,512]{1,0:T(8,128)(2,1)S(1)}, bf16[96,512]{1,0:T(8,128)(2,1)S(1)}, u32[]{:S(2)}, u32[]{:S(2)}) collective-permute-start(bf16[96,512]{1,0:T(8,128)(2,1)S(1)} %get-tuple-element.82.refs_0_), channel_id=1, source_target_pairs={{0,16},{1,6},{2,5},{3,19},{4,20},{5,2},{6,1},{7,23},{8,24},{9,14},... | collective-permute-start | bytes 294920 | tf_op jit(solution)/shard_map/ppermute | solution.py:170
  394.2 7.3 %collective-permute-start.54 = (bf16[96,2048]{1,0:T(8,128)(2,1)S(1)}, bf16[96,2048]{1,0:T(8,128)(2,1)S(1)}, u32[]{:S(2)}, u32[]{:S(2)}) collective-permute-start(bf16[96,2048]{1,0:T(8,128)(2,1)S(1)} %get-tuple-element.85), channel_id=1, source_target_pairs={{0,8},{1,9},{2,10},{3,11},{4,12},{5,13},{6,14},{7,15},{8,16},{9,17... | collective-permute-start | bytes 1179656 | tf_op jit(solution)/shard_map/ppermute | solution.py:170
  394.3 11.4 %collective-permute-start.55 = (bf16[96,2048]{1,0:T(8,128)(2,1)S(1)}, bf16[96,2048]{1,0:T(8,128)(2,1)S(1)}, u32[]{:S(2)}, u32[]{:S(2)}) collective-permute-start(bf16[96,2048]{1,0:T(8,128)(2,1)S(1)} %get-tuple-element.85), channel_id=1, source_target_pairs={{0,8},{1,9},{2,10},{3,11},{4,12},{5,13},{6,14},{7,15},{8,20},{9,21... | collective-permute-start | bytes 1179656 | tf_op jit(solution)/shard_map/ppermute | solution.py:170
  409.2 5.8 %collective-permute-start.56 = (bf16[96,512]{1,0:T(8,128)(2,1)S(1)}, bf16[96,512]{1,0:T(8,128)(2,1)S(1)}, u32[]{:S(2)}, u32[]{:S(2)}) collective-permute-start(bf16[96,512]{1,0:T(8,128)(2,1)S(1)} %get-tuple-element.86.refs_0_), channel_id=1, source_target_pairs={{0,16},{1,5},{2,6},{3,19},{4,20},{5,1},{6,2},{7,23},{8,24},{9,13},... | collective-permute-start | bytes 294920 | tf_op jit(solution)/shard_map/ppermute | solution.py:170
  411.5 5.7 %collective-permute-start.57 = (bf16[96,512]{1,0:T(8,128)(2,1)S(1)}, bf16[96,512]{1,0:T(8,128)(2,1)S(1)}, u32[]{:S(2)}, u32[]{:S(2)}) collective-permute-start(bf16[96,512]{1,0:T(8,128)(2,1)S(1)} %get-tuple-element.86.refs_0_), channel_id=1, source_target_pairs={{0,16},{1,2},{2,1},{3,19},{4,20},{5,6},{6,5},{7,23},{8,24},{9,10},... | collective-permute-start | bytes 294920 | tf_op jit(solution)/shard_map/ppermute | solution.py:170
  411.6 7.3 %collective-permute-start.58 = (bf16[96,512]{1,0:T(8,128)(2,1)S(1)}, bf16[96,512]{1,0:T(8,128)(2,1)S(1)}, u32[]{:S(2)}, u32[]{:S(2)}) collective-permute-start(bf16[96,512]{1,0:T(8,128)(2,1)S(1)} %get-tuple-element.86.refs_0_), channel_id=1, source_target_pairs={{0,16},{1,6},{2,5},{3,19},{4,20},{5,2},{6,1},{7,23},{8,24},{9,14},... | collective-permute-start | bytes 294920 | tf_op jit(solution)/shard_map/ppermute | solution.py:170
  426.9 9.0 %collective-permute-start.61 = (bf16[96,512]{1,0:T(8,128)(2,1)S(1)}, bf16[96,512]{1,0:T(8,128)(2,1)S(1)}, u32[]{:S(2)}, u32[]{:S(2)}) collective-permute-start(bf16[96,512]{1,0:T(8,128)(2,1)S(1)} %get-tuple-element.90), channel_id=1, source_target_pairs={{0,16},{1,5},{2,6},{3,19},{4,20},{5,1},{6,2},{7,23},{8,24},{9,13},... | collective-permute-start | bytes 294920 | tf_op jit(solution)/shard_map/ppermute | solution.py:170
  432.8 5.7 %collective-permute-start.62 = (bf16[96,512]{1,0:T(8,128)(2,1)S(1)}, bf16[96,512]{1,0:T(8,128)(2,1)S(1)}, u32[]{:S(2)}, u32[]{:S(2)}) collective-permute-start(bf16[96,512]{1,0:T(8,128)(2,1)S(1)} %get-tuple-element.90), channel_id=1, source_target_pairs={{0,16},{1,2},{2,1},{3,19},{4,20},{5,6},{6,5},{7,23},{8,24},{9,10},... | collective-permute-start | bytes 294920 | tf_op jit(solution)/shard_map/ppermute | solution.py:170
  432.9 7.8 %collective-permute-start.63 = (bf16[96,512]{1,0:T(8,128)(2,1)S(1)}, bf16[96,512]{1,0:T(8,128)(2,1)S(1)}, u32[]{:S(2)}, u32[]{:S(2)}) collective-permute-start(bf16[96,512]{1,0:T(8,128)(2,1)S(1)} %get-tuple-element.90), channel_id=1, source_target_pairs={{0,16},{1,6},{2,5},{3,19},{4,20},{5,2},{6,1},{7,23},{8,24},{9,14},... | collective-permute-start | bytes 294920 | tf_op jit(solution)/shard_map/ppermute | solution.py:170
  443.7 3.7 collective-permute-start.64
  443.8 4.3 collective-permute-start.65
  448.8 4.6 %collective-permute-start.67 = (f32[8,2048]{1,0:T(8,128)S(1)}, f32[8,2048]{1,0:T(8,128)S(1)}, u32[]{:S(2)}, u32[]{:S(2)}) collective-permute-start(f32[8,2048]{1,0:T(8,128)S(1)} %add_add_fusion.1), channel_id=1, source_target_pairs={{1,0},{2,3},{5,4},{6,7},{9,8},{10,11},{13,12},{14,15},{17,16},{18,... | collective-permute-start | bytes 196616 | tf_op jit(solution)/shard_map/ppermute | solution.py:170
  (38 other events, 1236.3 us)
